TPU v7x, 128 devices: a whole 4x4x4 slice. The times are simulated.
128 devices in a mesh: row: 8 (over z_lo, x), col: 16 (over z_hi, y, core).
Axes of the slice: x: 4, y: 4, z: 4 (z_hi: 2, z_lo: 2; z = z_hi * 2 + z_lo), core: 2. Of those that a mesh axis runs over, the one named last changes fastest.
Arguments:
- inputs: bfloat16 [512, 8192], P(('row', 'col')), may hold values from -36 to 36
- rms_gain_vector: float32 [8192], replicated, may hold values from 0.1 to 1.9
- gate_weight: bfloat16 [8192, 28672], P('row', 'col'), may hold values from -0.0625 to 0.0625
- up_weight: bfloat16 [8192, 28672], P('row', 'col'), may hold values from -0.0625 to 0.0625
- down_weight: bfloat16 [28672, 8192], P('col', 'row'), may hold values from -0.03125 to 0.03125
- out_grad: bfloat16 [512, 8192], P(('row', 'col')), may hold values from -6 to 6
Outputs:
- outputs: bfloat16 [512, 8192], P(('row', 'col'))
- input_gradient: bfloat16 [512, 8192], P(('row', 'col'))
- norm_gain_gradient: float32 [8192], replicated
- gate_weight_grad: bfloat16 [8192, 28672], P('row', 'col')
- up_weight_grad: bfloat16 [8192, 28672], P('row', 'col')
- down_weight_grad: bfloat16 [28672, 8192], P('col', 'row')
All inputs are finite; a program needn't handle non-finite values.
Results may differ from a plain program's by a relative error of at most 0.0067.
Values may be sent and summed in bfloat16 or wider, within the bound.
No kernel may reach another device: no remote copies, remote signals or barrier semaphores. Data moves between devices by JAX's collectives and lax.ppermute only.
A program may use at most 128 MiB of HBM per device.

v0:
```python
import jax
import jax.numpy as jnp
from jax import lax
from jax.sharding import PartitionSpec as P

EPS = 1e-05


def product(left, right):
    return jnp.dot(left, right, preferred_element_type=jnp.float32)


def product_right_t(left, right):
    return lax.dot_general(
        left, right, (((1,), (1,)), ((), ())), preferred_element_type=jnp.float32
    )


def product_left_t(left, right):
    return lax.dot_general(
        left, right, (((0,), (0,)), ((), ())), preferred_element_type=jnp.float32
    )


def swiglu_grads(gate, up, hidden_grad):
    sigma = jax.nn.sigmoid(gate)
    gate_grad = (hidden_grad * up * sigma * (1.0 + gate * (1.0 - sigma))).astype(jnp.bfloat16)
    up_grad = (hidden_grad * jax.nn.silu(gate)).astype(jnp.bfloat16)
    return (gate_grad, up_grad)


def per_device(inputs, rms_gain_vector, gate_weight, up_weight, down_weight, out_grad):
    width = gate_weight.shape[1]
    value_entries = inputs.astype(jnp.float32)
    inverse_root_mean_square = lax.rsqrt(
        jnp.mean(value_entries * value_entries, axis=1, keepdims=True) + EPS
    )
    normalized_estimate = value_entries * inverse_root_mean_square
    normalized_input = (normalized_estimate * rms_gain_vector).astype(jnp.bfloat16)
    grouped = (
        lax.all_gather(normalized_input, "col", axis=0, tiled=True),
        lax.all_gather(out_grad, "col", axis=0, tiled=True),
    )
    normed_full, grad_full = (
        lax.all_to_all(grouped[0], "row", split_axis=1, concat_axis=0, tiled=True),
        lax.all_to_all(grouped[1], "row", split_axis=1, concat_axis=0, tiled=True),
    )
    block = normed_full
    sums = lax.psum_scatter(
        jnp.concatenate([product(block, gate_weight), product(block, up_weight)], axis=1),
        "row",
        scatter_dimension=0,
        tiled=True,
    )
    gate = sums[:, :width]
    up = sums[:, width:]
    hidden_rows = (jax.nn.silu(gate) * up).astype(jnp.bfloat16)
    hidden_full = lax.all_gather(hidden_rows, "row", axis=0, tiled=True)
    moved = lax.all_to_all(
        product(hidden_full, down_weight), "row", split_axis=0, concat_axis=1, tiled=True
    )
    outputs = lax.psum_scatter(moved, "col", scatter_dimension=0, tiled=True).astype(jnp.bfloat16)
    down_weight_grad = product_left_t(hidden_full, grad_full).astype(jnp.bfloat16)
    block = grad_full
    hidden_grad = lax.psum_scatter(
        product_right_t(block, down_weight), "row", scatter_dimension=0, tiled=True
    )
    gate_rows, up_rows = swiglu_grads(gate, up, hidden_grad)
    gate_grad, up_grad = (
        lax.all_gather(gate_rows, "row", axis=0, tiled=True),
        lax.all_gather(up_rows, "row", axis=0, tiled=True),
    )
    gate_weight_grad = product_left_t(normed_full, gate_grad).astype(jnp.bfloat16)
    up_weight_grad = product_left_t(normed_full, up_grad).astype(jnp.bfloat16)
    partial_grad = product_right_t(gate_grad, gate_weight) + product_right_t(up_grad, up_weight)
    moved_grad = lax.all_to_all(partial_grad, "row", split_axis=0, concat_axis=1, tiled=True)
    normalized_gradient = lax.psum_scatter(moved_grad, "col", scatter_dimension=0, tiled=True)
    norm_gain_gradient = lax.psum(
        jnp.sum(normalized_gradient * normalized_estimate, axis=0), ("row", "col")
    )
    gain_scaled_input = normalized_gradient * rms_gain_vector
    input_gradient = inverse_root_mean_square * (
        gain_scaled_input
        - normalized_estimate
        * jnp.mean(gain_scaled_input * normalized_estimate, axis=1, keepdims=True)
    )
    return (
        outputs,
        input_gradient.astype(jnp.bfloat16),
        norm_gain_gradient,
        gate_weight_grad,
        up_weight_grad,
        down_weight_grad,
    )


def solution(mesh):
    in_specs = (
        P(("row", "col"), None),
        P(),
        P("row", "col"),
        P("row", "col"),
        P("col", "row"),
        P(("row", "col"), None),
    )
    out_specs = (
        P(("row", "col"), None),
        P(("row", "col"), None),
        P(),
        P("row", "col"),
        P("row", "col"),
        P("col", "row"),
    )
    return jax.shard_map(
        per_device, mesh=mesh, in_specs=in_specs, out_specs=out_specs, check_vma=False
    )
```

profile of v0, /device:TPU:0, one launch (start us, length us, event | category | flops | bytes accessed | tf_op | source)
XLA Modules:
  0.0 639.4 jit_solution(7226502155000512526)
XLA Ops:
  7.2 0.7 all-gather.16.cloned.1.call-update
  7.9 1.0 fusion.11
  9.0 1.6 fusion.12
  10.6 0.0 reduce-scatter.5.cloned.1.call-start
  10.6 47.5 %all-gather.16.cloned.1.call-done = bf16[16,4,8192]{2,1,0:T(4,128)(2,1)} async-done(((bf16[1,4,8192]{2,1,0:T(4,128)(2,1)}), bf16[16,4,8192]{2,1,0:T(4,128)(2,1)}) %all-gather.16.cloned.1.call-update) | async-done | bytes 1048592 | tf_op jit(solution)/shard_map/all_gather | solution.py:42
  58.1 1.8 all_to_all.64
  59.9 0.6 copy.22
  60.5 20.4 %all_to_all.76 = bf16[64,8,1024]{2,0,1:T(8,128)(2,1)S(1)} all-to-all(bf16[64,8,1024]{2,0,1:T(8,128)(2,1)S(1)} %copy.22), channel_id=1, replica_groups=mesh['row'=8,'col'=16] {'row'}, dimensions={1} | all-to-all | bytes 2097152 | tf_op jit(solution)/shard_map/all_to_all | solution.py:46
  80.9 3.9 fusion.16
  84.9 0.0 reduce-scatter.3.cloned.1.call-start
  84.9 23.9 %all-gather.14.cloned.1.call-done = bf16[16,4,8192]{2,1,0:T(4,128)(2,1)} async-done(((bf16[1,4,8192]{2,1,0:T(4,128)(2,1)}), bf16[16,4,8192]{2,1,0:T(4,128)(2,1)}) %all-gather.14.cloned.1.call-update) | async-done | bytes 1048592 | tf_op jit(solution)/shard_map/all_gather | solution.py:41
  108.9 1.8 all_to_all.56
  110.7 0.6 copy.20
  111.3 28.0 %all_to_all.77 = bf16[64,8,1024]{2,0,1:T(8,128)(2,1)S(1)} all-to-all(bf16[64,8,1024]{2,0,1:T(8,128)(2,1)S(1)} %copy.20), channel_id=1, replica_groups=mesh['row'=8,'col'=16] {'row'}, dimensions={1} | all-to-all | bytes 2097152 | tf_op jit(solution)/shard_map/all_to_all | solution.py:45
  139.3 2.1 fusion.13
  141.4 0.3 copy-done.5
  141.7 2.1 fusion.14
  143.8 4.0 pad_maximum_fusion
  147.9 0.0 all-gather.10.cloned.1.call-start
  147.9 19.3 %reduce-scatter.5.cloned.1.call-done = f32[64,1792]{1,0:T(8,128)} async-done(((f32[512,1792]{1,0:T(8,128)}), f32[64,1792]{1,0:T(8,128)}) %reduce-scatter.5.cloned.1.call-update) | async-done | bytes 458768 | tf_op jit(solution)/shard_map/reduce_scatter | solution.py:65
  167.2 82.3 %reduce-scatter.3.cloned.1.call-done = f32[64,3584]{1,0:T(8,128)} async-done(((f32[512,3584]{1,0:T(8,128)}), f32[64,3584]{1,0:T(8,128)}) %reduce-scatter.3.cloned.1.call-update) | async-done | bytes 917520 | tf_op jit(solution)/shard_map/reduce_scatter | solution.py:49
  249.4 2.3 multiply_convert_fusion
  251.8 0.0 all-gather.12.cloned.1.call-start
  251.9 0.5 all-gather.12.cloned.1.call-update
  252.4 0.0 all-gather.8.cloned.1.call-start
  252.4 0.7 all-gather.8.cloned.1.call-update
  253.1 38.6 %all-gather.10.cloned.1.call-done = bf16[512,1792]{1,0:T(8,128)(2,1)} async-done(((bf16[64,1792]{1,0:T(8,128)(2,1)}), bf16[512,1792]{1,0:T(8,128)(2,1)}) %all-gather.10.cloned.1.call-update) | async-done | bytes 1835024 | tf_op jit(solution)/shard_map/all_gather | solution.py:70
  291.7 4.7 fusion.17
  296.4 37.5 %all-gather.12.cloned.1.call-done = bf16[512,1792]{1,0:T(8,128)(2,1)} async-done(((bf16[64,1792]{1,0:T(8,128)(2,1)}), bf16[512,1792]{1,0:T(8,128)(2,1)}) %all-gather.12.cloned.1.call-update) | async-done | bytes 1835024 | tf_op jit(solution)/shard_map/all_gather | solution.py:71
  333.9 6.0 convolution_add_fusion
  339.9 3.8 all-to-all-start.3
  343.7 44.2 %all-gather.8.cloned.1.call-done = bf16[512,1792]{1,0:T(8,128)(2,1)} async-done(((bf16[64,1792]{1,0:T(8,128)(2,1)}), bf16[512,1792]{1,0:T(8,128)(2,1)}) %all-gather.8.cloned.1.call-update) | async-done | bytes 1835024 | tf_op jit(solution)/shard_map/all_gather | solution.py:58
  387.9 6.0 fusion.15
  393.8 4.5 all-to-all-start.1
  398.3 0.0 all-reduce.5.cloned.1.call-start
  398.4 0.6 dynamic-slice
  399.6 5.9 convolution_convert_fusion.1
  405.6 4.0 convolution_convert_fusion.2
  409.5 4.0 convolution_convert_fusion
  413.5 1.5 copy.25
  415.0 8.8 %all-to-all-done.1 = f32[8,64,1024]{2,1,0:T(8,128)} async-done(((f32[8,64,1024]{2,1,0:T(8,128)}), f32[8,64,1024]{2,1,0:T(8,128)}, u32[]{:S(2)}, u32[]{:S(2)}) %all-to-all-start.1) | async-done | bytes 2097184 | tf_op jit(solution)/shard_map/all_to_all | solution.py:59
  423.8 1.8 copy.24
  425.5 84.2 %all-reduce.6 = bf16[64,8192]{1,0:T(8,128)(2,1)S(1)} all-reduce(f32[64,8192]{1,0:T(8,128)S(1)} %bitcast.38), channel_id=3, replica_groups=mesh['row'=8,'col'=16] {'col'}, use_global_device_ids=true, to_apply=%region_2.3.clone | all-reduce | flops 524288 | bytes 3145728
  509.7 0.7 dynamic-slice_convert_fusion
  510.4 52.4 %all-reduce.5.cloned.1.call-done = f32[64,8192]{1,0:T(8,128)} async-done(((f32[64,8192]{1,0:T(8,128)}), f32[64,8192]{1,0:T(8,128)}) %all-reduce.5.cloned.1.call-update) | async-done | bytes 2097168
  562.8 1.3 fusion.10
  564.0 66.8 %psum.7 = f32[8192]{0:T(1024)} all-reduce(f32[8192]{0:T(1024)S(1)} %get-tuple-element.6), channel_id=1, replica_groups=mesh['row'=8,'col'=16] {'row','col'}, use_global_device_ids=true, to_apply=%region_7.8 | all-reduce | flops 8192 | bytes 65536 | tf_op jit(solution)/shard_map/psum | solution.py:78
  630.9 1.7 fusion.9
  (29 shorter events, 0.2 us)
Async XLA Ops:
  7.2 50.9 %all-gather.16.cloned.1.call-start = ((), (), s32[]{:S(2)}) async-start(), calls=%async_computation.12 | async-start | bytes 1114112 | tf_op jit(solution)/shard_map/all_gather | solution.py:42
  7.9 101.0 %all-gather.14.cloned.1.call-start = ((), (), s32[]{:S(2)}) async-start(), calls=%async_computation.11 | async-start | bytes 1114112 | tf_op jit(solution)/shard_map/all_gather | solution.py:41
  10.6 156.6 %reduce-scatter.5.cloned.1.call-start = ((), (), s32[]{:S(2)}) async-start(), calls=%async_computation.8 | async-start | bytes 4128768 | tf_op jit(solution)/shard_map/reduce_scatter | solution.py:65
  59.9 21.0 %copy-start.6 = (bf16[1792,1024]{1,0:T(8,128)(2,1)S(1)}, bf16[1792,1024]{1,0:T(8,128)(2,1)}, u32[]{:S(2)}) copy-start(bf16[1792,1024]{1,0:T(8,128)(2,1)} %param.10) | copy-start | bytes 11010052
  84.9 164.5 %reduce-scatter.3.cloned.1.call-start = ((), (), s32[]{:S(2)}) async-start(), calls=%async_computation.6 | async-start | bytes 8257536 | tf_op jit(solution)/shard_map/reduce_scatter | solution.py:49
  110.7 28.6 %copy-start.4 = (bf16[1024,1792]{1,0:T(8,128)(2,1)S(1)}, bf16[1024,1792]{1,0:T(8,128)(2,1)}, u32[]{:S(2)}) copy-start(bf16[1024,1792]{1,0:T(8,128)(2,1)} %param.8) | copy-start | bytes 11010052
  139.3 2.1 copy-start
  139.3 2.4 copy-start.5
  147.9 143.8 %all-gather.10.cloned.1.call-start = ((), (), s32[]{:S(2)}) async-start(), calls=%async_computation.9 | async-start | bytes 2064384 | tf_op jit(solution)/shard_map/all_gather | solution.py:70
  251.8 82.1 %all-gather.12.cloned.1.call-start = ((), (), s32[]{:S(2)}) async-start(), calls=%async_computation.10 | async-start | bytes 2064384 | tf_op jit(solution)/shard_map/all_gather | solution.py:71
  252.4 135.5 %all-gather.8.cloned.1.call-start = ((), (), s32[]{:S(2)}) async-start(), calls=%async_computation.7 | async-start | bytes 2064384 | tf_op jit(solution)/shard_map/all_gather | solution.py:58
  339.9 54.0 %all-to-all-start.3 = ((f32[8,64,1024]{2,1,0:T(8,128)}), f32[8,64,1024]{2,1,0:T(8,128)S(1)}, u32[]{:S(2)}, u32[]{:S(2)}) async-start(f32[8,64,1024]{2,1,0:T(8,128)} %bitcast.40), calls=%async_computation.5 | async-start | bytes 4194304 | tf_op jit(solution)/shard_map/all_to_all | solution.py:76
  393.8 4.5 copy-start.9
  393.8 29.9 %all-to-all-start.1 = ((f32[8,64,1024]{2,1,0:T(8,128)}), f32[8,64,1024]{2,1,0:T(8,128)}, u32[]{:S(2)}, u32[]{:S(2)}) async-start(f32[8,64,1024]{2,1,0:T(8,128)} %bitcast.39), calls=%async_computation.2 | async-start | bytes 4194304 | tf_op jit(solution)/shard_map/all_to_all | solution.py:59
  398.3 164.4 %all-reduce.5.cloned.1.call-start = ((), (), s32[]{:S(2)}) async-start(), calls=%async_computation.13 | async-start | bytes 4194304
  399.6 5.9 copy-start.1
  399.6 5.9 copy-start.7
  405.6 4.0 copy-start.8
  423.8 139.0 %copy-start.2 = (bf16[4,8192]{1,0:T(4,128)(2,1)S(1)}, bf16[4,8192]{1,0:T(4,128)(2,1)}, u32[]{:S(2)}) copy-start(bf16[4,8192]{1,0:T(4,128)(2,1)} %param.6) | copy-start | bytes 196612
  423.8 139.0 %copy-start.3 = (f32[8192]{0:T(1024)S(1)}, f32[8192]{0:T(1024)}, u32[]{:S(2)}) copy-start(f32[8192]{0:T(1024)} %param.7) | copy-start | bytes 98308
Sparse Core Ops, SparseCore 0:
  10.4 47.6 all-gather.15
  61.1 47.7 all-gather.13
  111.9 55.2 reduce-scatter.4
  169.4 79.9 reduce-scatter.2
  251.9 39.7 all-gather.9
  293.8 40.0 all-gather.11
  335.5 52.2 all-gather.7
  415.1 147.5 all-reduce.4
where the time goes:
time: 641 us; the launch traced here: 639 us
  waiting for transfers between devices  356 us (56%)
  blocking collectives  199 us (31%)
  matrix products  38.6 us (6%)
  between operations  14.9 us (2%)
  other arithmetic  11.9 us (2%)
  local copies, waits for them, and re-layouts  9.68 us (2%)
  starting transfers between devices  8.58 us (1%)
    unnamed x1, blocking collectives  84.2 us
    reduce_scatter x1, waiting for transfers between devices, per_device(): lax.psum_scatter(jnp.concatenate([product(block, gate_weight), product(bl...  82.3 us
    psum x1, blocking collectives, per_device(): lax.psum(jnp.sum(normalized_gradient * normalized_estimate, axis=0), ('ro...  66.8 us
    unnamed x9, waiting for transfers between devices  54.4 us
    all_gather x1, waiting for transfers between devices, per_device(): lax.all_gather(out_grad, 'col', axis=0, tiled=True)  47.5 us
    all_gather x1, waiting for transfers between devices, per_device(): hidden_full = lax.all_gather(hidden_rows, 'row', axis=0, tiled=True)  44.2 us
    all_gather x1, waiting for transfers between devices, per_device(): lax.all_gather(gate_rows, 'row', axis=0, tiled=True)  38.6 us
    all_gather x1, waiting for transfers between devices, per_device(): lax.all_gather(up_rows, 'row', axis=0, tiled=True)  37.5 us
  transfers between devices with their start and end apart: 10, of which 9 were waited for; matrix products, arithmetic and copies ran while one was open for 8% of the time, Pallas kernels for 0%

commit v1 on v0

v1 whole, which is shorter than its diff:
```python
import jax
import jax.numpy as jnp
from jax import lax
from jax.sharding import PartitionSpec as P

EPS = 1e-05
F32 = jnp.float32
BF16 = jnp.bfloat16
ZS, XS, HS, YS, CS = 2, 4, 2, 4, 2


def row_shift(dz, dx):
    return [
        (z * XS + x, (z + dz) % ZS * XS + (x + dx) % XS)
        for z in range(ZS)
        for x in range(XS)
    ]


def col_shift(dh, dy, dc):
    return [
        ((h * YS + y) * CS + c, ((h + dh) % HS * YS + (y + dy) % YS) * CS + (c + dc) % CS)
        for h in range(HS)
        for y in range(YS)
        for c in range(CS)
    ]


def to_row(value, dz, dx):
    return lax.ppermute(value, "row", row_shift(dz, dx))


def to_col(value, dh, dy, dc):
    return lax.ppermute(value, "col", col_shift(dh, dy, dc))


def product(left, right):
    return jnp.dot(left, right, preferred_element_type=F32)


def product_right_t(left, right):
    return lax.dot_general(left, right, (((1,), (1,)), ((), ())), preferred_element_type=F32)


def product_left_t(left, right):
    return lax.dot_general(left, right, (((0,), (0,)), ((), ())), preferred_element_type=F32)


def rounded(value):
    return lax.reduce_precision(value, 8, 7)


def parts_of(value, count):
    parts = []
    for _ in range(count):
        top = rounded(value)
        parts.append(top.astype(BF16))
        value = value - top
    return parts


def gather_tokens(block, x, z):
    n = block.shape[1]
    both = {0: block, 1: to_col(block, 1, 0, 0)}
    pair = jnp.concatenate([both[0], both[1]], axis=0)
    got = {0: pair}
    for dy in (1, 3, 2):
        got[(-dy) % YS] = to_col(pair, 0, dy, 0)
    own = jnp.zeros((256, n), BF16)
    for dy in range(YS):
        for dh in range(HS):
            slot = (dh * 2 + dy // 2 - x) % XS
            own = lax.dynamic_update_slice(
                own, got[dy][dh * 32 : dh * 32 + 32], (slot * 64 + dy % 2 * 32, 0)
            )
    other = to_col(own, 0, 0, 1)
    full = jnp.zeros((512, n), BF16)
    full = lax.dynamic_update_slice(full, own, (z * 256, 0))
    return lax.dynamic_update_slice(full, other, ((1 - z) * 256, 0))


def sum_over_row(near, far):
    m12 = to_row(far[2].astype(BF16), 1, 0).astype(F32)
    m11 = to_row(far[1].astype(BF16), 0, 1).astype(F32)
    m13 = to_row(far[3].astype(BF16), 0, 3).astype(F32)
    a02 = near[2] + m12
    h = a02.shape[0] // 2
    n1 = to_row(a02[:h].astype(BF16), 0, 1).astype(F32)
    n2 = to_row(a02[h:].astype(BF16), 0, 3).astype(F32)
    q = to_row((far[0] + m11 + m13).astype(BF16), 1, 0).astype(F32)
    a01 = jnp.concatenate([near[1][:h] + n1, near[1][h:]], axis=0)
    a03 = jnp.concatenate([near[3][:h], near[3][h:] + n2], axis=0)
    r1 = to_row(a01.astype(BF16), 0, 1).astype(F32)
    r2 = to_row(a03.astype(BF16), 0, 3).astype(F32)
    return near[0] + q + r1 + r2


def gather_over_row(own):
    h = own.shape[0] // 2
    a = to_row(own, 0, 1)
    b = to_row(own, 0, 3)
    p = to_row(own, 1, 0)
    a2 = to_row(a[:h], 0, 1)
    b2 = to_row(b[h:], 0, 3)
    pa = to_row(p, 0, 1)
    pb = to_row(p, 0, 3)
    across = jnp.concatenate([a2, b2], axis=0)
    p2 = to_row(across, 1, 0)
    return jnp.concatenate([own, b, across, a, p, pb, p2, pa], axis=0)


def sum_over_col(partial, gain_partial, x, z):
    keep = lax.dynamic_slice(partial, (z * 256, 0), (256, 2048))
    give = lax.dynamic_slice(partial, ((1 - z) * 256, 0), (256, 2048))
    give = jnp.concatenate([give, jnp.pad(gain_partial, ((0, 0), (0, 2048 - 128)))], axis=0)
    taken = to_col(give, 0, 0, 1)
    keep = keep + taken[:256]
    gain_partial = gain_partial + taken[256:, :128]
    gain_parts = jnp.concatenate(parts_of(gain_partial, 2) + [jnp.zeros((16, 128), BF16)], axis=0)

    def piece(dh, dy):
        slot = (dh * 2 + dy // 2 - x) % XS
        return lax.dynamic_slice(keep, (slot * 64 + dy % 2 * 32, 0), (32, 2048))

    def gain_of(parts):
        return parts[:8].astype(F32) + parts[8:16].astype(F32)

    total = piece(0, 0)
    gains = {(0, 0): gain_of(gain_parts)}
    for dh, dy in ((0, 1), (0, 3), (1, 0), (0, 2), (1, 1), (1, 3), (1, 2)):
        message = jnp.concatenate([piece(dh, dy).astype(BF16), gain_parts], axis=1)
        got = to_col(message, dh, dy, 0)
        total = total + got[:, :2048].astype(F32)
        gains[dh, dy] = gain_of(got[:, 2048:])
    over_y = [
        (gains[dh, 0] + gains[dh, 2]) + (gains[dh, 1] + gains[dh, 3]) for dh in range(HS)
    ]
    return total, over_y[0] + over_y[1]


def per_device(inputs, rms_gain_vector, gate_weight, up_weight, down_weight, out_grad):
    row = lax.axis_index("row")
    z, x = row // XS, row % XS
    width = gate_weight.shape[1]

    value_entries = inputs.astype(F32)
    inverse_rms = lax.rsqrt(jnp.mean(value_entries * value_entries, axis=1, keepdims=True) + EPS)
    side = jnp.concatenate(parts_of(inverse_rms, 3) + [jnp.zeros((4, 125), BF16)], axis=1)
    message = jnp.concatenate(
        [
            inputs.reshape(4, 8, 1024),
            out_grad.reshape(4, 8, 1024),
            jnp.broadcast_to(side[:, None, :], (4, 8, 128)),
        ],
        axis=2,
    )
    block = lax.all_to_all(message, "row", split_axis=1, concat_axis=0, tiled=True)
    tokens = gather_tokens(block.reshape(32, 2176), x, z)

    inverse_full = (
        tokens[:, 2048:2049].astype(F32)
        + tokens[:, 2049:2050].astype(F32)
        + tokens[:, 2050:2051].astype(F32)
    )
    gain_block = lax.dynamic_slice(rms_gain_vector, (row * 1024,), (1024,))
    estimate = tokens[:, :1024].astype(F32) * inverse_full
    normed = (estimate * gain_block).astype(BF16)
    grad_full = tokens[:, 1024:2048]

    def partials(rows):
        return jnp.concatenate(
            [
                product(normed[rows], gate_weight),
                product(normed[rows], up_weight),
                product_right_t(grad_full[rows], down_weight),
            ],
            axis=1,
        )

    far = partials(slice(256, 512)).reshape(4, 64, 3 * width)
    near = partials(slice(0, 256)).reshape(4, 64, 3 * width)
    sums = sum_over_row(near, far)
    gate, up, hidden_grad = sums[:, :width], sums[:, width : 2 * width], sums[:, 2 * width :]
    sigma = jax.nn.sigmoid(gate)
    silu = gate * sigma
    units = jnp.concatenate(
        [
            (silu * up).astype(BF16),
            (hidden_grad * up * sigma * (1.0 + gate * (1.0 - sigma))).astype(BF16),
            (hidden_grad * silu).astype(BF16),
        ],
        axis=1,
    )
    units = gather_over_row(units)
    hidden, gate_grad, up_grad = units[:, :width], units[:, width : 2 * width], units[:, 2 * width :]

    partial_out = product(hidden, down_weight)
    partial_grad = product_right_t(gate_grad, gate_weight) + product_right_t(up_grad, up_weight)
    gain_partial = jnp.sum(partial_grad * estimate, axis=0).reshape(8, 128)
    total, gain_total = sum_over_col(
        jnp.concatenate([partial_out, partial_grad], axis=1), gain_partial, x, z
    )
    down_weight_grad = product_left_t(hidden, grad_full).astype(BF16)
    gate_weight_grad = product_left_t(normed, gate_grad).astype(BF16)
    up_weight_grad = product_left_t(normed, up_grad).astype(BF16)

    grad_parts = parts_of(total[:, 1024:], 2)
    gain_parts = jnp.concatenate([p.reshape(4, 256) for p in parts_of(gain_total, 2)], axis=1)
    message = jnp.concatenate(
        [
            total[:, :1024].astype(BF16).reshape(8, 4, 1024),
            grad_parts[0].reshape(8, 4, 1024),
            grad_parts[1].reshape(8, 4, 1024),
            jnp.broadcast_to(gain_parts[None], (8, 4, 512)),
        ],
        axis=2,
    )
    back = lax.all_to_all(message, "row", split_axis=0, concat_axis=0, tiled=True)
    outputs = jnp.transpose(back[:, :, :1024], (1, 0, 2)).reshape(4, 8192)
    normed_grad = back[:, :, 1024:2048].astype(F32) + back[:, :, 2048:3072].astype(F32)
    normed_grad = jnp.transpose(normed_grad, (1, 0, 2)).reshape(4, 8192)
    gain_grad = back[:, :, 3072:3328].astype(F32) + back[:, :, 3328:].astype(F32)

    normalized = value_entries * inverse_rms
    scaled = normed_grad * rms_gain_vector
    input_gradient = inverse_rms * (
        scaled - normalized * jnp.mean(scaled * normalized, axis=1, keepdims=True)
    )
    return (
        outputs,
        input_gradient.astype(BF16),
        gain_grad.reshape(8192),
        gate_weight_grad,
        up_weight_grad,
        down_weight_grad,
    )


def solution(mesh):
    in_specs = (
        P(("row", "col"), None),
        P(),
        P("row", "col"),
        P("row", "col"),
        P("col", "row"),
        P(("row", "col"), None),
    )
    out_specs = (
        P(("row", "col"), None),
        P(("row", "col"), None),
        P(),
        P("row", "col"),
        P("row", "col"),
        P("col", "row"),
    )
    return jax.shard_map(
        per_device, mesh=mesh, in_specs=in_specs, out_specs=out_specs, check_vma=False
    )
```

time: 641 us -> 195 us (0.30)
  waiting for transfers between devices: 356 us -> 95.1 us
  blocking collectives: 199 us -> 0 us
  starting transfers between devices: 8.58 us -> 51.3 us
  between operations: 14.9 us -> 1.24 us
  matrix products: 38.6 us -> 28.8 us
    all_gather x5 -> x0, waiting for transfers between devices: 192 us -> none  [the longest x1 47.5 us: per_device(): lax.all_gather(out_grad, 'col', axis=0, tiled=True)]
    reduce_scatter x2 -> x0, waiting for transfers between devices: 102 us -> none  [the longest x1 82.3 us: per_device(): lax.psum_scatter(jnp.concatenate([product(block, gate_weight), product(bl...]
    ppermute x0 -> x29, waiting for transfers between devices: none -> 86.9 us  [the longest x16 66.6 us: to_row(): return lax.ppermute(value, 'row', row_shift(dz, dx))]
    unnamed x1 -> x0, blocking collectives: 84.2 us -> none
    psum x1 -> x0, blocking collectives: 66.8 us -> none  [per_device(): lax.psum(jnp.sum(normalized_gradient * normalized_estimate, axis=0), ('ro...]
    unnamed x9 -> x0, waiting for transfers between devices: 54.4 us -> none
    all_to_all x2 -> x0, blocking collectives: 48.4 us -> none  [the longest x1 28 us: per_device(): lax.all_to_all(grouped[0], 'row', split_axis=1, concat_axis=0, tiled=True)]
    ppermute x0 -> x29, starting transfers between devices: none -> 40.9 us  [the longest x13 22.4 us: to_col(): return lax.ppermute(value, 'col', col_shift(dh, dy, dc))]
  transfers between devices with their start and end apart: 10 -> 31, of which waited for: 9 -> 19; matrix products, arithmetic and copies ran while one was open for 8% -> 8% of each run, Pallas kernels for 0% -> 0%
where the time goes in v1:
time: 195 us; the launch traced here: 194 us
  waiting for transfers between devices  95.1 us (49%)
  starting transfers between devices  51.3 us (26%)
  matrix products  28.8 us (15%)
  local copies, waits for them, and re-layouts  9.01 us (5%)
  other arithmetic  8.55 us (4%)
    ppermute x16, waiting for transfers between devices, to_row(): return lax.ppermute(value, 'row', row_shift(dz, dx))  66.6 us
    ppermute x13, starting transfers between devices, to_col(): return lax.ppermute(value, 'col', col_shift(dh, dy, dc))  22.4 us
    ppermute x13, waiting for transfers between devices, to_col(): return lax.ppermute(value, 'col', col_shift(dh, dy, dc))  20.3 us
    ppermute x16, starting transfers between devices, to_row(): return lax.ppermute(value, 'row', row_shift(dz, dx))  18.4 us
    dot_general x3, matrix products, product_left_t(): lax.dot_general(left, right, (((0,), (0,)), ((), ())), preferred_element_...  13.4 us
    dot_general x5, matrix products, product(): return jnp.dot(left, right, preferred_element_type=F32)  8.8 us
    all_to_all x1, waiting for transfers between devices, per_device(): lax.all_to_all(message, 'row', split_axis=1, concat_axis=0, tiled=True)  6.63 us
    dot_general x4, matrix products, product_right_t(): lax.dot_general(left, right, (((1,), (1,)), ((), ())), preferred_element_...  6.58 us
  transfers between devices with their start and end apart: 31, of which 19 were waited for; matrix products, arithmetic and copies ran while one was open for 8% of the time, Pallas kernels for 0%

profile of v1, /device:TPU:0, one launch (start us, length us, event | category | flops | bytes accessed | tf_op | source)
XLA Modules:
  0.0 194.0 jit_solution(15920953365786672578)
XLA Ops:
  0.6 1.0 fusion.42
  2.2 1.6 pad_maximum_fusion.7
  3.8 5.7 %all-to-all-start = ((bf16[4,8,2176]{2,0,1:T(4,128)(2,1)}), bf16[4,8,2176]{2,0,1:T(4,128)(2,1)S(1)}, u32[]{:S(2)}, u32[]{:S(2)}) async-start(bf16[4,8,2176]{2,0,1:T(4,128)(2,1)} %pad_maximum_fusion.7), calls=%async_computation | async-start | bytes 278528 | tf_op jit(solution)/shard_map/all_to_all | solution.py:157
  9.5 6.6 %all-to-all-done = bf16[4,8,2176]{2,0,1:T(4,128)(2,1)S(1)} async-done(((bf16[4,8,2176]{2,0,1:T(4,128)(2,1)}), bf16[4,8,2176]{2,0,1:T(4,128)(2,1)S(1)}, u32[]{:S(2)}, u32[]{:S(2)}) %all-to-all-start) | async-done | bytes 139296 | tf_op jit(solution)/shard_map/all_to_all | solution.py:157
  16.2 3.7 %collective-permute-start = (bf16[32,2176]{1,0:T(8,128)(2,1)S(1)}, bf16[32,2176]{1,0:T(8,128)(2,1)S(1)}, u32[]{:S(2)}, u32[]{:S(2)}) collective-permute-start(bf16[32,2176]{1,0:T(8,128)(2,1)S(1)} %reshape.142), channel_id=1, source_target_pairs={{0,8},{1,9},{2,10},{3,11},{4,12},{5,13},{6,14},{7,15},{8,0},{9,1},... | collective-permute-start | bytes 417800 | tf_op jit(solution)/shard_map/ppermute | solution.py:34
  19.9 2.9 %collective-permute-done = bf16[32,2176]{1,0:T(8,128)(2,1)S(1)} collective-permute-done((bf16[32,2176]{1,0:T(8,128)(2,1)S(1)}, bf16[32,2176]{1,0:T(8,128)(2,1)S(1)}, u32[]{:S(2)}, u32[]{:S(2)}) %collective-permute-start) | collective-permute-done | bytes 139296 | tf_op jit(solution)/shard_map/ppermute | solution.py:34
  22.9 3.1 %collective-permute-start.1 = (bf16[64,2176]{1,0:T(8,128)(2,1)S(1)}, bf16[64,2176]{1,0:T(8,128)(2,1)S(1)}, u32[]{:S(2)}, u32[]{:S(2)}) collective-permute-start(bf16[64,2176]{1,0:T(8,128)(2,1)S(1)} %get-tuple-element.35), channel_id=1, source_target_pairs={{0,6},{1,7},{2,0},{3,1},{4,2},{5,3},{6,4},{7,5},{8,14},{9,15},{10,... | collective-permute-start | bytes 835592 | tf_op jit(solution)/shard_map/ppermute | solution.py:34
  26.6 1.0 collective-permute-start.3
  27.6 8.0 %collective-permute-done.1 = bf16[64,2176]{1,0:T(8,128)(2,1)S(1)} collective-permute-done((bf16[64,2176]{1,0:T(8,128)(2,1)S(1)}, bf16[64,2176]{1,0:T(8,128)(2,1)S(1)}, u32[]{:S(2)}, u32[]{:S(2)}) %collective-permute-start.1) | collective-permute-done | bytes 278560 | tf_op jit(solution)/shard_map/ppermute | solution.py:34
  36.4 2.8 %collective-permute-done.3 = bf16[64,2176]{1,0:T(8,128)(2,1)S(1)} collective-permute-done((bf16[64,2176]{1,0:T(8,128)(2,1)S(1)}, bf16[64,2176]{1,0:T(8,128)(2,1)S(1)}, u32[]{:S(2)}, u32[]{:S(2)}) %collective-permute-start.3) | collective-permute-done | bytes 278560 | tf_op jit(solution)/shard_map/ppermute | solution.py:34
  39.8 2.4 %collective-permute-done.4 = bf16[256,2176]{1,0:T(8,128)(2,1)S(1)} collective-permute-done((bf16[256,2176]{1,0:T(8,128)(2,1)S(1)}, bf16[256,2176]{1,0:T(8,128)(2,1)S(1)}, u32[]{:S(2)}, u32[]{:S(2)}) %collective-permute-start.4) | collective-permute-done | bytes 1114144 | tf_op jit(solution)/shard_map/ppermute | solution.py:34
  42.9 1.1 fusion.27
  44.9 1.1 fusion.29
  46.1 0.9 copy-done.5
  47.0 1.1 fusion.23
  48.8 3.3 %fusion.31 = f32[256,1792]{1,0:T(8,128)S(1)} fusion(bf16[1024,1792]{1,0:T(8,128)(2,1)} %param.9, bf16[512,1024]{1,0:T(8,128)(2,1)S(1)} %multiply_convert_fusion), kind=kOutput, calls=%fused_computation.52 | convolution fusion | flops 939524096 | bytes 6029312 | tf_op jit(solution)/shard_map/dot_general | solution.py:38
  52.1 1.1 fusion.33
  54.1 1.2 fusion.25
  55.3 1.2 fusion.53
  57.4 2.4 %collective-permute-start.6 = (bf16[64,5376]{1,0:T(8,128)(2,1)S(1)}, bf16[64,5376]{1,0:T(8,128)(2,1)S(1)}, u32[]{:S(2)}, u32[]{:S(2)}) collective-permute-start(bf16[64,5376]{1,0:T(8,128)(2,1)S(1)} %get-tuple-element.14), channel_id=1, source_target_pairs={{0,48},{16,0},{32,16},{48,32},{64,112},{80,64},{96,80},{112,96},{1... | collective-permute-start | bytes 2064392 | tf_op jit(solution)/shard_map/ppermute | solution.py:30
  60.7 16.5 %collective-permute-done.8 = bf16[64,5376]{1,0:T(8,128)(2,1)S(1)} collective-permute-done((bf16[64,5376]{1,0:T(8,128)(2,1)}, bf16[64,5376]{1,0:T(8,128)(2,1)S(1)}, u32[]{:S(2)}, u32[]{:S(2)}) %collective-permute-start.8) | collective-permute-done | bytes 688160 | tf_op jit(solution)/shard_map/ppermute | solution.py:30
  78.0 1.7 collective-permute-start.9
  80.4 6.0 %collective-permute-done.11 = bf16[32,5376]{1,0:T(8,128)(2,1)S(1)} collective-permute-done((bf16[32,5376]{1,0:T(8,128)(2,1)S(1)}, bf16[32,5376]{1,0:T(8,128)(2,1)S(1)}, u32[]{:S(2)}, u32[]{:S(2)}) %collective-permute-start.11) | collective-permute-done | bytes 344096 | tf_op jit(solution)/shard_map/ppermute | solution.py:30
  86.4 1.5 collective-permute-done.9
  88.4 3.0 %collective-permute-start.12 = (bf16[64,5376]{1,0:T(8,128)(2,1)S(1)}, bf16[64,5376]{1,0:T(8,128)(2,1)S(1)}, u32[]{:S(2)}, u32[]{:S(2)}) collective-permute-start(bf16[64,5376]{1,0:T(8,128)(2,1)S(1)} %pad_maximum_fusion.3), channel_id=1, source_target_pairs={{0,48},{16,0},{32,16},{48,32},{64,112},{80,64},{96,80},{112,96},{1... | collective-permute-start | bytes 2064392 | tf_op jit(solution)/shard_map/ppermute | solution.py:30
  91.5 4.1 %collective-permute-done.7 = bf16[64,5376]{1,0:T(8,128)(2,1)S(1)} collective-permute-done((bf16[64,5376]{1,0:T(8,128)(2,1)S(1)}, bf16[64,5376]{1,0:T(8,128)(2,1)S(1)}, u32[]{:S(2)}, u32[]{:S(2)}) %collective-permute-start.7) | collective-permute-done | bytes 688160 | tf_op jit(solution)/shard_map/ppermute | solution.py:30
  95.5 8.9 %collective-permute-done.10 = bf16[64,5376]{1,0:T(8,128)(2,1)S(1)} collective-permute-done((bf16[64,5376]{1,0:T(8,128)(2,1)S(1)}, bf16[64,5376]{1,0:T(8,128)(2,1)S(1)}, u32[]{:S(2)}, u32[]{:S(2)}) %collective-permute-start.10) | collective-permute-done | bytes 688160 | tf_op jit(solution)/shard_map/ppermute | solution.py:30
  105.1 3.2 %collective-permute-start.13 = (bf16[64,5376]{1,0:T(8,128)(2,1)S(1)}, bf16[64,5376]{1,0:T(8,128)(2,1)S(1)}, u32[]{:S(2)}, u32[]{:S(2)}) collective-permute-start(bf16[64,5376]{1,0:T(8,128)(2,1)S(1)} %get-tuple-element.29), channel_id=1, source_target_pairs={{0,48},{16,0},{32,16},{48,32},{64,112},{80,64},{96,80},{112,96},{1... | collective-permute-start | bytes 2064392 | tf_op jit(solution)/shard_map/ppermute | solution.py:30
  108.4 12.2 %collective-permute-done.14 = bf16[64,5376]{1,0:T(8,128)(2,1)S(1)} collective-permute-done((bf16[64,5376]{1,0:T(8,128)(2,1)S(1)}, bf16[64,5376]{1,0:T(8,128)(2,1)S(1)}, u32[]{:S(2)}, u32[]{:S(2)}) %collective-permute-start.14) | collective-permute-done | bytes 688160 | tf_op jit(solution)/shard_map/ppermute | solution.py:30
  120.7 3.3 %collective-permute-start.16 = (bf16[32,5376]{1,0:T(8,128)(2,1)S(1)}, bf16[32,5376]{1,0:T(8,128)(2,1)S(1)}, u32[]{:S(2)}, u32[]{:S(2)}) collective-permute-start(bf16[32,5376]{1,0:T(8,128)(2,1)S(1)} %slice.341), channel_id=1, source_target_pairs={{0,48},{16,0},{32,16},{48,32},{64,112},{80,64},{96,80},{112,96},{1... | collective-permute-start | bytes 1032200 | tf_op jit(solution)/shard_map/ppermute | solution.py:30
  124.0 1.9 collective-permute-start.18
  126.1 6.8 %collective-permute-done.15 = bf16[32,5376]{1,0:T(8,128)(2,1)S(1)} collective-permute-done((bf16[32,5376]{1,0:T(8,128)(2,1)S(1)}, bf16[32,5376]{1,0:T(8,128)(2,1)S(1)}, u32[]{:S(2)}, u32[]{:S(2)}) %collective-permute-start.15) | collective-permute-done | bytes 344096 | tf_op jit(solution)/shard_map/ppermute | solution.py:30
  133.3 8.6 %collective-permute-done.18 = bf16[64,5376]{1,0:T(8,128)(2,1)S(1)} collective-permute-done((bf16[64,5376]{1,0:T(8,128)(2,1)S(1)}, bf16[64,5376]{1,0:T(8,128)(2,1)S(1)}, u32[]{:S(2)}, u32[]{:S(2)}) %collective-permute-start.18) | collective-permute-done | bytes 688160 | tf_op jit(solution)/shard_map/ppermute | solution.py:30
  141.9 2.1 %collective-permute-done.19 = bf16[64,5376]{1,0:T(8,128)(2,1)S(1)} collective-permute-done((bf16[64,5376]{1,0:T(8,128)(2,1)S(1)}, bf16[64,5376]{1,0:T(8,128)(2,1)S(1)}, u32[]{:S(2)}, u32[]{:S(2)}) %collective-permute-start.19) | collective-permute-done | bytes 688160 | tf_op jit(solution)/shard_map/ppermute | solution.py:30
  144.1 2.1 %fusion.4 = f32[512,1024]{1,0:T(8,128)S(1)} fusion(bf16[1024,1792]{1,0:T(8,128)(2,1)S(1)} %copy-done.4, bf16[512,5376]{1,0:T(8,128)(2,1)S(1)} %constant_dynamic-update-slice_fusion.2), kind=kOutput, calls=%fused_computation.18 | convolution fusion | flops 1879048192 | bytes 7602176 | tf_op jit(solution)/shard_map/dot_general | solution.py:42
  146.2 1.9 copy-done.7
  148.1 2.1 %fusion.10 = f32[512,1024]{1,0:T(8,128)S(1)} fusion(bf16[1792,1024]{1,0:T(8,128)(2,1)S(1)} %copy-done.7, bf16[512,5376]{1,0:T(8,128)(2,1)S(1)} %constant_dynamic-update-slice_fusion.2), kind=kOutput, calls=%fused_computation.24 | convolution fusion | flops 1879048192 | bytes 7602176 | tf_op jit(solution)/shard_map/dot_general | solution.py:38
  150.2 2.2 %multiply_reduce_fusion = (f32[1024]{0:T(1024)S(1)}, f32[512,1024]{1,0:T(8,128)S(1)}) fusion(f32[512]{0:T(512)S(1)} %add_reduce_fusion, bf16[512,2176]{1,0:T(8,128)(2,1)S(1)} %constant_dynamic-update-slice_fusion.11, f32[512,1024]{1,0:T(8,128)S(1)} %fusion.4, bf16[1024,1792]{1,0:T(8,128)(2,1)S(1)} %copy-done.10, ...), kind=kOutput, calls=%fused_computation.14 | convolution fusion | flops 1881668608 | bytes 10754048 | tf_op jit(solution)/shard_map/dot_general | solution.py:42
  153.0 4.0 %convolution_convert_fusion.1 = bf16[1024,1792]{1,0:T(8,128)(2,1)} fusion(bf16[512,1024]{1,0:T(8,128)(2,1)S(1)} %multiply_convert_fusion, bf16[512,5376]{1,0:T(8,128)(2,1)S(1)} %constant_dynamic-update-slice_fusion.2), kind=kOutput, calls=%fused_computation.7 | convolution fusion | flops 1880883200 | bytes 6553600 | tf_op jit(solution)/shard_map/dot_general | solution.py:46
  158.5 3.2 %collective-permute-start.24 = (bf16[32,2176]{1,0:T(8,128)(2,1)S(1)}, bf16[32,2176]{1,0:T(8,128)(2,1)S(1)}, u32[]{:S(2)}, u32[]{:S(2)}) collective-permute-start(bf16[32,2176]{1,0:T(8,128)(2,1)S(1)} %get-tuple-element.41), channel_id=1, source_target_pairs={{0,8},{1,9},{2,10},{3,11},{4,12},{5,13},{6,14},{7,15},{8,0},{9,1},... | collective-permute-start | bytes 417800 | tf_op jit(solution)/shard_map/ppermute | solution.py:34
  163.0 2.1 %collective-permute-start.22 = (bf16[32,2176]{1,0:T(8,128)(2,1)S(1)}, bf16[32,2176]{1,0:T(8,128)(2,1)S(1)}, u32[]{:S(2)}, u32[]{:S(2)}) collective-permute-start(bf16[32,2176]{1,0:T(8,128)(2,1)S(1)} %get-tuple-element.43), channel_id=1, source_target_pairs={{0,2},{1,3},{2,4},{3,5},{4,6},{5,7},{6,0},{7,1},{8,10},{9,11},{10,... | collective-permute-start | bytes 417800 | tf_op jit(solution)/shard_map/ppermute | solution.py:34
  165.1 3.9 %collective-permute-start.27 = (bf16[32,2176]{1,0:T(8,128)(2,1)S(1)}, bf16[32,2176]{1,0:T(8,128)(2,1)S(1)}, u32[]{:S(2)}, u32[]{:S(2)}) collective-permute-start(bf16[32,2176]{1,0:T(8,128)(2,1)S(1)} %get-tuple-element.44), channel_id=1, source_target_pairs={{0,14},{1,15},{2,8},{3,9},{4,10},{5,11},{6,12},{7,13},{8,6},{9,7},... | collective-permute-start | bytes 417800 | tf_op jit(solution)/shard_map/ppermute | solution.py:34
  169.0 2.6 %collective-permute-start.28 = (bf16[32,2176]{1,0:T(8,128)(2,1)S(1)}, bf16[32,2176]{1,0:T(8,128)(2,1)S(1)}, u32[]{:S(2)}, u32[]{:S(2)}) collective-permute-start(bf16[32,2176]{1,0:T(8,128)(2,1)S(1)} %get-tuple-element.45), channel_id=1, source_target_pairs={{0,12},{1,13},{2,14},{3,15},{4,8},{5,9},{6,10},{7,11},{8,4},{9,5},... | collective-permute-start | bytes 417800 | tf_op jit(solution)/shard_map/ppermute | solution.py:34
  171.6 3.9 %convolution_convert_fusion = bf16[1792,1024]{1,0:T(8,128)(2,1)} fusion(bf16[512,5376]{1,0:T(8,128)(2,1)S(1)} %constant_dynamic-update-slice_fusion.2, bf16[512,2176]{1,0:T(8,128)(2,1)S(1)} %constant_dynamic-update-slice_fusion.11), kind=kOutput, calls=%fused_computation.6 | convolution fusion | flops 1880883200 | bytes 6553600 | tf_op jit(solution)/shard_map/dot_general | solution.py:46
  175.8 2.8 %collective-permute-done.28 = bf16[32,2176]{1,0:T(8,128)(2,1)S(1)} collective-permute-done((bf16[32,2176]{1,0:T(8,128)(2,1)S(1)}, bf16[32,2176]{1,0:T(8,128)(2,1)S(1)}, u32[]{:S(2)}, u32[]{:S(2)}) %collective-permute-start.28) | collective-permute-done | bytes 139296 | tf_op jit(solution)/shard_map/ppermute | solution.py:34
  179.8 4.7 %all-to-all-start.1 = ((bf16[8,4,3584]{2,1,0:T(4,128)(2,1)}), bf16[8,4,3584]{2,1,0:T(4,128)(2,1)S(1)}, u32[]{:S(2)}, u32[]{:S(2)}) async-start(bf16[8,4,3584]{2,1,0:T(4,128)(2,1)} %pad_maximum_fusion.6), calls=%async_computation.1 | async-start | bytes 458752 | tf_op jit(solution)/shard_map/all_to_all | solution.py:218
  184.5 5.5 %convolution_convert_fusion.2 = bf16[1024,1792]{1,0:T(8,128)(2,1)} fusion(bf16[512,1024]{1,0:T(8,128)(2,1)S(1)} %multiply_convert_fusion, bf16[512,5376]{1,0:T(8,128)(2,1)} %copy-done.2), kind=kOutput, calls=%fused_computation.8 | convolution fusion | flops 1880883200 | bytes 6553600 | tf_op jit(solution)/shard_map/dot_general | solution.py:46
  190.0 1.6 all-to-all-done.1
  (130 shorter events, 18.0 us)
Async XLA Ops:
  3.8 12.4 %all-to-all-start = ((bf16[4,8,2176]{2,0,1:T(4,128)(2,1)}), bf16[4,8,2176]{2,0,1:T(4,128)(2,1)S(1)}, u32[]{:S(2)}, u32[]{:S(2)}) async-start(bf16[4,8,2176]{2,0,1:T(4,128)(2,1)} %pad_maximum_fusion.7), calls=%async_computation | async-start | bytes 278528 | tf_op jit(solution)/shard_map/all_to_all | solution.py:157
  16.2 6.7 %collective-permute-start = (bf16[32,2176]{1,0:T(8,128)(2,1)S(1)}, bf16[32,2176]{1,0:T(8,128)(2,1)S(1)}, u32[]{:S(2)}, u32[]{:S(2)}) collective-permute-start(bf16[32,2176]{1,0:T(8,128)(2,1)S(1)} %reshape.142), channel_id=1, source_target_pairs={{0,8},{1,9},{2,10},{3,11},{4,12},{5,13},{6,14},{7,15},{8,0},{9,1},... | collective-permute-start | bytes 417800 | tf_op jit(solution)/shard_map/ppermute | solution.py:34
  22.9 12.7 %collective-permute-start.1 = (bf16[64,2176]{1,0:T(8,128)(2,1)S(1)}, bf16[64,2176]{1,0:T(8,128)(2,1)S(1)}, u32[]{:S(2)}, u32[]{:S(2)}) collective-permute-start(bf16[64,2176]{1,0:T(8,128)(2,1)S(1)} %get-tuple-element.35), channel_id=1, source_target_pairs={{0,6},{1,7},{2,0},{3,1},{4,2},{5,3},{6,4},{7,5},{8,14},{9,15},{10,... | collective-permute-start | bytes 835592 | tf_op jit(solution)/shard_map/ppermute | solution.py:34
  26.0 10.4 %collective-permute-start.2 = (bf16[64,2176]{1,0:T(8,128)(2,1)S(1)}, bf16[64,2176]{1,0:T(8,128)(2,1)S(1)}, u32[]{:S(2)}, u32[]{:S(2)}) collective-permute-start(bf16[64,2176]{1,0:T(8,128)(2,1)S(1)} %get-tuple-element.35), channel_id=1, source_target_pairs={{0,4},{1,5},{2,6},{3,7},{4,0},{5,1},{6,2},{7,3},{8,12},{9,13},{10,... | collective-permute-start | bytes 835592 | tf_op jit(solution)/shard_map/ppermute | solution.py:34
  26.6 12.7 %collective-permute-start.3 = (bf16[64,2176]{1,0:T(8,128)(2,1)S(1)}, bf16[64,2176]{1,0:T(8,128)(2,1)S(1)}, u32[]{:S(2)}, u32[]{:S(2)}) collective-permute-start(bf16[64,2176]{1,0:T(8,128)(2,1)S(1)} %get-tuple-element.35), channel_id=1, source_target_pairs={{0,2},{1,3},{2,4},{3,5},{4,6},{5,7},{6,0},{7,1},{8,10},{9,11},{10,... | collective-permute-start | bytes 835592 | tf_op jit(solution)/shard_map/ppermute | solution.py:34
  39.3 2.8 %collective-permute-start.4 = (bf16[256,2176]{1,0:T(8,128)(2,1)S(1)}, bf16[256,2176]{1,0:T(8,128)(2,1)S(1)}, u32[]{:S(2)}, u32[]{:S(2)}) collective-permute-start(bf16[256,2176]{1,0:T(8,128)(2,1)S(1)} %slice_dynamic-update-slice_fusion), channel_id=1, source_target_pairs={{0,1},{1,0},{2,3},{3,2},{4,5},{5,4},{6,7},{7,6},{8,9},{9,8},{10,11... | collective-permute-start | bytes 3342344 | tf_op jit(solution)/shard_map/ppermute | solution.py:34
  39.6 2.9 %dynamic-slice-start = ((f32[8192]{0:T(1024)}, s32[]{:T(128)}), f32[1024]{0:T(1024)S(1)}, s32[]{:S(2)}) async-start(f32[8192]{0:T(1024)} %param.7, s32[]{:T(128)} %select_n.110), calls=%async_computation.2 | async-start | bytes 8704 | tf_op jit(solution)/shard_map/dynamic_slice | solution.py:165
  39.8 3.1 %copy-start.3 = (bf16[1024,1792]{1,0:T(8,128)(2,1)S(1)}, bf16[1024,1792]{1,0:T(8,128)(2,1)}, u32[]{:S(2)}) copy-start(bf16[1024,1792]{1,0:T(8,128)(2,1)} %param.9) | copy-start | bytes 11010052
  42.9 2.0 %copy-start.8 = (bf16[1024,1792]{1,0:T(8,128)(2,1)S(1)}, bf16[1024,1792]{1,0:T(8,128)(2,1)}, u32[]{:S(2)}) copy-start(bf16[1024,1792]{1,0:T(8,128)(2,1)} %param.8) | copy-start | bytes 11010052
  44.9 2.0 %copy-start.5 = (bf16[1792,1024]{1,0:T(8,128)(2,1)S(1)}, bf16[1792,1024]{1,0:T(8,128)(2,1)}, u32[]{:S(2)}) copy-start(bf16[1792,1024]{1,0:T(8,128)(2,1)} %param.10) | copy-start | bytes 11010052
  48.8 3.3 %copy-start.9 = (bf16[1024,1792]{1,0:T(8,128)(2,1)S(1)}, bf16[1024,1792]{1,0:T(8,128)(2,1)}, u32[]{:S(2)}) copy-start(bf16[1024,1792]{1,0:T(8,128)(2,1)} %param.8) | copy-start | bytes 11010052
  52.1 2.0 %copy-start.6 = (bf16[1792,1024]{1,0:T(8,128)(2,1)S(1)}, bf16[1792,1024]{1,0:T(8,128)(2,1)}, u32[]{:S(2)}) copy-start(bf16[1792,1024]{1,0:T(8,128)(2,1)} %param.10) | copy-start | bytes 11010052
  56.5 23.2 %collective-permute-start.5 = (bf16[64,5376]{1,0:T(8,128)(2,1)}, bf16[64,5376]{1,0:T(8,128)(2,1)S(1)}, u32[]{:S(2)}, u32[]{:S(2)}) collective-permute-start(bf16[64,5376]{1,0:T(8,128)(2,1)} %get-tuple-element.12), channel_id=1, source_target_pairs={{0,16},{16,32},{32,48},{48,0},{64,80},{80,96},{96,112},{112,64},{1... | collective-permute-start | bytes 2064392 | tf_op jit(solution)/shard_map/ppermute | solution.py:30
  57.4 22.4 %collective-permute-start.6 = (bf16[64,5376]{1,0:T(8,128)(2,1)S(1)}, bf16[64,5376]{1,0:T(8,128)(2,1)S(1)}, u32[]{:S(2)}, u32[]{:S(2)}) collective-permute-start(bf16[64,5376]{1,0:T(8,128)(2,1)S(1)} %get-tuple-element.14), channel_id=1, source_target_pairs={{0,48},{16,0},{32,16},{48,32},{64,112},{80,64},{96,80},{112,96},{1... | collective-permute-start | bytes 2064392 | tf_op jit(solution)/shard_map/ppermute | solution.py:30
  60.1 17.2 %collective-permute-start.8 = (bf16[64,5376]{1,0:T(8,128)(2,1)}, bf16[64,5376]{1,0:T(8,128)(2,1)S(1)}, u32[]{:S(2)}, u32[]{:S(2)}) collective-permute-start(bf16[64,5376]{1,0:T(8,128)(2,1)} %get-tuple-element.13), channel_id=1, source_target_pairs={{0,64},{16,80},{32,96},{48,112},{64,0},{80,16},{96,32},{112,48},{1... | collective-permute-start | bytes 2064392 | tf_op jit(solution)/shard_map/ppermute | solution.py:30
  77.5 8.9 %collective-permute-start.11 = (bf16[32,5376]{1,0:T(8,128)(2,1)S(1)}, bf16[32,5376]{1,0:T(8,128)(2,1)S(1)}, u32[]{:S(2)}, u32[]{:S(2)}) collective-permute-start(bf16[32,5376]{1,0:T(8,128)(2,1)S(1)} %get-tuple-element.32), channel_id=1, source_target_pairs={{0,48},{16,0},{32,16},{48,32},{64,112},{80,64},{96,80},{112,96},{1... | collective-permute-start | bytes 1032200 | tf_op jit(solution)/shard_map/ppermute | solution.py:30
  78.0 9.8 %collective-permute-start.9 = (bf16[32,5376]{1,0:T(8,128)(2,1)S(1)}, bf16[32,5376]{1,0:T(8,128)(2,1)S(1)}, u32[]{:S(2)}, u32[]{:S(2)}) collective-permute-start(bf16[32,5376]{1,0:T(8,128)(2,1)S(1)} %get-tuple-element.31), channel_id=1, source_target_pairs={{0,16},{16,32},{32,48},{48,0},{64,80},{80,96},{96,112},{112,64},{1... | collective-permute-start | bytes 1032200 | tf_op jit(solution)/shard_map/ppermute | solution.py:30
  80.0 15.5 %collective-permute-start.7 = (bf16[64,5376]{1,0:T(8,128)(2,1)S(1)}, bf16[64,5376]{1,0:T(8,128)(2,1)S(1)}, u32[]{:S(2)}, u32[]{:S(2)}) collective-permute-start(bf16[64,5376]{1,0:T(8,128)(2,1)S(1)} %fusion.17), channel_id=1, source_target_pairs={{0,64},{16,80},{32,96},{48,112},{64,0},{80,16},{96,32},{112,48},{1... | collective-permute-start | bytes 2064392 | tf_op jit(solution)/shard_map/ppermute | solution.py:30
  88.0 16.3 %collective-permute-start.10 = (bf16[64,5376]{1,0:T(8,128)(2,1)S(1)}, bf16[64,5376]{1,0:T(8,128)(2,1)S(1)}, u32[]{:S(2)}, u32[]{:S(2)}) collective-permute-start(bf16[64,5376]{1,0:T(8,128)(2,1)S(1)} %pad_maximum_fusion.2), channel_id=1, source_target_pairs={{0,16},{16,32},{32,48},{48,0},{64,80},{80,96},{96,112},{112,64},{1... | collective-permute-start | bytes 2064392 | tf_op jit(solution)/shard_map/ppermute | solution.py:30
  88.4 16.0 %collective-permute-start.12 = (bf16[64,5376]{1,0:T(8,128)(2,1)S(1)}, bf16[64,5376]{1,0:T(8,128)(2,1)S(1)}, u32[]{:S(2)}, u32[]{:S(2)}) collective-permute-start(bf16[64,5376]{1,0:T(8,128)(2,1)S(1)} %pad_maximum_fusion.3), channel_id=1, source_target_pairs={{0,48},{16,0},{32,16},{48,32},{64,112},{80,64},{96,80},{112,96},{1... | collective-permute-start | bytes 2064392 | tf_op jit(solution)/shard_map/ppermute | solution.py:30
  105.0 15.6 %collective-permute-start.14 = (bf16[64,5376]{1,0:T(8,128)(2,1)S(1)}, bf16[64,5376]{1,0:T(8,128)(2,1)S(1)}, u32[]{:S(2)}, u32[]{:S(2)}) collective-permute-start(bf16[64,5376]{1,0:T(8,128)(2,1)S(1)} %get-tuple-element.29), channel_id=1, source_target_pairs={{0,16},{16,32},{32,48},{48,0},{64,80},{80,96},{96,112},{112,64},{1... | collective-permute-start | bytes 2064392 | tf_op jit(solution)/shard_map/ppermute | solution.py:30
  105.1 15.6 %collective-permute-start.13 = (bf16[64,5376]{1,0:T(8,128)(2,1)S(1)}, bf16[64,5376]{1,0:T(8,128)(2,1)S(1)}, u32[]{:S(2)}, u32[]{:S(2)}) collective-permute-start(bf16[64,5376]{1,0:T(8,128)(2,1)S(1)} %get-tuple-element.29), channel_id=1, source_target_pairs={{0,48},{16,0},{32,16},{48,32},{64,112},{80,64},{96,80},{112,96},{1... | collective-permute-start | bytes 2064392 | tf_op jit(solution)/shard_map/ppermute | solution.py:30
  108.3 15.7 %collective-permute-start.17 = (bf16[64,5376]{1,0:T(8,128)(2,1)S(1)}, bf16[64,5376]{1,0:T(8,128)(2,1)S(1)}, u32[]{:S(2)}, u32[]{:S(2)}) collective-permute-start(bf16[64,5376]{1,0:T(8,128)(2,1)S(1)} %get-tuple-element.29), channel_id=1, source_target_pairs={{0,64},{16,80},{32,96},{48,112},{64,0},{80,16},{96,32},{112,48},{1... | collective-permute-start | bytes 2064392 | tf_op jit(solution)/shard_map/ppermute | solution.py:30
  120.6 12.3 %collective-permute-start.15 = (bf16[32,5376]{1,0:T(8,128)(2,1)S(1)}, bf16[32,5376]{1,0:T(8,128)(2,1)S(1)}, u32[]{:S(2)}, u32[]{:S(2)}) collective-permute-start(bf16[32,5376]{1,0:T(8,128)(2,1)S(1)} %slice.340), channel_id=1, source_target_pairs={{0,16},{16,32},{32,48},{48,0},{64,80},{80,96},{96,112},{112,64},{1... | collective-permute-start | bytes 1032200 | tf_op jit(solution)/shard_map/ppermute | solution.py:30
  120.7 12.2 %collective-permute-start.16 = (bf16[32,5376]{1,0:T(8,128)(2,1)S(1)}, bf16[32,5376]{1,0:T(8,128)(2,1)S(1)}, u32[]{:S(2)}, u32[]{:S(2)}) collective-permute-start(bf16[32,5376]{1,0:T(8,128)(2,1)S(1)} %slice.341), channel_id=1, source_target_pairs={{0,48},{16,0},{32,16},{48,32},{64,112},{80,64},{96,80},{112,96},{1... | collective-permute-start | bytes 1032200 | tf_op jit(solution)/shard_map/ppermute | solution.py:30
  124.0 17.8 %collective-permute-start.18 = (bf16[64,5376]{1,0:T(8,128)(2,1)S(1)}, bf16[64,5376]{1,0:T(8,128)(2,1)S(1)}, u32[]{:S(2)}, u32[]{:S(2)}) collective-permute-start(bf16[64,5376]{1,0:T(8,128)(2,1)S(1)} %collective-permute-done.17), channel_id=1, source_target_pairs={{0,48},{16,0},{32,16},{48,32},{64,112},{80,64},{96,80},{112,96},{1... | collective-permute-start | bytes 2064392 | tf_op jit(solution)/shard_map/ppermute | solution.py:30
  125.9 18.1 %collective-permute-start.20 = (bf16[64,5376]{1,0:T(8,128)(2,1)S(1)}, bf16[64,5376]{1,0:T(8,128)(2,1)S(1)}, u32[]{:S(2)}, u32[]{:S(2)}) collective-permute-start(bf16[64,5376]{1,0:T(8,128)(2,1)S(1)} %collective-permute-done.17), channel_id=1, source_target_pairs={{0,16},{16,32},{32,48},{48,0},{64,80},{80,96},{96,112},{112,64},{1... | collective-permute-start | bytes 2064392 | tf_op jit(solution)/shard_map/ppermute | solution.py:30
  133.0 11.0 %collective-permute-start.19 = (bf16[64,5376]{1,0:T(8,128)(2,1)S(1)}, bf16[64,5376]{1,0:T(8,128)(2,1)S(1)}, u32[]{:S(2)}, u32[]{:S(2)}) collective-permute-start(bf16[64,5376]{1,0:T(8,128)(2,1)S(1)} %pad_maximum_fusion.4), channel_id=1, source_target_pairs={{0,64},{16,80},{32,96},{48,112},{64,0},{80,16},{96,32},{112,48},{1... | collective-permute-start | bytes 2064392 | tf_op jit(solution)/shard_map/ppermute | solution.py:30
  133.3 10.8 %copy-start.4 = (bf16[1024,1792]{1,0:T(8,128)(2,1)S(1)}, bf16[1024,1792]{1,0:T(8,128)(2,1)}, u32[]{:S(2)}) copy-start(bf16[1024,1792]{1,0:T(8,128)(2,1)} %param.9) | copy-start | bytes 11010052
  144.1 27.5 %copy-start.2 = (bf16[512,5376]{1,0:T(8,128)(2,1)}, bf16[512,5376]{1,0:T(8,128)(2,1)S(1)}, u32[]{:S(2)}) copy-start(bf16[512,5376]{1,0:T(8,128)(2,1)S(1)} %constant_dynamic-update-slice_fusion.2) | copy-start | bytes 16515076
  144.1 4.0 %copy-start.7 = (bf16[1792,1024]{1,0:T(8,128)(2,1)S(1)}, bf16[1792,1024]{1,0:T(8,128)(2,1)}, u32[]{:S(2)}) copy-start(bf16[1792,1024]{1,0:T(8,128)(2,1)} %param.10) | copy-start | bytes 11010052
  148.1 2.1 %copy-start.10 = (bf16[1024,1792]{1,0:T(8,128)(2,1)S(1)}, bf16[1024,1792]{1,0:T(8,128)(2,1)}, u32[]{:S(2)}) copy-start(bf16[1024,1792]{1,0:T(8,128)(2,1)} %param.8) | copy-start | bytes 11010052
  152.7 4.6 %collective-permute-start.21 = (f32[264,2048]{1,0:T(8,128)S(1)}, f32[264,2048]{1,0:T(8,128)S(1)}, u32[]{:S(2)}, u32[]{:S(2)}) collective-permute-start(f32[264,2048]{1,0:T(8,128)S(1)} %select_maximum_fusion), channel_id=1, source_target_pairs={{0,1},{1,0},{2,3},{3,2},{4,5},{5,4},{6,7},{7,6},{8,9},{9,8},{10,11... | collective-permute-start | bytes 6488072 | tf_op jit(solution)/shard_map/ppermute | solution.py:34
  157.8 7.2 %collective-permute-start.23 = (bf16[32,2176]{1,0:T(8,128)(2,1)S(1)}, bf16[32,2176]{1,0:T(8,128)(2,1)S(1)}, u32[]{:S(2)}, u32[]{:S(2)}) collective-permute-start(bf16[32,2176]{1,0:T(8,128)(2,1)S(1)} %get-tuple-element.40), channel_id=1, source_target_pairs={{0,6},{1,7},{2,0},{3,1},{4,2},{5,3},{6,4},{7,5},{8,14},{9,15},{10,... | collective-permute-start | bytes 417800 | tf_op jit(solution)/shard_map/ppermute | solution.py:34
  158.5 10.4 %collective-permute-start.24 = (bf16[32,2176]{1,0:T(8,128)(2,1)S(1)}, bf16[32,2176]{1,0:T(8,128)(2,1)S(1)}, u32[]{:S(2)}, u32[]{:S(2)}) collective-permute-start(bf16[32,2176]{1,0:T(8,128)(2,1)S(1)} %get-tuple-element.41), channel_id=1, source_target_pairs={{0,8},{1,9},{2,10},{3,11},{4,12},{5,13},{6,14},{7,15},{8,0},{9,1},... | collective-permute-start | bytes 417800 | tf_op jit(solution)/shard_map/ppermute | solution.py:34
  161.7 13.8 %collective-permute-start.25 = (bf16[32,2176]{1,0:T(8,128)(2,1)S(1)}, bf16[32,2176]{1,0:T(8,128)(2,1)S(1)}, u32[]{:S(2)}, u32[]{:S(2)}) collective-permute-start(bf16[32,2176]{1,0:T(8,128)(2,1)S(1)} %get-tuple-element.39), channel_id=1, source_target_pairs={{0,4},{1,5},{2,6},{3,7},{4,0},{5,1},{6,2},{7,3},{8,12},{9,13},{10,... | collective-permute-start | bytes 417800 | tf_op jit(solution)/shard_map/ppermute | solution.py:34
  162.4 13.1 %collective-permute-start.26 = (bf16[32,2176]{1,0:T(8,128)(2,1)S(1)}, bf16[32,2176]{1,0:T(8,128)(2,1)S(1)}, u32[]{:S(2)}, u32[]{:S(2)}) collective-permute-start(bf16[32,2176]{1,0:T(8,128)(2,1)S(1)} %get-tuple-element.42), channel_id=1, source_target_pairs={{0,10},{1,11},{2,12},{3,13},{4,14},{5,15},{6,8},{7,9},{8,2},{9,3},... | collective-permute-start | bytes 417800 | tf_op jit(solution)/shard_map/ppermute | solution.py:34
  163.0 12.8 %collective-permute-start.22 = (bf16[32,2176]{1,0:T(8,128)(2,1)S(1)}, bf16[32,2176]{1,0:T(8,128)(2,1)S(1)}, u32[]{:S(2)}, u32[]{:S(2)}) collective-permute-start(bf16[32,2176]{1,0:T(8,128)(2,1)S(1)} %get-tuple-element.43), channel_id=1, source_target_pairs={{0,2},{1,3},{2,4},{3,5},{4,6},{5,7},{6,0},{7,1},{8,10},{9,11},{10,... | collective-permute-start | bytes 417800 | tf_op jit(solution)/shard_map/ppermute | solution.py:34
  165.1 10.7 %collective-permute-start.27 = (bf16[32,2176]{1,0:T(8,128)(2,1)S(1)}, bf16[32,2176]{1,0:T(8,128)(2,1)S(1)}, u32[]{:S(2)}, u32[]{:S(2)}) collective-permute-start(bf16[32,2176]{1,0:T(8,128)(2,1)S(1)} %get-tuple-element.44), channel_id=1, source_target_pairs={{0,14},{1,15},{2,8},{3,9},{4,10},{5,11},{6,12},{7,13},{8,6},{9,7},... | collective-permute-start | bytes 417800 | tf_op jit(solution)/shard_map/ppermute | solution.py:34
  169.0 9.7 %collective-permute-start.28 = (bf16[32,2176]{1,0:T(8,128)(2,1)S(1)}, bf16[32,2176]{1,0:T(8,128)(2,1)S(1)}, u32[]{:S(2)}, u32[]{:S(2)}) collective-permute-start(bf16[32,2176]{1,0:T(8,128)(2,1)S(1)} %get-tuple-element.45), channel_id=1, source_target_pairs={{0,12},{1,13},{2,14},{3,15},{4,8},{5,9},{6,10},{7,11},{8,4},{9,5},... | collective-permute-start | bytes 417800 | tf_op jit(solution)/shard_map/ppermute | solution.py:34
  179.8 11.8 %all-to-all-start.1 = ((bf16[8,4,3584]{2,1,0:T(4,128)(2,1)}), bf16[8,4,3584]{2,1,0:T(4,128)(2,1)S(1)}, u32[]{:S(2)}, u32[]{:S(2)}) async-start(bf16[8,4,3584]{2,1,0:T(4,128)(2,1)} %pad_maximum_fusion.6), calls=%async_computation.1 | async-start | bytes 458752 | tf_op jit(solution)/shard_map/all_to_all | solution.py:218
  184.5 7.2 %copy-start = (bf16[4,8192]{1,0:T(4,128)(2,1)S(1)}, bf16[4,8192]{1,0:T(4,128)(2,1)}, u32[]{:S(2)}) copy-start(bf16[4,8192]{1,0:T(4,128)(2,1)} %param.6) | copy-start | bytes 196612
  184.5 7.2 %copy-start.1 = (f32[8192]{0:T(1024)S(1)}, f32[8192]{0:T(1024)}, u32[]{:S(2)}) copy-start(f32[8192]{0:T(1024)} %param.7) | copy-start | bytes 98308

commit v2 on v1

v2 whole, which is shorter than its diff:
```python
import jax
import jax.numpy as jnp
from jax import lax
from jax.sharding import PartitionSpec as P

EPS = 1e-05
F32 = jnp.float32
BF16 = jnp.bfloat16
ZS, XS, HS, YS, CS = 2, 4, 2, 4, 2


def send(value, z=0, x=0, h=0, y=0, c=0):
    pairs = []
    for z0 in range(ZS):
        for x0 in range(XS):
            for h0 in range(HS):
                for y0 in range(YS):
                    for c0 in range(CS):
                        source = (((z0 * XS + x0) * HS + h0) * YS + y0) * CS + c0
                        z1, x1, h1 = (z0 + z) % ZS, (x0 + x) % XS, (h0 + h) % HS
                        y1, c1 = (y0 + y) % YS, (c0 + c) % CS
                        pairs.append((source, (((z1 * XS + x1) * HS + h1) * YS + y1) * CS + c1))
    return lax.ppermute(value, ("row", "col"), pairs)


def product(left, right):
    return jnp.dot(left, right, preferred_element_type=F32)


def product_right_t(left, right):
    return lax.dot_general(left, right, (((1,), (1,)), ((), ())), preferred_element_type=F32)


def product_left_t(left, right):
    return lax.dot_general(left, right, (((0,), (0,)), ((), ())), preferred_element_type=F32)


def rounded(value):
    return lax.reduce_precision(value, 8, 7)


def parts_of(value, count):
    parts = []
    for _ in range(count):
        top = rounded(value)
        parts.append(top.astype(BF16))
        value = value - top
    return parts


def gather_tokens(inputs, inverse_rms, out_grad, z, x):
    side = jnp.concatenate(parts_of(inverse_rms, 3) + [jnp.zeros((4, 125), BF16)], axis=1)
    halves = [
        jnp.concatenate(
            [inputs[:, i * 4096 : i * 4096 + 4096], out_grad[:, i * 4096 : i * 4096 + 4096], side],
            axis=1,
        )
        for i in range(ZS)
    ]
    same = jnp.where(z == 0, halves[0], halves[1])
    cross = jnp.where(z == 0, halves[1], halves[0])
    got = [
        [same, send(same, h=1)],
        [send(cross, z=1), send(cross, z=1, h=1)],
    ]
    rows = jnp.concatenate([got[0][0], got[0][1], got[1][0], got[1][1]], axis=0)
    blocks = jnp.stack(
        [
            jnp.concatenate(
                [
                    rows[:, i * 1024 : i * 1024 + 1024],
                    rows[:, 4096 + i * 1024 : 5120 + i * 1024],
                    rows[:, 8192:],
                ],
                axis=1,
            )
            for i in range(XS)
        ]
    )

    def block_for(dx):
        return lax.dynamic_index_in_dim(blocks, (x + dx) % XS, 0, keepdims=False)

    over_x = {0: block_for(0)}
    for dx in (1, 3, 2):
        over_x[-dx % XS] = send(block_for(dx), x=dx)
    own = jnp.concatenate([over_x[i][s : s + 8] for s in (0, 8) for i in range(XS)], axis=0)
    over_y = {0: own}
    for dy in (1, 3, 2):
        over_y[-dy % YS] = send(own, y=dy)
    core = jnp.stack([over_y[i].reshape(8, 8, -1) for i in range(YS)], axis=1)
    core = core.reshape(256, -1)
    other = send(core, c=1)
    both = jnp.stack([core.reshape(8, 32, -1), other.reshape(8, 32, -1)], axis=1)
    return both.reshape(512, -1)


def sum_over_row(near, far):
    m12 = send(far[2].astype(BF16), z=1).astype(F32)
    m11 = send(far[1].astype(BF16), x=1).astype(F32)
    m13 = send(far[3].astype(BF16), x=3).astype(F32)
    a02 = near[2] + m12
    h = a02.shape[0] // 2
    n1 = send(a02[:h].astype(BF16), x=1).astype(F32)
    n2 = send(a02[h:].astype(BF16), x=3).astype(F32)
    q = send((far[0] + m11 + m13).astype(BF16), z=1).astype(F32)
    a01 = jnp.concatenate([near[1][:h] + n1, near[1][h:]], axis=0)
    a03 = jnp.concatenate([near[3][:h], near[3][h:] + n2], axis=0)
    r1 = send(a01.astype(BF16), x=1).astype(F32)
    r2 = send(a03.astype(BF16), x=3).astype(F32)
    return near[0] + q + r1 + r2


def gather_over_row(own):
    h = own.shape[0] // 2
    a = send(own, x=1)
    b = send(own, x=3)
    p = send(own, z=1)
    a2 = send(a[:h], x=1)
    b2 = send(b[h:], x=3)
    pa = send(p, x=1)
    pb = send(p, x=3)
    across = jnp.concatenate([a2, b2], axis=0)
    p2 = send(across, z=1)
    return (
        jnp.concatenate([own, b, across, a], axis=0),
        jnp.concatenate([p, pb, p2, pa], axis=0),
    )


def sum_to_owners(partial, gain_partial):
    side = jnp.pad(gain_partial, ((0, 248), (0, 0)))
    split = partial.reshape(8, 2, 32, 2048)
    message = jnp.concatenate([split[:, 1].reshape(256, 2048), side], axis=1)
    taken = send(message, c=1)
    keep = split[:, 0].reshape(256, 2048) + taken[:, :2048]
    gain = gain_partial + taken[:8, 2048:]
    gain_parts = jnp.concatenate(parts_of(gain, 2) + [jnp.zeros((48, 128), BF16)], axis=0)

    def gain_of(parts):
        return parts[:8].astype(F32) + parts[8:16].astype(F32)

    over_y = keep.reshape(8, 4, 8, 2048)
    total = over_y[:, 0].reshape(64, 2048)
    gains = {0: gain_of(gain_parts)}
    for dy in (1, 3, 2):
        message = over_y[:, dy].reshape(64, 2048).astype(BF16)
        got = send(jnp.concatenate([message, gain_parts], axis=1), y=dy)
        total = total + got[:, :2048].astype(F32)
        gains[dy] = gain_of(got[:, 2048:])
    gain = (gains[0] + gains[2]) + (gains[1] + gains[3])

    over_z = total.reshape(2, 4, 2, 4, 2048)
    side = jnp.pad(gain, ((0, 8), (0, 0)))

    def message_for(dz, dh):
        return jnp.concatenate([over_z[dz, :, dh].reshape(16, 2048), side], axis=1)

    sums = []
    for dz in range(ZS):
        mine = message_for(dz, 0)
        if dz:
            mine = send(mine, z=dz)
        sums.append(mine + send(message_for(dz, 1), z=dz, h=1))

    def last(total):
        grad = parts_of(total[:, 1024:2048], 2)
        return jnp.concatenate([total[:, :1024].astype(BF16), grad[0], grad[1]], axis=1)

    def gain_rows(total):
        return jnp.concatenate([p.reshape(4, 256) for p in parts_of(total[:8, 2048:], 2)], axis=1)

    ready = [last(total).reshape(4, 4, 3072) for total in sums]
    gains = [gain_rows(total) for total in sums]
    result = {}
    for dx in (0, 1, 3, 2):
        message = jnp.concatenate(
            [jnp.concatenate([ready[dz][dx], gains[dz]], axis=1) for dz in range(ZS)], axis=0
        )
        got = send(message, x=dx) if dx else message
        for dz in range(ZS):
            part = got[dz * 4 : dz * 4 + 4]
            result[dz, -dx % XS] = (
                part[:, :1024],
                part[:, 1024:2048].astype(F32) + part[:, 2048:3072].astype(F32),
                part[:, 3072:3328].astype(F32) + part[:, 3328:].astype(F32),
            )
    return result


def in_order(pieces, z, x):
    first = pieces[0, 0]
    stacked = jnp.zeros((8,) + first.shape, first.dtype)
    for (dz, dx), piece in pieces.items():
        place = (z + dz) % ZS * XS + (x + dx) % XS
        stacked = lax.dynamic_update_slice(stacked, piece[None], (place, 0, 0))
    return stacked


def per_device(inputs, rms_gain_vector, gate_weight, up_weight, down_weight, out_grad):
    row = lax.axis_index("row")
    z, x = row // XS, row % XS
    width = gate_weight.shape[1]

    value_entries = inputs.astype(F32)
    inverse_rms = lax.rsqrt(jnp.mean(value_entries * value_entries, axis=1, keepdims=True) + EPS)
    tokens = gather_tokens(inputs, inverse_rms, out_grad, z, x)
    inverse_full = (
        tokens[:, 2048:2049].astype(F32)
        + tokens[:, 2049:2050].astype(F32)
        + tokens[:, 2050:2051].astype(F32)
    )
    gain_block = lax.dynamic_slice(rms_gain_vector, (row * 1024,), (1024,))
    estimate = tokens[:, :1024].astype(F32) * inverse_full
    normed = (estimate * gain_block).astype(BF16)
    grad_full = tokens[:, 1024:2048]

    def partials(normed, grad):
        return jnp.concatenate(
            [
                product(normed, gate_weight),
                product(normed, up_weight),
                product_right_t(grad, down_weight),
            ],
            axis=1,
        ).reshape(4, 64, 3 * width)

    far = partials(normed[256:], grad_full[256:])
    near = partials(normed[:256], grad_full[:256])
    sums = sum_over_row(near, far)
    gate, up, hidden_grad = sums[:, :width], sums[:, width : 2 * width], sums[:, 2 * width :]
    sigma = jax.nn.sigmoid(gate)
    silu = gate * sigma
    units = jnp.concatenate(
        [
            (silu * up).astype(BF16),
            (hidden_grad * up * sigma * (1.0 + gate * (1.0 - sigma))).astype(BF16),
            (hidden_grad * silu).astype(BF16),
        ],
        axis=1,
    )
    units = gather_over_row(units)

    def back(units):
        hidden, gate_grad, up_grad = units[:, :width], units[:, width : 2 * width], units[:, 2 * width :]
        grad = product_right_t(gate_grad, gate_weight) + product_right_t(up_grad, up_weight)
        return jnp.concatenate([product(hidden, down_weight), grad], axis=1)

    partial = jnp.concatenate([back(units[0]), back(units[1])], axis=0)
    gain_partial = jnp.sum(partial[:, 1024:] * estimate, axis=0).reshape(8, 128)
    result = sum_to_owners(partial, gain_partial)

    units = jnp.concatenate(units, axis=0)
    hidden, gate_grad, up_grad = units[:, :width], units[:, width : 2 * width], units[:, 2 * width :]
    down_weight_grad = product_left_t(hidden, grad_full).astype(BF16)
    gate_weight_grad = product_left_t(normed, gate_grad).astype(BF16)
    up_weight_grad = product_left_t(normed, up_grad).astype(BF16)

    def tokens_of(index):
        stacked = in_order({k: v[index] for k, v in result.items()}, z, x)
        return jnp.transpose(stacked, (1, 0, 2)).reshape(4, 8192)

    outputs = tokens_of(0)
    normed_grad = tokens_of(1)
    gain_grad = in_order({k: v[2] for k, v in result.items()}, z, x).reshape(8192)

    normalized = value_entries * inverse_rms
    scaled = normed_grad * rms_gain_vector
    input_gradient = inverse_rms * (
        scaled - normalized * jnp.mean(scaled * normalized, axis=1, keepdims=True)
    )
    return (
        outputs,
        input_gradient.astype(BF16),
        gain_grad,
        gate_weight_grad,
        up_weight_grad,
        down_weight_grad,
    )


def solution(mesh):
    in_specs = (
        P(("row", "col"), None),
        P(),
        P("row", "col"),
        P("row", "col"),
        P("col", "row"),
        P(("row", "col"), None),
    )
    out_specs = (
        P(("row", "col"), None),
        P(("row", "col"), None),
        P(),
        P("row", "col"),
        P("row", "col"),
        P("col", "row"),
    )
    return jax.shard_map(
        per_device, mesh=mesh, in_specs=in_specs, out_specs=out_specs, check_vma=False
    )
```

time: 195 us -> 213 us (1.092); the launches traced: 194 us -> 209 us
  starting transfers between devices: 51.3 us -> 57.9 us
  local copies, waits for them, and re-layouts: 9.01 us -> 14.6 us
  other arithmetic: 8.55 us -> 12.8 us
  waiting for transfers between devices: 95.1 us -> 90.9 us
    ppermute x29 -> x36, starting transfers between devices: 40.9 us -> 57.9 us  [send(): return lax.ppermute(value, ('row', 'col'), pairs)]
    all_to_all x2 -> x0, starting transfers between devices: 10.4 us -> none  [the longest x1 5.74 us: per_device(): lax.all_to_all(message, 'row', split_axis=1, concat_axis=0, tiled=True)]
    all_to_all x2 -> x0, waiting for transfers between devices: 8.23 us -> none  [the longest x1 6.63 us: per_device(): lax.all_to_all(message, 'row', split_axis=1, concat_axis=0, tiled=True)]
    ppermute x29 -> x36, waiting for transfers between devices: 86.9 us -> 90.9 us  [send(): return lax.ppermute(value, ('row', 'col'), pairs)]
    dot_general x3, matrix products: 13.4 us -> 16.5 us  [product_left_t(): lax.dot_general(left, right, (((0,), (0,)), ((), ())), preferred_element_...]
    another operation x4 -> x13, other arithmetic: 0.83 us -> 2.97 us  [the longest x2 1.8 us: gather_tokens(): jnp.stack([core.reshape(8, 32, -1), other.reshape(8, 32, -1)], axis=1)]
    dot_general x5 -> x6, matrix products: 8.8 us -> 6.8 us  [product(): return jnp.dot(left, right, preferred_element_type=F32)]
    unnamed x31 -> x39, local copies, waits for them, and re-layouts: 5.54 us -> 7.13 us
  transfers between devices with their start and end apart: 31 -> 36, of which waited for: 19 -> 24; matrix products, arithmetic and copies ran while one was open for 8% -> 11% of each run, Pallas kernels for 0% -> 0%
where the time goes in v2:
time: 213 us; the launch traced here: 209 us
  waiting for transfers between devices  90.9 us (43%)
  starting transfers between devices  57.9 us (27%)
  matrix products  30.2 us (14%)
  local copies, waits for them, and re-layouts  14.6 us (7%)
  other arithmetic  12.8 us (6%)
  between operations  2.18 us (1%)
    ppermute x36, waiting for transfers between devices, send(): return lax.ppermute(value, ('row', 'col'), pairs)  90.9 us
    ppermute x36, starting transfers between devices, send(): return lax.ppermute(value, ('row', 'col'), pairs)  57.9 us
    dot_general x3, matrix products, product_left_t(): lax.dot_general(left, right, (((0,), (0,)), ((), ())), preferred_element_...  16.5 us
    unnamed x39, local copies, waits for them, and re-layouts  7.13 us
    dot_general x6, matrix products, product_right_t(): lax.dot_general(left, right, (((1,), (1,)), ((), ())), preferred_element_...  6.94 us
    dot_general x6, matrix products, product(): return jnp.dot(left, right, preferred_element_type=F32)  6.8 us
  transfers between devices with their start and end apart: 36, of which 24 were waited for; matrix products, arithmetic and copies ran while one was open for 11% of the time, Pallas kernels for 0%

profile of v2, /device:TPU:0, one launch (start us, length us, event | category | flops | bytes accessed | tf_op | source)
XLA Modules:
  0.0 208.6 jit_solution(3533990437147750966)
XLA Ops:
  3.2 4.2 %collective-permute-start.2 = (bf16[4,8320]{1,0:T(4,128)(2,1)S(1)}, bf16[4,8320]{1,0:T(4,128)(2,1)S(1)}, u32[]{:S(2)}, u32[]{:S(2)}) collective-permute-start(bf16[4,8320]{1,0:T(4,128)(2,1)S(1)} %get-tuple-element.74), channel_id=1, source_target_pairs={{0,72},{1,73},{2,74},{3,75},{4,76},{5,77},{6,78},{7,79},{8,64},{9,... | collective-permute-start | bytes 199688 | tf_op jit(solution)/shard_map/ppermute | solution.py:23
  7.4 1.6 collective-permute-start
  9.6 2.0 collective-permute-done.1
  11.6 1.5 collective-permute-done
  13.6 1.6 collective-permute-start.5
  15.1 2.7 %collective-permute-start.4 = (bf16[16,2176]{1,0:T(8,128)(2,1)S(1)}, bf16[16,2176]{1,0:T(8,128)(2,1)S(1)}, u32[]{:S(2)}, u32[]{:S(2)}) collective-permute-start(bf16[16,2176]{1,0:T(8,128)(2,1)S(1)} %get-tuple-element.63), channel_id=1, source_target_pairs={{0,32},{1,33},{2,34},{3,35},{4,36},{5,37},{6,38},{7,39},{8,40},{9,... | collective-permute-start | bytes 208904 | tf_op jit(solution)/shard_map/ppermute | solution.py:23
  17.9 1.4 collective-permute-start.3
  19.3 2.9 %collective-permute-done.3 = bf16[16,2176]{1,0:T(8,128)(2,1)S(1)} collective-permute-done((bf16[16,2176]{1,0:T(8,128)(2,1)S(1)}, bf16[16,2176]{1,0:T(8,128)(2,1)S(1)}, u32[]{:S(2)}, u32[]{:S(2)}) %collective-permute-start.3) | collective-permute-done | bytes 69664 | tf_op jit(solution)/shard_map/ppermute | solution.py:23
  22.3 1.6 collective-permute-start.8
  23.9 2.9 %collective-permute-start.7 = (bf16[64,2176]{1,0:T(8,128)(2,1)S(1)}, bf16[64,2176]{1,0:T(8,128)(2,1)S(1)}, u32[]{:S(2)}, u32[]{:S(2)}) collective-permute-start(bf16[64,2176]{1,0:T(8,128)(2,1)S(1)} %constant_dynamic-update-slice_fusion), channel_id=1, source_target_pairs={{0,4},{1,5},{2,6},{3,7},{4,0},{5,1},{6,2},{7,3},{8,12},{9,13},{10,... | collective-permute-start | bytes 835592 | tf_op jit(solution)/shard_map/ppermute | solution.py:23
  26.8 1.3 collective-permute-start.6
  28.2 4.9 %collective-permute-done.8 = bf16[64,2176]{1,0:T(8,128)(2,1)S(1)} collective-permute-done((bf16[64,2176]{1,0:T(8,128)(2,1)S(1)}, bf16[64,2176]{1,0:T(8,128)(2,1)S(1)}, u32[]{:S(2)}, u32[]{:S(2)}) %collective-permute-start.8) | collective-permute-done | bytes 278560 | tf_op jit(solution)/shard_map/ppermute | solution.py:23
  33.1 3.4 %collective-permute-done.7 = bf16[64,2176]{1,0:T(8,128)(2,1)S(1)} collective-permute-done((bf16[64,2176]{1,0:T(8,128)(2,1)S(1)}, bf16[64,2176]{1,0:T(8,128)(2,1)S(1)}, u32[]{:S(2)}, u32[]{:S(2)}) %collective-permute-start.7) | collective-permute-done | bytes 278560 | tf_op jit(solution)/shard_map/ppermute | solution.py:23
  37.0 2.7 %collective-permute-done.9 = bf16[256,2176]{1,0:T(8,128)(2,1)S(1)} collective-permute-done((bf16[256,2176]{1,0:T(8,128)(2,1)S(1)}, bf16[256,2176]{1,0:T(8,128)(2,1)S(1)}, u32[]{:S(2)}, u32[]{:S(2)}) %collective-permute-start.9) | collective-permute-done | bytes 1114144 | tf_op jit(solution)/shard_map/ppermute | solution.py:23
  40.7 1.6 pad_maximum_fusion.2
  54.4 1.5 collective-permute-start.13
  55.9 2.9 %collective-permute-start.11 = (bf16[64,5376]{1,0:T(8,128)(2,1)}, bf16[64,5376]{1,0:T(8,128)(2,1)S(1)}, u32[]{:S(2)}, u32[]{:S(2)}) collective-permute-start(bf16[64,5376]{1,0:T(8,128)(2,1)} %get-tuple-element.24), channel_id=1, source_target_pairs={{0,48},{1,49},{2,50},{3,51},{4,52},{5,53},{6,54},{7,55},{8,56},{9,... | collective-permute-start | bytes 2064392 | tf_op jit(solution)/shard_map/ppermute | solution.py:23
  59.2 12.4 %collective-permute-done.13 = bf16[64,5376]{1,0:T(8,128)(2,1)S(1)} collective-permute-done((bf16[64,5376]{1,0:T(8,128)(2,1)S(1)}, bf16[64,5376]{1,0:T(8,128)(2,1)S(1)}, u32[]{:S(2)}, u32[]{:S(2)}) %collective-permute-start.13) | collective-permute-done | bytes 688160 | tf_op jit(solution)/shard_map/ppermute | solution.py:23
  71.7 1.9 collective-permute-start.14
  73.6 1.4 collective-permute-start.16
  75.3 1.6 collective-permute-start.12
  76.9 5.1 %collective-permute-done.14 = bf16[32,5376]{1,0:T(8,128)(2,1)S(1)} collective-permute-done((bf16[32,5376]{1,0:T(8,128)(2,1)S(1)}, bf16[32,5376]{1,0:T(8,128)(2,1)S(1)}, u32[]{:S(2)}, u32[]{:S(2)}) %collective-permute-start.14) | collective-permute-done | bytes 344096 | tf_op jit(solution)/shard_map/ppermute | solution.py:23
  82.5 2.7 %collective-permute-start.17 = (bf16[64,5376]{1,0:T(8,128)(2,1)S(1)}, bf16[64,5376]{1,0:T(8,128)(2,1)S(1)}, u32[]{:S(2)}, u32[]{:S(2)}) collective-permute-start(bf16[64,5376]{1,0:T(8,128)(2,1)S(1)} %pad_maximum_fusion.5), channel_id=1, source_target_pairs={{0,48},{1,49},{2,50},{3,51},{4,52},{5,53},{6,54},{7,55},{8,56},{9,... | collective-permute-start | bytes 2064392 | tf_op jit(solution)/shard_map/ppermute | solution.py:23
  85.3 5.8 %collective-permute-done.12 = bf16[64,5376]{1,0:T(8,128)(2,1)S(1)} collective-permute-done((bf16[64,5376]{1,0:T(8,128)(2,1)S(1)}, bf16[64,5376]{1,0:T(8,128)(2,1)S(1)}, u32[]{:S(2)}, u32[]{:S(2)}) %collective-permute-start.12) | collective-permute-done | bytes 688160 | tf_op jit(solution)/shard_map/ppermute | solution.py:23
  91.1 6.7 %collective-permute-done.17 = bf16[64,5376]{1,0:T(8,128)(2,1)S(1)} collective-permute-done((bf16[64,5376]{1,0:T(8,128)(2,1)S(1)}, bf16[64,5376]{1,0:T(8,128)(2,1)S(1)}, u32[]{:S(2)}, u32[]{:S(2)}) %collective-permute-start.17) | collective-permute-done | bytes 688160 | tf_op jit(solution)/shard_map/ppermute | solution.py:23
  97.9 3.5 %collective-permute-done.15 = bf16[64,5376]{1,0:T(8,128)(2,1)S(1)} collective-permute-done((bf16[64,5376]{1,0:T(8,128)(2,1)S(1)}, bf16[64,5376]{1,0:T(8,128)(2,1)S(1)}, u32[]{:S(2)}, u32[]{:S(2)}) %collective-permute-start.15) | collective-permute-done | bytes 688160 | tf_op jit(solution)/shard_map/ppermute | solution.py:23
  102.4 3.2 %collective-permute-start.18 = (bf16[64,5376]{1,0:T(8,128)(2,1)S(1)}, bf16[64,5376]{1,0:T(8,128)(2,1)S(1)}, u32[]{:S(2)}, u32[]{:S(2)}) collective-permute-start(bf16[64,5376]{1,0:T(8,128)(2,1)S(1)} %get-tuple-element.51), channel_id=1, source_target_pairs={{0,48},{1,49},{2,50},{3,51},{4,52},{5,53},{6,54},{7,55},{8,56},{9,... | collective-permute-start | bytes 2064392 | tf_op jit(solution)/shard_map/ppermute | solution.py:23
  105.6 1.6 collective-permute-start.22
  107.2 10.7 %collective-permute-done.19 = bf16[64,5376]{1,0:T(8,128)(2,1)S(1)} collective-permute-done((bf16[64,5376]{1,0:T(8,128)(2,1)S(1)}, bf16[64,5376]{1,0:T(8,128)(2,1)S(1)}, u32[]{:S(2)}, u32[]{:S(2)}) %collective-permute-start.19) | collective-permute-done | bytes 688160 | tf_op jit(solution)/shard_map/ppermute | solution.py:23
  118.0 3.3 %collective-permute-start.21 = (bf16[32,5376]{1,0:T(8,128)(2,1)S(1)}, bf16[32,5376]{1,0:T(8,128)(2,1)S(1)}, u32[]{:S(2)}, u32[]{:S(2)}) collective-permute-start(bf16[32,5376]{1,0:T(8,128)(2,1)S(1)} %slice.649), channel_id=1, source_target_pairs={{0,48},{1,49},{2,50},{3,51},{4,52},{5,53},{6,54},{7,55},{8,56},{9,... | collective-permute-start | bytes 1032200 | tf_op jit(solution)/shard_map/ppermute | solution.py:23
  121.3 3.2 %collective-permute-start.23 = (bf16[64,5376]{1,0:T(8,128)(2,1)S(1)}, bf16[64,5376]{1,0:T(8,128)(2,1)S(1)}, u32[]{:S(2)}, u32[]{:S(2)}) collective-permute-start(bf16[64,5376]{1,0:T(8,128)(2,1)S(1)} %collective-permute-done.22), channel_id=1, source_target_pairs={{0,48},{1,49},{2,50},{3,51},{4,52},{5,53},{6,54},{7,55},{8,56},{9,... | collective-permute-start | bytes 2064392 | tf_op jit(solution)/shard_map/ppermute | solution.py:23
  124.6 5.5 %collective-permute-done.20 = bf16[32,5376]{1,0:T(8,128)(2,1)S(1)} collective-permute-done((bf16[32,5376]{1,0:T(8,128)(2,1)S(1)}, bf16[32,5376]{1,0:T(8,128)(2,1)S(1)}, u32[]{:S(2)}, u32[]{:S(2)}) %collective-permute-start.20) | collective-permute-done | bytes 344096 | tf_op jit(solution)/shard_map/ppermute | solution.py:23
  133.6 1.7 collective-permute-start.24
  136.6 2.4 %collective-permute-done.23 = bf16[64,5376]{1,0:T(8,128)(2,1)S(1)} collective-permute-done((bf16[64,5376]{1,0:T(8,128)(2,1)S(1)}, bf16[64,5376]{1,0:T(8,128)(2,1)S(1)}, u32[]{:S(2)}, u32[]{:S(2)}) %collective-permute-start.23) | collective-permute-done | bytes 688160 | tf_op jit(solution)/shard_map/ppermute | solution.py:23
  139.0 5.6 %collective-permute-done.24 = bf16[64,5376]{1,0:T(8,128)(2,1)S(1)} collective-permute-done((bf16[64,5376]{1,0:T(8,128)(2,1)S(1)}, bf16[64,5376]{1,0:T(8,128)(2,1)S(1)}, u32[]{:S(2)}, u32[]{:S(2)}) %collective-permute-start.24) | collective-permute-done | bytes 688160 | tf_op jit(solution)/shard_map/ppermute | solution.py:23
  150.4 1.7 fusion.160
  152.1 1.5 select_maximum_fusion
  153.6 5.6 %convolution_convert_fusion = bf16[1792,1024]{1,0:T(8,128)(2,1)} fusion(bf16[512,5376]{1,0:T(8,128)(2,1)} %copy-done.4, bf16[512,2176]{1,0:T(8,128)(2,1)S(1)} %bitcast.136), kind=kOutput, calls=%fused_computation.3 | convolution fusion | flops 1880883200 | bytes 6553600 | tf_op jit(solution)/shard_map/dot_general | solution.py:35
  159.2 1.8 slice_add_fusion
  162.0 3.0 %collective-permute-start.29 = (bf16[64,2176]{1,0:T(8,128)(2,1)S(1)}, bf16[64,2176]{1,0:T(8,128)(2,1)S(1)}, u32[]{:S(2)}, u32[]{:S(2)}) collective-permute-start(bf16[64,2176]{1,0:T(8,128)(2,1)S(1)} %get-tuple-element.91), channel_id=1, source_target_pairs={{0,4},{1,5},{2,6},{3,7},{4,0},{5,1},{6,2},{7,3},{8,12},{9,13},{10,... | collective-permute-start | bytes 835592 | tf_op jit(solution)/shard_map/ppermute | solution.py:23
  167.0 5.5 %convolution_convert_fusion.1 = bf16[1024,1792]{1,0:T(8,128)(2,1)} fusion(bf16[512,1024]{1,0:T(8,128)(2,1)S(1)} %multiply_convert_fusion, bf16[512,5376]{1,0:T(8,128)(2,1)} %copy-done.4), kind=kOutput, calls=%fused_computation.4 | convolution fusion | flops 1880883200 | bytes 6553600 | tf_op jit(solution)/shard_map/dot_general | solution.py:35
  173.3 5.1 %collective-permute-done.28 = bf16[64,2176]{1,0:T(8,128)(2,1)S(1)} collective-permute-done((bf16[64,2176]{1,0:T(8,128)(2,1)S(1)}, bf16[64,2176]{1,0:T(8,128)(2,1)S(1)}, u32[]{:S(2)}, u32[]{:S(2)}) %collective-permute-start.28) | collective-permute-done | bytes 278560 | tf_op jit(solution)/shard_map/ppermute | solution.py:23
  179.2 3.0 %collective-permute-start.30 = (f32[16,2176]{1,0:T(8,128)S(1)}, f32[16,2176]{1,0:T(8,128)S(1)}, u32[]{:S(2)}, u32[]{:S(2)}) collective-permute-start(f32[16,2176]{1,0:T(8,128)S(1)} %fusion.46), channel_id=1, source_target_pairs={{0,8},{1,9},{2,10},{3,11},{4,12},{5,13},{6,14},{7,15},{8,0},{9,1},... | collective-permute-start | bytes 417800 | tf_op jit(solution)/shard_map/ppermute | solution.py:23
  182.3 5.5 %convolution_convert_fusion.2 = bf16[1024,1792]{1,0:T(8,128)(2,1)} fusion(bf16[512,1024]{1,0:T(8,128)(2,1)S(1)} %multiply_convert_fusion, bf16[512,5376]{1,0:T(8,128)(2,1)} %copy-done.4), kind=kOutput, calls=%fused_computation.5 | convolution fusion | flops 1880883200 | bytes 6553600 | tf_op jit(solution)/shard_map/dot_general | solution.py:35
  188.0 1.4 collective-permute-start.32
  189.9 4.7 %collective-permute-done.32 = f32[16,2176]{1,0:T(8,128)S(1)} collective-permute-done((f32[16,2176]{1,0:T(8,128)S(1)}, f32[16,2176]{1,0:T(8,128)S(1)}, u32[]{:S(2)}, u32[]{:S(2)}) %collective-permute-start.32) | collective-permute-done | bytes 139296 | tf_op jit(solution)/shard_map/ppermute | solution.py:23
  195.0 4.7 %collective-permute-start.35 = (bf16[8,3584]{1,0:T(8,128)(2,1)S(1)}, bf16[8,3584]{1,0:T(8,128)(2,1)S(1)}, u32[]{:S(2)}, u32[]{:S(2)}) collective-permute-start(bf16[8,3584]{1,0:T(8,128)(2,1)S(1)} %fusion.118), channel_id=1, source_target_pairs={{0,32},{1,33},{2,34},{3,35},{4,36},{5,37},{6,38},{7,39},{8,40},{9,... | collective-permute-start | bytes 172040 | tf_op jit(solution)/shard_map/ppermute | solution.py:23
  201.0 1.5 collective-permute-done.35
  (214 shorter events, 42.3 us)
Async XLA Ops:
  3.2 6.5 %collective-permute-start.2 = (bf16[4,8320]{1,0:T(4,128)(2,1)S(1)}, bf16[4,8320]{1,0:T(4,128)(2,1)S(1)}, u32[]{:S(2)}, u32[]{:S(2)}) collective-permute-start(bf16[4,8320]{1,0:T(4,128)(2,1)S(1)} %get-tuple-element.74), channel_id=1, source_target_pairs={{0,72},{1,73},{2,74},{3,75},{4,76},{5,77},{6,78},{7,79},{8,64},{9,... | collective-permute-start | bytes 199688 | tf_op jit(solution)/shard_map/ppermute | solution.py:23
  7.4 4.3 %collective-permute-start.1 = (bf16[4,8320]{1,0:T(4,128)(2,1)S(1)}, bf16[4,8320]{1,0:T(4,128)(2,1)S(1)}, u32[]{:S(2)}, u32[]{:S(2)}) collective-permute-start(bf16[4,8320]{1,0:T(4,128)(2,1)S(1)} %get-tuple-element.74), channel_id=1, source_target_pairs={{0,64},{1,65},{2,66},{3,67},{4,68},{5,69},{6,70},{7,71},{8,72},{9,... | collective-permute-start | bytes 199688 | tf_op jit(solution)/shard_map/ppermute | solution.py:23
  7.4 5.8 %collective-permute-start = (bf16[4,8320]{1,0:T(4,128)(2,1)S(1)}, bf16[4,8320]{1,0:T(4,128)(2,1)S(1)}, u32[]{:S(2)}, u32[]{:S(2)}) collective-permute-start(bf16[4,8320]{1,0:T(4,128)(2,1)S(1)} %get-tuple-element.73), channel_id=1, source_target_pairs={{0,8},{1,9},{2,10},{3,11},{4,12},{5,13},{6,14},{7,15},{8,0},{9,1},... | collective-permute-start | bytes 199688 | tf_op jit(solution)/shard_map/ppermute | solution.py:23
  13.6 8.6 %collective-permute-start.5 = (bf16[16,2176]{1,0:T(8,128)(2,1)S(1)}, bf16[16,2176]{1,0:T(8,128)(2,1)S(1)}, u32[]{:S(2)}, u32[]{:S(2)}) collective-permute-start(bf16[16,2176]{1,0:T(8,128)(2,1)S(1)} %get-tuple-element.62), channel_id=1, source_target_pairs={{0,16},{1,17},{2,18},{3,19},{4,20},{5,21},{6,22},{7,23},{8,24},{9,... | collective-permute-start | bytes 208904 | tf_op jit(solution)/shard_map/ppermute | solution.py:23
  15.1 7.1 %collective-permute-start.4 = (bf16[16,2176]{1,0:T(8,128)(2,1)S(1)}, bf16[16,2176]{1,0:T(8,128)(2,1)S(1)}, u32[]{:S(2)}, u32[]{:S(2)}) collective-permute-start(bf16[16,2176]{1,0:T(8,128)(2,1)S(1)} %get-tuple-element.63), channel_id=1, source_target_pairs={{0,32},{1,33},{2,34},{3,35},{4,36},{5,37},{6,38},{7,39},{8,40},{9,... | collective-permute-start | bytes 208904 | tf_op jit(solution)/shard_map/ppermute | solution.py:23
  17.9 4.3 %collective-permute-start.3 = (bf16[16,2176]{1,0:T(8,128)(2,1)S(1)}, bf16[16,2176]{1,0:T(8,128)(2,1)S(1)}, u32[]{:S(2)}, u32[]{:S(2)}) collective-permute-start(bf16[16,2176]{1,0:T(8,128)(2,1)S(1)} %get-tuple-element.64), channel_id=1, source_target_pairs={{0,48},{1,49},{2,50},{3,51},{4,52},{5,53},{6,54},{7,55},{8,56},{9,... | collective-permute-start | bytes 208904 | tf_op jit(solution)/shard_map/ppermute | solution.py:23
  22.3 10.8 %collective-permute-start.8 = (bf16[64,2176]{1,0:T(8,128)(2,1)S(1)}, bf16[64,2176]{1,0:T(8,128)(2,1)S(1)}, u32[]{:S(2)}, u32[]{:S(2)}) collective-permute-start(bf16[64,2176]{1,0:T(8,128)(2,1)S(1)} %constant_dynamic-update-slice_fusion), channel_id=1, source_target_pairs={{0,2},{1,3},{2,4},{3,5},{4,6},{5,7},{6,0},{7,1},{8,10},{9,11},{10,... | collective-permute-start | bytes 835592 | tf_op jit(solution)/shard_map/ppermute | solution.py:23
  23.9 12.5 %collective-permute-start.7 = (bf16[64,2176]{1,0:T(8,128)(2,1)S(1)}, bf16[64,2176]{1,0:T(8,128)(2,1)S(1)}, u32[]{:S(2)}, u32[]{:S(2)}) collective-permute-start(bf16[64,2176]{1,0:T(8,128)(2,1)S(1)} %constant_dynamic-update-slice_fusion), channel_id=1, source_target_pairs={{0,4},{1,5},{2,6},{3,7},{4,0},{5,1},{6,2},{7,3},{8,12},{9,13},{10,... | collective-permute-start | bytes 835592 | tf_op jit(solution)/shard_map/ppermute | solution.py:23
  26.8 9.6 %collective-permute-start.6 = (bf16[64,2176]{1,0:T(8,128)(2,1)S(1)}, bf16[64,2176]{1,0:T(8,128)(2,1)S(1)}, u32[]{:S(2)}, u32[]{:S(2)}) collective-permute-start(bf16[64,2176]{1,0:T(8,128)(2,1)S(1)} %constant_dynamic-update-slice_fusion), channel_id=1, source_target_pairs={{0,6},{1,7},{2,0},{3,1},{4,2},{5,3},{6,4},{7,5},{8,14},{9,15},{10,... | collective-permute-start | bytes 835592 | tf_op jit(solution)/shard_map/ppermute | solution.py:23
  36.7 3.0 %collective-permute-start.9 = (bf16[256,2176]{1,0:T(8,128)(2,1)S(1)}, bf16[256,2176]{1,0:T(8,128)(2,1)S(1)}, u32[]{:S(2)}, u32[]{:S(2)}) collective-permute-start(bf16[256,2176]{1,0:T(8,128)(2,1)S(1)} %bitcast.140), channel_id=1, source_target_pairs={{0,1},{1,0},{2,3},{3,2},{4,5},{5,4},{6,7},{7,6},{8,9},{9,8},{10,11... | collective-permute-start | bytes 3342344 | tf_op jit(solution)/shard_map/ppermute | solution.py:23
  36.9 5.6 %dynamic-slice-start = ((f32[8192]{0:T(1024)}, s32[]{:T(128)}), f32[1024]{0:T(1024)S(1)}, s32[]{:S(2)}) async-start(f32[8192]{0:T(1024)} %param.7, s32[]{:T(128)} %select_n.208), calls=%async_computation | async-start | bytes 8704 | tf_op jit(solution)/shard_map/dynamic_slice | solution.py:213
  39.7 1.0 copy-start.1
  40.7 2.4 %copy-start.5 = (bf16[1024,1792]{1,0:T(8,128)(2,1)S(1)}, bf16[1024,1792]{1,0:T(8,128)(2,1)}, u32[]{:S(2)}) copy-start(bf16[1024,1792]{1,0:T(8,128)(2,1)} %param.9) | copy-start | bytes 11010052
  44.2 2.0 copy-start.9
  47.4 2.0 copy-start.7
  54.0 21.0 %collective-permute-start.10 = (bf16[64,5376]{1,0:T(8,128)(2,1)}, bf16[64,5376]{1,0:T(8,128)(2,1)S(1)}, u32[]{:S(2)}, u32[]{:S(2)}) collective-permute-start(bf16[64,5376]{1,0:T(8,128)(2,1)} %get-tuple-element.22), channel_id=1, source_target_pairs={{0,16},{1,17},{2,18},{3,19},{4,20},{5,21},{6,22},{7,23},{8,24},{9,... | collective-permute-start | bytes 2064392 | tf_op jit(solution)/shard_map/ppermute | solution.py:23
  54.4 17.2 %collective-permute-start.13 = (bf16[64,5376]{1,0:T(8,128)(2,1)S(1)}, bf16[64,5376]{1,0:T(8,128)(2,1)S(1)}, u32[]{:S(2)}, u32[]{:S(2)}) collective-permute-start(bf16[64,5376]{1,0:T(8,128)(2,1)S(1)} %get-tuple-element.23), channel_id=1, source_target_pairs={{0,64},{1,65},{2,66},{3,67},{4,68},{5,69},{6,70},{7,71},{8,72},{9,... | collective-permute-start | bytes 2064392 | tf_op jit(solution)/shard_map/ppermute | solution.py:23
  55.9 19.1 %collective-permute-start.11 = (bf16[64,5376]{1,0:T(8,128)(2,1)}, bf16[64,5376]{1,0:T(8,128)(2,1)S(1)}, u32[]{:S(2)}, u32[]{:S(2)}) collective-permute-start(bf16[64,5376]{1,0:T(8,128)(2,1)} %get-tuple-element.24), channel_id=1, source_target_pairs={{0,48},{1,49},{2,50},{3,51},{4,52},{5,53},{6,54},{7,55},{8,56},{9,... | collective-permute-start | bytes 2064392 | tf_op jit(solution)/shard_map/ppermute | solution.py:23
  71.7 10.2 %collective-permute-start.14 = (bf16[32,5376]{1,0:T(8,128)(2,1)S(1)}, bf16[32,5376]{1,0:T(8,128)(2,1)S(1)}, u32[]{:S(2)}, u32[]{:S(2)}) collective-permute-start(bf16[32,5376]{1,0:T(8,128)(2,1)S(1)} %get-tuple-element.52), channel_id=1, source_target_pairs={{0,16},{1,17},{2,18},{3,19},{4,20},{5,21},{6,22},{7,23},{8,24},{9,... | collective-permute-start | bytes 1032200 | tf_op jit(solution)/shard_map/ppermute | solution.py:23
  73.6 8.7 %collective-permute-start.16 = (bf16[32,5376]{1,0:T(8,128)(2,1)S(1)}, bf16[32,5376]{1,0:T(8,128)(2,1)S(1)}, u32[]{:S(2)}, u32[]{:S(2)}) collective-permute-start(bf16[32,5376]{1,0:T(8,128)(2,1)S(1)} %get-tuple-element.53), channel_id=1, source_target_pairs={{0,48},{1,49},{2,50},{3,51},{4,52},{5,53},{6,54},{7,55},{8,56},{9,... | collective-permute-start | bytes 1032200 | tf_op jit(solution)/shard_map/ppermute | solution.py:23
  75.3 15.9 %collective-permute-start.12 = (bf16[64,5376]{1,0:T(8,128)(2,1)S(1)}, bf16[64,5376]{1,0:T(8,128)(2,1)S(1)}, u32[]{:S(2)}, u32[]{:S(2)}) collective-permute-start(bf16[64,5376]{1,0:T(8,128)(2,1)S(1)} %fusion.6), channel_id=1, source_target_pairs={{0,64},{1,65},{2,66},{3,67},{4,68},{5,69},{6,70},{7,71},{8,72},{9,... | collective-permute-start | bytes 2064392 | tf_op jit(solution)/shard_map/ppermute | solution.py:23
  82.5 15.4 %collective-permute-start.17 = (bf16[64,5376]{1,0:T(8,128)(2,1)S(1)}, bf16[64,5376]{1,0:T(8,128)(2,1)S(1)}, u32[]{:S(2)}, u32[]{:S(2)}) collective-permute-start(bf16[64,5376]{1,0:T(8,128)(2,1)S(1)} %pad_maximum_fusion.5), channel_id=1, source_target_pairs={{0,48},{1,49},{2,50},{3,51},{4,52},{5,53},{6,54},{7,55},{8,56},{9,... | collective-permute-start | bytes 2064392 | tf_op jit(solution)/shard_map/ppermute | solution.py:23
  85.3 16.2 %collective-permute-start.15 = (bf16[64,5376]{1,0:T(8,128)(2,1)S(1)}, bf16[64,5376]{1,0:T(8,128)(2,1)S(1)}, u32[]{:S(2)}, u32[]{:S(2)}) collective-permute-start(bf16[64,5376]{1,0:T(8,128)(2,1)S(1)} %pad_maximum_fusion.4), channel_id=1, source_target_pairs={{0,16},{1,17},{2,18},{3,19},{4,20},{5,21},{6,22},{7,23},{8,24},{9,... | collective-permute-start | bytes 2064392 | tf_op jit(solution)/shard_map/ppermute | solution.py:23
  102.1 15.8 %collective-permute-start.19 = (bf16[64,5376]{1,0:T(8,128)(2,1)S(1)}, bf16[64,5376]{1,0:T(8,128)(2,1)S(1)}, u32[]{:S(2)}, u32[]{:S(2)}) collective-permute-start(bf16[64,5376]{1,0:T(8,128)(2,1)S(1)} %get-tuple-element.51), channel_id=1, source_target_pairs={{0,16},{1,17},{2,18},{3,19},{4,20},{5,21},{6,22},{7,23},{8,24},{9,... | collective-permute-start | bytes 2064392 | tf_op jit(solution)/shard_map/ppermute | solution.py:23
  102.4 15.6 %collective-permute-start.18 = (bf16[64,5376]{1,0:T(8,128)(2,1)S(1)}, bf16[64,5376]{1,0:T(8,128)(2,1)S(1)}, u32[]{:S(2)}, u32[]{:S(2)}) collective-permute-start(bf16[64,5376]{1,0:T(8,128)(2,1)S(1)} %get-tuple-element.51), channel_id=1, source_target_pairs={{0,48},{1,49},{2,50},{3,51},{4,52},{5,53},{6,54},{7,55},{8,56},{9,... | collective-permute-start | bytes 2064392 | tf_op jit(solution)/shard_map/ppermute | solution.py:23
  105.6 15.7 %collective-permute-start.22 = (bf16[64,5376]{1,0:T(8,128)(2,1)S(1)}, bf16[64,5376]{1,0:T(8,128)(2,1)S(1)}, u32[]{:S(2)}, u32[]{:S(2)}) collective-permute-start(bf16[64,5376]{1,0:T(8,128)(2,1)S(1)} %get-tuple-element.51), channel_id=1, source_target_pairs={{0,64},{1,65},{2,66},{3,67},{4,68},{5,69},{6,70},{7,71},{8,72},{9,... | collective-permute-start | bytes 2064392 | tf_op jit(solution)/shard_map/ppermute | solution.py:23
  117.9 12.3 %collective-permute-start.20 = (bf16[32,5376]{1,0:T(8,128)(2,1)S(1)}, bf16[32,5376]{1,0:T(8,128)(2,1)S(1)}, u32[]{:S(2)}, u32[]{:S(2)}) collective-permute-start(bf16[32,5376]{1,0:T(8,128)(2,1)S(1)} %slice.648), channel_id=1, source_target_pairs={{0,16},{1,17},{2,18},{3,19},{4,20},{5,21},{6,22},{7,23},{8,24},{9,... | collective-permute-start | bytes 1032200 | tf_op jit(solution)/shard_map/ppermute | solution.py:23
  118.0 12.2 %collective-permute-start.21 = (bf16[32,5376]{1,0:T(8,128)(2,1)S(1)}, bf16[32,5376]{1,0:T(8,128)(2,1)S(1)}, u32[]{:S(2)}, u32[]{:S(2)}) collective-permute-start(bf16[32,5376]{1,0:T(8,128)(2,1)S(1)} %slice.649), channel_id=1, source_target_pairs={{0,48},{1,49},{2,50},{3,51},{4,52},{5,53},{6,54},{7,55},{8,56},{9,... | collective-permute-start | bytes 1032200 | tf_op jit(solution)/shard_map/ppermute | solution.py:23
  121.3 23.4 %collective-permute-start.25 = (bf16[64,5376]{1,0:T(8,128)(2,1)S(1)}, bf16[64,5376]{1,0:T(8,128)(2,1)S(1)}, u32[]{:S(2)}, u32[]{:S(2)}) collective-permute-start(bf16[64,5376]{1,0:T(8,128)(2,1)S(1)} %collective-permute-done.22), channel_id=1, source_target_pairs={{0,16},{1,17},{2,18},{3,19},{4,20},{5,21},{6,22},{7,23},{8,24},{9,... | collective-permute-start | bytes 2064392 | tf_op jit(solution)/shard_map/ppermute | solution.py:23
  121.3 17.6 %collective-permute-start.23 = (bf16[64,5376]{1,0:T(8,128)(2,1)S(1)}, bf16[64,5376]{1,0:T(8,128)(2,1)S(1)}, u32[]{:S(2)}, u32[]{:S(2)}) collective-permute-start(bf16[64,5376]{1,0:T(8,128)(2,1)S(1)} %collective-permute-done.22), channel_id=1, source_target_pairs={{0,48},{1,49},{2,50},{3,51},{4,52},{5,53},{6,54},{7,55},{8,56},{9,... | collective-permute-start | bytes 2064392 | tf_op jit(solution)/shard_map/ppermute | solution.py:23
  124.5 5.8 %copy-start.6 = (bf16[1024,1792]{1,0:T(8,128)(2,1)S(1)}, bf16[1024,1792]{1,0:T(8,128)(2,1)}, u32[]{:S(2)}) copy-start(bf16[1024,1792]{1,0:T(8,128)(2,1)} %param.9) | copy-start | bytes 11010052
  130.4 2.0 copy-start.8
  132.4 2.9 %copy-start.10 = (bf16[1024,1792]{1,0:T(8,128)(2,1)S(1)}, bf16[1024,1792]{1,0:T(8,128)(2,1)}, u32[]{:S(2)}) copy-start(bf16[1024,1792]{1,0:T(8,128)(2,1)} %param.8) | copy-start | bytes 11010052
  133.6 11.0 %collective-permute-start.24 = (bf16[64,5376]{1,0:T(8,128)(2,1)S(1)}, bf16[64,5376]{1,0:T(8,128)(2,1)S(1)}, u32[]{:S(2)}, u32[]{:S(2)}) collective-permute-start(bf16[64,5376]{1,0:T(8,128)(2,1)S(1)} %pad_maximum_fusion.7), channel_id=1, source_target_pairs={{0,64},{1,65},{2,66},{3,67},{4,68},{5,69},{6,70},{7,71},{8,72},{9,... | collective-permute-start | bytes 2064392 | tf_op jit(solution)/shard_map/ppermute | solution.py:23
  144.8 2.4 %copy-start.4 = (bf16[512,5376]{1,0:T(8,128)(2,1)}, bf16[512,5376]{1,0:T(8,128)(2,1)S(1)}, u32[]{:S(2)}) copy-start(bf16[512,5376]{1,0:T(8,128)(2,1)S(1)} %get-tuple-element.37) | copy-start | bytes 16515076
  153.6 5.6 %collective-permute-start.26 = (f32[256,2176]{1,0:T(8,128)}, f32[256,2176]{1,0:T(8,128)}, u32[]{:S(2)}, u32[]{:S(2)}) collective-permute-start(f32[256,2176]{1,0:T(8,128)} %select_maximum_fusion), channel_id=1, source_target_pairs={{0,1},{1,0},{2,3},{3,2},{4,5},{5,4},{6,7},{7,6},{8,9},{9,8},{10,11... | collective-permute-start | bytes 6684680 | tf_op jit(solution)/shard_map/ppermute | solution.py:23
  153.6 5.6 %copy-start = (f32[8,1,32,2048]{3,2,1,0:T(8,128)S(1)}, f32[8,1,32,2048]{3,2,1,0:T(8,128)}, u32[]{:S(2)}) copy-start(f32[8,1,32,2048]{3,2,1,0:T(8,128)} %get-tuple-element.20) | copy-start | bytes 6291460
  162.0 11.3 %collective-permute-start.29 = (bf16[64,2176]{1,0:T(8,128)(2,1)S(1)}, bf16[64,2176]{1,0:T(8,128)(2,1)S(1)}, u32[]{:S(2)}, u32[]{:S(2)}) collective-permute-start(bf16[64,2176]{1,0:T(8,128)(2,1)S(1)} %get-tuple-element.91), channel_id=1, source_target_pairs={{0,4},{1,5},{2,6},{3,7},{4,0},{5,1},{6,2},{7,3},{8,12},{9,13},{10,... | collective-permute-start | bytes 835592 | tf_op jit(solution)/shard_map/ppermute | solution.py:23
  165.0 13.4 %collective-permute-start.28 = (bf16[64,2176]{1,0:T(8,128)(2,1)S(1)}, bf16[64,2176]{1,0:T(8,128)(2,1)S(1)}, u32[]{:S(2)}, u32[]{:S(2)}) collective-permute-start(bf16[64,2176]{1,0:T(8,128)(2,1)S(1)} %get-tuple-element.92), channel_id=1, source_target_pairs={{0,6},{1,7},{2,0},{3,1},{4,2},{5,3},{6,4},{7,5},{8,14},{9,15},{10,... | collective-permute-start | bytes 835592 | tf_op jit(solution)/shard_map/ppermute | solution.py:23
  166.2 12.6 %collective-permute-start.27 = (bf16[64,2176]{1,0:T(8,128)(2,1)S(1)}, bf16[64,2176]{1,0:T(8,128)(2,1)S(1)}, u32[]{:S(2)}, u32[]{:S(2)}) collective-permute-start(bf16[64,2176]{1,0:T(8,128)(2,1)S(1)} %get-tuple-element.93), channel_id=1, source_target_pairs={{0,2},{1,3},{2,4},{3,5},{4,6},{5,7},{6,0},{7,1},{8,10},{9,11},{10,... | collective-permute-start | bytes 835592 | tf_op jit(solution)/shard_map/ppermute | solution.py:23
  179.2 8.6 %collective-permute-start.30 = (f32[16,2176]{1,0:T(8,128)S(1)}, f32[16,2176]{1,0:T(8,128)S(1)}, u32[]{:S(2)}, u32[]{:S(2)}) collective-permute-start(f32[16,2176]{1,0:T(8,128)S(1)} %fusion.46), channel_id=1, source_target_pairs={{0,8},{1,9},{2,10},{3,11},{4,12},{5,13},{6,14},{7,15},{8,0},{9,1},... | collective-permute-start | bytes 417800 | tf_op jit(solution)/shard_map/ppermute | solution.py:23
  187.8 19.3 %copy-start.2 = (bf16[4,8192]{1,0:T(4,128)(2,1)S(1)}, bf16[4,8192]{1,0:T(4,128)(2,1)}, u32[]{:S(2)}) copy-start(bf16[4,8192]{1,0:T(4,128)(2,1)} %param.6) | copy-start | bytes 196612
  187.8 19.3 %copy-start.3 = (f32[8192]{0:T(1024)S(1)}, f32[8192]{0:T(1024)}, u32[]{:S(2)}) copy-start(f32[8192]{0:T(1024)} %param.7) | copy-start | bytes 98308
  188.0 6.6 %collective-permute-start.32 = (f32[16,2176]{1,0:T(8,128)S(1)}, f32[16,2176]{1,0:T(8,128)S(1)}, u32[]{:S(2)}, u32[]{:S(2)}) collective-permute-start(f32[16,2176]{1,0:T(8,128)S(1)} %get-tuple-element.94), channel_id=1, source_target_pairs={{0,72},{1,73},{2,74},{3,75},{4,76},{5,77},{6,78},{7,79},{8,64},{9,... | collective-permute-start | bytes 417800 | tf_op jit(solution)/shard_map/ppermute | solution.py:23
  189.4 5.2 %collective-permute-start.31 = (f32[16,2176]{1,0:T(8,128)S(1)}, f32[16,2176]{1,0:T(8,128)S(1)}, u32[]{:S(2)}, u32[]{:S(2)}) collective-permute-start(f32[16,2176]{1,0:T(8,128)S(1)} %get-tuple-element.95), channel_id=1, source_target_pairs={{0,64},{1,65},{2,66},{3,67},{4,68},{5,69},{6,70},{7,71},{8,72},{9,... | collective-permute-start | bytes 417800 | tf_op jit(solution)/shard_map/ppermute | solution.py:23
  194.9 6.1 %collective-permute-start.33 = (bf16[8,3584]{1,0:T(8,128)(2,1)S(1)}, bf16[8,3584]{1,0:T(8,128)(2,1)S(1)}, u32[]{:S(2)}, u32[]{:S(2)}) collective-permute-start(bf16[8,3584]{1,0:T(8,128)(2,1)S(1)} %fusion.116), channel_id=1, source_target_pairs={{0,16},{1,17},{2,18},{3,19},{4,20},{5,21},{6,22},{7,23},{8,24},{9,... | collective-permute-start | bytes 172040 | tf_op jit(solution)/shard_map/ppermute | solution.py:23
  195.0 7.5 %collective-permute-start.35 = (bf16[8,3584]{1,0:T(8,128)(2,1)S(1)}, bf16[8,3584]{1,0:T(8,128)(2,1)S(1)}, u32[]{:S(2)}, u32[]{:S(2)}) collective-permute-start(bf16[8,3584]{1,0:T(8,128)(2,1)S(1)} %fusion.118), channel_id=1, source_target_pairs={{0,32},{1,33},{2,34},{3,35},{4,36},{5,37},{6,38},{7,39},{8,40},{9,... | collective-permute-start | bytes 172040 | tf_op jit(solution)/shard_map/ppermute | solution.py:23
  199.7 4.2 %collective-permute-start.34 = (bf16[8,3584]{1,0:T(8,128)(2,1)S(1)}, bf16[8,3584]{1,0:T(8,128)(2,1)S(1)}, u32[]{:S(2)}, u32[]{:S(2)}) collective-permute-start(bf16[8,3584]{1,0:T(8,128)(2,1)S(1)} %fusion.117), channel_id=1, source_target_pairs={{0,48},{1,49},{2,50},{3,51},{4,52},{5,53},{6,54},{7,55},{8,56},{9,... | collective-permute-start | bytes 172040 | tf_op jit(solution)/shard_map/ppermute | solution.py:23

commit v3 on v2

v3 whole, which is shorter than its diff:
```python
import jax
import jax.numpy as jnp
from jax import lax
from jax.sharding import Mesh, PartitionSpec as P

EPS = 1e-05
F32 = jnp.float32
BF16 = jnp.bfloat16
ZS, XS, HS, YS, CS = 2, 4, 2, 4, 2
AXES = ("z", "x", "h", "y", "core")


def send(value, z=0, x=0, h=0, y=0, c=0):
    pairs = []
    for z0 in range(ZS):
        for x0 in range(XS):
            for h0 in range(HS):
                for y0 in range(YS):
                    for c0 in range(CS):
                        source = (((z0 * XS + x0) * HS + h0) * YS + y0) * CS + c0
                        z1, x1, h1 = (z0 + z) % ZS, (x0 + x) % XS, (h0 + h) % HS
                        y1, c1 = (y0 + y) % YS, (c0 + c) % CS
                        pairs.append((source, (((z1 * XS + x1) * HS + h1) * YS + y1) * CS + c1))
    return lax.ppermute(value, AXES, pairs)


def product(left, right):
    return jnp.dot(left, right, preferred_element_type=F32)


def product_right_t(left, right):
    return lax.dot_general(left, right, (((1,), (1,)), ((), ())), preferred_element_type=F32)


def product_left_t(left, right):
    return lax.dot_general(left, right, (((0,), (0,)), ((), ())), preferred_element_type=F32)


def rounded(value):
    return lax.reduce_precision(value, 8, 7)


def parts_of(value, count):
    parts = []
    for _ in range(count):
        top = rounded(value)
        parts.append(top.astype(BF16))
        value = value - top
    return parts


def gather_tokens(own, z, x):
    n = own.shape[1]
    over_y = {0: own}
    for dy in (1, 3, 2):
        over_y[-dy % YS] = send(own, y=dy)
    core = jnp.zeros((256, n), own.dtype)
    for dy in range(YS):
        core = lax.dynamic_update_slice(core, over_y[dy], ((dy - x) % XS * 64, 0))
    other = send(core, c=1)
    both = jnp.zeros((512, n), own.dtype)
    both = lax.dynamic_update_slice(both, core, (z * 256, 0))
    return lax.dynamic_update_slice(both, other, ((1 - z) * 256, 0)), over_y[3]


def sum_over_row(near, arrived):
    m12, a10 = arrived
    a02 = near[2] + m12
    h = a02.shape[0] // 2
    n1 = send(a02[:h].astype(BF16), x=1).astype(F32)
    n2 = send(a02[h:].astype(BF16), x=3).astype(F32)
    q = send(a10.astype(BF16), z=1).astype(F32)
    a01 = jnp.concatenate([near[1][:h] + n1, near[1][h:]], axis=0)
    a03 = jnp.concatenate([near[3][:h], near[3][h:] + n2], axis=0)
    r1 = send(a01.astype(BF16), x=1).astype(F32)
    r2 = send(a03.astype(BF16), x=3).astype(F32)
    return near[0] + q + r1 + r2


def first_step(far, messages):
    m12 = send(messages[2], z=1).astype(F32)
    m11 = send(messages[1], x=1).astype(F32)
    m13 = send(messages[3], x=3).astype(F32)
    return m12, far[0] + m11 + m13


def gather_over_row(own):
    h = own.shape[0] // 2
    a = send(own, x=1)
    b = send(own, x=3)
    p = send(own, z=1)
    a2 = send(a[:h], x=1)
    b2 = send(b[h:], x=3)
    pa = send(p, x=1)
    pb = send(p, x=3)
    across = jnp.concatenate([a2, b2], axis=0)
    p2 = send(across, z=1)
    return (
        jnp.concatenate([own, b, across, a], axis=0),
        jnp.concatenate([p, pb, p2, pa], axis=0),
    )


def sum_over_core_y(partial, gain_partial, z, x):
    give = lax.dynamic_slice(partial, ((1 - z) * 256, 0), (256, 2048))
    give = jnp.concatenate([give, jnp.pad(gain_partial, ((0, 0), (0, 2048 - 128)))], axis=0)
    taken = send(give, c=1)
    keep = lax.dynamic_slice(partial, (z * 256, 0), (256, 2048)) + taken[:256]
    gain = gain_partial + taken[256:, :128]
    gain_parts = jnp.concatenate(parts_of(gain, 2) + [jnp.zeros((48, 128), BF16)], axis=0)

    def gain_of(parts):
        return parts[:8].astype(F32) + parts[8:16].astype(F32)

    def piece(dy):
        return lax.dynamic_slice(keep, ((dy - x) % XS * 64, 0), (64, 2048))

    total = piece(0)
    gains = {0: gain_of(gain_parts)}
    for dy in (1, 3, 2):
        message = jnp.concatenate([piece(dy).astype(BF16), gain_parts], axis=1)
        got = send(message, y=dy)
        total = total + got[:, :2048].astype(F32)
        gains[dy] = gain_of(got[:, 2048:])
    gain = (gains[0] + gains[2]) + (gains[1] + gains[3])
    return total, gain


def per_device(inputs, rms_gain_vector, gate_weight, up_weight, down_weight, out_grad):
    z, x = lax.axis_index("z"), lax.axis_index("x")
    row = z * XS + x
    width = gate_weight.shape[1]

    value_entries = inputs.astype(F32)
    inverse_rms = lax.rsqrt(jnp.mean(value_entries * value_entries, axis=1, keepdims=True) + EPS)
    side = jnp.concatenate(parts_of(inverse_rms, 3) + [jnp.zeros((4, 125), BF16)], axis=1)
    message = jnp.concatenate(
        [
            inputs.reshape(4, 8, 1024),
            jnp.broadcast_to(side[:, None, :], (4, 8, 128)),
            out_grad.reshape(4, 8, 1024),
        ],
        axis=2,
    )
    message = jnp.broadcast_to(jnp.transpose(message, (1, 0, 2))[:, None], (8, HS, 4, 2176))
    block = lax.all_to_all(
        message.reshape(16, 4, 2176), ("z", "x", "h"), split_axis=0, concat_axis=0, tiled=True
    )
    block = block.reshape(64, 2176)
    tokens, first = gather_tokens(block[:, :1152], z, x)
    grad_block, _ = lax.optimization_barrier((block[:, 1152:], first))
    grad_full, _ = gather_tokens(grad_block, z, x)

    inverse_full = (
        tokens[:, 1024:1025].astype(F32)
        + tokens[:, 1025:1026].astype(F32)
        + tokens[:, 1026:1027].astype(F32)
    )
    gain_block = lax.dynamic_slice(rms_gain_vector, (row * 1024,), (1024,))
    estimate = tokens[:, :1024].astype(F32) * inverse_full
    normed = (estimate * gain_block).astype(BF16)

    def gate_up(normed):
        both = [product(normed, gate_weight), product(normed, up_weight)]
        return jnp.concatenate(both, axis=1).reshape(4, 64, 2 * width)

    def for_hidden(grad):
        return product_right_t(grad, down_weight).reshape(4, 64, width)

    far = gate_up(normed[256:])
    messages = [far[i].astype(BF16) for i in range(XS)]
    far_grad = for_hidden(grad_full[256:])
    grad_messages = [far_grad[i].astype(BF16) for i in range(XS)]
    normed_near, grad_near, *messages = lax.optimization_barrier(
        (normed[:256], grad_full[:256], *messages)
    )
    arrived = first_step(far, messages)
    arrived_grad = first_step(far_grad, grad_messages)
    near = jnp.concatenate([gate_up(normed_near), for_hidden(grad_near)], axis=2)
    sums = sum_over_row(
        near, [jnp.concatenate(pair, axis=1) for pair in zip(arrived, arrived_grad, strict=True)]
    )
    gate, up, hidden_grad = sums[:, :width], sums[:, width : 2 * width], sums[:, 2 * width :]
    sigma = jax.nn.sigmoid(gate)
    silu = gate * sigma
    units = jnp.concatenate(
        [
            (silu * up).astype(BF16),
            (hidden_grad * up * sigma * (1.0 + gate * (1.0 - sigma))).astype(BF16),
            (hidden_grad * silu).astype(BF16),
        ],
        axis=1,
    )
    units = gather_over_row(units)

    def backward(units):
        hidden, gate_grad, up_grad = units[:, :width], units[:, width : 2 * width], units[:, 2 * width :]
        grad = product_right_t(gate_grad, gate_weight) + product_right_t(up_grad, up_weight)
        return jnp.concatenate([product(hidden, down_weight), grad], axis=1)

    partial = jnp.concatenate([backward(units[0]), backward(units[1])], axis=0)
    gain_partial = jnp.sum(partial[:, 1024:] * estimate, axis=0).reshape(8, 128)
    total, gain = sum_over_core_y(partial, gain_partial, z, x)
    units = jnp.concatenate(units, axis=0)
    hidden, gate_grad, up_grad = units[:, :width], units[:, width : 2 * width], units[:, 2 * width :]
    down_weight_grad = product_left_t(hidden, grad_full).astype(BF16)
    gate_weight_grad = product_left_t(normed, gate_grad).astype(BF16)
    up_weight_grad = product_left_t(normed, up_grad).astype(BF16)
    total, down_weight_grad, gate_weight_grad = lax.optimization_barrier(
        (total, down_weight_grad, gate_weight_grad)
    )
    gain_parts = [p.reshape(4, 256) for p in parts_of(gain, 2)]
    gain_rows = jnp.broadcast_to(jnp.concatenate(gain_parts, axis=1)[None], (16, 4, 512))
    message = total.astype(BF16).reshape(16, 4, 2048)
    message = jnp.concatenate([message, gain_rows], axis=2)
    back = lax.all_to_all(message, ("z", "x", "h"), split_axis=0, concat_axis=0, tiled=True)
    back = back.reshape(8, HS, 4, 2560).astype(F32)
    gain_grad = back[..., 2048:2304] + back[..., 2304:]
    gain_grad = (gain_grad[:, 0] + gain_grad[:, 1]).reshape(8192)
    back = back[:, 0, :, :2048] + back[:, 1, :, :2048]
    outputs = jnp.transpose(back[..., :1024].astype(BF16), (1, 0, 2)).reshape(4, 8192)
    normed_grad = jnp.transpose(back[..., 1024:], (1, 0, 2)).reshape(4, 8192)

    normalized = value_entries * inverse_rms
    scaled = normed_grad * rms_gain_vector
    input_gradient = inverse_rms * (
        scaled - normalized * jnp.mean(scaled * normalized, axis=1, keepdims=True)
    )
    return (
        outputs,
        input_gradient.astype(BF16),
        gain_grad,
        gate_weight_grad,
        up_weight_grad,
        down_weight_grad,
    )


def solution(mesh):
    fine = Mesh(mesh.devices.reshape(ZS, XS, HS, YS, CS), AXES)
    row, col = AXES[:2], AXES[2:]
    in_specs = (P(AXES, None), P(), P(row, col), P(row, col), P(col, row), P(AXES, None))
    out_specs = (P(AXES, None), P(AXES, None), P(), P(row, col), P(row, col), P(col, row))
    return jax.shard_map(
        per_device, mesh=fine, in_specs=in_specs, out_specs=out_specs, check_vma=False
    )
```

time: 213 us -> 192 us (0.901); the launches traced: 209 us -> 191 us
  local copies, waits for them, and re-layouts: 14.6 us -> 8.96 us
  other arithmetic: 12.8 us -> 8.74 us
  starting transfers between devices: 57.9 us -> 54 us
  matrix products: 30.2 us -> 26.9 us
    ppermute x36 -> x31, starting transfers between devices: 57.9 us -> 40.8 us  [send(): return lax.ppermute(value, AXES, pairs)]
    all_to_all x0 -> x2, starting transfers between devices: none -> 13.2 us  [the longest x1 7.96 us: per_device(): lax.all_to_all(message.reshape(16, 4, 2176), ('z', 'x', 'h'), split_axis=...]
    ppermute x36 -> x31, waiting for transfers between devices: 90.9 us -> 78.1 us  [send(): return lax.ppermute(value, AXES, pairs)]
    all_to_all x0 -> x2, waiting for transfers between devices: none -> 12.7 us  [the longest x1 8.93 us: per_device(): lax.all_to_all(message.reshape(16, 4, 2176), ('z', 'x', 'h'), split_axis=...]
    slice x7, local copies, waits for them, and re-layouts: 3.83 us -> 0.31 us  [the longest x1 0.1 us: per_device(): messages = [far[i].astype(BF16) for i in range(XS)]]
    dot_general x3, matrix products: 16.5 us -> 13.3 us  [product_left_t(): lax.dot_general(left, right, (((0,), (0,)), ((), ())), preferred_element_...]
    unnamed x39 -> x34, local copies, waits for them, and re-layouts: 7.13 us -> 5 us
  transfers between devices with their start and end apart: 36 -> 33, of which waited for: 24 -> 17; matrix products, arithmetic and copies ran while one was open for 11% -> 13% of each run, Pallas kernels for 0% -> 0%
where the time goes in v3:
time: 192 us; the launch traced here: 191 us
  waiting for transfers between devices  90.8 us (47%)
  starting transfers between devices  54 us (28%)
  matrix products  26.9 us (14%)
  local copies, waits for them, and re-layouts  8.96 us (5%)
  other arithmetic  8.74 us (5%)
    ppermute x31, waiting for transfers between devices, send(): return lax.ppermute(value, AXES, pairs)  78.1 us
    ppermute x31, starting transfers between devices, send(): return lax.ppermute(value, AXES, pairs)  40.8 us
    dot_general x3, matrix products, product_left_t(): lax.dot_general(left, right, (((0,), (0,)), ((), ())), preferred_element_...  13.3 us
    all_to_all x1, waiting for transfers between devices, per_device(): lax.all_to_all(message.reshape(16, 4, 2176), ('z', 'x', 'h'), split_axis=...  8.93 us
    all_to_all x1, starting transfers between devices, per_device(): lax.all_to_all(message.reshape(16, 4, 2176), ('z', 'x', 'h'), split_axis=...  7.96 us
    dot_general x6, matrix products, product_right_t(): lax.dot_general(left, right, (((1,), (1,)), ((), ())), preferred_element_...  6.88 us
    dot_general x6, matrix products, product(): return jnp.dot(left, right, preferred_element_type=F32)  6.68 us
    all_to_all x1, starting transfers between devices, per_device(): lax.all_to_all(message, ('z', 'x', 'h'), split_axis=0, concat_axis=0, til...  5.27 us
  transfers between devices with their start and end apart: 33, of which 17 were waited for; matrix products, arithmetic and copies ran while one was open for 13% of the time, Pallas kernels for 0%

profile of v3, /device:TPU:0, one launch (start us, length us, event | category | flops | bytes accessed | tf_op | source)
XLA Modules:
  0.0 190.9 jit_solution(6111184709532916877)
XLA Ops:
  4.0 8.0 %all-to-all-start = ((bf16[16,4,2176]{2,1,0:T(4,128)(2,1)}), bf16[16,4,2176]{2,1,0:T(4,128)(2,1)S(1)}, u32[]{:S(2)}, u32[]{:S(2)}) async-start(bf16[16,4,2176]{2,1,0:T(4,128)(2,1)} %bitcast.2), calls=%async_computation | async-start | bytes 557056 | tf_op jit(solution)/shard_map/all_to_all | solution.py:146
  11.9 8.9 %all-to-all-done = bf16[16,4,2176]{2,1,0:T(4,128)(2,1)S(1)} async-done(((bf16[16,4,2176]{2,1,0:T(4,128)(2,1)}), bf16[16,4,2176]{2,1,0:T(4,128)(2,1)S(1)}, u32[]{:S(2)}, u32[]{:S(2)}) %all-to-all-start) | async-done | bytes 278560 | tf_op jit(solution)/shard_map/all_to_all | solution.py:146
  21.0 1.6 collective-permute-start.2
  22.7 1.7 collective-permute-start
  24.4 2.1 %collective-permute-start.1 = (bf16[64,1152]{1,0:T(8,128)(2,1)S(1)}, bf16[64,1152]{1,0:T(8,128)(2,1)S(1)}, u32[]{:S(2)}, u32[]{:S(2)}) collective-permute-start(bf16[64,1152]{1,0:T(8,128)(2,1)S(1)} %get-tuple-element.69), channel_id=1, source_target_pairs={{0,4},{1,5},{2,6},{3,7},{4,0},{5,1},{6,2},{7,3},{8,12},{9,13},{10,... | collective-permute-start | bytes 442376 | tf_op jit(solution)/shard_map/ppermute | solution.py:24
  26.4 2.8 %collective-permute-done.2 = bf16[64,1152]{1,0:T(8,128)(2,1)S(1)} collective-permute-done((bf16[64,1152]{1,0:T(8,128)(2,1)S(1)}, bf16[64,1152]{1,0:T(8,128)(2,1)S(1)}, u32[]{:S(2)}, u32[]{:S(2)}) %collective-permute-start.2) | collective-permute-done | bytes 147488 | tf_op jit(solution)/shard_map/ppermute | solution.py:24
  29.2 3.0 %collective-permute-start.5 = (bf16[64,1024]{1,0:T(8,128)(2,1)S(1)}, bf16[64,1024]{1,0:T(8,128)(2,1)S(1)}, u32[]{:S(2)}, u32[]{:S(2)}) collective-permute-start(bf16[64,1024]{1,0:T(8,128)(2,1)S(1)} %slice.299), channel_id=1, source_target_pairs={{0,4},{1,5},{2,6},{3,7},{4,0},{5,1},{6,2},{7,3},{8,12},{9,13},{10,... | collective-permute-start | bytes 393224 | tf_op jit(solution)/shard_map/ppermute | solution.py:24
  32.3 2.1 %collective-permute-start.4 = (bf16[64,1024]{1,0:T(8,128)(2,1)S(1)}, bf16[64,1024]{1,0:T(8,128)(2,1)S(1)}, u32[]{:S(2)}, u32[]{:S(2)}) collective-permute-start(bf16[64,1024]{1,0:T(8,128)(2,1)S(1)} %slice.299), channel_id=1, source_target_pairs={{0,6},{1,7},{2,0},{3,1},{4,2},{5,3},{6,4},{7,5},{8,14},{9,15},{10,... | collective-permute-start | bytes 393224 | tf_op jit(solution)/shard_map/ppermute | solution.py:24
  34.9 2.8 %collective-permute-done.4 = bf16[64,1024]{1,0:T(8,128)(2,1)S(1)} collective-permute-done((bf16[64,1024]{1,0:T(8,128)(2,1)S(1)}, bf16[64,1024]{1,0:T(8,128)(2,1)S(1)}, u32[]{:S(2)}, u32[]{:S(2)}) %collective-permute-start.4) | collective-permute-done | bytes 131104 | tf_op jit(solution)/shard_map/ppermute | solution.py:24
  38.7 1.3 copy-done.7
  40.0 1.1 fusion.39
  43.6 1.1 fusion.69
  44.7 1.1 fusion.68
  46.5 2.7 %collective-permute-start.9 = (bf16[64,3584]{1,0:T(8,128)(2,1)S(1)}, bf16[64,3584]{1,0:T(8,128)(2,1)S(1)}, u32[]{:S(2)}, u32[]{:S(2)}) collective-permute-start(bf16[64,3584]{1,0:T(8,128)(2,1)S(1)} %get-tuple-element.19), channel_id=1, source_target_pairs={{0,48},{1,49},{2,50},{3,51},{4,52},{5,53},{6,54},{7,55},{8,56},{9,... | collective-permute-start | bytes 1376264 | tf_op jit(solution)/shard_map/ppermute | solution.py:24
  49.3 1.2 fusion.67
  50.4 1.1 fusion.70
  51.9 3.2 %collective-permute-start.11 = (bf16[64,1792]{1,0:T(8,128)(2,1)S(1)}, bf16[64,1792]{1,0:T(8,128)(2,1)S(1)}, u32[]{:S(2)}, u32[]{:S(2)}) collective-permute-start(bf16[64,1792]{1,0:T(8,128)(2,1)S(1)} %get-tuple-element.45), channel_id=1, source_target_pairs={{0,48},{1,49},{2,50},{3,51},{4,52},{5,53},{6,54},{7,55},{8,56},{9,... | collective-permute-start | bytes 688136 | tf_op jit(solution)/shard_map/ppermute | solution.py:24
  55.9 9.0 %collective-permute-done.10 = bf16[64,1792]{1,0:T(8,128)(2,1)S(1)} collective-permute-done((bf16[64,1792]{1,0:T(8,128)(2,1)S(1)}, bf16[64,1792]{1,0:T(8,128)(2,1)S(1)}, u32[]{:S(2)}, u32[]{:S(2)}) %collective-permute-start.10) | collective-permute-done | bytes 229408 | tf_op jit(solution)/shard_map/ppermute | solution.py:24
  65.1 7.0 %collective-permute-done.14 = bf16[64,1792]{1,0:T(8,128)(2,1)S(1)} collective-permute-done((bf16[64,1792]{1,0:T(8,128)(2,1)S(1)}, bf16[64,1792]{1,0:T(8,128)(2,1)S(1)}, u32[]{:S(2)}, u32[]{:S(2)}) %collective-permute-start.14) | collective-permute-done | bytes 229408 | tf_op jit(solution)/shard_map/ppermute | solution.py:24
  72.4 3.2 %collective-permute-start.17 = (bf16[32,5376]{1,0:T(8,128)(2,1)S(1)}, bf16[32,5376]{1,0:T(8,128)(2,1)S(1)}, u32[]{:S(2)}, u32[]{:S(2)}) collective-permute-start(bf16[32,5376]{1,0:T(8,128)(2,1)S(1)} %get-tuple-element.62), channel_id=1, source_target_pairs={{0,48},{1,49},{2,50},{3,51},{4,52},{5,53},{6,54},{7,55},{8,56},{9,... | collective-permute-start | bytes 1032200 | tf_op jit(solution)/shard_map/ppermute | solution.py:24
  76.2 6.2 %collective-permute-done.15 = bf16[32,5376]{1,0:T(8,128)(2,1)S(1)} collective-permute-done((bf16[32,5376]{1,0:T(8,128)(2,1)S(1)}, bf16[32,5376]{1,0:T(8,128)(2,1)S(1)}, u32[]{:S(2)}, u32[]{:S(2)}) %collective-permute-start.15) | collective-permute-done | bytes 344096 | tf_op jit(solution)/shard_map/ppermute | solution.py:24
  82.6 3.0 %collective-permute-start.18 = (bf16[64,5376]{1,0:T(8,128)(2,1)S(1)}, bf16[64,5376]{1,0:T(8,128)(2,1)S(1)}, u32[]{:S(2)}, u32[]{:S(2)}) collective-permute-start(bf16[64,5376]{1,0:T(8,128)(2,1)S(1)} %pad_maximum_fusion.5), channel_id=1, source_target_pairs={{0,48},{1,49},{2,50},{3,51},{4,52},{5,53},{6,54},{7,55},{8,56},{9,... | collective-permute-start | bytes 2064392 | tf_op jit(solution)/shard_map/ppermute | solution.py:24
  85.8 5.8 %collective-permute-done.12 = bf16[64,5376]{1,0:T(8,128)(2,1)S(1)} collective-permute-done((bf16[64,5376]{1,0:T(8,128)(2,1)S(1)}, bf16[64,5376]{1,0:T(8,128)(2,1)S(1)}, u32[]{:S(2)}, u32[]{:S(2)}) %collective-permute-start.12) | collective-permute-done | bytes 688160 | tf_op jit(solution)/shard_map/ppermute | solution.py:24
  91.6 6.6 %collective-permute-done.18 = bf16[64,5376]{1,0:T(8,128)(2,1)S(1)} collective-permute-done((bf16[64,5376]{1,0:T(8,128)(2,1)S(1)}, bf16[64,5376]{1,0:T(8,128)(2,1)S(1)}, u32[]{:S(2)}, u32[]{:S(2)}) %collective-permute-start.18) | collective-permute-done | bytes 688160 | tf_op jit(solution)/shard_map/ppermute | solution.py:24
  98.1 3.5 %collective-permute-done.16 = bf16[64,5376]{1,0:T(8,128)(2,1)S(1)} collective-permute-done((bf16[64,5376]{1,0:T(8,128)(2,1)S(1)}, bf16[64,5376]{1,0:T(8,128)(2,1)S(1)}, u32[]{:S(2)}, u32[]{:S(2)}) %collective-permute-start.16) | collective-permute-done | bytes 688160 | tf_op jit(solution)/shard_map/ppermute | solution.py:24
  102.4 3.2 %collective-permute-start.19 = (bf16[64,5376]{1,0:T(8,128)(2,1)S(1)}, bf16[64,5376]{1,0:T(8,128)(2,1)S(1)}, u32[]{:S(2)}, u32[]{:S(2)}) collective-permute-start(bf16[64,5376]{1,0:T(8,128)(2,1)S(1)} %get-tuple-element.60), channel_id=1, source_target_pairs={{0,48},{1,49},{2,50},{3,51},{4,52},{5,53},{6,54},{7,55},{8,56},{9,... | collective-permute-start | bytes 2064392 | tf_op jit(solution)/shard_map/ppermute | solution.py:24
  106.3 11.6 %collective-permute-done.20 = bf16[64,5376]{1,0:T(8,128)(2,1)S(1)} collective-permute-done((bf16[64,5376]{1,0:T(8,128)(2,1)S(1)}, bf16[64,5376]{1,0:T(8,128)(2,1)S(1)}, u32[]{:S(2)}, u32[]{:S(2)}) %collective-permute-start.20) | collective-permute-done | bytes 688160 | tf_op jit(solution)/shard_map/ppermute | solution.py:24
  118.0 3.3 %collective-permute-start.22 = (bf16[32,5376]{1,0:T(8,128)(2,1)S(1)}, bf16[32,5376]{1,0:T(8,128)(2,1)S(1)}, u32[]{:S(2)}, u32[]{:S(2)}) collective-permute-start(bf16[32,5376]{1,0:T(8,128)(2,1)S(1)} %slice.328), channel_id=1, source_target_pairs={{0,48},{1,49},{2,50},{3,51},{4,52},{5,53},{6,54},{7,55},{8,56},{9,... | collective-permute-start | bytes 1032200 | tf_op jit(solution)/shard_map/ppermute | solution.py:24
  121.3 3.2 %collective-permute-start.24 = (bf16[64,5376]{1,0:T(8,128)(2,1)S(1)}, bf16[64,5376]{1,0:T(8,128)(2,1)S(1)}, u32[]{:S(2)}, u32[]{:S(2)}) collective-permute-start(bf16[64,5376]{1,0:T(8,128)(2,1)S(1)} %collective-permute-done.23), channel_id=1, source_target_pairs={{0,48},{1,49},{2,50},{3,51},{4,52},{5,53},{6,54},{7,55},{8,56},{9,... | collective-permute-start | bytes 2064392 | tf_op jit(solution)/shard_map/ppermute | solution.py:24
  124.7 5.5 %collective-permute-done.21 = bf16[32,5376]{1,0:T(8,128)(2,1)S(1)} collective-permute-done((bf16[32,5376]{1,0:T(8,128)(2,1)S(1)}, bf16[32,5376]{1,0:T(8,128)(2,1)S(1)}, u32[]{:S(2)}, u32[]{:S(2)}) %collective-permute-start.21) | collective-permute-done | bytes 344096 | tf_op jit(solution)/shard_map/ppermute | solution.py:24
  130.4 1.1 fusion.24
  131.6 1.1 fusion.27
  133.8 1.1 convolution_add_fusion.1
  135.0 3.7 %collective-permute-done.24 = bf16[64,5376]{1,0:T(8,128)(2,1)S(1)} collective-permute-done((bf16[64,5376]{1,0:T(8,128)(2,1)S(1)}, bf16[64,5376]{1,0:T(8,128)(2,1)S(1)}, u32[]{:S(2)}, u32[]{:S(2)}) %collective-permute-start.24) | collective-permute-done | bytes 688160 | tf_op jit(solution)/shard_map/ppermute | solution.py:24
  138.8 5.2 %collective-permute-done.25 = bf16[64,5376]{1,0:T(8,128)(2,1)S(1)} collective-permute-done((bf16[64,5376]{1,0:T(8,128)(2,1)S(1)}, bf16[64,5376]{1,0:T(8,128)(2,1)S(1)}, u32[]{:S(2)}, u32[]{:S(2)}) %collective-permute-start.25) | collective-permute-done | bytes 688160 | tf_op jit(solution)/shard_map/ppermute | solution.py:24
  144.2 1.1 fusion.19
  145.4 1.1 fusion.22
  146.5 1.1 convolution_add_fusion
  149.0 3.9 %convolution_convert_fusion.2 = bf16[1792,1024]{1,0:T(8,128)(2,1)} fusion(bf16[512,1024]{1,0:T(8,128)(2,1)S(1)} %constant_dynamic-update-slice_fusion.18, bf16[512,5376]{1,0:T(8,128)(2,1)S(1)} %get-tuple-element.46), kind=kOutput, calls=%fused_computation.16 | convolution fusion | flops 1880883200 | bytes 6553600 | tf_op jit(solution)/shard_map/dot_general | solution.py:36
  153.8 2.6 %collective-permute-start.30 = (bf16[64,2176]{1,0:T(8,128)(2,1)S(1)}, bf16[64,2176]{1,0:T(8,128)(2,1)S(1)}, u32[]{:S(2)}, u32[]{:S(2)}) collective-permute-start(bf16[64,2176]{1,0:T(8,128)(2,1)S(1)} %get-tuple-element.71), channel_id=1, source_target_pairs={{0,4},{1,5},{2,6},{3,7},{4,0},{5,1},{6,2},{7,3},{8,12},{9,13},{10,... | collective-permute-start | bytes 835592 | tf_op jit(solution)/shard_map/ppermute | solution.py:24
  156.4 2.1 %collective-permute-start.29 = (bf16[64,2176]{1,0:T(8,128)(2,1)S(1)}, bf16[64,2176]{1,0:T(8,128)(2,1)S(1)}, u32[]{:S(2)}, u32[]{:S(2)}) collective-permute-start(bf16[64,2176]{1,0:T(8,128)(2,1)S(1)} %get-tuple-element.72), channel_id=1, source_target_pairs={{0,6},{1,7},{2,0},{3,1},{4,2},{5,3},{6,4},{7,5},{8,14},{9,15},{10,... | collective-permute-start | bytes 835592 | tf_op jit(solution)/shard_map/ppermute | solution.py:24
  158.4 4.0 %convolution_convert_fusion.1 = bf16[1024,1792]{1,0:T(8,128)(2,1)} fusion(bf16[512,1024]{1,0:T(8,128)(2,1)S(1)} %multiply_convert_fusion, bf16[512,5376]{1,0:T(8,128)(2,1)S(1)} %get-tuple-element.46), kind=kOutput, calls=%fused_computation.15 | convolution fusion | flops 1880883200 | bytes 6553600 | tf_op jit(solution)/shard_map/dot_general | solution.py:36
  162.4 2.5 %collective-permute-done.30 = bf16[64,2176]{1,0:T(8,128)(2,1)S(1)} collective-permute-done((bf16[64,2176]{1,0:T(8,128)(2,1)S(1)}, bf16[64,2176]{1,0:T(8,128)(2,1)S(1)}, u32[]{:S(2)}, u32[]{:S(2)}) %collective-permute-start.30) | collective-permute-done | bytes 278560 | tf_op jit(solution)/shard_map/ppermute | solution.py:24
  164.9 5.5 %collective-permute-done.29 = bf16[64,2176]{1,0:T(8,128)(2,1)S(1)} collective-permute-done((bf16[64,2176]{1,0:T(8,128)(2,1)S(1)}, bf16[64,2176]{1,0:T(8,128)(2,1)S(1)}, u32[]{:S(2)}, u32[]{:S(2)}) %collective-permute-start.29) | collective-permute-done | bytes 278560 | tf_op jit(solution)/shard_map/ppermute | solution.py:24
  171.2 1.2 convert_add_fusion
  173.5 5.3 %all-to-all-start.1 = ((bf16[16,4,2560]{2,1,0:T(4,128)(2,1)}), bf16[16,4,2560]{2,1,0:T(4,128)(2,1)S(1)}, u32[]{:S(2)}, u32[]{:S(2)}) async-start(bf16[16,4,2560]{2,1,0:T(4,128)(2,1)} %pad_maximum_fusion.8), calls=%async_computation.1 | async-start | bytes 655360 | tf_op jit(solution)/shard_map/all_to_all | solution.py:216
  178.7 5.5 %convolution_convert_fusion = bf16[1024,1792]{1,0:T(8,128)(2,1)} fusion(bf16[512,1024]{1,0:T(8,128)(2,1)S(1)} %multiply_convert_fusion, bf16[512,5376]{1,0:T(8,128)(2,1)} %copy-done.6), kind=kOutput, calls=%fused_computation.14 | convolution fusion | flops 1880883200 | bytes 6553600 | tf_op jit(solution)/shard_map/dot_general | solution.py:36
  184.2 3.8 %all-to-all-done.1 = bf16[16,4,2560]{2,1,0:T(4,128)(2,1)S(1)} async-done(((bf16[16,4,2560]{2,1,0:T(4,128)(2,1)}), bf16[16,4,2560]{2,1,0:T(4,128)(2,1)S(1)}, u32[]{:S(2)}, u32[]{:S(2)}) %all-to-all-start.1) | async-done | bytes 327712 | tf_op jit(solution)/shard_map/all_to_all | solution.py:216
  (152 shorter events, 20.3 us)
Async XLA Ops:
  4.0 16.9 %all-to-all-start = ((bf16[16,4,2176]{2,1,0:T(4,128)(2,1)}), bf16[16,4,2176]{2,1,0:T(4,128)(2,1)S(1)}, u32[]{:S(2)}, u32[]{:S(2)}) async-start(bf16[16,4,2176]{2,1,0:T(4,128)(2,1)} %bitcast.2), calls=%async_computation | async-start | bytes 557056 | tf_op jit(solution)/shard_map/all_to_all | solution.py:146
  21.0 8.2 %collective-permute-start.2 = (bf16[64,1152]{1,0:T(8,128)(2,1)S(1)}, bf16[64,1152]{1,0:T(8,128)(2,1)S(1)}, u32[]{:S(2)}, u32[]{:S(2)}) collective-permute-start(bf16[64,1152]{1,0:T(8,128)(2,1)S(1)} %get-tuple-element.69), channel_id=1, source_target_pairs={{0,2},{1,3},{2,4},{3,5},{4,6},{5,7},{6,0},{7,1},{8,10},{9,11},{10,... | collective-permute-start | bytes 442376 | tf_op jit(solution)/shard_map/ppermute | solution.py:24
  22.7 11.7 %collective-permute-start = (bf16[64,1152]{1,0:T(8,128)(2,1)S(1)}, bf16[64,1152]{1,0:T(8,128)(2,1)S(1)}, u32[]{:S(2)}, u32[]{:S(2)}) collective-permute-start(bf16[64,1152]{1,0:T(8,128)(2,1)S(1)} %get-tuple-element.69), channel_id=1, source_target_pairs={{0,6},{1,7},{2,0},{3,1},{4,2},{5,3},{6,4},{7,5},{8,14},{9,15},{10,... | collective-permute-start | bytes 442376 | tf_op jit(solution)/shard_map/ppermute | solution.py:24
  24.4 10.1 %collective-permute-start.1 = (bf16[64,1152]{1,0:T(8,128)(2,1)S(1)}, bf16[64,1152]{1,0:T(8,128)(2,1)S(1)}, u32[]{:S(2)}, u32[]{:S(2)}) collective-permute-start(bf16[64,1152]{1,0:T(8,128)(2,1)S(1)} %get-tuple-element.69), channel_id=1, source_target_pairs={{0,4},{1,5},{2,6},{3,7},{4,0},{5,1},{6,2},{7,3},{8,12},{9,13},{10,... | collective-permute-start | bytes 442376 | tf_op jit(solution)/shard_map/ppermute | solution.py:24
  29.2 8.5 %collective-permute-start.6 = (bf16[64,1024]{1,0:T(8,128)(2,1)S(1)}, bf16[64,1024]{1,0:T(8,128)(2,1)S(1)}, u32[]{:S(2)}, u32[]{:S(2)}) collective-permute-start(bf16[64,1024]{1,0:T(8,128)(2,1)S(1)} %slice.299), channel_id=1, source_target_pairs={{0,2},{1,3},{2,4},{3,5},{4,6},{5,7},{6,0},{7,1},{8,10},{9,11},{10,... | collective-permute-start | bytes 393224 | tf_op jit(solution)/shard_map/ppermute | solution.py:24
  29.2 8.5 %collective-permute-start.5 = (bf16[64,1024]{1,0:T(8,128)(2,1)S(1)}, bf16[64,1024]{1,0:T(8,128)(2,1)S(1)}, u32[]{:S(2)}, u32[]{:S(2)}) collective-permute-start(bf16[64,1024]{1,0:T(8,128)(2,1)S(1)} %slice.299), channel_id=1, source_target_pairs={{0,4},{1,5},{2,6},{3,7},{4,0},{5,1},{6,2},{7,3},{8,12},{9,13},{10,... | collective-permute-start | bytes 393224 | tf_op jit(solution)/shard_map/ppermute | solution.py:24
  32.3 5.4 %collective-permute-start.4 = (bf16[64,1024]{1,0:T(8,128)(2,1)S(1)}, bf16[64,1024]{1,0:T(8,128)(2,1)S(1)}, u32[]{:S(2)}, u32[]{:S(2)}) collective-permute-start(bf16[64,1024]{1,0:T(8,128)(2,1)S(1)} %slice.299), channel_id=1, source_target_pairs={{0,6},{1,7},{2,0},{3,1},{4,2},{5,3},{6,4},{7,5},{8,14},{9,15},{10,... | collective-permute-start | bytes 393224 | tf_op jit(solution)/shard_map/ppermute | solution.py:24
  34.5 3.5 %collective-permute-start.3 = (bf16[256,1152]{1,0:T(8,128)(2,1)S(1)}, bf16[256,1152]{1,0:T(8,128)(2,1)S(1)}, u32[]{:S(2)}, u32[]{:S(2)}) collective-permute-start(bf16[256,1152]{1,0:T(8,128)(2,1)S(1)} %constant_dynamic-update-slice_fusion.26), channel_id=1, source_target_pairs={{0,1},{1,0},{2,3},{3,2},{4,5},{5,4},{6,7},{7,6},{8,9},{9,8},{10,11... | collective-permute-start | bytes 1769480 | tf_op jit(solution)/shard_map/ppermute | solution.py:24
  34.8 3.6 %dynamic-slice-start = ((f32[8192]{0:T(1024)}, s32[]{:T(128)}), f32[1024]{0:T(1024)S(1)}, s32[]{:S(2)}) async-start(f32[8192]{0:T(1024)} %param.7, s32[]{:T(128)} %select_n.78), calls=%async_computation.2 | async-start | bytes 8704 | tf_op jit(solution)/shard_map/dynamic_slice | solution.py:159
  37.8 5.7 %collective-permute-start.7 = (bf16[256,1024]{1,0:T(8,128)(2,1)S(1)}, bf16[256,1024]{1,0:T(8,128)(2,1)S(1)}, u32[]{:S(2)}, u32[]{:S(2)}) collective-permute-start(bf16[256,1024]{1,0:T(8,128)(2,1)S(1)} %constant_dynamic-update-slice_fusion.20), channel_id=1, source_target_pairs={{0,1},{1,0},{2,3},{3,2},{4,5},{5,4},{6,7},{7,6},{8,9},{9,8},{10,11... | collective-permute-start | bytes 1572872 | tf_op jit(solution)/shard_map/ppermute | solution.py:24
  38.0 2.0 %copy-start.7 = (bf16[1024,1792]{1,0:T(8,128)(2,1)S(1)}, bf16[1024,1792]{1,0:T(8,128)(2,1)}, u32[]{:S(2)}) copy-start(bf16[1024,1792]{1,0:T(8,128)(2,1)} %param.9) | copy-start | bytes 11010052
  40.0 2.0 %copy-start.9 = (bf16[1024,1792]{1,0:T(8,128)(2,1)S(1)}, bf16[1024,1792]{1,0:T(8,128)(2,1)}, u32[]{:S(2)}) copy-start(bf16[1024,1792]{1,0:T(8,128)(2,1)} %param.8) | copy-start | bytes 11010052
  44.7 4.6 %copy-start = (bf16[1792,1024]{1,0:T(8,128)(2,1)S(1)}, bf16[1792,1024]{1,0:T(8,128)(2,1)}, u32[]{:S(2)}) copy-start(bf16[1792,1024]{1,0:T(8,128)(2,1)} %param.10) | copy-start | bytes 11010052
  45.8 29.8 %collective-permute-start.8 = (bf16[64,3584]{1,0:T(8,128)(2,1)S(1)}, bf16[64,3584]{1,0:T(8,128)(2,1)S(1)}, u32[]{:S(2)}, u32[]{:S(2)}) collective-permute-start(bf16[64,3584]{1,0:T(8,128)(2,1)S(1)} %get-tuple-element.18), channel_id=1, source_target_pairs={{0,16},{1,17},{2,18},{3,19},{4,20},{5,21},{6,22},{7,23},{8,24},{9,... | collective-permute-start | bytes 1376264 | tf_op jit(solution)/shard_map/ppermute | solution.py:24
  46.5 29.2 %collective-permute-start.9 = (bf16[64,3584]{1,0:T(8,128)(2,1)S(1)}, bf16[64,3584]{1,0:T(8,128)(2,1)S(1)}, u32[]{:S(2)}, u32[]{:S(2)}) collective-permute-start(bf16[64,3584]{1,0:T(8,128)(2,1)S(1)} %get-tuple-element.19), channel_id=1, source_target_pairs={{0,48},{1,49},{2,50},{3,51},{4,52},{5,53},{6,54},{7,55},{8,56},{9,... | collective-permute-start | bytes 1376264 | tf_op jit(solution)/shard_map/ppermute | solution.py:24
  49.1 23.0 %collective-permute-start.13 = (bf16[64,3584]{1,0:T(8,128)(2,1)S(1)}, bf16[64,3584]{1,0:T(8,128)(2,1)S(1)}, u32[]{:S(2)}, u32[]{:S(2)}) collective-permute-start(bf16[64,3584]{1,0:T(8,128)(2,1)S(1)} %get-tuple-element.20), channel_id=1, source_target_pairs={{0,64},{1,65},{2,66},{3,67},{4,68},{5,69},{6,70},{7,71},{8,72},{9,... | collective-permute-start | bytes 1376264 | tf_op jit(solution)/shard_map/ppermute | solution.py:24
  51.6 13.3 %collective-permute-start.10 = (bf16[64,1792]{1,0:T(8,128)(2,1)S(1)}, bf16[64,1792]{1,0:T(8,128)(2,1)S(1)}, u32[]{:S(2)}, u32[]{:S(2)}) collective-permute-start(bf16[64,1792]{1,0:T(8,128)(2,1)S(1)} %get-tuple-element.43), channel_id=1, source_target_pairs={{0,16},{1,17},{2,18},{3,19},{4,20},{5,21},{6,22},{7,23},{8,24},{9,... | collective-permute-start | bytes 688136 | tf_op jit(solution)/shard_map/ppermute | solution.py:24
  51.9 13.2 %collective-permute-start.11 = (bf16[64,1792]{1,0:T(8,128)(2,1)S(1)}, bf16[64,1792]{1,0:T(8,128)(2,1)S(1)}, u32[]{:S(2)}, u32[]{:S(2)}) collective-permute-start(bf16[64,1792]{1,0:T(8,128)(2,1)S(1)} %get-tuple-element.45), channel_id=1, source_target_pairs={{0,48},{1,49},{2,50},{3,51},{4,52},{5,53},{6,54},{7,55},{8,56},{9,... | collective-permute-start | bytes 688136 | tf_op jit(solution)/shard_map/ppermute | solution.py:24
  65.0 7.2 %collective-permute-start.14 = (bf16[64,1792]{1,0:T(8,128)(2,1)S(1)}, bf16[64,1792]{1,0:T(8,128)(2,1)S(1)}, u32[]{:S(2)}, u32[]{:S(2)}) collective-permute-start(bf16[64,1792]{1,0:T(8,128)(2,1)S(1)} %get-tuple-element.44), channel_id=1, source_target_pairs={{0,64},{1,65},{2,66},{3,67},{4,68},{5,69},{6,70},{7,71},{8,72},{9,... | collective-permute-start | bytes 688136 | tf_op jit(solution)/shard_map/ppermute | solution.py:24
  72.4 10.1 %collective-permute-start.15 = (bf16[32,5376]{1,0:T(8,128)(2,1)S(1)}, bf16[32,5376]{1,0:T(8,128)(2,1)S(1)}, u32[]{:S(2)}, u32[]{:S(2)}) collective-permute-start(bf16[32,5376]{1,0:T(8,128)(2,1)S(1)} %get-tuple-element.61), channel_id=1, source_target_pairs={{0,16},{1,17},{2,18},{3,19},{4,20},{5,21},{6,22},{7,23},{8,24},{9,... | collective-permute-start | bytes 1032200 | tf_op jit(solution)/shard_map/ppermute | solution.py:24
  72.4 10.0 %collective-permute-start.17 = (bf16[32,5376]{1,0:T(8,128)(2,1)S(1)}, bf16[32,5376]{1,0:T(8,128)(2,1)S(1)}, u32[]{:S(2)}, u32[]{:S(2)}) collective-permute-start(bf16[32,5376]{1,0:T(8,128)(2,1)S(1)} %get-tuple-element.62), channel_id=1, source_target_pairs={{0,48},{1,49},{2,50},{3,51},{4,52},{5,53},{6,54},{7,55},{8,56},{9,... | collective-permute-start | bytes 1032200 | tf_op jit(solution)/shard_map/ppermute | solution.py:24
  75.9 15.7 %collective-permute-start.12 = (bf16[64,5376]{1,0:T(8,128)(2,1)S(1)}, bf16[64,5376]{1,0:T(8,128)(2,1)S(1)}, u32[]{:S(2)}, u32[]{:S(2)}) collective-permute-start(bf16[64,5376]{1,0:T(8,128)(2,1)S(1)} %pad_maximum_fusion.3), channel_id=1, source_target_pairs={{0,64},{1,65},{2,66},{3,67},{4,68},{5,69},{6,70},{7,71},{8,72},{9,... | collective-permute-start | bytes 2064392 | tf_op jit(solution)/shard_map/ppermute | solution.py:24
  82.6 15.5 %collective-permute-start.18 = (bf16[64,5376]{1,0:T(8,128)(2,1)S(1)}, bf16[64,5376]{1,0:T(8,128)(2,1)S(1)}, u32[]{:S(2)}, u32[]{:S(2)}) collective-permute-start(bf16[64,5376]{1,0:T(8,128)(2,1)S(1)} %pad_maximum_fusion.5), channel_id=1, source_target_pairs={{0,48},{1,49},{2,50},{3,51},{4,52},{5,53},{6,54},{7,55},{8,56},{9,... | collective-permute-start | bytes 2064392 | tf_op jit(solution)/shard_map/ppermute | solution.py:24
  85.7 16.0 %collective-permute-start.16 = (bf16[64,5376]{1,0:T(8,128)(2,1)S(1)}, bf16[64,5376]{1,0:T(8,128)(2,1)S(1)}, u32[]{:S(2)}, u32[]{:S(2)}) collective-permute-start(bf16[64,5376]{1,0:T(8,128)(2,1)S(1)} %pad_maximum_fusion.4), channel_id=1, source_target_pairs={{0,16},{1,17},{2,18},{3,19},{4,20},{5,21},{6,22},{7,23},{8,24},{9,... | collective-permute-start | bytes 2064392 | tf_op jit(solution)/shard_map/ppermute | solution.py:24
  102.3 15.6 %collective-permute-start.20 = (bf16[64,5376]{1,0:T(8,128)(2,1)S(1)}, bf16[64,5376]{1,0:T(8,128)(2,1)S(1)}, u32[]{:S(2)}, u32[]{:S(2)}) collective-permute-start(bf16[64,5376]{1,0:T(8,128)(2,1)S(1)} %get-tuple-element.60), channel_id=1, source_target_pairs={{0,16},{1,17},{2,18},{3,19},{4,20},{5,21},{6,22},{7,23},{8,24},{9,... | collective-permute-start | bytes 2064392 | tf_op jit(solution)/shard_map/ppermute | solution.py:24
  102.4 15.6 %collective-permute-start.19 = (bf16[64,5376]{1,0:T(8,128)(2,1)S(1)}, bf16[64,5376]{1,0:T(8,128)(2,1)S(1)}, u32[]{:S(2)}, u32[]{:S(2)}) collective-permute-start(bf16[64,5376]{1,0:T(8,128)(2,1)S(1)} %get-tuple-element.60), channel_id=1, source_target_pairs={{0,48},{1,49},{2,50},{3,51},{4,52},{5,53},{6,54},{7,55},{8,56},{9,... | collective-permute-start | bytes 2064392 | tf_op jit(solution)/shard_map/ppermute | solution.py:24
  105.6 15.7 %collective-permute-start.23 = (bf16[64,5376]{1,0:T(8,128)(2,1)S(1)}, bf16[64,5376]{1,0:T(8,128)(2,1)S(1)}, u32[]{:S(2)}, u32[]{:S(2)}) collective-permute-start(bf16[64,5376]{1,0:T(8,128)(2,1)S(1)} %get-tuple-element.60), channel_id=1, source_target_pairs={{0,64},{1,65},{2,66},{3,67},{4,68},{5,69},{6,70},{7,71},{8,72},{9,... | collective-permute-start | bytes 2064392 | tf_op jit(solution)/shard_map/ppermute | solution.py:24
  117.9 12.3 %collective-permute-start.21 = (bf16[32,5376]{1,0:T(8,128)(2,1)S(1)}, bf16[32,5376]{1,0:T(8,128)(2,1)S(1)}, u32[]{:S(2)}, u32[]{:S(2)}) collective-permute-start(bf16[32,5376]{1,0:T(8,128)(2,1)S(1)} %slice.327), channel_id=1, source_target_pairs={{0,16},{1,17},{2,18},{3,19},{4,20},{5,21},{6,22},{7,23},{8,24},{9,... | collective-permute-start | bytes 1032200 | tf_op jit(solution)/shard_map/ppermute | solution.py:24
  118.0 12.2 %collective-permute-start.22 = (bf16[32,5376]{1,0:T(8,128)(2,1)S(1)}, bf16[32,5376]{1,0:T(8,128)(2,1)S(1)}, u32[]{:S(2)}, u32[]{:S(2)}) collective-permute-start(bf16[32,5376]{1,0:T(8,128)(2,1)S(1)} %slice.328), channel_id=1, source_target_pairs={{0,48},{1,49},{2,50},{3,51},{4,52},{5,53},{6,54},{7,55},{8,56},{9,... | collective-permute-start | bytes 1032200 | tf_op jit(solution)/shard_map/ppermute | solution.py:24
  121.3 22.8 %collective-permute-start.26 = (bf16[64,5376]{1,0:T(8,128)(2,1)S(1)}, bf16[64,5376]{1,0:T(8,128)(2,1)S(1)}, u32[]{:S(2)}, u32[]{:S(2)}) collective-permute-start(bf16[64,5376]{1,0:T(8,128)(2,1)S(1)} %collective-permute-done.23), channel_id=1, source_target_pairs={{0,16},{1,17},{2,18},{3,19},{4,20},{5,21},{6,22},{7,23},{8,24},{9,... | collective-permute-start | bytes 2064392 | tf_op jit(solution)/shard_map/ppermute | solution.py:24
  121.3 17.4 %collective-permute-start.24 = (bf16[64,5376]{1,0:T(8,128)(2,1)S(1)}, bf16[64,5376]{1,0:T(8,128)(2,1)S(1)}, u32[]{:S(2)}, u32[]{:S(2)}) collective-permute-start(bf16[64,5376]{1,0:T(8,128)(2,1)S(1)} %collective-permute-done.23), channel_id=1, source_target_pairs={{0,48},{1,49},{2,50},{3,51},{4,52},{5,53},{6,54},{7,55},{8,56},{9,... | collective-permute-start | bytes 2064392 | tf_op jit(solution)/shard_map/ppermute | solution.py:24
  124.6 5.8 %copy-start.8 = (bf16[1024,1792]{1,0:T(8,128)(2,1)S(1)}, bf16[1024,1792]{1,0:T(8,128)(2,1)}, u32[]{:S(2)}) copy-start(bf16[1024,1792]{1,0:T(8,128)(2,1)} %param.9) | copy-start | bytes 11010052
  131.6 2.2 %copy-start.10 = (bf16[1024,1792]{1,0:T(8,128)(2,1)S(1)}, bf16[1024,1792]{1,0:T(8,128)(2,1)}, u32[]{:S(2)}) copy-start(bf16[1024,1792]{1,0:T(8,128)(2,1)} %param.8) | copy-start | bytes 11010052
  132.8 11.2 %collective-permute-start.25 = (bf16[64,5376]{1,0:T(8,128)(2,1)S(1)}, bf16[64,5376]{1,0:T(8,128)(2,1)S(1)}, u32[]{:S(2)}, u32[]{:S(2)}) collective-permute-start(bf16[64,5376]{1,0:T(8,128)(2,1)S(1)} %pad_maximum_fusion.7), channel_id=1, source_target_pairs={{0,64},{1,65},{2,66},{3,67},{4,68},{5,69},{6,70},{7,71},{8,72},{9,... | collective-permute-start | bytes 2064392 | tf_op jit(solution)/shard_map/ppermute | solution.py:24
  144.2 14.2 %copy-start.6 = (bf16[512,5376]{1,0:T(8,128)(2,1)}, bf16[512,5376]{1,0:T(8,128)(2,1)S(1)}, u32[]{:S(2)}) copy-start(bf16[512,5376]{1,0:T(8,128)(2,1)S(1)} %get-tuple-element.46) | copy-start | bytes 16515076
  149.0 4.3 %collective-permute-start.27 = (f32[264,2048]{1,0:T(8,128)S(1)}, f32[264,2048]{1,0:T(8,128)S(1)}, u32[]{:S(2)}, u32[]{:S(2)}) collective-permute-start(f32[264,2048]{1,0:T(8,128)S(1)} %select_maximum_fusion), channel_id=1, source_target_pairs={{0,1},{1,0},{2,3},{3,2},{4,5},{5,4},{6,7},{7,6},{8,9},{9,8},{10,11... | collective-permute-start | bytes 6488072 | tf_op jit(solution)/shard_map/ppermute | solution.py:24
  153.8 11.1 %collective-permute-start.30 = (bf16[64,2176]{1,0:T(8,128)(2,1)S(1)}, bf16[64,2176]{1,0:T(8,128)(2,1)S(1)}, u32[]{:S(2)}, u32[]{:S(2)}) collective-permute-start(bf16[64,2176]{1,0:T(8,128)(2,1)S(1)} %get-tuple-element.71), channel_id=1, source_target_pairs={{0,4},{1,5},{2,6},{3,7},{4,0},{5,1},{6,2},{7,3},{8,12},{9,13},{10,... | collective-permute-start | bytes 835592 | tf_op jit(solution)/shard_map/ppermute | solution.py:24
  156.4 14.0 %collective-permute-start.29 = (bf16[64,2176]{1,0:T(8,128)(2,1)S(1)}, bf16[64,2176]{1,0:T(8,128)(2,1)S(1)}, u32[]{:S(2)}, u32[]{:S(2)}) collective-permute-start(bf16[64,2176]{1,0:T(8,128)(2,1)S(1)} %get-tuple-element.72), channel_id=1, source_target_pairs={{0,6},{1,7},{2,0},{3,1},{4,2},{5,3},{6,4},{7,5},{8,14},{9,15},{10,... | collective-permute-start | bytes 835592 | tf_op jit(solution)/shard_map/ppermute | solution.py:24
  158.4 11.9 %collective-permute-start.28 = (bf16[64,2176]{1,0:T(8,128)(2,1)S(1)}, bf16[64,2176]{1,0:T(8,128)(2,1)S(1)}, u32[]{:S(2)}, u32[]{:S(2)}) collective-permute-start(bf16[64,2176]{1,0:T(8,128)(2,1)S(1)} %get-tuple-element.73), channel_id=1, source_target_pairs={{0,2},{1,3},{2,4},{3,5},{4,6},{5,7},{6,0},{7,1},{8,10},{9,11},{10,... | collective-permute-start | bytes 835592 | tf_op jit(solution)/shard_map/ppermute | solution.py:24
  164.9 5.5 %copy-start.2 = (bf16[64,2176]{1,0:T(8,128)(2,1)}, bf16[64,2176]{1,0:T(8,128)(2,1)S(1)}, u32[]{:S(2)}) copy-start(bf16[64,2176]{1,0:T(8,128)(2,1)S(1)} %collective-permute-done.30) | copy-start | bytes 835588
  170.4 0.7 copy-start.3
  170.4 0.8 copy-start.4
  173.5 14.5 %all-to-all-start.1 = ((bf16[16,4,2560]{2,1,0:T(4,128)(2,1)}), bf16[16,4,2560]{2,1,0:T(4,128)(2,1)S(1)}, u32[]{:S(2)}, u32[]{:S(2)}) async-start(bf16[16,4,2560]{2,1,0:T(4,128)(2,1)} %pad_maximum_fusion.8), calls=%async_computation.1 | async-start | bytes 655360 | tf_op jit(solution)/shard_map/all_to_all | solution.py:216
  184.2 5.0 %copy-start.1 = (bf16[4,8192]{1,0:T(4,128)(2,1)S(1)}, bf16[4,8192]{1,0:T(4,128)(2,1)}, u32[]{:S(2)}) copy-start(bf16[4,8192]{1,0:T(4,128)(2,1)} %param.6) | copy-start | bytes 196612
  184.2 5.0 %copy-start.5 = (f32[8192]{0:T(1024)S(1)}, f32[8192]{0:T(1024)}, u32[]{:S(2)}) copy-start(f32[8192]{0:T(1024)} %param.7) | copy-start | bytes 98308

commit v4 on v3

v4 whole, which is shorter than its diff:
```python
import jax
import jax.numpy as jnp
from jax import lax
from jax.sharding import Mesh, PartitionSpec as P

EPS = 1e-05
F32 = jnp.float32
BF16 = jnp.bfloat16
ZS, XS, HS, YS, CS = 2, 4, 2, 4, 2
AXES = ("z", "x", "h", "y", "core")


def send(value, z=0, x=0, h=0, y=0, c=0):
    pairs = []
    for z0 in range(ZS):
        for x0 in range(XS):
            for h0 in range(HS):
                for y0 in range(YS):
                    for c0 in range(CS):
                        source = (((z0 * XS + x0) * HS + h0) * YS + y0) * CS + c0
                        z1, x1, h1 = (z0 + z) % ZS, (x0 + x) % XS, (h0 + h) % HS
                        y1, c1 = (y0 + y) % YS, (c0 + c) % CS
                        pairs.append((source, (((z1 * XS + x1) * HS + h1) * YS + y1) * CS + c1))
    return lax.ppermute(value, AXES, pairs)


def product(left, right):
    return jnp.dot(left, right, preferred_element_type=F32)


def product_right_t(left, right):
    return lax.dot_general(left, right, (((1,), (1,)), ((), ())), preferred_element_type=F32)


def product_left_t(left, right):
    return lax.dot_general(left, right, (((0,), (0,)), ((), ())), preferred_element_type=F32)


def rounded(value):
    return lax.reduce_precision(value, 8, 7)


def parts_of(value, count):
    parts = []
    for _ in range(count):
        top = rounded(value)
        parts.append(top.astype(BF16))
        value = value - top
    return parts


def gather_half(own, x):
    n = own.shape[1]
    over_y = {0: own}
    for dy in (1, 3, 2):
        over_y[-dy % YS] = send(own, y=dy)
    core = jnp.zeros((128, n), own.dtype)
    for dy in range(YS):
        core = lax.dynamic_update_slice(core, over_y[dy], ((dy - x) % XS * 32, 0))
    return core, over_y[3]


def both_cores(core):
    both = (core, send(core, c=1))
    return jnp.concatenate([v[i * 32 : i * 32 + 32] for i in range(XS) for v in both], axis=0)


def sum_over_core(partial, gain_partial):
    n = partial.shape[1]
    split = [partial[i * 32 : i * 32 + 32] for i in range(2 * XS)]
    give = split[1::2]
    if gain_partial is not None:
        give = give + [jnp.pad(gain_partial, ((0, 0), (0, n - 128)))]
    taken = send(jnp.concatenate(give, axis=0), c=1)
    keep = jnp.concatenate(split[::2], axis=0) + taken[:128]
    if gain_partial is not None:
        gain_partial = gain_partial + taken[128:, :128]
    return keep, gain_partial


def sum_over_y(keep, gain, x):
    n = keep.shape[1]

    def piece(dy):
        return lax.dynamic_slice(keep, ((dy - x) % XS * 32, 0), (32, n))

    def gain_of(parts):
        return parts[:8].astype(F32) + parts[8:16].astype(F32)

    if gain is not None:
        parts = jnp.concatenate(parts_of(gain, 2) + [jnp.zeros((16, 128), BF16)], axis=0)
        gains = {0: gain_of(parts)}
    total = piece(0)
    for dy in (1, 3, 2):
        message = piece(dy).astype(BF16)
        if gain is not None:
            message = jnp.concatenate([message, parts], axis=1)
        got = send(message, y=dy)
        total = total + got[:, :n].astype(F32)
        if gain is not None:
            gains[dy] = gain_of(got[:, n:])
    if gain is not None:
        gain = (gains[0] + gains[2]) + (gains[1] + gains[3])
    return total, gain


def sum_over_row(near, far):
    m12 = send(far[2].astype(BF16), z=1).astype(F32)
    m11 = send(far[1].astype(BF16), x=1).astype(F32)
    m13 = send(far[3].astype(BF16), x=3).astype(F32)
    a02 = near[2] + m12
    h = a02.shape[0] // 2
    n1 = send(a02[:h].astype(BF16), x=1).astype(F32)
    n2 = send(a02[h:].astype(BF16), x=3).astype(F32)
    q = send((far[0] + m11 + m13).astype(BF16), z=1).astype(F32)
    a01 = jnp.concatenate([near[1][:h] + n1, near[1][h:]], axis=0)
    a03 = jnp.concatenate([near[3][:h], near[3][h:] + n2], axis=0)
    r1 = send(a01.astype(BF16), x=1).astype(F32)
    r2 = send(a03.astype(BF16), x=3).astype(F32)
    return near[0] + q + r1 + r2


def gather_over_row(own):
    h = own.shape[0] // 2
    a = send(own, x=1)
    b = send(own, x=3)
    p = send(own, z=1)
    a2 = send(a[:h], x=1)
    b2 = send(b[h:], x=3)
    pa = send(p, x=1)
    pb = send(p, x=3)
    across = jnp.concatenate([a2, b2], axis=0)
    p2 = send(across, z=1)
    return (
        jnp.concatenate([own, b, across, a], axis=0),
        jnp.concatenate([p, pb, p2, pa], axis=0),
    )


def per_device(inputs, rms_gain_vector, gate_weight, up_weight, down_weight, out_grad):
    z, x = lax.axis_index("z"), lax.axis_index("x")
    row = z * XS + x
    width = gate_weight.shape[1]

    value_entries = inputs.astype(F32)
    inverse_rms = lax.rsqrt(jnp.mean(value_entries * value_entries, axis=1, keepdims=True) + EPS)
    side = jnp.concatenate(parts_of(inverse_rms, 3) + [jnp.zeros((4, 125), BF16)], axis=1)
    message = jnp.concatenate(
        [
            inputs.reshape(4, 8, 1024),
            out_grad.reshape(4, 8, 1024),
            jnp.broadcast_to(side[:, None, :], (4, 8, 128)),
        ],
        axis=2,
    )
    message = jnp.broadcast_to(jnp.transpose(message, (1, 0, 2))[None], (HS, 8, 4, 2176))
    block = lax.all_to_all(
        message.reshape(16, 4, 2176), ("h", "z", "x"), split_axis=0, concat_axis=0, tiled=True
    )
    block = block.reshape(64, 2176)
    gain_block = lax.dynamic_slice(rms_gain_vector, (row * 1024,), (1024,))

    def normed_of(tokens):
        inverse = (
            tokens[:, 2048:2049].astype(F32)
            + tokens[:, 2049:2050].astype(F32)
            + tokens[:, 2050:2051].astype(F32)
        )
        estimate = tokens[:, :1024].astype(F32) * inverse
        return estimate, (estimate * gain_block).astype(BF16), tokens[:, 1024:2048]

    def partials(normed, grad):
        return jnp.concatenate(
            [
                product(normed, gate_weight),
                product(normed, up_weight),
                product_right_t(grad, down_weight),
            ],
            axis=1,
        ).reshape(4, 64, 3 * width)

    far_core, first = gather_half(lax.dynamic_slice(block, ((1 - z) * 32, 0), (32, 2176)), x)
    near_block, _ = lax.optimization_barrier(
        (lax.dynamic_slice(block, (z * 32, 0), (32, 2176)), first)
    )
    near_core, _ = gather_half(near_block, x)
    far_estimate, far_normed, far_grad = normed_of(both_cores(far_core))
    far = partials(far_normed, far_grad)
    near_core, far = lax.optimization_barrier((near_core, far))
    near_estimate, near_normed, near_grad = normed_of(both_cores(near_core))
    near = partials(near_normed, near_grad)
    sums = sum_over_row(near, far)
    gate, up, hidden_grad = sums[:, :width], sums[:, width : 2 * width], sums[:, 2 * width :]
    sigma = jax.nn.sigmoid(gate)
    silu = gate * sigma
    units = jnp.concatenate(
        [
            (silu * up).astype(BF16),
            (hidden_grad * up * sigma * (1.0 + gate * (1.0 - sigma))).astype(BF16),
            (hidden_grad * silu).astype(BF16),
        ],
        axis=1,
    )
    units = gather_over_row(units)

    def backward(units):
        hidden, gate_grad, up_grad = units[:, :width], units[:, width : 2 * width], units[:, 2 * width :]
        grad = product_right_t(gate_grad, gate_weight) + product_right_t(up_grad, up_weight)
        return jnp.concatenate([product(hidden, down_weight), grad], axis=1)

    near_partial = backward(units[0])
    near_total, _ = sum_over_y(sum_over_core(near_partial, None)[0], None, x)
    far_partial = backward(units[1])
    gain_partial = jnp.sum(near_partial[:, 1024:] * near_estimate, axis=0) + jnp.sum(
        far_partial[:, 1024:] * far_estimate, axis=0
    )
    far_total, gain = sum_over_y(*sum_over_core(far_partial, gain_partial.reshape(8, 128)), x)

    units = jnp.concatenate(units, axis=0)
    hidden, gate_grad, up_grad = units[:, :width], units[:, width : 2 * width], units[:, 2 * width :]
    normed = jnp.concatenate([near_normed, far_normed], axis=0)
    grad_full = jnp.concatenate([near_grad, far_grad], axis=0)
    down_weight_grad = product_left_t(hidden, grad_full).astype(BF16)
    gate_weight_grad = product_left_t(normed, gate_grad).astype(BF16)
    up_weight_grad = product_left_t(normed, up_grad).astype(BF16)
    far_total, down_weight_grad, gate_weight_grad = lax.optimization_barrier(
        (far_total, down_weight_grad, gate_weight_grad)
    )

    gain_parts = [p.reshape(4, 256) for p in parts_of(gain, 2)]
    gain_rows = jnp.broadcast_to(jnp.concatenate(gain_parts, axis=1)[None], (16, 4, 512))
    total = jnp.zeros((64, 2048), BF16)
    total = lax.dynamic_update_slice(total, near_total.astype(BF16), (z * 32, 0))
    total = lax.dynamic_update_slice(total, far_total.astype(BF16), ((1 - z) * 32, 0))
    message = jnp.concatenate([total.reshape(16, 4, 2048), gain_rows], axis=2)
    back = lax.all_to_all(message, ("h", "z", "x"), split_axis=0, concat_axis=0, tiled=True)
    back = back.reshape(HS, 8, 4, 2560).astype(F32)
    gain_grad = back[..., 2048:2304] + back[..., 2304:]
    gain_grad = (gain_grad[0] + gain_grad[1]).reshape(8192)
    back = back[0, :, :, :2048] + back[1, :, :, :2048]
    outputs = jnp.transpose(back[..., :1024].astype(BF16), (1, 0, 2)).reshape(4, 8192)
    normed_grad = jnp.transpose(back[..., 1024:], (1, 0, 2)).reshape(4, 8192)

    normalized = value_entries * inverse_rms
    scaled = normed_grad * rms_gain_vector
    input_gradient = inverse_rms * (
        scaled - normalized * jnp.mean(scaled * normalized, axis=1, keepdims=True)
    )
    return (
        outputs,
        input_gradient.astype(BF16),
        gain_grad,
        gate_weight_grad,
        up_weight_grad,
        down_weight_grad,
    )


def solution(mesh):
    fine = Mesh(mesh.devices.reshape(ZS, XS, HS, YS, CS), AXES)
    row, col = AXES[:2], AXES[2:]
    in_specs = (P(AXES, None), P(), P(row, col), P(row, col), P(col, row), P(AXES, None))
    out_specs = (P(AXES, None), P(AXES, None), P(), P(row, col), P(row, col), P(col, row))
    return jax.shard_map(
        per_device, mesh=fine, in_specs=in_specs, out_specs=out_specs, check_vma=False
    )
```

time: 192 us -> 185 us (0.964)
  waiting for transfers between devices: 90.8 us -> 83.3 us
    ppermute x31 -> x32, waiting for transfers between devices: 78.1 us -> 70.6 us  [send(): return lax.ppermute(value, AXES, pairs)]
    unnamed x34 -> x52, local copies, waits for them, and re-layouts: 5 us -> 6.93 us
    ppermute x31 -> x32, starting transfers between devices: 40.8 us -> 41.5 us  [send(): return lax.ppermute(value, AXES, pairs)]
  transfers between devices with their start and end apart: 33 -> 34, of which waited for: 17 -> 17; matrix products, arithmetic and copies ran while one was open for 13% -> 15% of each run, Pallas kernels for 0% -> 0%
where the time goes in v4:
time: 185 us; the launch traced here: 184 us
  waiting for transfers between devices  83.3 us (45%)
  starting transfers between devices  54.6 us (30%)
  matrix products  27.2 us (15%)
  local copies, waits for them, and re-layouts  10.3 us (6%)
  other arithmetic  7.27 us (4%)
    ppermute x32, waiting for transfers between devices, send(): return lax.ppermute(value, AXES, pairs)  70.6 us
    ppermute x32, starting transfers between devices, send(): return lax.ppermute(value, AXES, pairs)  41.5 us
    dot_general x3, matrix products, product_left_t(): lax.dot_general(left, right, (((0,), (0,)), ((), ())), preferred_element_...  13.4 us
    all_to_all x1, waiting for transfers between devices, per_device(): lax.all_to_all(message.reshape(16, 4, 2176), ('h', 'z', 'x'), split_axis=...  8.83 us
    all_to_all x1, starting transfers between devices, per_device(): lax.all_to_all(message.reshape(16, 4, 2176), ('h', 'z', 'x'), split_axis=...  7.96 us
    dot_general x6, matrix products, product_right_t(): lax.dot_general(left, right, (((1,), (1,)), ((), ())), preferred_element_...  7.03 us
    unnamed x52, local copies, waits for them, and re-layouts  6.93 us
    dot_general x6, matrix products, product(): return jnp.dot(left, right, preferred_element_type=F32)  6.8 us
  transfers between devices with their start and end apart: 34, of which 17 were waited for; matrix products, arithmetic and copies ran while one was open for 15% of the time, Pallas kernels for 0%

profile of v4, /device:TPU:0, one launch (start us, length us, event | category | flops | bytes accessed | tf_op | source)
XLA Modules:
  0.0 184.3 jit_solution(11870041770542168033)
XLA Ops:
  4.0 8.0 %all-to-all-start = ((bf16[16,4,2176]{2,1,0:T(4,128)(2,1)}), bf16[16,4,2176]{2,1,0:T(4,128)(2,1)S(1)}, u32[]{:S(2)}, u32[]{:S(2)}) async-start(bf16[16,4,2176]{2,1,0:T(4,128)(2,1)} %bitcast.2), calls=%async_computation | async-start | bytes 557056 | tf_op jit(solution)/shard_map/all_to_all | solution.py:157
  12.0 8.8 %all-to-all-done = bf16[16,4,2176]{2,1,0:T(4,128)(2,1)S(1)} async-done(((bf16[16,4,2176]{2,1,0:T(4,128)(2,1)}), bf16[16,4,2176]{2,1,0:T(4,128)(2,1)S(1)}, u32[]{:S(2)}, u32[]{:S(2)}) %all-to-all-start) | async-done | bytes 278560 | tf_op jit(solution)/shard_map/all_to_all | solution.py:157
  21.0 1.6 collective-permute-start
  22.6 1.7 collective-permute-start.4
  24.3 2.0 %collective-permute-start.5 = (bf16[32,2176]{1,0:T(8,128)(2,1)S(1)}, bf16[32,2176]{1,0:T(8,128)(2,1)S(1)}, u32[]{:S(2)}, u32[]{:S(2)}) collective-permute-start(bf16[32,2176]{1,0:T(8,128)(2,1)S(1)} %get-tuple-element.21), channel_id=1, source_target_pairs={{0,4},{1,5},{2,6},{3,7},{4,0},{5,1},{6,2},{7,3},{8,12},{9,13},{10,... | collective-permute-start | bytes 417800 | tf_op jit(solution)/shard_map/ppermute | solution.py:24
  26.3 2.7 %collective-permute-done = bf16[32,2176]{1,0:T(8,128)(2,1)S(1)} collective-permute-done((bf16[32,2176]{1,0:T(8,128)(2,1)S(1)}, bf16[32,2176]{1,0:T(8,128)(2,1)S(1)}, u32[]{:S(2)}, u32[]{:S(2)}) %collective-permute-start) | collective-permute-done | bytes 139296 | tf_op jit(solution)/shard_map/ppermute | solution.py:24
  28.9 3.1 %collective-permute-start.2 = (bf16[32,2176]{1,0:T(8,128)(2,1)S(1)}, bf16[32,2176]{1,0:T(8,128)(2,1)S(1)}, u32[]{:S(2)}, u32[]{:S(2)}) collective-permute-start(bf16[32,2176]{1,0:T(8,128)(2,1)S(1)} %get-tuple-element.12), channel_id=1, source_target_pairs={{0,4},{1,5},{2,6},{3,7},{4,0},{5,1},{6,2},{7,3},{8,12},{9,13},{10,... | collective-permute-start | bytes 417800 | tf_op jit(solution)/shard_map/ppermute | solution.py:24
  32.0 2.0 %collective-permute-start.1 = (bf16[32,2176]{1,0:T(8,128)(2,1)S(1)}, bf16[32,2176]{1,0:T(8,128)(2,1)S(1)}, u32[]{:S(2)}, u32[]{:S(2)}) collective-permute-start(bf16[32,2176]{1,0:T(8,128)(2,1)S(1)} %get-tuple-element.12), channel_id=1, source_target_pairs={{0,6},{1,7},{2,0},{3,1},{4,2},{5,3},{6,4},{7,5},{8,14},{9,15},{10,... | collective-permute-start | bytes 417800 | tf_op jit(solution)/shard_map/ppermute | solution.py:24
  34.3 3.3 %collective-permute-done.1 = bf16[32,2176]{1,0:T(8,128)(2,1)S(1)} collective-permute-done((bf16[32,2176]{1,0:T(8,128)(2,1)S(1)}, bf16[32,2176]{1,0:T(8,128)(2,1)S(1)}, u32[]{:S(2)}, u32[]{:S(2)}) %collective-permute-start.1) | collective-permute-done | bytes 139296 | tf_op jit(solution)/shard_map/ppermute | solution.py:24
  38.2 1.1 fusion.70
  40.3 1.1 fusion.69
  42.3 1.2 fusion.64
  45.1 3.1 %collective-permute-start.9 = (bf16[64,5376]{1,0:T(8,128)(2,1)S(1)}, bf16[64,5376]{1,0:T(8,128)(2,1)S(1)}, u32[]{:S(2)}, u32[]{:S(2)}) collective-permute-start(bf16[64,5376]{1,0:T(8,128)(2,1)S(1)} %get-tuple-element.28), channel_id=1, source_target_pairs={{0,48},{1,49},{2,50},{3,51},{4,52},{5,53},{6,54},{7,55},{8,56},{9,... | collective-permute-start | bytes 2064392 | tf_op jit(solution)/shard_map/ppermute | solution.py:24
  48.9 1.1 fusion.72
  51.1 1.1 fusion.71
  53.1 1.1 fusion.62
  55.0 7.4 %collective-permute-done.11 = bf16[64,5376]{1,0:T(8,128)(2,1)S(1)} collective-permute-done((bf16[64,5376]{1,0:T(8,128)(2,1)S(1)}, bf16[64,5376]{1,0:T(8,128)(2,1)S(1)}, u32[]{:S(2)}, u32[]{:S(2)}) %collective-permute-start.11) | collective-permute-done | bytes 688160 | tf_op jit(solution)/shard_map/ppermute | solution.py:24
  62.7 3.2 %collective-permute-start.14 = (bf16[32,5376]{1,0:T(8,128)(2,1)S(1)}, bf16[32,5376]{1,0:T(8,128)(2,1)S(1)}, u32[]{:S(2)}, u32[]{:S(2)}) collective-permute-start(bf16[32,5376]{1,0:T(8,128)(2,1)S(1)} %get-tuple-element.70), channel_id=1, source_target_pairs={{0,48},{1,49},{2,50},{3,51},{4,52},{5,53},{6,54},{7,55},{8,56},{9,... | collective-permute-start | bytes 1032200 | tf_op jit(solution)/shard_map/ppermute | solution.py:24
  66.7 6.8 %collective-permute-done.12 = bf16[32,5376]{1,0:T(8,128)(2,1)S(1)} collective-permute-done((bf16[32,5376]{1,0:T(8,128)(2,1)S(1)}, bf16[32,5376]{1,0:T(8,128)(2,1)S(1)}, u32[]{:S(2)}, u32[]{:S(2)}) %collective-permute-start.12) | collective-permute-done | bytes 344096 | tf_op jit(solution)/shard_map/ppermute | solution.py:24
  73.7 3.0 %collective-permute-start.15 = (bf16[64,5376]{1,0:T(8,128)(2,1)S(1)}, bf16[64,5376]{1,0:T(8,128)(2,1)S(1)}, u32[]{:S(2)}, u32[]{:S(2)}) collective-permute-start(bf16[64,5376]{1,0:T(8,128)(2,1)S(1)} %pad_maximum_fusion.4), channel_id=1, source_target_pairs={{0,48},{1,49},{2,50},{3,51},{4,52},{5,53},{6,54},{7,55},{8,56},{9,... | collective-permute-start | bytes 2064392 | tf_op jit(solution)/shard_map/ppermute | solution.py:24
  76.8 5.8 %collective-permute-done.10 = bf16[64,5376]{1,0:T(8,128)(2,1)S(1)} collective-permute-done((bf16[64,5376]{1,0:T(8,128)(2,1)S(1)}, bf16[64,5376]{1,0:T(8,128)(2,1)S(1)}, u32[]{:S(2)}, u32[]{:S(2)}) %collective-permute-start.10) | collective-permute-done | bytes 688160 | tf_op jit(solution)/shard_map/ppermute | solution.py:24
  82.6 7.4 %collective-permute-done.15 = bf16[64,5376]{1,0:T(8,128)(2,1)S(1)} collective-permute-done((bf16[64,5376]{1,0:T(8,128)(2,1)S(1)}, bf16[64,5376]{1,0:T(8,128)(2,1)S(1)}, u32[]{:S(2)}, u32[]{:S(2)}) %collective-permute-start.15) | collective-permute-done | bytes 688160 | tf_op jit(solution)/shard_map/ppermute | solution.py:24
  90.1 3.5 %collective-permute-done.13 = bf16[64,5376]{1,0:T(8,128)(2,1)S(1)} collective-permute-done((bf16[64,5376]{1,0:T(8,128)(2,1)S(1)}, bf16[64,5376]{1,0:T(8,128)(2,1)S(1)}, u32[]{:S(2)}, u32[]{:S(2)}) %collective-permute-start.13) | collective-permute-done | bytes 688160 | tf_op jit(solution)/shard_map/ppermute | solution.py:24
  94.3 3.2 %collective-permute-start.16 = (bf16[64,5376]{1,0:T(8,128)(2,1)S(1)}, bf16[64,5376]{1,0:T(8,128)(2,1)S(1)}, u32[]{:S(2)}, u32[]{:S(2)}) collective-permute-start(bf16[64,5376]{1,0:T(8,128)(2,1)S(1)} %get-tuple-element.68), channel_id=1, source_target_pairs={{0,48},{1,49},{2,50},{3,51},{4,52},{5,53},{6,54},{7,55},{8,56},{9,... | collective-permute-start | bytes 2064392 | tf_op jit(solution)/shard_map/ppermute | solution.py:24
  98.3 11.9 %collective-permute-done.17 = bf16[64,5376]{1,0:T(8,128)(2,1)S(1)} collective-permute-done((bf16[64,5376]{1,0:T(8,128)(2,1)S(1)}, bf16[64,5376]{1,0:T(8,128)(2,1)S(1)}, u32[]{:S(2)}, u32[]{:S(2)}) %collective-permute-start.17) | collective-permute-done | bytes 688160 | tf_op jit(solution)/shard_map/ppermute | solution.py:24
  110.3 3.3 %collective-permute-start.19 = (bf16[32,5376]{1,0:T(8,128)(2,1)S(1)}, bf16[32,5376]{1,0:T(8,128)(2,1)S(1)}, u32[]{:S(2)}, u32[]{:S(2)}) collective-permute-start(bf16[32,5376]{1,0:T(8,128)(2,1)S(1)} %slice.416), channel_id=1, source_target_pairs={{0,48},{1,49},{2,50},{3,51},{4,52},{5,53},{6,54},{7,55},{8,56},{9,... | collective-permute-start | bytes 1032200 | tf_op jit(solution)/shard_map/ppermute | solution.py:24
  113.6 3.2 %collective-permute-start.25 = (bf16[64,5376]{1,0:T(8,128)(2,1)S(1)}, bf16[64,5376]{1,0:T(8,128)(2,1)S(1)}, u32[]{:S(2)}, u32[]{:S(2)}) collective-permute-start(bf16[64,5376]{1,0:T(8,128)(2,1)S(1)} %collective-permute-done.24), channel_id=1, source_target_pairs={{0,48},{1,49},{2,50},{3,51},{4,52},{5,53},{6,54},{7,55},{8,56},{9,... | collective-permute-start | bytes 2064392 | tf_op jit(solution)/shard_map/ppermute | solution.py:24
  117.0 5.5 %collective-permute-done.18 = bf16[32,5376]{1,0:T(8,128)(2,1)S(1)} collective-permute-done((bf16[32,5376]{1,0:T(8,128)(2,1)S(1)}, bf16[32,5376]{1,0:T(8,128)(2,1)S(1)}, u32[]{:S(2)}, u32[]{:S(2)}) %collective-permute-start.18) | collective-permute-done | bytes 344096 | tf_op jit(solution)/shard_map/ppermute | solution.py:24
  122.7 1.2 fusion.20
  124.8 1.1 fusion.17
  126.9 1.2 multiply_reduce_fusion.1
  128.6 3.4 %collective-permute-done.25 = bf16[64,5376]{1,0:T(8,128)(2,1)S(1)} collective-permute-done((bf16[64,5376]{1,0:T(8,128)(2,1)S(1)}, bf16[64,5376]{1,0:T(8,128)(2,1)S(1)}, u32[]{:S(2)}, u32[]{:S(2)}) %collective-permute-start.25) | collective-permute-done | bytes 688160 | tf_op jit(solution)/shard_map/ppermute | solution.py:24
  132.0 5.2 %collective-permute-done.26 = bf16[64,5376]{1,0:T(8,128)(2,1)S(1)} collective-permute-done((bf16[64,5376]{1,0:T(8,128)(2,1)S(1)}, bf16[64,5376]{1,0:T(8,128)(2,1)S(1)}, u32[]{:S(2)}, u32[]{:S(2)}) %collective-permute-start.26) | collective-permute-done | bytes 688160 | tf_op jit(solution)/shard_map/ppermute | solution.py:24
  137.4 1.2 fusion.15
  138.6 1.1 fusion.12
  139.7 1.2 multiply_reduce_fusion
  141.3 4.0 %convolution_convert_fusion.2 = bf16[1792,1024]{1,0:T(8,128)(2,1)} fusion(bf16[512,5376]{1,0:T(8,128)(2,1)S(1)} %get-tuple-element.54, bf16[256,1024]{1,0:T(8,128)(2,1)S(1)} %slice.391, bf16[256,1024]{1,0:T(8,128)(2,1)S(1)} %slice.400), kind=kOutput, calls=%fused_computation.32 | convolution fusion | flops 1882980352 | bytes 6553600 | tf_op jit(solution)/shard_map/dot_general | solution.py:36
  145.3 4.0 %convolution_convert_fusion.1 = bf16[1024,1792]{1,0:T(8,128)(2,1)} fusion(bf16[512,5376]{1,0:T(8,128)(2,1)S(1)} %get-tuple-element.54, bf16[256,1024]{1,0:T(8,128)(2,1)S(1)} %multiply_convert_fusion.1, bf16[256,1024]{1,0:T(8,128)(2,1)S(1)} %copy-done.2), kind=kOutput, calls=%fused_computation.31 | convolution fusion | flops 1882980352 | bytes 6553600 | tf_op jit(solution)/shard_map/dot_general | solution.py:36
  149.4 1.9 %collective-permute-start.21 = (bf16[32,2048]{1,0:T(8,128)(2,1)S(1)}, bf16[32,2048]{1,0:T(8,128)(2,1)S(1)}, u32[]{:S(2)}, u32[]{:S(2)}) collective-permute-start(bf16[32,2048]{1,0:T(8,128)(2,1)S(1)} %get-tuple-element.48), channel_id=1, source_target_pairs={{0,2},{1,3},{2,4},{3,5},{4,6},{5,7},{6,0},{7,1},{8,10},{9,11},{10,... | collective-permute-start | bytes 393224 | tf_op jit(solution)/shard_map/ppermute | solution.py:24
  151.3 1.8 collective-permute-start.23
  154.3 1.7 collective-permute-start.31
  156.0 2.2 %collective-permute-start.30 = (bf16[32,2176]{1,0:T(8,128)(2,1)S(1)}, bf16[32,2176]{1,0:T(8,128)(2,1)S(1)}, u32[]{:S(2)}, u32[]{:S(2)}) collective-permute-start(bf16[32,2176]{1,0:T(8,128)(2,1)S(1)} %get-tuple-element.77), channel_id=1, source_target_pairs={{0,6},{1,7},{2,0},{3,1},{4,2},{5,3},{6,4},{7,5},{8,14},{9,15},{10,... | collective-permute-start | bytes 417800 | tf_op jit(solution)/shard_map/ppermute | solution.py:24
  158.2 2.0 %collective-permute-done.23 = bf16[32,2048]{1,0:T(8,128)(2,1)S(1)} collective-permute-done((bf16[32,2048]{1,0:T(8,128)(2,1)S(1)}, bf16[32,2048]{1,0:T(8,128)(2,1)S(1)}, u32[]{:S(2)}, u32[]{:S(2)}) %collective-permute-start.23) | collective-permute-done | bytes 131104 | tf_op jit(solution)/shard_map/ppermute | solution.py:24
  160.8 2.4 %collective-permute-done.31 = bf16[32,2176]{1,0:T(8,128)(2,1)S(1)} collective-permute-done((bf16[32,2176]{1,0:T(8,128)(2,1)S(1)}, bf16[32,2176]{1,0:T(8,128)(2,1)S(1)}, u32[]{:S(2)}, u32[]{:S(2)}) %collective-permute-start.31) | collective-permute-done | bytes 139296 | tf_op jit(solution)/shard_map/ppermute | solution.py:24
  163.2 2.8 %collective-permute-done.30 = bf16[32,2176]{1,0:T(8,128)(2,1)S(1)} collective-permute-done((bf16[32,2176]{1,0:T(8,128)(2,1)S(1)}, bf16[32,2176]{1,0:T(8,128)(2,1)S(1)}, u32[]{:S(2)}, u32[]{:S(2)}) %collective-permute-start.30) | collective-permute-done | bytes 139296 | tf_op jit(solution)/shard_map/ppermute | solution.py:24
  167.2 5.2 %all-to-all-start.1 = ((bf16[16,4,2560]{2,1,0:T(4,128)(2,1)}), bf16[16,4,2560]{2,1,0:T(4,128)(2,1)S(1)}, u32[]{:S(2)}, u32[]{:S(2)}) async-start(bf16[16,4,2560]{2,1,0:T(4,128)(2,1)} %pad_maximum_fusion.9), calls=%async_computation.1 | async-start | bytes 655360 | tf_op jit(solution)/shard_map/all_to_all | solution.py:236
  172.3 5.5 %convolution_convert_fusion = bf16[1024,1792]{1,0:T(8,128)(2,1)} fusion(bf16[512,5376]{1,0:T(8,128)(2,1)} %copy-done.4, bf16[256,1024]{1,0:T(8,128)(2,1)S(1)} %multiply_convert_fusion.1, bf16[256,1024]{1,0:T(8,128)(2,1)S(1)} %copy-done.2), kind=kOutput, calls=%fused_computation.30 | convolution fusion | flops 1882980352 | bytes 6553600 | tf_op jit(solution)/shard_map/dot_general | solution.py:36
  177.8 3.9 %all-to-all-done.1 = bf16[16,4,2560]{2,1,0:T(4,128)(2,1)S(1)} async-done(((bf16[16,4,2560]{2,1,0:T(4,128)(2,1)}), bf16[16,4,2560]{2,1,0:T(4,128)(2,1)S(1)}, u32[]{:S(2)}, u32[]{:S(2)}) %all-to-all-start.1) | async-done | bytes 327712 | tf_op jit(solution)/shard_map/all_to_all | solution.py:236
  (175 shorter events, 22.6 us)
Async XLA Ops:
  0.6 23.6 %copy-start.3 = (f32[8192]{0:T(1024)S(1)}, f32[8192]{0:T(1024)}, u32[]{:S(2)}) copy-start(f32[8192]{0:T(1024)} %param.7) | copy-start | bytes 98308
  4.0 16.8 %all-to-all-start = ((bf16[16,4,2176]{2,1,0:T(4,128)(2,1)}), bf16[16,4,2176]{2,1,0:T(4,128)(2,1)S(1)}, u32[]{:S(2)}, u32[]{:S(2)}) async-start(bf16[16,4,2176]{2,1,0:T(4,128)(2,1)} %bitcast.2), calls=%async_computation | async-start | bytes 557056 | tf_op jit(solution)/shard_map/all_to_all | solution.py:157
  21.0 8.0 %collective-permute-start = (bf16[32,2176]{1,0:T(8,128)(2,1)S(1)}, bf16[32,2176]{1,0:T(8,128)(2,1)S(1)}, u32[]{:S(2)}, u32[]{:S(2)}) collective-permute-start(bf16[32,2176]{1,0:T(8,128)(2,1)S(1)} %get-tuple-element.21), channel_id=1, source_target_pairs={{0,2},{1,3},{2,4},{3,5},{4,6},{5,7},{6,0},{7,1},{8,10},{9,11},{10,... | collective-permute-start | bytes 417800 | tf_op jit(solution)/shard_map/ppermute | solution.py:24
  22.6 11.4 %collective-permute-start.4 = (bf16[32,2176]{1,0:T(8,128)(2,1)S(1)}, bf16[32,2176]{1,0:T(8,128)(2,1)S(1)}, u32[]{:S(2)}, u32[]{:S(2)}) collective-permute-start(bf16[32,2176]{1,0:T(8,128)(2,1)S(1)} %get-tuple-element.21), channel_id=1, source_target_pairs={{0,6},{1,7},{2,0},{3,1},{4,2},{5,3},{6,4},{7,5},{8,14},{9,15},{10,... | collective-permute-start | bytes 417800 | tf_op jit(solution)/shard_map/ppermute | solution.py:24
  24.3 9.7 %collective-permute-start.5 = (bf16[32,2176]{1,0:T(8,128)(2,1)S(1)}, bf16[32,2176]{1,0:T(8,128)(2,1)S(1)}, u32[]{:S(2)}, u32[]{:S(2)}) collective-permute-start(bf16[32,2176]{1,0:T(8,128)(2,1)S(1)} %get-tuple-element.21), channel_id=1, source_target_pairs={{0,4},{1,5},{2,6},{3,7},{4,0},{5,1},{6,2},{7,3},{8,12},{9,13},{10,... | collective-permute-start | bytes 417800 | tf_op jit(solution)/shard_map/ppermute | solution.py:24
  28.9 8.7 %collective-permute-start.3 = (bf16[32,2176]{1,0:T(8,128)(2,1)S(1)}, bf16[32,2176]{1,0:T(8,128)(2,1)S(1)}, u32[]{:S(2)}, u32[]{:S(2)}) collective-permute-start(bf16[32,2176]{1,0:T(8,128)(2,1)S(1)} %get-tuple-element.12), channel_id=1, source_target_pairs={{0,2},{1,3},{2,4},{3,5},{4,6},{5,7},{6,0},{7,1},{8,10},{9,11},{10,... | collective-permute-start | bytes 417800 | tf_op jit(solution)/shard_map/ppermute | solution.py:24
  28.9 8.6 %collective-permute-start.2 = (bf16[32,2176]{1,0:T(8,128)(2,1)S(1)}, bf16[32,2176]{1,0:T(8,128)(2,1)S(1)}, u32[]{:S(2)}, u32[]{:S(2)}) collective-permute-start(bf16[32,2176]{1,0:T(8,128)(2,1)S(1)} %get-tuple-element.12), channel_id=1, source_target_pairs={{0,4},{1,5},{2,6},{3,7},{4,0},{5,1},{6,2},{7,3},{8,12},{9,13},{10,... | collective-permute-start | bytes 417800 | tf_op jit(solution)/shard_map/ppermute | solution.py:24
  32.0 5.5 %collective-permute-start.1 = (bf16[32,2176]{1,0:T(8,128)(2,1)S(1)}, bf16[32,2176]{1,0:T(8,128)(2,1)S(1)}, u32[]{:S(2)}, u32[]{:S(2)}) collective-permute-start(bf16[32,2176]{1,0:T(8,128)(2,1)S(1)} %get-tuple-element.12), channel_id=1, source_target_pairs={{0,6},{1,7},{2,0},{3,1},{4,2},{5,3},{6,4},{7,5},{8,14},{9,15},{10,... | collective-permute-start | bytes 417800 | tf_op jit(solution)/shard_map/ppermute | solution.py:24
  34.1 3.6 %collective-permute-start.6 = (bf16[128,2176]{1,0:T(8,128)(2,1)S(1)}, bf16[128,2176]{1,0:T(8,128)(2,1)S(1)}, u32[]{:S(2)}, u32[]{:S(2)}) collective-permute-start(bf16[128,2176]{1,0:T(8,128)(2,1)S(1)} %constant_dynamic-update-slice_fusion.19), channel_id=1, source_target_pairs={{0,1},{1,0},{2,3},{3,2},{4,5},{5,4},{6,7},{7,6},{8,9},{9,8},{10,11... | collective-permute-start | bytes 1671176 | tf_op jit(solution)/shard_map/ppermute | solution.py:24
  34.3 4.0 %copy-start.8 = (bf16[1024,1792]{1,0:T(8,128)(2,1)S(1)}, bf16[1024,1792]{1,0:T(8,128)(2,1)}, u32[]{:S(2)}) copy-start(bf16[1024,1792]{1,0:T(8,128)(2,1)} %param.9) | copy-start | bytes 11010052
  38.2 2.0 %copy-start.10 = (bf16[1024,1792]{1,0:T(8,128)(2,1)S(1)}, bf16[1024,1792]{1,0:T(8,128)(2,1)}, u32[]{:S(2)}) copy-start(bf16[1024,1792]{1,0:T(8,128)(2,1)} %param.8) | copy-start | bytes 11010052
  40.3 2.0 %copy-start.5 = (bf16[1792,1024]{1,0:T(8,128)(2,1)S(1)}, bf16[1792,1024]{1,0:T(8,128)(2,1)}, u32[]{:S(2)}) copy-start(bf16[1792,1024]{1,0:T(8,128)(2,1)} %param.10) | copy-start | bytes 11010052
  43.9 4.4 %collective-permute-start.7 = (bf16[128,2176]{1,0:T(8,128)(2,1)S(1)}, bf16[128,2176]{1,0:T(8,128)(2,1)S(1)}, u32[]{:S(2)}, u32[]{:S(2)}) collective-permute-start(bf16[128,2176]{1,0:T(8,128)(2,1)S(1)} %constant_dynamic-update-slice_fusion.23), channel_id=1, source_target_pairs={{0,1},{1,0},{2,3},{3,2},{4,5},{5,4},{6,7},{7,6},{8,9},{9,8},{10,11... | collective-permute-start | bytes 1671176 | tf_op jit(solution)/shard_map/ppermute | solution.py:24
  44.4 21.5 %collective-permute-start.8 = (bf16[64,5376]{1,0:T(8,128)(2,1)S(1)}, bf16[64,5376]{1,0:T(8,128)(2,1)S(1)}, u32[]{:S(2)}, u32[]{:S(2)}) collective-permute-start(bf16[64,5376]{1,0:T(8,128)(2,1)S(1)} %get-tuple-element.26), channel_id=1, source_target_pairs={{0,16},{1,17},{2,18},{3,19},{4,20},{5,21},{6,22},{7,23},{8,24},{9,... | collective-permute-start | bytes 2064392 | tf_op jit(solution)/shard_map/ppermute | solution.py:24
  44.5 17.9 %collective-permute-start.11 = (bf16[64,5376]{1,0:T(8,128)(2,1)S(1)}, bf16[64,5376]{1,0:T(8,128)(2,1)S(1)}, u32[]{:S(2)}, u32[]{:S(2)}) collective-permute-start(bf16[64,5376]{1,0:T(8,128)(2,1)S(1)} %get-tuple-element.27), channel_id=1, source_target_pairs={{0,64},{1,65},{2,66},{3,67},{4,68},{5,69},{6,70},{7,71},{8,72},{9,... | collective-permute-start | bytes 2064392 | tf_op jit(solution)/shard_map/ppermute | solution.py:24
  45.1 20.7 %collective-permute-start.9 = (bf16[64,5376]{1,0:T(8,128)(2,1)S(1)}, bf16[64,5376]{1,0:T(8,128)(2,1)S(1)}, u32[]{:S(2)}, u32[]{:S(2)}) collective-permute-start(bf16[64,5376]{1,0:T(8,128)(2,1)S(1)} %get-tuple-element.28), channel_id=1, source_target_pairs={{0,48},{1,49},{2,50},{3,51},{4,52},{5,53},{6,54},{7,55},{8,56},{9,... | collective-permute-start | bytes 2064392 | tf_op jit(solution)/shard_map/ppermute | solution.py:24
  48.8 1.2 copy-start.1
  48.9 2.2 %copy-start.11 = (bf16[1024,1792]{1,0:T(8,128)(2,1)S(1)}, bf16[1024,1792]{1,0:T(8,128)(2,1)}, u32[]{:S(2)}) copy-start(bf16[1024,1792]{1,0:T(8,128)(2,1)} %param.8) | copy-start | bytes 11010052
  51.1 2.0 %copy-start.6 = (bf16[1792,1024]{1,0:T(8,128)(2,1)S(1)}, bf16[1792,1024]{1,0:T(8,128)(2,1)}, u32[]{:S(2)}) copy-start(bf16[1792,1024]{1,0:T(8,128)(2,1)} %param.10) | copy-start | bytes 11010052
  62.5 11.0 %collective-permute-start.12 = (bf16[32,5376]{1,0:T(8,128)(2,1)S(1)}, bf16[32,5376]{1,0:T(8,128)(2,1)S(1)}, u32[]{:S(2)}, u32[]{:S(2)}) collective-permute-start(bf16[32,5376]{1,0:T(8,128)(2,1)S(1)} %get-tuple-element.69), channel_id=1, source_target_pairs={{0,16},{1,17},{2,18},{3,19},{4,20},{5,21},{6,22},{7,23},{8,24},{9,... | collective-permute-start | bytes 1032200 | tf_op jit(solution)/shard_map/ppermute | solution.py:24
  62.7 10.8 %collective-permute-start.14 = (bf16[32,5376]{1,0:T(8,128)(2,1)S(1)}, bf16[32,5376]{1,0:T(8,128)(2,1)S(1)}, u32[]{:S(2)}, u32[]{:S(2)}) collective-permute-start(bf16[32,5376]{1,0:T(8,128)(2,1)S(1)} %get-tuple-element.70), channel_id=1, source_target_pairs={{0,48},{1,49},{2,50},{3,51},{4,52},{5,53},{6,54},{7,55},{8,56},{9,... | collective-permute-start | bytes 1032200 | tf_op jit(solution)/shard_map/ppermute | solution.py:24
  66.1 16.6 %collective-permute-start.10 = (bf16[64,5376]{1,0:T(8,128)(2,1)S(1)}, bf16[64,5376]{1,0:T(8,128)(2,1)S(1)}, u32[]{:S(2)}, u32[]{:S(2)}) collective-permute-start(bf16[64,5376]{1,0:T(8,128)(2,1)S(1)} %fusion.7), channel_id=1, source_target_pairs={{0,64},{1,65},{2,66},{3,67},{4,68},{5,69},{6,70},{7,71},{8,72},{9,... | collective-permute-start | bytes 2064392 | tf_op jit(solution)/shard_map/ppermute | solution.py:24
  73.7 16.4 %collective-permute-start.15 = (bf16[64,5376]{1,0:T(8,128)(2,1)S(1)}, bf16[64,5376]{1,0:T(8,128)(2,1)S(1)}, u32[]{:S(2)}, u32[]{:S(2)}) collective-permute-start(bf16[64,5376]{1,0:T(8,128)(2,1)S(1)} %pad_maximum_fusion.4), channel_id=1, source_target_pairs={{0,48},{1,49},{2,50},{3,51},{4,52},{5,53},{6,54},{7,55},{8,56},{9,... | collective-permute-start | bytes 2064392 | tf_op jit(solution)/shard_map/ppermute | solution.py:24
  76.7 16.8 %collective-permute-start.13 = (bf16[64,5376]{1,0:T(8,128)(2,1)S(1)}, bf16[64,5376]{1,0:T(8,128)(2,1)S(1)}, u32[]{:S(2)}, u32[]{:S(2)}) collective-permute-start(bf16[64,5376]{1,0:T(8,128)(2,1)S(1)} %pad_maximum_fusion.3), channel_id=1, source_target_pairs={{0,16},{1,17},{2,18},{3,19},{4,20},{5,21},{6,22},{7,23},{8,24},{9,... | collective-permute-start | bytes 2064392 | tf_op jit(solution)/shard_map/ppermute | solution.py:24
  94.3 15.9 %collective-permute-start.17 = (bf16[64,5376]{1,0:T(8,128)(2,1)S(1)}, bf16[64,5376]{1,0:T(8,128)(2,1)S(1)}, u32[]{:S(2)}, u32[]{:S(2)}) collective-permute-start(bf16[64,5376]{1,0:T(8,128)(2,1)S(1)} %get-tuple-element.68), channel_id=1, source_target_pairs={{0,16},{1,17},{2,18},{3,19},{4,20},{5,21},{6,22},{7,23},{8,24},{9,... | collective-permute-start | bytes 2064392 | tf_op jit(solution)/shard_map/ppermute | solution.py:24
  94.3 16.0 %collective-permute-start.16 = (bf16[64,5376]{1,0:T(8,128)(2,1)S(1)}, bf16[64,5376]{1,0:T(8,128)(2,1)S(1)}, u32[]{:S(2)}, u32[]{:S(2)}) collective-permute-start(bf16[64,5376]{1,0:T(8,128)(2,1)S(1)} %get-tuple-element.68), channel_id=1, source_target_pairs={{0,48},{1,49},{2,50},{3,51},{4,52},{5,53},{6,54},{7,55},{8,56},{9,... | collective-permute-start | bytes 2064392 | tf_op jit(solution)/shard_map/ppermute | solution.py:24
  97.6 16.1 %collective-permute-start.24 = (bf16[64,5376]{1,0:T(8,128)(2,1)S(1)}, bf16[64,5376]{1,0:T(8,128)(2,1)S(1)}, u32[]{:S(2)}, u32[]{:S(2)}) collective-permute-start(bf16[64,5376]{1,0:T(8,128)(2,1)S(1)} %get-tuple-element.68), channel_id=1, source_target_pairs={{0,64},{1,65},{2,66},{3,67},{4,68},{5,69},{6,70},{7,71},{8,72},{9,... | collective-permute-start | bytes 2064392 | tf_op jit(solution)/shard_map/ppermute | solution.py:24
  110.2 12.3 %collective-permute-start.18 = (bf16[32,5376]{1,0:T(8,128)(2,1)S(1)}, bf16[32,5376]{1,0:T(8,128)(2,1)S(1)}, u32[]{:S(2)}, u32[]{:S(2)}) collective-permute-start(bf16[32,5376]{1,0:T(8,128)(2,1)S(1)} %slice.415), channel_id=1, source_target_pairs={{0,16},{1,17},{2,18},{3,19},{4,20},{5,21},{6,22},{7,23},{8,24},{9,... | collective-permute-start | bytes 1032200 | tf_op jit(solution)/shard_map/ppermute | solution.py:24
  110.3 12.2 %collective-permute-start.19 = (bf16[32,5376]{1,0:T(8,128)(2,1)S(1)}, bf16[32,5376]{1,0:T(8,128)(2,1)S(1)}, u32[]{:S(2)}, u32[]{:S(2)}) collective-permute-start(bf16[32,5376]{1,0:T(8,128)(2,1)S(1)} %slice.416), channel_id=1, source_target_pairs={{0,48},{1,49},{2,50},{3,51},{4,52},{5,53},{6,54},{7,55},{8,56},{9,... | collective-permute-start | bytes 1032200 | tf_op jit(solution)/shard_map/ppermute | solution.py:24
  113.6 23.7 %collective-permute-start.27 = (bf16[64,5376]{1,0:T(8,128)(2,1)S(1)}, bf16[64,5376]{1,0:T(8,128)(2,1)S(1)}, u32[]{:S(2)}, u32[]{:S(2)}) collective-permute-start(bf16[64,5376]{1,0:T(8,128)(2,1)S(1)} %collective-permute-done.24), channel_id=1, source_target_pairs={{0,16},{1,17},{2,18},{3,19},{4,20},{5,21},{6,22},{7,23},{8,24},{9,... | collective-permute-start | bytes 2064392 | tf_op jit(solution)/shard_map/ppermute | solution.py:24
  113.6 18.3 %collective-permute-start.25 = (bf16[64,5376]{1,0:T(8,128)(2,1)S(1)}, bf16[64,5376]{1,0:T(8,128)(2,1)S(1)}, u32[]{:S(2)}, u32[]{:S(2)}) collective-permute-start(bf16[64,5376]{1,0:T(8,128)(2,1)S(1)} %collective-permute-done.24), channel_id=1, source_target_pairs={{0,48},{1,49},{2,50},{3,51},{4,52},{5,53},{6,54},{7,55},{8,56},{9,... | collective-permute-start | bytes 2064392 | tf_op jit(solution)/shard_map/ppermute | solution.py:24
  117.0 5.8 %copy-start.7 = (bf16[1792,1024]{1,0:T(8,128)(2,1)S(1)}, bf16[1792,1024]{1,0:T(8,128)(2,1)}, u32[]{:S(2)}) copy-start(bf16[1792,1024]{1,0:T(8,128)(2,1)} %param.10) | copy-start | bytes 11010052
  122.7 2.0 %copy-start.9 = (bf16[1024,1792]{1,0:T(8,128)(2,1)S(1)}, bf16[1024,1792]{1,0:T(8,128)(2,1)}, u32[]{:S(2)}) copy-start(bf16[1024,1792]{1,0:T(8,128)(2,1)} %param.9) | copy-start | bytes 11010052
  124.8 2.1 %copy-start.12 = (bf16[1024,1792]{1,0:T(8,128)(2,1)S(1)}, bf16[1024,1792]{1,0:T(8,128)(2,1)}, u32[]{:S(2)}) copy-start(bf16[1024,1792]{1,0:T(8,128)(2,1)} %param.8) | copy-start | bytes 11010052
  126.0 11.2 %collective-permute-start.26 = (bf16[64,5376]{1,0:T(8,128)(2,1)S(1)}, bf16[64,5376]{1,0:T(8,128)(2,1)S(1)}, u32[]{:S(2)}, u32[]{:S(2)}) collective-permute-start(bf16[64,5376]{1,0:T(8,128)(2,1)S(1)} %pad_maximum_fusion.6), channel_id=1, source_target_pairs={{0,64},{1,65},{2,66},{3,67},{4,68},{5,69},{6,70},{7,71},{8,72},{9,... | collective-permute-start | bytes 2064392 | tf_op jit(solution)/shard_map/ppermute | solution.py:24
  128.4 20.9 %collective-permute-start.20 = (f32[128,2048]{1,0:T(8,128)S(1)}, f32[128,2048]{1,0:T(8,128)S(1)}, u32[]{:S(2)}, u32[]{:S(2)}) collective-permute-start(f32[128,2048]{1,0:T(8,128)S(1)} %fusion.8), channel_id=1, source_target_pairs={{0,1},{1,0},{2,3},{3,2},{4,5},{5,4},{6,7},{7,6},{8,9},{9,8},{10,11... | collective-permute-start | bytes 3145736 | tf_op jit(solution)/shard_map/ppermute | solution.py:24
  137.4 7.8 %copy-start.4 = (bf16[512,5376]{1,0:T(8,128)(2,1)}, bf16[512,5376]{1,0:T(8,128)(2,1)S(1)}, u32[]{:S(2)}) copy-start(bf16[512,5376]{1,0:T(8,128)(2,1)S(1)} %get-tuple-element.54) | copy-start | bytes 16515076
  141.2 12.9 %collective-permute-start.28 = (f32[136,2048]{1,0:T(8,128)S(1)}, f32[136,2048]{1,0:T(8,128)S(1)}, u32[]{:S(2)}, u32[]{:S(2)}) collective-permute-start(f32[136,2048]{1,0:T(8,128)S(1)} %constant_dynamic-update-slice_fusion.9), channel_id=1, source_target_pairs={{0,1},{1,0},{2,3},{3,2},{4,5},{5,4},{6,7},{7,6},{8,9},{9,8},{10,11... | collective-permute-start | bytes 3342344 | tf_op jit(solution)/shard_map/ppermute | solution.py:24
  141.3 4.0 %copy-start.2 = (bf16[256,1024]{1,0:T(8,128)(2,1)S(1)}, bf16[256,1024]{1,0:T(8,128)(2,1)}, u32[]{:S(2)}) copy-start(bf16[256,1024]{1,0:T(8,128)(2,1)} %copy-done.1) | copy-start | bytes 1572868
  149.4 8.7 %collective-permute-start.21 = (bf16[32,2048]{1,0:T(8,128)(2,1)S(1)}, bf16[32,2048]{1,0:T(8,128)(2,1)S(1)}, u32[]{:S(2)}, u32[]{:S(2)}) collective-permute-start(bf16[32,2048]{1,0:T(8,128)(2,1)S(1)} %get-tuple-element.48), channel_id=1, source_target_pairs={{0,2},{1,3},{2,4},{3,5},{4,6},{5,7},{6,0},{7,1},{8,10},{9,11},{10,... | collective-permute-start | bytes 393224 | tf_op jit(solution)/shard_map/ppermute | solution.py:24
  151.3 8.9 %collective-permute-start.23 = (bf16[32,2048]{1,0:T(8,128)(2,1)S(1)}, bf16[32,2048]{1,0:T(8,128)(2,1)S(1)}, u32[]{:S(2)}, u32[]{:S(2)}) collective-permute-start(bf16[32,2048]{1,0:T(8,128)(2,1)S(1)} %get-tuple-element.49), channel_id=1, source_target_pairs={{0,4},{1,5},{2,6},{3,7},{4,0},{5,1},{6,2},{7,3},{8,12},{9,13},{10,... | collective-permute-start | bytes 393224 | tf_op jit(solution)/shard_map/ppermute | solution.py:24
  153.1 7.6 %collective-permute-start.22 = (bf16[32,2048]{1,0:T(8,128)(2,1)S(1)}, bf16[32,2048]{1,0:T(8,128)(2,1)S(1)}, u32[]{:S(2)}, u32[]{:S(2)}) collective-permute-start(bf16[32,2048]{1,0:T(8,128)(2,1)S(1)} %get-tuple-element.50), channel_id=1, source_target_pairs={{0,6},{1,7},{2,0},{3,1},{4,2},{5,3},{6,4},{7,5},{8,14},{9,15},{10,... | collective-permute-start | bytes 393224 | tf_op jit(solution)/shard_map/ppermute | solution.py:24
  154.3 8.9 %collective-permute-start.31 = (bf16[32,2176]{1,0:T(8,128)(2,1)S(1)}, bf16[32,2176]{1,0:T(8,128)(2,1)S(1)}, u32[]{:S(2)}, u32[]{:S(2)}) collective-permute-start(bf16[32,2176]{1,0:T(8,128)(2,1)S(1)} %get-tuple-element.76), channel_id=1, source_target_pairs={{0,4},{1,5},{2,6},{3,7},{4,0},{5,1},{6,2},{7,3},{8,12},{9,13},{10,... | collective-permute-start | bytes 417800 | tf_op jit(solution)/shard_map/ppermute | solution.py:24
  156.0 10.0 %collective-permute-start.30 = (bf16[32,2176]{1,0:T(8,128)(2,1)S(1)}, bf16[32,2176]{1,0:T(8,128)(2,1)S(1)}, u32[]{:S(2)}, u32[]{:S(2)}) collective-permute-start(bf16[32,2176]{1,0:T(8,128)(2,1)S(1)} %get-tuple-element.77), channel_id=1, source_target_pairs={{0,6},{1,7},{2,0},{3,1},{4,2},{5,3},{6,4},{7,5},{8,14},{9,15},{10,... | collective-permute-start | bytes 417800 | tf_op jit(solution)/shard_map/ppermute | solution.py:24
  158.2 7.8 %collective-permute-start.29 = (bf16[32,2176]{1,0:T(8,128)(2,1)S(1)}, bf16[32,2176]{1,0:T(8,128)(2,1)S(1)}, u32[]{:S(2)}, u32[]{:S(2)}) collective-permute-start(bf16[32,2176]{1,0:T(8,128)(2,1)S(1)} %get-tuple-element.78), channel_id=1, source_target_pairs={{0,2},{1,3},{2,4},{3,5},{4,6},{5,7},{6,0},{7,1},{8,10},{9,11},{10,... | collective-permute-start | bytes 417800 | tf_op jit(solution)/shard_map/ppermute | solution.py:24
  167.2 14.5 %all-to-all-start.1 = ((bf16[16,4,2560]{2,1,0:T(4,128)(2,1)}), bf16[16,4,2560]{2,1,0:T(4,128)(2,1)S(1)}, u32[]{:S(2)}, u32[]{:S(2)}) async-start(bf16[16,4,2560]{2,1,0:T(4,128)(2,1)} %pad_maximum_fusion.9), calls=%async_computation.1 | async-start | bytes 655360 | tf_op jit(solution)/shard_map/all_to_all | solution.py:236
  177.8 5.5 %copy-start = (bf16[4,8192]{1,0:T(4,128)(2,1)S(1)}, bf16[4,8192]{1,0:T(4,128)(2,1)}, u32[]{:S(2)}) copy-start(bf16[4,8192]{1,0:T(4,128)(2,1)} %param.6) | copy-start | bytes 196612

commit v5 on v4

--- a/solution.py
+++ b/solution.py
@@ -108,15 +108,18 @@
     m12 = send(far[2].astype(BF16), z=1).astype(F32)
     m11 = send(far[1].astype(BF16), x=1).astype(F32)
     m13 = send(far[3].astype(BF16), x=3).astype(F32)
+    h = near[0].shape[0] // 2
+    first1 = send(near[1][h:].astype(BF16), x=1)
+    first2 = send(near[3][:h].astype(BF16), x=3)
     a02 = near[2] + m12
-    h = a02.shape[0] // 2
     n1 = send(a02[:h].astype(BF16), x=1).astype(F32)
     n2 = send(a02[h:].astype(BF16), x=3).astype(F32)
     q = send((far[0] + m11 + m13).astype(BF16), z=1).astype(F32)
-    a01 = jnp.concatenate([near[1][:h] + n1, near[1][h:]], axis=0)
-    a03 = jnp.concatenate([near[3][:h], near[3][h:] + n2], axis=0)
-    r1 = send(a01.astype(BF16), x=1).astype(F32)
-    r2 = send(a03.astype(BF16), x=3).astype(F32)
+    last1 = (near[1][:h] + n1).astype(BF16)
+    last2 = (near[3][h:] + n2).astype(BF16)
+    last1, last2, first1, first2 = lax.optimization_barrier((last1, last2, first1, first2))
+    r1 = jnp.concatenate([send(last1, x=1), first1], axis=0).astype(F32)
+    r2 = jnp.concatenate([first2, send(last2, x=3)], axis=0).astype(F32)
     return near[0] + q + r1 + r2
 
 
@@ -209,23 +212,25 @@
         return jnp.concatenate([product(hidden, down_weight), grad], axis=1)
 
     near_partial = backward(units[0])
-    near_total, _ = sum_over_y(sum_over_core(near_partial, None)[0], None, x)
-    far_partial = backward(units[1])
+    near_keep, _ = sum_over_core(near_partial, None)
+    near_total, _ = sum_over_y(near_keep, None, x)
+    far_units, near_total = lax.optimization_barrier((units[1], near_total))
+    far_partial = backward(far_units)
     gain_partial = jnp.sum(near_partial[:, 1024:] * near_estimate, axis=0) + jnp.sum(
         far_partial[:, 1024:] * far_estimate, axis=0
     )
-    far_total, gain = sum_over_y(*sum_over_core(far_partial, gain_partial.reshape(8, 128)), x)
-
-    units = jnp.concatenate(units, axis=0)
+    far_keep, gain = sum_over_core(far_partial, gain_partial.reshape(8, 128))
+
+    units = jnp.concatenate([units[0], far_units], axis=0)
     hidden, gate_grad, up_grad = units[:, :width], units[:, width : 2 * width], units[:, 2 * width :]
     normed = jnp.concatenate([near_normed, far_normed], axis=0)
     grad_full = jnp.concatenate([near_grad, far_grad], axis=0)
     down_weight_grad = product_left_t(hidden, grad_full).astype(BF16)
+    far_keep, down_weight_grad = lax.optimization_barrier((far_keep, down_weight_grad))
+    far_total, gain = sum_over_y(far_keep, gain, x)
+    normed, far_total = lax.optimization_barrier((normed, far_total))
     gate_weight_grad = product_left_t(normed, gate_grad).astype(BF16)
     up_weight_grad = product_left_t(normed, up_grad).astype(BF16)
-    far_total, down_weight_grad, gate_weight_grad = lax.optimization_barrier(
-        (far_total, down_weight_grad, gate_weight_grad)
-    )
 
     gain_parts = [p.reshape(4, 256) for p in parts_of(gain, 2)]
     gain_rows = jnp.broadcast_to(jnp.concatenate(gain_parts, axis=1)[None], (16, 4, 512))

time: 185 us -> 196 us (1.059)
  waiting for transfers between devices: 83.3 us -> 93.6 us
    ppermute x32 -> x34, waiting for transfers between devices: 70.6 us -> 81.2 us  [send(): return lax.ppermute(value, AXES, pairs)]
    ppermute x32 -> x34, starting transfers between devices: 41.5 us -> 39.7 us  [send(): return lax.ppermute(value, AXES, pairs)]
    unnamed x52 -> x45, local copies, waits for them, and re-layouts: 6.93 us -> 7.42 us
  transfers between devices with their start and end apart: 34 -> 36, of which waited for: 17 -> 20; matrix products, arithmetic and copies ran while one was open for 15% -> 11% of each run, Pallas kernels for 0% -> 0%
where the time goes in v5:
time: 196 us
  waiting for transfers between devices  93.6 us (48%)
  starting transfers between devices  53.5 us (27%)
  matrix products  27 us (14%)
  local copies, waits for them, and re-layouts  11.7 us (6%)
  other arithmetic  8.51 us (4%)
    ppermute x34, waiting for transfers between devices, send(): return lax.ppermute(value, AXES, pairs)  81.2 us
    ppermute x34, starting transfers between devices, send(): return lax.ppermute(value, AXES, pairs)  39.7 us
    dot_general x3, matrix products, product_left_t(): lax.dot_general(left, right, (((0,), (0,)), ((), ())), preferred_element_...  13.4 us
    all_to_all x1, waiting for transfers between devices, per_device(): lax.all_to_all(message.reshape(16, 4, 2176), ('h', 'z', 'x'), split_axis=...  8.83 us
    all_to_all x1, starting transfers between devices, per_device(): lax.all_to_all(message.reshape(16, 4, 2176), ('h', 'z', 'x'), split_axis=...  7.96 us
    unnamed x45, local copies, waits for them, and re-layouts  7.42 us
    dot_general x6, matrix products, product_right_t(): lax.dot_general(left, right, (((1,), (1,)), ((), ())), preferred_element_...  6.96 us
    dot_general x6, matrix products, product(): return jnp.dot(left, right, preferred_element_type=F32)  6.69 us
  transfers between devices with their start and end apart: 36, of which 20 were waited for; matrix products, arithmetic and copies ran while one was open for 11% of the time, Pallas kernels for 0%

profile of v5, /device:TPU:0, one launch (start us, length us, event | category | flops | bytes accessed | tf_op | source)
XLA Modules:
  0.0 195.8 jit_solution(10542933758836912724)
XLA Ops:
  0.6 1.0 fusion.50
  4.0 8.0 %all-to-all-start = ((bf16[16,4,2176]{2,1,0:T(4,128)(2,1)}), bf16[16,4,2176]{2,1,0:T(4,128)(2,1)S(1)}, u32[]{:S(2)}, u32[]{:S(2)}) async-start(bf16[16,4,2176]{2,1,0:T(4,128)(2,1)} %bitcast.2), calls=%async_computation | async-start | bytes 557056 | tf_op jit(solution)/shard_map/all_to_all | solution.py:160
  12.0 8.8 %all-to-all-done = bf16[16,4,2176]{2,1,0:T(4,128)(2,1)S(1)} async-done(((bf16[16,4,2176]{2,1,0:T(4,128)(2,1)}), bf16[16,4,2176]{2,1,0:T(4,128)(2,1)S(1)}, u32[]{:S(2)}, u32[]{:S(2)}) %all-to-all-start) | async-done | bytes 278560 | tf_op jit(solution)/shard_map/all_to_all | solution.py:160
  21.0 3.1 %collective-permute-start.4 = (bf16[32,2176]{1,0:T(8,128)(2,1)S(1)}, bf16[32,2176]{1,0:T(8,128)(2,1)S(1)}, u32[]{:S(2)}, u32[]{:S(2)}) collective-permute-start(bf16[32,2176]{1,0:T(8,128)(2,1)S(1)} %get-tuple-element.35), channel_id=1, source_target_pairs={{0,6},{1,7},{2,0},{3,1},{4,2},{5,3},{6,4},{7,5},{8,14},{9,15},{10,... | collective-permute-start | bytes 417800 | tf_op jit(solution)/shard_map/ppermute | solution.py:24
  25.7 3.0 %collective-permute-done.4 = bf16[32,2176]{1,0:T(8,128)(2,1)S(1)} collective-permute-done((bf16[32,2176]{1,0:T(8,128)(2,1)S(1)}, bf16[32,2176]{1,0:T(8,128)(2,1)S(1)}, u32[]{:S(2)}, u32[]{:S(2)}) %collective-permute-start.4) | collective-permute-done | bytes 139296 | tf_op jit(solution)/shard_map/ppermute | solution.py:24
  28.6 2.2 %collective-permute-done.5 = bf16[32,2176]{1,0:T(8,128)(2,1)S(1)} collective-permute-done((bf16[32,2176]{1,0:T(8,128)(2,1)S(1)}, bf16[32,2176]{1,0:T(8,128)(2,1)S(1)}, u32[]{:S(2)}, u32[]{:S(2)}) %collective-permute-start.5) | collective-permute-done | bytes 139296 | tf_op jit(solution)/shard_map/ppermute | solution.py:24
  30.9 1.4 collective-permute-done
  34.6 4.3 %collective-permute-done.1 = bf16[32,2176]{1,0:T(8,128)(2,1)S(1)} collective-permute-done((bf16[32,2176]{1,0:T(8,128)(2,1)S(1)}, bf16[32,2176]{1,0:T(8,128)(2,1)S(1)}, u32[]{:S(2)}, u32[]{:S(2)}) %collective-permute-start.1) | collective-permute-done | bytes 139296 | tf_op jit(solution)/shard_map/ppermute | solution.py:24
  39.0 2.1 %collective-permute-done.2 = bf16[32,2176]{1,0:T(8,128)(2,1)S(1)} collective-permute-done((bf16[32,2176]{1,0:T(8,128)(2,1)S(1)}, bf16[32,2176]{1,0:T(8,128)(2,1)S(1)}, u32[]{:S(2)}, u32[]{:S(2)}) %collective-permute-start.2) | collective-permute-done | bytes 139296 | tf_op jit(solution)/shard_map/ppermute | solution.py:24
  41.1 2.2 %collective-permute-done.3 = bf16[32,2176]{1,0:T(8,128)(2,1)S(1)} collective-permute-done((bf16[32,2176]{1,0:T(8,128)(2,1)S(1)}, bf16[32,2176]{1,0:T(8,128)(2,1)S(1)}, u32[]{:S(2)}, u32[]{:S(2)}) %collective-permute-start.3) | collective-permute-done | bytes 139296 | tf_op jit(solution)/shard_map/ppermute | solution.py:24
  43.8 1.1 fusion.66
  45.9 1.1 fusion.67
  47.9 1.1 fusion.61
  51.0 2.4 %collective-permute-start.9 = (bf16[64,5376]{1,0:T(8,128)(2,1)S(1)}, bf16[64,5376]{1,0:T(8,128)(2,1)S(1)}, u32[]{:S(2)}, u32[]{:S(2)}) collective-permute-start(bf16[64,5376]{1,0:T(8,128)(2,1)S(1)} %get-tuple-element.43), channel_id=1, source_target_pairs={{0,48},{1,49},{2,50},{3,51},{4,52},{5,53},{6,54},{7,55},{8,56},{9,... | collective-permute-start | bytes 2064392 | tf_op jit(solution)/shard_map/ppermute | solution.py:24
  54.0 1.1 fusion.68
  56.0 1.1 fusion.69
  58.0 1.2 fusion.59
  60.4 3.2 %collective-permute-start.15 = (bf16[32,5376]{1,0:T(8,128)(2,1)}, bf16[32,5376]{1,0:T(8,128)(2,1)}, u32[]{:S(2)}, u32[]{:S(2)}) collective-permute-start(bf16[32,5376]{1,0:T(8,128)(2,1)} %get-tuple-element.40), channel_id=1, source_target_pairs={{0,48},{1,49},{2,50},{3,51},{4,52},{5,53},{6,54},{7,55},{8,56},{9,... | collective-permute-start | bytes 1032200 | tf_op jit(solution)/shard_map/ppermute | solution.py:24
  64.0 3.9 %collective-permute-done.11 = bf16[64,5376]{1,0:T(8,128)(2,1)S(1)} collective-permute-done((bf16[64,5376]{1,0:T(8,128)(2,1)S(1)}, bf16[64,5376]{1,0:T(8,128)(2,1)S(1)}, u32[]{:S(2)}, u32[]{:S(2)}) %collective-permute-start.11) | collective-permute-done | bytes 688160 | tf_op jit(solution)/shard_map/ppermute | solution.py:24
  69.6 1.8 collective-permute-start.13
  71.9 12.0 %collective-permute-done.12 = bf16[32,5376]{1,0:T(8,128)(2,1)S(1)} collective-permute-done((bf16[32,5376]{1,0:T(8,128)(2,1)S(1)}, bf16[32,5376]{1,0:T(8,128)(2,1)S(1)}, u32[]{:S(2)}, u32[]{:S(2)}) %collective-permute-start.12) | collective-permute-done | bytes 344096 | tf_op jit(solution)/shard_map/ppermute | solution.py:24
  84.1 3.2 %collective-permute-start.17 = (bf16[32,5376]{1,0:T(8,128)(2,1)S(1)}, bf16[32,5376]{1,0:T(8,128)(2,1)S(1)}, u32[]{:S(2)}, u32[]{:S(2)}) collective-permute-start(bf16[32,5376]{1,0:T(8,128)(2,1)S(1)} %get-tuple-element.25), channel_id=1, source_target_pairs={{0,48},{1,49},{2,50},{3,51},{4,52},{5,53},{6,54},{7,55},{8,56},{9,... | collective-permute-start | bytes 1032200 | tf_op jit(solution)/shard_map/ppermute | solution.py:24
  87.4 7.6 %collective-permute-done.16 = bf16[32,5376]{1,0:T(8,128)(2,1)S(1)} collective-permute-done((bf16[32,5376]{1,0:T(8,128)(2,1)S(1)}, bf16[32,5376]{1,0:T(8,128)(2,1)S(1)}, u32[]{:S(2)}, u32[]{:S(2)}) %collective-permute-start.16) | collective-permute-done | bytes 344096 | tf_op jit(solution)/shard_map/ppermute | solution.py:24
  95.0 1.4 fusion.5
  97.7 2.4 %collective-permute-start.22 = (bf16[64,5376]{1,0:T(8,128)(2,1)S(1)}, bf16[64,5376]{1,0:T(8,128)(2,1)S(1)}, u32[]{:S(2)}, u32[]{:S(2)}) collective-permute-start(bf16[64,5376]{1,0:T(8,128)(2,1)S(1)} %get-tuple-element.74), channel_id=1, source_target_pairs={{0,48},{1,49},{2,50},{3,51},{4,52},{5,53},{6,54},{7,55},{8,56},{9,... | collective-permute-start | bytes 2064392 | tf_op jit(solution)/shard_map/ppermute | solution.py:24
  100.1 1.3 collective-permute-start.18
  101.4 12.8 %collective-permute-done.20 = bf16[64,5376]{1,0:T(8,128)(2,1)S(1)} collective-permute-done((bf16[64,5376]{1,0:T(8,128)(2,1)S(1)}, bf16[64,5376]{1,0:T(8,128)(2,1)S(1)}, u32[]{:S(2)}, u32[]{:S(2)}) %collective-permute-start.20) | collective-permute-done | bytes 688160 | tf_op jit(solution)/shard_map/ppermute | solution.py:24
  114.3 3.5 %collective-permute-start.23 = (bf16[32,5376]{1,0:T(8,128)(2,1)S(1)}, bf16[32,5376]{1,0:T(8,128)(2,1)S(1)}, u32[]{:S(2)}, u32[]{:S(2)}) collective-permute-start(bf16[32,5376]{1,0:T(8,128)(2,1)S(1)} %slice.416), channel_id=1, source_target_pairs={{0,48},{1,49},{2,50},{3,51},{4,52},{5,53},{6,54},{7,55},{8,56},{9,... | collective-permute-start | bytes 1032200 | tf_op jit(solution)/shard_map/ppermute | solution.py:24
  118.0 5.4 %collective-permute-done.21 = bf16[32,5376]{1,0:T(8,128)(2,1)S(1)} collective-permute-done((bf16[32,5376]{1,0:T(8,128)(2,1)S(1)}, bf16[32,5376]{1,0:T(8,128)(2,1)S(1)}, u32[]{:S(2)}, u32[]{:S(2)}) %collective-permute-start.21) | collective-permute-done | bytes 344096 | tf_op jit(solution)/shard_map/ppermute | solution.py:24
  123.6 1.1 fusion.12
  125.6 1.1 fusion.15
  127.6 1.2 multiply_reduce_fusion.1
  129.4 3.3 %collective-permute-start.19 = (bf16[64,5376]{1,0:T(8,128)(2,1)S(1)}, bf16[64,5376]{1,0:T(8,128)(2,1)S(1)}, u32[]{:S(2)}, u32[]{:S(2)}) collective-permute-start(bf16[64,5376]{1,0:T(8,128)(2,1)S(1)} %collective-permute-done.18), channel_id=1, source_target_pairs={{0,48},{1,49},{2,50},{3,51},{4,52},{5,53},{6,54},{7,55},{8,56},{9,... | collective-permute-start | bytes 2064392 | tf_op jit(solution)/shard_map/ppermute | solution.py:24
  133.7 3.2 %collective-permute-start.28 = (bf16[32,2048]{1,0:T(8,128)(2,1)S(1)}, bf16[32,2048]{1,0:T(8,128)(2,1)S(1)}, u32[]{:S(2)}, u32[]{:S(2)}) collective-permute-start(bf16[32,2048]{1,0:T(8,128)(2,1)S(1)} %get-tuple-element.67), channel_id=1, source_target_pairs={{0,6},{1,7},{2,0},{3,1},{4,2},{5,3},{6,4},{7,5},{8,14},{9,15},{10,... | collective-permute-start | bytes 393224 | tf_op jit(solution)/shard_map/ppermute | solution.py:24
  137.0 11.0 %collective-permute-done.19 = bf16[64,5376]{1,0:T(8,128)(2,1)S(1)} collective-permute-done((bf16[64,5376]{1,0:T(8,128)(2,1)S(1)}, bf16[64,5376]{1,0:T(8,128)(2,1)S(1)}, u32[]{:S(2)}, u32[]{:S(2)}) %collective-permute-start.19) | collective-permute-done | bytes 688160 | tf_op jit(solution)/shard_map/ppermute | solution.py:24
  148.7 2.7 %collective-permute-done.25 = bf16[64,5376]{1,0:T(8,128)(2,1)S(1)} collective-permute-done((bf16[64,5376]{1,0:T(8,128)(2,1)S(1)}, bf16[64,5376]{1,0:T(8,128)(2,1)S(1)}, u32[]{:S(2)}, u32[]{:S(2)}) %collective-permute-start.25) | collective-permute-done | bytes 688160 | tf_op jit(solution)/shard_map/ppermute | solution.py:24
  151.7 3.0 %collective-permute-done.29 = bf16[32,2048]{1,0:T(8,128)(2,1)S(1)} collective-permute-done((bf16[32,2048]{1,0:T(8,128)(2,1)S(1)}, bf16[32,2048]{1,0:T(8,128)(2,1)S(1)}, u32[]{:S(2)}, u32[]{:S(2)}) %collective-permute-start.29) | collective-permute-done | bytes 131104 | tf_op jit(solution)/shard_map/ppermute | solution.py:24
  154.7 1.1 fusion.18
  155.8 1.1 fusion.20
  157.0 1.2 multiply_reduce_fusion
  158.7 4.0 %convolution_convert_fusion.2 = bf16[1792,1024]{1,0:T(8,128)(2,1)} fusion(bf16[512,5376]{1,0:T(8,128)(2,1)S(1)} %constant_dynamic-update-slice_fusion.6, bf16[256,1024]{1,0:T(8,128)(2,1)S(1)} %slice.391, bf16[256,1024]{1,0:T(8,128)(2,1)S(1)} %slice.400), kind=kOutput, calls=%fused_computation.32 | convolution fusion | flops 1882980352 | bytes 6553600 | tf_op jit(solution)/shard_map/dot_general | solution.py:36
  163.0 3.2 %collective-permute-start.32 = (bf16[32,2176]{1,0:T(8,128)(2,1)S(1)}, bf16[32,2176]{1,0:T(8,128)(2,1)S(1)}, u32[]{:S(2)}, u32[]{:S(2)}) collective-permute-start(bf16[32,2176]{1,0:T(8,128)(2,1)S(1)} %get-tuple-element.83), channel_id=1, source_target_pairs={{0,6},{1,7},{2,0},{3,1},{4,2},{5,3},{6,4},{7,5},{8,14},{9,15},{10,... | collective-permute-start | bytes 417800 | tf_op jit(solution)/shard_map/ppermute | solution.py:24
  166.3 4.0 %collective-permute-done.31 = bf16[32,2176]{1,0:T(8,128)(2,1)S(1)} collective-permute-done((bf16[32,2176]{1,0:T(8,128)(2,1)S(1)}, bf16[32,2176]{1,0:T(8,128)(2,1)S(1)}, u32[]{:S(2)}, u32[]{:S(2)}) %collective-permute-start.31) | collective-permute-done | bytes 139296 | tf_op jit(solution)/shard_map/ppermute | solution.py:24
  170.3 2.2 %collective-permute-done.32 = bf16[32,2176]{1,0:T(8,128)(2,1)S(1)} collective-permute-done((bf16[32,2176]{1,0:T(8,128)(2,1)S(1)}, bf16[32,2176]{1,0:T(8,128)(2,1)S(1)}, u32[]{:S(2)}, u32[]{:S(2)}) %collective-permute-start.32) | collective-permute-done | bytes 139296 | tf_op jit(solution)/shard_map/ppermute | solution.py:24
  173.3 4.0 %convolution_convert_fusion = bf16[1024,1792]{1,0:T(8,128)(2,1)} fusion(bf16[512,1024]{1,0:T(8,128)(2,1)S(1)} %pad_maximum_fusion.3, bf16[512,5376]{1,0:T(8,128)(2,1)S(1)} %constant_dynamic-update-slice_fusion.6), kind=kOutput, calls=%fused_computation.30 | convolution fusion | flops 1880883200 | bytes 6553600 | tf_op jit(solution)/shard_map/dot_general | solution.py:36
  178.4 5.8 %all-to-all-start.1 = ((bf16[16,4,2560]{2,1,0:T(4,128)(2,1)}), bf16[16,4,2560]{2,1,0:T(4,128)(2,1)S(1)}, u32[]{:S(2)}, u32[]{:S(2)}) async-start(bf16[16,4,2560]{2,1,0:T(4,128)(2,1)} %pad_maximum_fusion.6), calls=%async_computation.1 | async-start | bytes 655360 | tf_op jit(solution)/shard_map/all_to_all | solution.py:241
  184.2 5.5 %convolution_convert_fusion.1 = bf16[1024,1792]{1,0:T(8,128)(2,1)} fusion(bf16[512,1024]{1,0:T(8,128)(2,1)S(1)} %pad_maximum_fusion.3, bf16[512,5376]{1,0:T(8,128)(2,1)} %copy-done.2), kind=kOutput, calls=%fused_computation.31 | convolution fusion | flops 1880883200 | bytes 6553600 | tf_op jit(solution)/shard_map/dot_general | solution.py:36
  189.6 3.6 %all-to-all-done.1 = bf16[16,4,2560]{2,1,0:T(4,128)(2,1)S(1)} async-done(((bf16[16,4,2560]{2,1,0:T(4,128)(2,1)}), bf16[16,4,2560]{2,1,0:T(4,128)(2,1)S(1)}, u32[]{:S(2)}, u32[]{:S(2)}) %all-to-all-start.1) | async-done | bytes 327712 | tf_op jit(solution)/shard_map/all_to_all | solution.py:241
  (173 shorter events, 28.2 us)
Async XLA Ops:
  0.6 23.4 %copy-start.1 = (f32[8192]{0:T(1024)S(1)}, f32[8192]{0:T(1024)}, u32[]{:S(2)}) copy-start(f32[8192]{0:T(1024)} %param.7) | copy-start | bytes 98308
  4.0 16.8 %all-to-all-start = ((bf16[16,4,2176]{2,1,0:T(4,128)(2,1)}), bf16[16,4,2176]{2,1,0:T(4,128)(2,1)S(1)}, u32[]{:S(2)}, u32[]{:S(2)}) async-start(bf16[16,4,2176]{2,1,0:T(4,128)(2,1)} %bitcast.2), calls=%async_computation | async-start | bytes 557056 | tf_op jit(solution)/shard_map/all_to_all | solution.py:160
  21.0 7.7 %collective-permute-start.4 = (bf16[32,2176]{1,0:T(8,128)(2,1)S(1)}, bf16[32,2176]{1,0:T(8,128)(2,1)S(1)}, u32[]{:S(2)}, u32[]{:S(2)}) collective-permute-start(bf16[32,2176]{1,0:T(8,128)(2,1)S(1)} %get-tuple-element.35), channel_id=1, source_target_pairs={{0,6},{1,7},{2,0},{3,1},{4,2},{5,3},{6,4},{7,5},{8,14},{9,15},{10,... | collective-permute-start | bytes 417800 | tf_op jit(solution)/shard_map/ppermute | solution.py:24
  24.1 6.8 %collective-permute-start.5 = (bf16[32,2176]{1,0:T(8,128)(2,1)S(1)}, bf16[32,2176]{1,0:T(8,128)(2,1)S(1)}, u32[]{:S(2)}, u32[]{:S(2)}) collective-permute-start(bf16[32,2176]{1,0:T(8,128)(2,1)S(1)} %get-tuple-element.35), channel_id=1, source_target_pairs={{0,4},{1,5},{2,6},{3,7},{4,0},{5,1},{6,2},{7,3},{8,12},{9,13},{10,... | collective-permute-start | bytes 417800 | tf_op jit(solution)/shard_map/ppermute | solution.py:24
  24.7 7.6 %collective-permute-start = (bf16[32,2176]{1,0:T(8,128)(2,1)S(1)}, bf16[32,2176]{1,0:T(8,128)(2,1)S(1)}, u32[]{:S(2)}, u32[]{:S(2)}) collective-permute-start(bf16[32,2176]{1,0:T(8,128)(2,1)S(1)} %get-tuple-element.35), channel_id=1, source_target_pairs={{0,2},{1,3},{2,4},{3,5},{4,6},{5,7},{6,0},{7,1},{8,10},{9,11},{10,... | collective-permute-start | bytes 417800 | tf_op jit(solution)/shard_map/ppermute | solution.py:24
  32.3 11.0 %collective-permute-start.6 = (bf16[128,2176]{1,0:T(8,128)(2,1)S(1)}, bf16[128,2176]{1,0:T(8,128)(2,1)S(1)}, u32[]{:S(2)}, u32[]{:S(2)}) collective-permute-start(bf16[128,2176]{1,0:T(8,128)(2,1)S(1)} %constant_dynamic-update-slice_fusion.12), channel_id=1, source_target_pairs={{0,1},{1,0},{2,3},{3,2},{4,5},{5,4},{6,7},{7,6},{8,9},{9,8},{10,11... | collective-permute-start | bytes 1671176 | tf_op jit(solution)/shard_map/ppermute | solution.py:24
  32.4 6.5 %collective-permute-start.1 = (bf16[32,2176]{1,0:T(8,128)(2,1)S(1)}, bf16[32,2176]{1,0:T(8,128)(2,1)S(1)}, u32[]{:S(2)}, u32[]{:S(2)}) collective-permute-start(bf16[32,2176]{1,0:T(8,128)(2,1)S(1)} %get-tuple-element.19), channel_id=1, source_target_pairs={{0,6},{1,7},{2,0},{3,1},{4,2},{5,3},{6,4},{7,5},{8,14},{9,15},{10,... | collective-permute-start | bytes 417800 | tf_op jit(solution)/shard_map/ppermute | solution.py:24
  33.0 8.0 %collective-permute-start.2 = (bf16[32,2176]{1,0:T(8,128)(2,1)S(1)}, bf16[32,2176]{1,0:T(8,128)(2,1)S(1)}, u32[]{:S(2)}, u32[]{:S(2)}) collective-permute-start(bf16[32,2176]{1,0:T(8,128)(2,1)S(1)} %get-tuple-element.19), channel_id=1, source_target_pairs={{0,4},{1,5},{2,6},{3,7},{4,0},{5,1},{6,2},{7,3},{8,12},{9,13},{10,... | collective-permute-start | bytes 417800 | tf_op jit(solution)/shard_map/ppermute | solution.py:24
  33.7 9.6 %collective-permute-start.3 = (bf16[32,2176]{1,0:T(8,128)(2,1)S(1)}, bf16[32,2176]{1,0:T(8,128)(2,1)S(1)}, u32[]{:S(2)}, u32[]{:S(2)}) collective-permute-start(bf16[32,2176]{1,0:T(8,128)(2,1)S(1)} %get-tuple-element.19), channel_id=1, source_target_pairs={{0,2},{1,3},{2,4},{3,5},{4,6},{5,7},{6,0},{7,1},{8,10},{9,11},{10,... | collective-permute-start | bytes 417800 | tf_op jit(solution)/shard_map/ppermute | solution.py:24
  34.6 9.3 %copy-start.3 = (bf16[1024,1792]{1,0:T(8,128)(2,1)S(1)}, bf16[1024,1792]{1,0:T(8,128)(2,1)}, u32[]{:S(2)}) copy-start(bf16[1024,1792]{1,0:T(8,128)(2,1)} %param.8) | copy-start | bytes 11010052
  43.8 2.0 %copy-start.8 = (bf16[1024,1792]{1,0:T(8,128)(2,1)S(1)}, bf16[1024,1792]{1,0:T(8,128)(2,1)}, u32[]{:S(2)}) copy-start(bf16[1024,1792]{1,0:T(8,128)(2,1)} %param.9) | copy-start | bytes 11010052
  45.9 2.0 %copy-start.5 = (bf16[1792,1024]{1,0:T(8,128)(2,1)S(1)}, bf16[1792,1024]{1,0:T(8,128)(2,1)}, u32[]{:S(2)}) copy-start(bf16[1792,1024]{1,0:T(8,128)(2,1)} %param.10) | copy-start | bytes 11010052
  49.4 4.0 %collective-permute-start.7 = (bf16[128,2176]{1,0:T(8,128)(2,1)S(1)}, bf16[128,2176]{1,0:T(8,128)(2,1)S(1)}, u32[]{:S(2)}, u32[]{:S(2)}) collective-permute-start(bf16[128,2176]{1,0:T(8,128)(2,1)S(1)} %constant_dynamic-update-slice_fusion.16), channel_id=1, source_target_pairs={{0,1},{1,0},{2,3},{3,2},{4,5},{5,4},{6,7},{7,6},{8,9},{9,8},{10,11... | collective-permute-start | bytes 1671176 | tf_op jit(solution)/shard_map/ppermute | solution.py:24
  50.0 17.9 %collective-permute-start.11 = (bf16[64,5376]{1,0:T(8,128)(2,1)S(1)}, bf16[64,5376]{1,0:T(8,128)(2,1)S(1)}, u32[]{:S(2)}, u32[]{:S(2)}) collective-permute-start(bf16[64,5376]{1,0:T(8,128)(2,1)S(1)} %get-tuple-element.42), channel_id=1, source_target_pairs={{0,64},{1,65},{2,66},{3,67},{4,68},{5,69},{6,70},{7,71},{8,72},{9,... | collective-permute-start | bytes 2064392 | tf_op jit(solution)/shard_map/ppermute | solution.py:24
  50.1 19.5 %collective-permute-start.8 = (bf16[64,5376]{1,0:T(8,128)(2,1)S(1)}, bf16[64,5376]{1,0:T(8,128)(2,1)S(1)}, u32[]{:S(2)}, u32[]{:S(2)}) collective-permute-start(bf16[64,5376]{1,0:T(8,128)(2,1)S(1)} %get-tuple-element.44), channel_id=1, source_target_pairs={{0,16},{1,17},{2,18},{3,19},{4,20},{5,21},{6,22},{7,23},{8,24},{9,... | collective-permute-start | bytes 2064392 | tf_op jit(solution)/shard_map/ppermute | solution.py:24
  51.0 20.4 %collective-permute-start.9 = (bf16[64,5376]{1,0:T(8,128)(2,1)S(1)}, bf16[64,5376]{1,0:T(8,128)(2,1)S(1)}, u32[]{:S(2)}, u32[]{:S(2)}) collective-permute-start(bf16[64,5376]{1,0:T(8,128)(2,1)S(1)} %get-tuple-element.43), channel_id=1, source_target_pairs={{0,48},{1,49},{2,50},{3,51},{4,52},{5,53},{6,54},{7,55},{8,56},{9,... | collective-permute-start | bytes 2064392 | tf_op jit(solution)/shard_map/ppermute | solution.py:24
  53.9 2.0 %copy-start.9 = (bf16[1024,1792]{1,0:T(8,128)(2,1)S(1)}, bf16[1024,1792]{1,0:T(8,128)(2,1)}, u32[]{:S(2)}) copy-start(bf16[1024,1792]{1,0:T(8,128)(2,1)} %param.9) | copy-start | bytes 11010052
  56.0 2.0 %copy-start.6 = (bf16[1792,1024]{1,0:T(8,128)(2,1)S(1)}, bf16[1792,1024]{1,0:T(8,128)(2,1)}, u32[]{:S(2)}) copy-start(bf16[1792,1024]{1,0:T(8,128)(2,1)} %param.10) | copy-start | bytes 11010052
  60.4 23.7 %collective-permute-start.14 = (bf16[32,5376]{1,0:T(8,128)(2,1)}, bf16[32,5376]{1,0:T(8,128)(2,1)}, u32[]{:S(2)}, u32[]{:S(2)}) collective-permute-start(bf16[32,5376]{1,0:T(8,128)(2,1)} %get-tuple-element.41), channel_id=1, source_target_pairs={{0,16},{1,17},{2,18},{3,19},{4,20},{5,21},{6,22},{7,23},{8,24},{9,... | collective-permute-start | bytes 1032200 | tf_op jit(solution)/shard_map/ppermute | solution.py:24
  60.4 23.7 %collective-permute-start.15 = (bf16[32,5376]{1,0:T(8,128)(2,1)}, bf16[32,5376]{1,0:T(8,128)(2,1)}, u32[]{:S(2)}, u32[]{:S(2)}) collective-permute-start(bf16[32,5376]{1,0:T(8,128)(2,1)} %get-tuple-element.40), channel_id=1, source_target_pairs={{0,48},{1,49},{2,50},{3,51},{4,52},{5,53},{6,54},{7,55},{8,56},{9,... | collective-permute-start | bytes 1032200 | tf_op jit(solution)/shard_map/ppermute | solution.py:24
  68.0 15.9 %collective-permute-start.12 = (bf16[32,5376]{1,0:T(8,128)(2,1)S(1)}, bf16[32,5376]{1,0:T(8,128)(2,1)S(1)}, u32[]{:S(2)}, u32[]{:S(2)}) collective-permute-start(bf16[32,5376]{1,0:T(8,128)(2,1)S(1)} %get-tuple-element.76), channel_id=1, source_target_pairs={{0,16},{1,17},{2,18},{3,19},{4,20},{5,21},{6,22},{7,23},{8,24},{9,... | collective-permute-start | bytes 1032200 | tf_op jit(solution)/shard_map/ppermute | solution.py:24
  69.6 14.3 %collective-permute-start.13 = (bf16[32,5376]{1,0:T(8,128)(2,1)S(1)}, bf16[32,5376]{1,0:T(8,128)(2,1)S(1)}, u32[]{:S(2)}, u32[]{:S(2)}) collective-permute-start(bf16[32,5376]{1,0:T(8,128)(2,1)S(1)} %get-tuple-element.75), channel_id=1, source_target_pairs={{0,48},{1,49},{2,50},{3,51},{4,52},{5,53},{6,54},{7,55},{8,56},{9,... | collective-permute-start | bytes 1032200 | tf_op jit(solution)/shard_map/ppermute | solution.py:24
  71.6 23.4 %collective-permute-start.10 = (bf16[64,5376]{1,0:T(8,128)(2,1)S(1)}, bf16[64,5376]{1,0:T(8,128)(2,1)S(1)}, u32[]{:S(2)}, u32[]{:S(2)}) collective-permute-start(bf16[64,5376]{1,0:T(8,128)(2,1)S(1)} %fusion.7), channel_id=1, source_target_pairs={{0,64},{1,65},{2,66},{3,67},{4,68},{5,69},{6,70},{7,71},{8,72},{9,... | collective-permute-start | bytes 2064392 | tf_op jit(solution)/shard_map/ppermute | solution.py:24
  84.0 10.9 %collective-permute-start.16 = (bf16[32,5376]{1,0:T(8,128)(2,1)S(1)}, bf16[32,5376]{1,0:T(8,128)(2,1)S(1)}, u32[]{:S(2)}, u32[]{:S(2)}) collective-permute-start(bf16[32,5376]{1,0:T(8,128)(2,1)S(1)} %get-tuple-element.22), channel_id=1, source_target_pairs={{0,16},{1,17},{2,18},{3,19},{4,20},{5,21},{6,22},{7,23},{8,24},{9,... | collective-permute-start | bytes 1032200 | tf_op jit(solution)/shard_map/ppermute | solution.py:24
  84.1 10.9 %collective-permute-start.17 = (bf16[32,5376]{1,0:T(8,128)(2,1)S(1)}, bf16[32,5376]{1,0:T(8,128)(2,1)S(1)}, u32[]{:S(2)}, u32[]{:S(2)}) collective-permute-start(bf16[32,5376]{1,0:T(8,128)(2,1)S(1)} %get-tuple-element.25), channel_id=1, source_target_pairs={{0,48},{1,49},{2,50},{3,51},{4,52},{5,53},{6,54},{7,55},{8,56},{9,... | collective-permute-start | bytes 1032200 | tf_op jit(solution)/shard_map/ppermute | solution.py:24
  96.8 17.4 %collective-permute-start.20 = (bf16[64,5376]{1,0:T(8,128)(2,1)S(1)}, bf16[64,5376]{1,0:T(8,128)(2,1)S(1)}, u32[]{:S(2)}, u32[]{:S(2)}) collective-permute-start(bf16[64,5376]{1,0:T(8,128)(2,1)S(1)} %get-tuple-element.74), channel_id=1, source_target_pairs={{0,16},{1,17},{2,18},{3,19},{4,20},{5,21},{6,22},{7,23},{8,24},{9,... | collective-permute-start | bytes 2064392 | tf_op jit(solution)/shard_map/ppermute | solution.py:24
  97.7 16.6 %collective-permute-start.22 = (bf16[64,5376]{1,0:T(8,128)(2,1)S(1)}, bf16[64,5376]{1,0:T(8,128)(2,1)S(1)}, u32[]{:S(2)}, u32[]{:S(2)}) collective-permute-start(bf16[64,5376]{1,0:T(8,128)(2,1)S(1)} %get-tuple-element.74), channel_id=1, source_target_pairs={{0,48},{1,49},{2,50},{3,51},{4,52},{5,53},{6,54},{7,55},{8,56},{9,... | collective-permute-start | bytes 2064392 | tf_op jit(solution)/shard_map/ppermute | solution.py:24
  100.1 29.3 %collective-permute-start.18 = (bf16[64,5376]{1,0:T(8,128)(2,1)S(1)}, bf16[64,5376]{1,0:T(8,128)(2,1)S(1)}, u32[]{:S(2)}, u32[]{:S(2)}) collective-permute-start(bf16[64,5376]{1,0:T(8,128)(2,1)S(1)} %get-tuple-element.74), channel_id=1, source_target_pairs={{0,64},{1,65},{2,66},{3,67},{4,68},{5,69},{6,70},{7,71},{8,72},{9,... | collective-permute-start | bytes 2064392 | tf_op jit(solution)/shard_map/ppermute | solution.py:24
  114.2 9.1 %collective-permute-start.21 = (bf16[32,5376]{1,0:T(8,128)(2,1)S(1)}, bf16[32,5376]{1,0:T(8,128)(2,1)S(1)}, u32[]{:S(2)}, u32[]{:S(2)}) collective-permute-start(bf16[32,5376]{1,0:T(8,128)(2,1)S(1)} %slice.415), channel_id=1, source_target_pairs={{0,16},{1,17},{2,18},{3,19},{4,20},{5,21},{6,22},{7,23},{8,24},{9,... | collective-permute-start | bytes 1032200 | tf_op jit(solution)/shard_map/ppermute | solution.py:24
  114.3 9.0 %collective-permute-start.23 = (bf16[32,5376]{1,0:T(8,128)(2,1)S(1)}, bf16[32,5376]{1,0:T(8,128)(2,1)S(1)}, u32[]{:S(2)}, u32[]{:S(2)}) collective-permute-start(bf16[32,5376]{1,0:T(8,128)(2,1)S(1)} %slice.416), channel_id=1, source_target_pairs={{0,48},{1,49},{2,50},{3,51},{4,52},{5,53},{6,54},{7,55},{8,56},{9,... | collective-permute-start | bytes 1032200 | tf_op jit(solution)/shard_map/ppermute | solution.py:24
  117.9 5.6 %copy-start.10 = (bf16[1024,1792]{1,0:T(8,128)(2,1)S(1)}, bf16[1024,1792]{1,0:T(8,128)(2,1)}, u32[]{:S(2)}) copy-start(bf16[1024,1792]{1,0:T(8,128)(2,1)} %param.9) | copy-start | bytes 11010052
  123.6 2.0 %copy-start.7 = (bf16[1792,1024]{1,0:T(8,128)(2,1)S(1)}, bf16[1792,1024]{1,0:T(8,128)(2,1)}, u32[]{:S(2)}) copy-start(bf16[1792,1024]{1,0:T(8,128)(2,1)} %param.10) | copy-start | bytes 11010052
  125.6 2.0 %copy-start.4 = (bf16[1024,1792]{1,0:T(8,128)(2,1)S(1)}, bf16[1024,1792]{1,0:T(8,128)(2,1)}, u32[]{:S(2)}) copy-start(bf16[1024,1792]{1,0:T(8,128)(2,1)} %param.8) | copy-start | bytes 11010052
  129.1 4.4 %collective-permute-start.26 = (f32[128,2048]{1,0:T(8,128)S(1)}, f32[128,2048]{1,0:T(8,128)S(1)}, u32[]{:S(2)}, u32[]{:S(2)}) collective-permute-start(f32[128,2048]{1,0:T(8,128)S(1)} %fusion.8), channel_id=1, source_target_pairs={{0,1},{1,0},{2,3},{3,2},{4,5},{5,4},{6,7},{7,6},{8,9},{9,8},{10,11... | collective-permute-start | bytes 3145736 | tf_op jit(solution)/shard_map/ppermute | solution.py:24
  129.4 18.6 %collective-permute-start.19 = (bf16[64,5376]{1,0:T(8,128)(2,1)S(1)}, bf16[64,5376]{1,0:T(8,128)(2,1)S(1)}, u32[]{:S(2)}, u32[]{:S(2)}) collective-permute-start(bf16[64,5376]{1,0:T(8,128)(2,1)S(1)} %collective-permute-done.18), channel_id=1, source_target_pairs={{0,48},{1,49},{2,50},{3,51},{4,52},{5,53},{6,54},{7,55},{8,56},{9,... | collective-permute-start | bytes 2064392 | tf_op jit(solution)/shard_map/ppermute | solution.py:24
  132.7 18.8 %collective-permute-start.25 = (bf16[64,5376]{1,0:T(8,128)(2,1)S(1)}, bf16[64,5376]{1,0:T(8,128)(2,1)S(1)}, u32[]{:S(2)}, u32[]{:S(2)}) collective-permute-start(bf16[64,5376]{1,0:T(8,128)(2,1)S(1)} %collective-permute-done.18), channel_id=1, source_target_pairs={{0,16},{1,17},{2,18},{3,19},{4,20},{5,21},{6,22},{7,23},{8,24},{9,... | collective-permute-start | bytes 2064392 | tf_op jit(solution)/shard_map/ppermute | solution.py:24
  132.7 18.7 %collective-permute-start.24 = (bf16[64,5376]{1,0:T(8,128)(2,1)S(1)}, bf16[64,5376]{1,0:T(8,128)(2,1)S(1)}, u32[]{:S(2)}, u32[]{:S(2)}) collective-permute-start(bf16[64,5376]{1,0:T(8,128)(2,1)S(1)} %pad_maximum_fusion.5), channel_id=1, source_target_pairs={{0,64},{1,65},{2,66},{3,67},{4,68},{5,69},{6,70},{7,71},{8,72},{9,... | collective-permute-start | bytes 2064392 | tf_op jit(solution)/shard_map/ppermute | solution.py:24
  133.7 18.0 %collective-permute-start.27 = (bf16[32,2048]{1,0:T(8,128)(2,1)S(1)}, bf16[32,2048]{1,0:T(8,128)(2,1)S(1)}, u32[]{:S(2)}, u32[]{:S(2)}) collective-permute-start(bf16[32,2048]{1,0:T(8,128)(2,1)S(1)} %get-tuple-element.65), channel_id=1, source_target_pairs={{0,2},{1,3},{2,4},{3,5},{4,6},{5,7},{6,0},{7,1},{8,10},{9,11},{10,... | collective-permute-start | bytes 393224 | tf_op jit(solution)/shard_map/ppermute | solution.py:24
  133.7 17.9 %collective-permute-start.28 = (bf16[32,2048]{1,0:T(8,128)(2,1)S(1)}, bf16[32,2048]{1,0:T(8,128)(2,1)S(1)}, u32[]{:S(2)}, u32[]{:S(2)}) collective-permute-start(bf16[32,2048]{1,0:T(8,128)(2,1)S(1)} %get-tuple-element.67), channel_id=1, source_target_pairs={{0,6},{1,7},{2,0},{3,1},{4,2},{5,3},{6,4},{7,5},{8,14},{9,15},{10,... | collective-permute-start | bytes 393224 | tf_op jit(solution)/shard_map/ppermute | solution.py:24
  148.0 6.6 %collective-permute-start.29 = (bf16[32,2048]{1,0:T(8,128)(2,1)S(1)}, bf16[32,2048]{1,0:T(8,128)(2,1)S(1)}, u32[]{:S(2)}, u32[]{:S(2)}) collective-permute-start(bf16[32,2048]{1,0:T(8,128)(2,1)S(1)} %get-tuple-element.66), channel_id=1, source_target_pairs={{0,4},{1,5},{2,6},{3,7},{4,0},{5,1},{6,2},{7,3},{8,12},{9,13},{10,... | collective-permute-start | bytes 393224 | tf_op jit(solution)/shard_map/ppermute | solution.py:24
  158.4 4.2 %collective-permute-start.30 = (f32[136,2048]{1,0:T(8,128)S(1)}, f32[136,2048]{1,0:T(8,128)S(1)}, u32[]{:S(2)}, u32[]{:S(2)}) collective-permute-start(f32[136,2048]{1,0:T(8,128)S(1)} %constant_dynamic-update-slice_fusion.5), channel_id=1, source_target_pairs={{0,1},{1,0},{2,3},{3,2},{4,5},{5,4},{6,7},{7,6},{8,9},{9,8},{10,11... | collective-permute-start | bytes 3342344 | tf_op jit(solution)/shard_map/ppermute | solution.py:24
  158.7 14.6 %copy-start.2 = (bf16[512,5376]{1,0:T(8,128)(2,1)}, bf16[512,5376]{1,0:T(8,128)(2,1)S(1)}, u32[]{:S(2)}) copy-start(bf16[512,5376]{1,0:T(8,128)(2,1)S(1)} %constant_dynamic-update-slice_fusion.6) | copy-start | bytes 16515076
  162.9 7.4 %collective-permute-start.31 = (bf16[32,2176]{1,0:T(8,128)(2,1)S(1)}, bf16[32,2176]{1,0:T(8,128)(2,1)S(1)}, u32[]{:S(2)}, u32[]{:S(2)}) collective-permute-start(bf16[32,2176]{1,0:T(8,128)(2,1)S(1)} %get-tuple-element.84), channel_id=1, source_target_pairs={{0,2},{1,3},{2,4},{3,5},{4,6},{5,7},{6,0},{7,1},{8,10},{9,11},{10,... | collective-permute-start | bytes 417800 | tf_op jit(solution)/shard_map/ppermute | solution.py:24
  163.0 9.5 %collective-permute-start.32 = (bf16[32,2176]{1,0:T(8,128)(2,1)S(1)}, bf16[32,2176]{1,0:T(8,128)(2,1)S(1)}, u32[]{:S(2)}, u32[]{:S(2)}) collective-permute-start(bf16[32,2176]{1,0:T(8,128)(2,1)S(1)} %get-tuple-element.83), channel_id=1, source_target_pairs={{0,6},{1,7},{2,0},{3,1},{4,2},{5,3},{6,4},{7,5},{8,14},{9,15},{10,... | collective-permute-start | bytes 417800 | tf_op jit(solution)/shard_map/ppermute | solution.py:24
  166.2 7.0 %collective-permute-start.33 = (bf16[32,2176]{1,0:T(8,128)(2,1)S(1)}, bf16[32,2176]{1,0:T(8,128)(2,1)S(1)}, u32[]{:S(2)}, u32[]{:S(2)}) collective-permute-start(bf16[32,2176]{1,0:T(8,128)(2,1)S(1)} %get-tuple-element.82), channel_id=1, source_target_pairs={{0,4},{1,5},{2,6},{3,7},{4,0},{5,1},{6,2},{7,3},{8,12},{9,13},{10,... | collective-permute-start | bytes 417800 | tf_op jit(solution)/shard_map/ppermute | solution.py:24
  178.4 14.8 %all-to-all-start.1 = ((bf16[16,4,2560]{2,1,0:T(4,128)(2,1)}), bf16[16,4,2560]{2,1,0:T(4,128)(2,1)S(1)}, u32[]{:S(2)}, u32[]{:S(2)}) async-start(bf16[16,4,2560]{2,1,0:T(4,128)(2,1)} %pad_maximum_fusion.6), calls=%async_computation.1 | async-start | bytes 655360 | tf_op jit(solution)/shard_map/all_to_all | solution.py:241
  189.6 3.8 %copy-start = (bf16[4,8192]{1,0:T(4,128)(2,1)S(1)}, bf16[4,8192]{1,0:T(4,128)(2,1)}, u32[]{:S(2)}) copy-start(bf16[4,8192]{1,0:T(4,128)(2,1)} %param.6) | copy-start | bytes 196612

commit v6 on v5

--- a/solution.py
+++ b/solution.py
@@ -57,7 +57,7 @@
     core = jnp.zeros((128, n), own.dtype)
     for dy in range(YS):
         core = lax.dynamic_update_slice(core, over_y[dy], ((dy - x) % XS * 32, 0))
-    return core, over_y[3]
+    return core
 
 
 def both_cores(core):
@@ -65,43 +65,38 @@
     return jnp.concatenate([v[i * 32 : i * 32 + 32] for i in range(XS) for v in both], axis=0)
 
 
-def sum_over_core(partial, gain_partial):
-    n = partial.shape[1]
-    split = [partial[i * 32 : i * 32 + 32] for i in range(2 * XS)]
-    give = split[1::2]
-    if gain_partial is not None:
-        give = give + [jnp.pad(gain_partial, ((0, 0), (0, n - 128)))]
-    taken = send(jnp.concatenate(give, axis=0), c=1)
-    keep = jnp.concatenate(split[::2], axis=0) + taken[:128]
-    if gain_partial is not None:
-        gain_partial = gain_partial + taken[128:, :128]
-    return keep, gain_partial
+def sum_over_core(near, far, gain):
+    n = near.shape[1]
+
+    def rows_of(core):
+        return [
+            half[i * 64 + core * 32 : i * 64 + core * 32 + 32]
+            for i in range(XS)
+            for half in (near, far)
+        ]
+
+    gain_rows = jnp.pad(gain, ((0, 0), (0, n - 128)))
+    taken = send(jnp.concatenate(rows_of(1) + [gain_rows], axis=0), c=1)
+    return jnp.concatenate(rows_of(0), axis=0) + taken[:256], gain + taken[256:, :128]
 
 
 def sum_over_y(keep, gain, x):
     n = keep.shape[1]
 
     def piece(dy):
-        return lax.dynamic_slice(keep, ((dy - x) % XS * 32, 0), (32, n))
+        return lax.dynamic_slice(keep, ((dy - x) % XS * 64, 0), (64, n))
 
     def gain_of(parts):
         return parts[:8].astype(F32) + parts[8:16].astype(F32)
 
-    if gain is not None:
-        parts = jnp.concatenate(parts_of(gain, 2) + [jnp.zeros((16, 128), BF16)], axis=0)
-        gains = {0: gain_of(parts)}
+    parts = jnp.concatenate(parts_of(gain, 2) + [jnp.zeros((48, 128), BF16)], axis=0)
+    gains = {0: gain_of(parts)}
     total = piece(0)
     for dy in (1, 3, 2):
-        message = piece(dy).astype(BF16)
-        if gain is not None:
-            message = jnp.concatenate([message, parts], axis=1)
-        got = send(message, y=dy)
+        got = send(jnp.concatenate([piece(dy).astype(BF16), parts], axis=1), y=dy)
         total = total + got[:, :n].astype(F32)
-        if gain is not None:
-            gains[dy] = gain_of(got[:, n:])
-    if gain is not None:
-        gain = (gains[0] + gains[2]) + (gains[1] + gains[3])
-    return total, gain
+        gains[dy] = gain_of(got[:, n:])
+    return total, (gains[0] + gains[2]) + (gains[1] + gains[3])
 
 
 def sum_over_row(near, far):
@@ -134,10 +129,9 @@
     pb = send(p, x=3)
     across = jnp.concatenate([a2, b2], axis=0)
     p2 = send(across, z=1)
-    return (
-        jnp.concatenate([own, b, across, a], axis=0),
-        jnp.concatenate([p, pb, p2, pa], axis=0),
-    )
+    near = jnp.concatenate([own, b, across, a], axis=0)
+    near, pb = lax.optimization_barrier((near, pb))
+    return near, jnp.concatenate([p, pb, p2, pa], axis=0)
 
 
 def per_device(inputs, rms_gain_vector, gate_weight, up_weight, down_weight, out_grad):
@@ -182,17 +176,17 @@
             axis=1,
         ).reshape(4, 64, 3 * width)
 
-    far_core, first = gather_half(lax.dynamic_slice(block, ((1 - z) * 32, 0), (32, 2176)), x)
-    near_block, _ = lax.optimization_barrier(
-        (lax.dynamic_slice(block, (z * 32, 0), (32, 2176)), first)
-    )
-    near_core, _ = gather_half(near_block, x)
+    far_core = gather_half(lax.dynamic_slice(block, ((1 - z) * 32, 0), (32, 2176)), x)
+    near_block, far_core = lax.optimization_barrier(
+        (lax.dynamic_slice(block, (z * 32, 0), (32, 2176)), far_core)
+    )
+    near_core = gather_half(near_block, x)
     far_estimate, far_normed, far_grad = normed_of(both_cores(far_core))
     far = partials(far_normed, far_grad)
-    near_core, far = lax.optimization_barrier((near_core, far))
+    near_core, far_own = lax.optimization_barrier((near_core, far[0]))
     near_estimate, near_normed, near_grad = normed_of(both_cores(near_core))
     near = partials(near_normed, near_grad)
-    sums = sum_over_row(near, far)
+    sums = sum_over_row(near, [far_own, far[1], far[2], far[3]])
     gate, up, hidden_grad = sums[:, :width], sums[:, width : 2 * width], sums[:, 2 * width :]
     sigma = jax.nn.sigmoid(gate)
     silu = gate * sigma
@@ -212,31 +206,27 @@
         return jnp.concatenate([product(hidden, down_weight), grad], axis=1)
 
     near_partial = backward(units[0])
-    near_keep, _ = sum_over_core(near_partial, None)
-    near_total, _ = sum_over_y(near_keep, None, x)
-    far_units, near_total = lax.optimization_barrier((units[1], near_total))
-    far_partial = backward(far_units)
+    far_partial = backward(units[1])
     gain_partial = jnp.sum(near_partial[:, 1024:] * near_estimate, axis=0) + jnp.sum(
         far_partial[:, 1024:] * far_estimate, axis=0
     )
-    far_keep, gain = sum_over_core(far_partial, gain_partial.reshape(8, 128))
-
-    units = jnp.concatenate([units[0], far_units], axis=0)
+    keep, gain = sum_over_core(near_partial, far_partial, gain_partial.reshape(8, 128))
+
+    units = jnp.concatenate(units, axis=0)
     hidden, gate_grad, up_grad = units[:, :width], units[:, width : 2 * width], units[:, 2 * width :]
     normed = jnp.concatenate([near_normed, far_normed], axis=0)
     grad_full = jnp.concatenate([near_grad, far_grad], axis=0)
     down_weight_grad = product_left_t(hidden, grad_full).astype(BF16)
-    far_keep, down_weight_grad = lax.optimization_barrier((far_keep, down_weight_grad))
-    far_total, gain = sum_over_y(far_keep, gain, x)
-    normed, far_total = lax.optimization_barrier((normed, far_total))
+    keep, down_weight_grad = lax.optimization_barrier((keep, down_weight_grad))
+    total, gain = sum_over_y(keep, gain, x)
+    normed, total = lax.optimization_barrier((normed, total))
     gate_weight_grad = product_left_t(normed, gate_grad).astype(BF16)
     up_weight_grad = product_left_t(normed, up_grad).astype(BF16)
 
     gain_parts = [p.reshape(4, 256) for p in parts_of(gain, 2)]
     gain_rows = jnp.broadcast_to(jnp.concatenate(gain_parts, axis=1)[None], (16, 4, 512))
-    total = jnp.zeros((64, 2048), BF16)
-    total = lax.dynamic_update_slice(total, near_total.astype(BF16), (z * 32, 0))
-    total = lax.dynamic_update_slice(total, far_total.astype(BF16), ((1 - z) * 32, 0))
+    total = total.astype(BF16)
+    total = jnp.where(z == 0, total, jnp.concatenate([total[32:], total[:32]], axis=0))
     message = jnp.concatenate([total.reshape(16, 4, 2048), gain_rows], axis=2)
     back = lax.all_to_all(message, ("h", "z", "x"), split_axis=0, concat_axis=0, tiled=True)
     back = back.reshape(HS, 8, 4, 2560).astype(F32)

time: 196 us -> 216 us (1.10)
  other arithmetic: 8.51 us -> 22.5 us
  starting transfers between devices: 53.5 us -> 48.2 us
  local copies, waits for them, and re-layouts: 11.7 us -> 16.5 us
  matrix products: 27 us -> 30.2 us
  waiting for transfers between devices: 93.6 us -> 95.9 us
    unnamed x4 -> x14, other arithmetic: 0.2 us -> 9.64 us
    ppermute x34 -> x30, starting transfers between devices: 39.7 us -> 34.5 us  [send(): return lax.ppermute(value, AXES, pairs)]
    dot_general x3, matrix products: 13.4 us -> 16.5 us  [product_left_t(): lax.dot_general(left, right, (((0,), (0,)), ((), ())), preferred_element_...]
    unnamed x45 -> x72, local copies, waits for them, and re-layouts: 7.42 us -> 10.4 us
    ppermute x34 -> x30, waiting for transfers between devices: 81.2 us -> 83.2 us  [send(): return lax.ppermute(value, AXES, pairs)]
  transfers between devices with their start and end apart: 36 -> 32, of which waited for: 20 -> 16; matrix products, arithmetic and copies ran while one was open for 11% -> 13% of each run, Pallas kernels for 0% -> 0%
where the time goes in v6:
time: 216 us; the launch traced here: 215 us
  waiting for transfers between devices  95.9 us (44%)
  starting transfers between devices  48.2 us (22%)
  matrix products  30.2 us (14%)
  other arithmetic  22.5 us (10%)
  local copies, waits for them, and re-layouts  16.5 us (8%)
    ppermute x30, waiting for transfers between devices, send(): return lax.ppermute(value, AXES, pairs)  83.2 us
    ppermute x30, starting transfers between devices, send(): return lax.ppermute(value, AXES, pairs)  34.5 us
    dot_general x3, matrix products, product_left_t(): lax.dot_general(left, right, (((0,), (0,)), ((), ())), preferred_element_...  16.5 us
    unnamed x72, local copies, waits for them, and re-layouts  10.4 us
    unnamed x14, other arithmetic  9.64 us
    all_to_all x1, waiting for transfers between devices, per_device(): lax.all_to_all(message.reshape(16, 4, 2176), ('h', 'z', 'x'), split_axis=...  8.83 us
    all_to_all x1, starting transfers between devices, per_device(): lax.all_to_all(message.reshape(16, 4, 2176), ('h', 'z', 'x'), split_axis=...  7.96 us
    dot_general x6, matrix products, product_right_t(): lax.dot_general(left, right, (((1,), (1,)), ((), ())), preferred_element_...  6.98 us
  transfers between devices with their start and end apart: 32, of which 16 were waited for; matrix products, arithmetic and copies ran while one was open for 13% of the time, Pallas kernels for 0%

profile of v6, /device:TPU:0, one launch (start us, length us, event | category | flops | bytes accessed | tf_op | source)
XLA Modules:
  0.0 214.9 jit_solution(2326237450274636993)
XLA Ops:
  4.0 8.0 %all-to-all-start = ((bf16[16,4,2176]{2,1,0:T(4,128)(2,1)}), bf16[16,4,2176]{2,1,0:T(4,128)(2,1)S(1)}, u32[]{:S(2)}, u32[]{:S(2)}) async-start(bf16[16,4,2176]{2,1,0:T(4,128)(2,1)} %bitcast.2), calls=%async_computation | async-start | bytes 557056 | tf_op jit(solution)/shard_map/all_to_all | solution.py:154
  12.0 8.8 %all-to-all-done = bf16[16,4,2176]{2,1,0:T(4,128)(2,1)S(1)} async-done(((bf16[16,4,2176]{2,1,0:T(4,128)(2,1)}), bf16[16,4,2176]{2,1,0:T(4,128)(2,1)S(1)}, u32[]{:S(2)}, u32[]{:S(2)}) %all-to-all-start) | async-done | bytes 278560 | tf_op jit(solution)/shard_map/all_to_all | solution.py:154
  21.0 3.1 %collective-permute-start = (bf16[32,2176]{1,0:T(8,128)(2,1)S(1)}, bf16[32,2176]{1,0:T(8,128)(2,1)S(1)}, u32[]{:S(2)}, u32[]{:S(2)}) collective-permute-start(bf16[32,2176]{1,0:T(8,128)(2,1)S(1)} %get-tuple-element.37), channel_id=1, source_target_pairs={{0,6},{1,7},{2,0},{3,1},{4,2},{5,3},{6,4},{7,5},{8,14},{9,15},{10,... | collective-permute-start | bytes 417800 | tf_op jit(solution)/shard_map/ppermute | solution.py:24
  25.7 3.0 %collective-permute-done = bf16[32,2176]{1,0:T(8,128)(2,1)S(1)} collective-permute-done((bf16[32,2176]{1,0:T(8,128)(2,1)S(1)}, bf16[32,2176]{1,0:T(8,128)(2,1)S(1)}, u32[]{:S(2)}, u32[]{:S(2)}) %collective-permute-start) | collective-permute-done | bytes 139296 | tf_op jit(solution)/shard_map/ppermute | solution.py:24
  28.6 2.2 %collective-permute-done.1 = bf16[32,2176]{1,0:T(8,128)(2,1)S(1)} collective-permute-done((bf16[32,2176]{1,0:T(8,128)(2,1)S(1)}, bf16[32,2176]{1,0:T(8,128)(2,1)S(1)}, u32[]{:S(2)}, u32[]{:S(2)}) %collective-permute-start.1) | collective-permute-done | bytes 139296 | tf_op jit(solution)/shard_map/ppermute | solution.py:24
  30.9 1.4 collective-permute-done.2
  34.6 4.3 %collective-permute-done.3 = bf16[32,2176]{1,0:T(8,128)(2,1)S(1)} collective-permute-done((bf16[32,2176]{1,0:T(8,128)(2,1)S(1)}, bf16[32,2176]{1,0:T(8,128)(2,1)S(1)}, u32[]{:S(2)}, u32[]{:S(2)}) %collective-permute-start.3) | collective-permute-done | bytes 139296 | tf_op jit(solution)/shard_map/ppermute | solution.py:24
  39.0 2.1 collective-permute-done.4
  41.1 2.2 %collective-permute-done.5 = bf16[32,2176]{1,0:T(8,128)(2,1)S(1)} collective-permute-done((bf16[32,2176]{1,0:T(8,128)(2,1)S(1)}, bf16[32,2176]{1,0:T(8,128)(2,1)S(1)}, u32[]{:S(2)}, u32[]{:S(2)}) %collective-permute-start.5) | collective-permute-done | bytes 139296 | tf_op jit(solution)/shard_map/ppermute | solution.py:24
  43.9 1.1 fusion.80
  46.1 1.1 fusion.81
  48.1 1.1 fusion.71
  49.9 2.1 copy-done.2
  53.3 2.4 %collective-permute-start.9 = (bf16[64,5376]{1,0:T(8,128)(2,1)S(1)}, bf16[64,5376]{1,0:T(8,128)(2,1)S(1)}, u32[]{:S(2)}, u32[]{:S(2)}) collective-permute-start(bf16[64,5376]{1,0:T(8,128)(2,1)S(1)} %get-tuple-element.45), channel_id=1, source_target_pairs={{0,48},{1,49},{2,50},{3,51},{4,52},{5,53},{6,54},{7,55},{8,56},{9,... | collective-permute-start | bytes 2064392 | tf_op jit(solution)/shard_map/ppermute | solution.py:24
  56.3 1.1 fusion.82
  57.4 1.1 fusion.83
  59.4 1.2 fusion.69
  61.0 3.2 %collective-permute-start.15 = (bf16[32,5376]{1,0:T(8,128)(2,1)S(1)}, bf16[32,5376]{1,0:T(8,128)(2,1)S(1)}, u32[]{:S(2)}, u32[]{:S(2)}) collective-permute-start(bf16[32,5376]{1,0:T(8,128)(2,1)S(1)} %get-tuple-element.42), channel_id=1, source_target_pairs={{0,48},{1,49},{2,50},{3,51},{4,52},{5,53},{6,54},{7,55},{8,56},{9,... | collective-permute-start | bytes 1032200 | tf_op jit(solution)/shard_map/ppermute | solution.py:24
  64.6 5.5 %collective-permute-done.11 = bf16[64,5376]{1,0:T(8,128)(2,1)S(1)} collective-permute-done((bf16[64,5376]{1,0:T(8,128)(2,1)S(1)}, bf16[64,5376]{1,0:T(8,128)(2,1)S(1)}, u32[]{:S(2)}, u32[]{:S(2)}) %collective-permute-start.11) | collective-permute-done | bytes 688160 | tf_op jit(solution)/shard_map/ppermute | solution.py:24
  71.9 1.8 collective-permute-start.13
  74.2 12.0 %collective-permute-done.12 = bf16[32,5376]{1,0:T(8,128)(2,1)S(1)} collective-permute-done((bf16[32,5376]{1,0:T(8,128)(2,1)S(1)}, bf16[32,5376]{1,0:T(8,128)(2,1)S(1)}, u32[]{:S(2)}, u32[]{:S(2)}) %collective-permute-start.12) | collective-permute-done | bytes 344096 | tf_op jit(solution)/shard_map/ppermute | solution.py:24
  86.4 3.2 %collective-permute-start.17 = (bf16[32,5376]{1,0:T(8,128)(2,1)S(1)}, bf16[32,5376]{1,0:T(8,128)(2,1)S(1)}, u32[]{:S(2)}, u32[]{:S(2)}) collective-permute-start(bf16[32,5376]{1,0:T(8,128)(2,1)S(1)} %get-tuple-element.27), channel_id=1, source_target_pairs={{0,48},{1,49},{2,50},{3,51},{4,52},{5,53},{6,54},{7,55},{8,56},{9,... | collective-permute-start | bytes 1032200 | tf_op jit(solution)/shard_map/ppermute | solution.py:24
  89.6 7.6 %collective-permute-done.16 = bf16[32,5376]{1,0:T(8,128)(2,1)S(1)} collective-permute-done((bf16[32,5376]{1,0:T(8,128)(2,1)S(1)}, bf16[32,5376]{1,0:T(8,128)(2,1)S(1)}, u32[]{:S(2)}, u32[]{:S(2)}) %collective-permute-start.16) | collective-permute-done | bytes 344096 | tf_op jit(solution)/shard_map/ppermute | solution.py:24
  98.8 2.4 %collective-permute-start.18 = (bf16[64,5376]{1,0:T(8,128)(2,1)S(1)}, bf16[64,5376]{1,0:T(8,128)(2,1)S(1)}, u32[]{:S(2)}, u32[]{:S(2)}) collective-permute-start(bf16[64,5376]{1,0:T(8,128)(2,1)S(1)} %get-tuple-element.67), channel_id=1, source_target_pairs={{0,48},{1,49},{2,50},{3,51},{4,52},{5,53},{6,54},{7,55},{8,56},{9,... | collective-permute-start | bytes 2064392 | tf_op jit(solution)/shard_map/ppermute | solution.py:24
  101.2 1.3 collective-permute-start.22
  102.5 12.8 %collective-permute-done.19 = bf16[64,5376]{1,0:T(8,128)(2,1)S(1)} collective-permute-done((bf16[64,5376]{1,0:T(8,128)(2,1)S(1)}, bf16[64,5376]{1,0:T(8,128)(2,1)S(1)}, u32[]{:S(2)}, u32[]{:S(2)}) %collective-permute-start.19) | collective-permute-done | bytes 688160 | tf_op jit(solution)/shard_map/ppermute | solution.py:24
  115.5 3.3 %collective-permute-start.21 = (bf16[32,5376]{1,0:T(8,128)(2,1)S(1)}, bf16[32,5376]{1,0:T(8,128)(2,1)S(1)}, u32[]{:S(2)}, u32[]{:S(2)}) collective-permute-start(bf16[32,5376]{1,0:T(8,128)(2,1)S(1)} %slice.425), channel_id=1, source_target_pairs={{0,48},{1,49},{2,50},{3,51},{4,52},{5,53},{6,54},{7,55},{8,56},{9,... | collective-permute-start | bytes 1032200 | tf_op jit(solution)/shard_map/ppermute | solution.py:24
  119.0 1.8 collective-permute-start.25
  120.8 6.8 %collective-permute-done.20 = bf16[32,5376]{1,0:T(8,128)(2,1)S(1)} collective-permute-done((bf16[32,5376]{1,0:T(8,128)(2,1)S(1)}, bf16[32,5376]{1,0:T(8,128)(2,1)S(1)}, u32[]{:S(2)}, u32[]{:S(2)}) %collective-permute-start.20) | collective-permute-done | bytes 344096 | tf_op jit(solution)/shard_map/ppermute | solution.py:24
  127.7 1.3 collective-permute-start.24
  129.1 9.5 %collective-permute-done.23 = bf16[64,5376]{1,0:T(8,128)(2,1)S(1)} collective-permute-done((bf16[64,5376]{1,0:T(8,128)(2,1)S(1)}, bf16[64,5376]{1,0:T(8,128)(2,1)S(1)}, u32[]{:S(2)}, u32[]{:S(2)}) %collective-permute-start.23) | collective-permute-done | bytes 688160 | tf_op jit(solution)/shard_map/ppermute | solution.py:24
  138.8 1.1 fusion.14
  140.8 1.1 fusion.17
  142.8 1.2 multiply_reduce_fusion.1
  145.2 1.2 fusion.9
  146.3 1.3 copy-done.10
  147.6 1.1 fusion.12
  148.7 1.2 multiply_reduce_fusion
  155.9 1.2 slice.399
  162.5 5.6 %convolution_convert_fusion.2 = bf16[1792,1024]{1,0:T(8,128)(2,1)} fusion(bf16[512,5376]{1,0:T(8,128)(2,1)} %copy-done.10, bf16[256,1024]{1,0:T(8,128)(2,1)S(1)} %slice.399, bf16[256,1024]{1,0:T(8,128)(2,1)S(1)} %slice.409), kind=kOutput, calls=%fused_computation.32 | convolution fusion | flops 1882980352 | bytes 6553600 | tf_op jit(solution)/shard_map/dot_general | solution.py:36
  168.1 1.8 slice_add_fusion
  171.7 3.2 %collective-permute-start.28 = (bf16[64,2176]{1,0:T(8,128)(2,1)}, bf16[64,2176]{1,0:T(8,128)(2,1)}, u32[]{:S(2)}, u32[]{:S(2)}) collective-permute-start(bf16[64,2176]{1,0:T(8,128)(2,1)} %get-tuple-element.77), channel_id=1, source_target_pairs={{0,6},{1,7},{2,0},{3,1},{4,2},{5,3},{6,4},{7,5},{8,14},{9,15},{10,... | collective-permute-start | bytes 835592 | tf_op jit(solution)/shard_map/ppermute | solution.py:24
  175.0 13.2 %collective-permute-done.27 = bf16[64,2176]{1,0:T(8,128)(2,1)} collective-permute-done((bf16[64,2176]{1,0:T(8,128)(2,1)}, bf16[64,2176]{1,0:T(8,128)(2,1)}, u32[]{:S(2)}, u32[]{:S(2)}) %collective-permute-start.27) | collective-permute-done | bytes 278560 | tf_op jit(solution)/shard_map/ppermute | solution.py:24
  188.3 1.2 convert_add_fusion
  189.5 5.5 %convolution_convert_fusion = bf16[1024,1792]{1,0:T(8,128)(2,1)} fusion(bf16[512,1024]{1,0:T(8,128)(2,1)S(1)} %pad_maximum_fusion.2, bf16[512,5376]{1,0:T(8,128)(2,1)} %copy-done.10), kind=kOutput, calls=%fused_computation.30 | convolution fusion | flops 1880883200 | bytes 6553600 | tf_op jit(solution)/shard_map/dot_general | solution.py:36
  196.9 5.7 %all-to-all-start.1 = ((bf16[16,4,2560]{2,1,0:T(4,128)(2,1)}), bf16[16,4,2560]{2,1,0:T(4,128)(2,1)S(1)}, u32[]{:S(2)}, u32[]{:S(2)}) async-start(bf16[16,4,2560]{2,1,0:T(4,128)(2,1)} %pad_maximum_fusion.5), calls=%async_computation.1 | async-start | bytes 655360 | tf_op jit(solution)/shard_map/all_to_all | solution.py:231
  202.7 5.5 %convolution_convert_fusion.1 = bf16[1024,1792]{1,0:T(8,128)(2,1)} fusion(bf16[512,1024]{1,0:T(8,128)(2,1)S(1)} %copy-done.12, bf16[512,5376]{1,0:T(8,128)(2,1)} %copy-done.10), kind=kOutput, calls=%fused_computation.31 | convolution fusion | flops 1880883200 | bytes 6553600 | tf_op jit(solution)/shard_map/dot_general | solution.py:36
  208.1 3.8 %all-to-all-done.1 = bf16[16,4,2560]{2,1,0:T(4,128)(2,1)S(1)} async-done(((bf16[16,4,2560]{2,1,0:T(4,128)(2,1)}), bf16[16,4,2560]{2,1,0:T(4,128)(2,1)S(1)}, u32[]{:S(2)}, u32[]{:S(2)}) %all-to-all-start.1) | async-done | bytes 327712 | tf_op jit(solution)/shard_map/all_to_all | solution.py:231
  (198 shorter events, 39.6 us)
Async XLA Ops:
  0.6 23.4 %copy-start.14 = (f32[8192]{0:T(1024)S(1)}, f32[8192]{0:T(1024)}, u32[]{:S(2)}) copy-start(f32[8192]{0:T(1024)} %param.7) | copy-start | bytes 98308
  4.0 16.8 %all-to-all-start = ((bf16[16,4,2176]{2,1,0:T(4,128)(2,1)}), bf16[16,4,2176]{2,1,0:T(4,128)(2,1)S(1)}, u32[]{:S(2)}, u32[]{:S(2)}) async-start(bf16[16,4,2176]{2,1,0:T(4,128)(2,1)} %bitcast.2), calls=%async_computation | async-start | bytes 557056 | tf_op jit(solution)/shard_map/all_to_all | solution.py:154
  21.0 7.7 %collective-permute-start = (bf16[32,2176]{1,0:T(8,128)(2,1)S(1)}, bf16[32,2176]{1,0:T(8,128)(2,1)S(1)}, u32[]{:S(2)}, u32[]{:S(2)}) collective-permute-start(bf16[32,2176]{1,0:T(8,128)(2,1)S(1)} %get-tuple-element.37), channel_id=1, source_target_pairs={{0,6},{1,7},{2,0},{3,1},{4,2},{5,3},{6,4},{7,5},{8,14},{9,15},{10,... | collective-permute-start | bytes 417800 | tf_op jit(solution)/shard_map/ppermute | solution.py:24
  24.1 6.8 %collective-permute-start.1 = (bf16[32,2176]{1,0:T(8,128)(2,1)S(1)}, bf16[32,2176]{1,0:T(8,128)(2,1)S(1)}, u32[]{:S(2)}, u32[]{:S(2)}) collective-permute-start(bf16[32,2176]{1,0:T(8,128)(2,1)S(1)} %get-tuple-element.37), channel_id=1, source_target_pairs={{0,4},{1,5},{2,6},{3,7},{4,0},{5,1},{6,2},{7,3},{8,12},{9,13},{10,... | collective-permute-start | bytes 417800 | tf_op jit(solution)/shard_map/ppermute | solution.py:24
  24.7 7.6 %collective-permute-start.2 = (bf16[32,2176]{1,0:T(8,128)(2,1)S(1)}, bf16[32,2176]{1,0:T(8,128)(2,1)S(1)}, u32[]{:S(2)}, u32[]{:S(2)}) collective-permute-start(bf16[32,2176]{1,0:T(8,128)(2,1)S(1)} %get-tuple-element.37), channel_id=1, source_target_pairs={{0,2},{1,3},{2,4},{3,5},{4,6},{5,7},{6,0},{7,1},{8,10},{9,11},{10,... | collective-permute-start | bytes 417800 | tf_op jit(solution)/shard_map/ppermute | solution.py:24
  32.3 11.0 %collective-permute-start.6 = (bf16[128,2176]{1,0:T(8,128)(2,1)S(1)}, bf16[128,2176]{1,0:T(8,128)(2,1)S(1)}, u32[]{:S(2)}, u32[]{:S(2)}) collective-permute-start(bf16[128,2176]{1,0:T(8,128)(2,1)S(1)} %constant_dynamic-update-slice_fusion.19), channel_id=1, source_target_pairs={{0,1},{1,0},{2,3},{3,2},{4,5},{5,4},{6,7},{7,6},{8,9},{9,8},{10,11... | collective-permute-start | bytes 1671176 | tf_op jit(solution)/shard_map/ppermute | solution.py:24
  32.4 6.5 %collective-permute-start.3 = (bf16[32,2176]{1,0:T(8,128)(2,1)S(1)}, bf16[32,2176]{1,0:T(8,128)(2,1)S(1)}, u32[]{:S(2)}, u32[]{:S(2)}) collective-permute-start(bf16[32,2176]{1,0:T(8,128)(2,1)S(1)} %get-tuple-element.20), channel_id=1, source_target_pairs={{0,6},{1,7},{2,0},{3,1},{4,2},{5,3},{6,4},{7,5},{8,14},{9,15},{10,... | collective-permute-start | bytes 417800 | tf_op jit(solution)/shard_map/ppermute | solution.py:24
  33.0 8.0 %collective-permute-start.4 = (bf16[32,2176]{1,0:T(8,128)(2,1)S(1)}, bf16[32,2176]{1,0:T(8,128)(2,1)S(1)}, u32[]{:S(2)}, u32[]{:S(2)}) collective-permute-start(bf16[32,2176]{1,0:T(8,128)(2,1)S(1)} %get-tuple-element.20), channel_id=1, source_target_pairs={{0,4},{1,5},{2,6},{3,7},{4,0},{5,1},{6,2},{7,3},{8,12},{9,13},{10,... | collective-permute-start | bytes 417800 | tf_op jit(solution)/shard_map/ppermute | solution.py:24
  33.7 9.6 %collective-permute-start.5 = (bf16[32,2176]{1,0:T(8,128)(2,1)S(1)}, bf16[32,2176]{1,0:T(8,128)(2,1)S(1)}, u32[]{:S(2)}, u32[]{:S(2)}) collective-permute-start(bf16[32,2176]{1,0:T(8,128)(2,1)S(1)} %get-tuple-element.20), channel_id=1, source_target_pairs={{0,2},{1,3},{2,4},{3,5},{4,6},{5,7},{6,0},{7,1},{8,10},{9,11},{10,... | collective-permute-start | bytes 417800 | tf_op jit(solution)/shard_map/ppermute | solution.py:24
  34.6 9.3 %copy-start.20 = (bf16[1024,1792]{1,0:T(8,128)(2,1)S(1)}, bf16[1024,1792]{1,0:T(8,128)(2,1)}, u32[]{:S(2)}) copy-start(bf16[1024,1792]{1,0:T(8,128)(2,1)} %param.8) | copy-start | bytes 11010052
  43.4 105.3 %copy-start.8 = (bf16[256,2176]{1,0:T(8,128)(2,1)}, bf16[256,2176]{1,0:T(8,128)(2,1)S(1)}, u32[]{:S(2)}) copy-start(bf16[256,2176]{1,0:T(8,128)(2,1)S(1)} %slice_dynamic-update-slice_fusion.4) | copy-start | bytes 3342340
  49.6 2.4 %copy-start.2 = (f32[256,5376]{1,0:T(8,128)}, f32[256,5376]{1,0:T(8,128)S(1)}, u32[]{:S(2)}) copy-start(f32[256,5376]{1,0:T(8,128)S(1)} %pad_maximum_fusion) | copy-start | bytes 16515076
  52.1 3.6 %collective-permute-start.7 = (bf16[128,2176]{1,0:T(8,128)(2,1)S(1)}, bf16[128,2176]{1,0:T(8,128)(2,1)S(1)}, u32[]{:S(2)}, u32[]{:S(2)}) collective-permute-start(bf16[128,2176]{1,0:T(8,128)(2,1)S(1)} %constant_dynamic-update-slice_fusion.15), channel_id=1, source_target_pairs={{0,1},{1,0},{2,3},{3,2},{4,5},{5,4},{6,7},{7,6},{8,9},{9,8},{10,11... | collective-permute-start | bytes 1671176 | tf_op jit(solution)/shard_map/ppermute | solution.py:24
  52.1 4.1 %copy-start.21 = (bf16[1024,1792]{1,0:T(8,128)(2,1)S(1)}, bf16[1024,1792]{1,0:T(8,128)(2,1)}, u32[]{:S(2)}) copy-start(bf16[1024,1792]{1,0:T(8,128)(2,1)} %param.8) | copy-start | bytes 11010052
  52.3 17.9 %collective-permute-start.11 = (bf16[64,5376]{1,0:T(8,128)(2,1)S(1)}, bf16[64,5376]{1,0:T(8,128)(2,1)S(1)}, u32[]{:S(2)}, u32[]{:S(2)}) collective-permute-start(bf16[64,5376]{1,0:T(8,128)(2,1)S(1)} %get-tuple-element.44), channel_id=1, source_target_pairs={{0,64},{1,65},{2,66},{3,67},{4,68},{5,69},{6,70},{7,71},{8,72},{9,... | collective-permute-start | bytes 2064392 | tf_op jit(solution)/shard_map/ppermute | solution.py:24
  52.3 19.5 %collective-permute-start.8 = (bf16[64,5376]{1,0:T(8,128)(2,1)S(1)}, bf16[64,5376]{1,0:T(8,128)(2,1)S(1)}, u32[]{:S(2)}, u32[]{:S(2)}) collective-permute-start(bf16[64,5376]{1,0:T(8,128)(2,1)S(1)} %get-tuple-element.46), channel_id=1, source_target_pairs={{0,16},{1,17},{2,18},{3,19},{4,20},{5,21},{6,22},{7,23},{8,24},{9,... | collective-permute-start | bytes 2064392 | tf_op jit(solution)/shard_map/ppermute | solution.py:24
  53.3 20.4 %collective-permute-start.9 = (bf16[64,5376]{1,0:T(8,128)(2,1)S(1)}, bf16[64,5376]{1,0:T(8,128)(2,1)S(1)}, u32[]{:S(2)}, u32[]{:S(2)}) collective-permute-start(bf16[64,5376]{1,0:T(8,128)(2,1)S(1)} %get-tuple-element.45), channel_id=1, source_target_pairs={{0,48},{1,49},{2,50},{3,51},{4,52},{5,53},{6,54},{7,55},{8,56},{9,... | collective-permute-start | bytes 2064392 | tf_op jit(solution)/shard_map/ppermute | solution.py:24
  55.8 86.1 %copy-start.9 = (bf16[256,2176]{1,0:T(8,128)(2,1)}, bf16[256,2176]{1,0:T(8,128)(2,1)S(1)}, u32[]{:S(2)}) copy-start(bf16[256,2176]{1,0:T(8,128)(2,1)S(1)} %slice_dynamic-update-slice_fusion) | copy-start | bytes 3342340
  61.0 25.4 %collective-permute-start.14 = (bf16[32,5376]{1,0:T(8,128)(2,1)S(1)}, bf16[32,5376]{1,0:T(8,128)(2,1)S(1)}, u32[]{:S(2)}, u32[]{:S(2)}) collective-permute-start(bf16[32,5376]{1,0:T(8,128)(2,1)S(1)} %get-tuple-element.43), channel_id=1, source_target_pairs={{0,16},{1,17},{2,18},{3,19},{4,20},{5,21},{6,22},{7,23},{8,24},{9,... | collective-permute-start | bytes 1032200 | tf_op jit(solution)/shard_map/ppermute | solution.py:24
  61.0 25.3 %collective-permute-start.15 = (bf16[32,5376]{1,0:T(8,128)(2,1)S(1)}, bf16[32,5376]{1,0:T(8,128)(2,1)S(1)}, u32[]{:S(2)}, u32[]{:S(2)}) collective-permute-start(bf16[32,5376]{1,0:T(8,128)(2,1)S(1)} %get-tuple-element.42), channel_id=1, source_target_pairs={{0,48},{1,49},{2,50},{3,51},{4,52},{5,53},{6,54},{7,55},{8,56},{9,... | collective-permute-start | bytes 1032200 | tf_op jit(solution)/shard_map/ppermute | solution.py:24
  64.6 9.0 %slice-start = ((f32[256,5376]{1,0:T(8,128)}), f32[64,5376]{1,0:T(8,128)S(1)}, s32[]{:S(2)}) async-start(f32[256,5376]{1,0:T(8,128)} %copy-done.2), calls=%async_computation.2 | async-start | bytes 2752512 | tf_op jit(solution)/shard_map/slice | solution.py:186
  70.3 15.9 %collective-permute-start.12 = (bf16[32,5376]{1,0:T(8,128)(2,1)S(1)}, bf16[32,5376]{1,0:T(8,128)(2,1)S(1)}, u32[]{:S(2)}, u32[]{:S(2)}) collective-permute-start(bf16[32,5376]{1,0:T(8,128)(2,1)S(1)} %get-tuple-element.70), channel_id=1, source_target_pairs={{0,16},{1,17},{2,18},{3,19},{4,20},{5,21},{6,22},{7,23},{8,24},{9,... | collective-permute-start | bytes 1032200 | tf_op jit(solution)/shard_map/ppermute | solution.py:24
  71.9 14.3 %collective-permute-start.13 = (bf16[32,5376]{1,0:T(8,128)(2,1)S(1)}, bf16[32,5376]{1,0:T(8,128)(2,1)S(1)}, u32[]{:S(2)}, u32[]{:S(2)}) collective-permute-start(bf16[32,5376]{1,0:T(8,128)(2,1)S(1)} %get-tuple-element.69), channel_id=1, source_target_pairs={{0,48},{1,49},{2,50},{3,51},{4,52},{5,53},{6,54},{7,55},{8,56},{9,... | collective-permute-start | bytes 1032200 | tf_op jit(solution)/shard_map/ppermute | solution.py:24
  73.8 23.4 %collective-permute-start.10 = (bf16[64,5376]{1,0:T(8,128)(2,1)S(1)}, bf16[64,5376]{1,0:T(8,128)(2,1)S(1)}, u32[]{:S(2)}, u32[]{:S(2)}) collective-permute-start(bf16[64,5376]{1,0:T(8,128)(2,1)S(1)} %add_convert_fusion), channel_id=1, source_target_pairs={{0,64},{1,65},{2,66},{3,67},{4,68},{5,69},{6,70},{7,71},{8,72},{9,... | collective-permute-start | bytes 2064392 | tf_op jit(solution)/shard_map/ppermute | solution.py:24
  86.3 10.9 %collective-permute-start.16 = (bf16[32,5376]{1,0:T(8,128)(2,1)S(1)}, bf16[32,5376]{1,0:T(8,128)(2,1)S(1)}, u32[]{:S(2)}, u32[]{:S(2)}) collective-permute-start(bf16[32,5376]{1,0:T(8,128)(2,1)S(1)} %get-tuple-element.24), channel_id=1, source_target_pairs={{0,16},{1,17},{2,18},{3,19},{4,20},{5,21},{6,22},{7,23},{8,24},{9,... | collective-permute-start | bytes 1032200 | tf_op jit(solution)/shard_map/ppermute | solution.py:24
  86.4 10.9 %collective-permute-start.17 = (bf16[32,5376]{1,0:T(8,128)(2,1)S(1)}, bf16[32,5376]{1,0:T(8,128)(2,1)S(1)}, u32[]{:S(2)}, u32[]{:S(2)}) collective-permute-start(bf16[32,5376]{1,0:T(8,128)(2,1)S(1)} %get-tuple-element.27), channel_id=1, source_target_pairs={{0,48},{1,49},{2,50},{3,51},{4,52},{5,53},{6,54},{7,55},{8,56},{9,... | collective-permute-start | bytes 1032200 | tf_op jit(solution)/shard_map/ppermute | solution.py:24
  97.9 17.4 %collective-permute-start.19 = (bf16[64,5376]{1,0:T(8,128)(2,1)S(1)}, bf16[64,5376]{1,0:T(8,128)(2,1)S(1)}, u32[]{:S(2)}, u32[]{:S(2)}) collective-permute-start(bf16[64,5376]{1,0:T(8,128)(2,1)S(1)} %get-tuple-element.67), channel_id=1, source_target_pairs={{0,16},{1,17},{2,18},{3,19},{4,20},{5,21},{6,22},{7,23},{8,24},{9,... | collective-permute-start | bytes 2064392 | tf_op jit(solution)/shard_map/ppermute | solution.py:24
  98.8 16.6 %collective-permute-start.18 = (bf16[64,5376]{1,0:T(8,128)(2,1)S(1)}, bf16[64,5376]{1,0:T(8,128)(2,1)S(1)}, u32[]{:S(2)}, u32[]{:S(2)}) collective-permute-start(bf16[64,5376]{1,0:T(8,128)(2,1)S(1)} %get-tuple-element.67), channel_id=1, source_target_pairs={{0,48},{1,49},{2,50},{3,51},{4,52},{5,53},{6,54},{7,55},{8,56},{9,... | collective-permute-start | bytes 2064392 | tf_op jit(solution)/shard_map/ppermute | solution.py:24
  101.2 17.5 %collective-permute-start.22 = (bf16[64,5376]{1,0:T(8,128)(2,1)S(1)}, bf16[64,5376]{1,0:T(8,128)(2,1)S(1)}, u32[]{:S(2)}, u32[]{:S(2)}) collective-permute-start(bf16[64,5376]{1,0:T(8,128)(2,1)S(1)} %get-tuple-element.67), channel_id=1, source_target_pairs={{0,64},{1,65},{2,66},{3,67},{4,68},{5,69},{6,70},{7,71},{8,72},{9,... | collective-permute-start | bytes 2064392 | tf_op jit(solution)/shard_map/ppermute | solution.py:24
  115.3 12.3 %collective-permute-start.20 = (bf16[32,5376]{1,0:T(8,128)(2,1)S(1)}, bf16[32,5376]{1,0:T(8,128)(2,1)S(1)}, u32[]{:S(2)}, u32[]{:S(2)}) collective-permute-start(bf16[32,5376]{1,0:T(8,128)(2,1)S(1)} %slice.424), channel_id=1, source_target_pairs={{0,16},{1,17},{2,18},{3,19},{4,20},{5,21},{6,22},{7,23},{8,24},{9,... | collective-permute-start | bytes 1032200 | tf_op jit(solution)/shard_map/ppermute | solution.py:24
  115.5 12.2 %collective-permute-start.21 = (bf16[32,5376]{1,0:T(8,128)(2,1)S(1)}, bf16[32,5376]{1,0:T(8,128)(2,1)S(1)}, u32[]{:S(2)}, u32[]{:S(2)}) collective-permute-start(bf16[32,5376]{1,0:T(8,128)(2,1)S(1)} %slice.425), channel_id=1, source_target_pairs={{0,48},{1,49},{2,50},{3,51},{4,52},{5,53},{6,54},{7,55},{8,56},{9,... | collective-permute-start | bytes 1032200 | tf_op jit(solution)/shard_map/ppermute | solution.py:24
  118.7 19.8 %collective-permute-start.23 = (bf16[64,5376]{1,0:T(8,128)(2,1)S(1)}, bf16[64,5376]{1,0:T(8,128)(2,1)S(1)}, u32[]{:S(2)}, u32[]{:S(2)}) collective-permute-start(bf16[64,5376]{1,0:T(8,128)(2,1)S(1)} %collective-permute-done.22), channel_id=1, source_target_pairs={{0,48},{1,49},{2,50},{3,51},{4,52},{5,53},{6,54},{7,55},{8,56},{9,... | collective-permute-start | bytes 2064392 | tf_op jit(solution)/shard_map/ppermute | solution.py:24
  119.0 26.1 %collective-permute-start.25 = (bf16[64,5376]{1,0:T(8,128)(2,1)S(1)}, bf16[64,5376]{1,0:T(8,128)(2,1)S(1)}, u32[]{:S(2)}, u32[]{:S(2)}) collective-permute-start(bf16[64,5376]{1,0:T(8,128)(2,1)S(1)} %collective-permute-done.22), channel_id=1, source_target_pairs={{0,16},{1,17},{2,18},{3,19},{4,20},{5,21},{6,22},{7,23},{8,24},{9,... | collective-permute-start | bytes 2064392 | tf_op jit(solution)/shard_map/ppermute | solution.py:24
  127.7 17.3 %collective-permute-start.24 = (bf16[64,5376]{1,0:T(8,128)(2,1)S(1)}, bf16[64,5376]{1,0:T(8,128)(2,1)S(1)}, u32[]{:S(2)}, u32[]{:S(2)}) collective-permute-start(bf16[64,5376]{1,0:T(8,128)(2,1)S(1)} %pad_maximum_fusion.4), channel_id=1, source_target_pairs={{0,64},{1,65},{2,66},{3,67},{4,68},{5,69},{6,70},{7,71},{8,72},{9,... | collective-permute-start | bytes 2064392 | tf_op jit(solution)/shard_map/ppermute | solution.py:24
  129.1 9.7 %copy-start.16 = (bf16[1024,1792]{1,0:T(8,128)(2,1)S(1)}, bf16[1024,1792]{1,0:T(8,128)(2,1)}, u32[]{:S(2)}) copy-start(bf16[1024,1792]{1,0:T(8,128)(2,1)} %param.9) | copy-start | bytes 11010052
  149.9 4.5 %copy-start = (f32[256,1024]{1,0:T(8,128)}, f32[256,1024]{1,0:T(8,128)S(1)}, u32[]{:S(2)}) copy-start(f32[256,1024]{1,0:T(8,128)S(1)} %get-tuple-element.84) | copy-start | bytes 3145732
  155.9 12.2 %collective-permute-start.26 = (f32[264,2048]{1,0:T(8,128)}, f32[264,2048]{1,0:T(8,128)}, u32[]{:S(2)}, u32[]{:S(2)}) collective-permute-start(f32[264,2048]{1,0:T(8,128)} %constant_dynamic-update-slice_fusion.9), channel_id=1, source_target_pairs={{0,1},{1,0},{2,3},{3,2},{4,5},{5,4},{6,7},{7,6},{8,9},{9,8},{10,11... | collective-permute-start | bytes 6488072 | tf_op jit(solution)/shard_map/ppermute | solution.py:24
  155.9 3.0 %copy-start.1 = (f32[256,1024]{1,0:T(8,128)S(1)}, f32[256,1024]{1,0:T(8,128)}, u32[]{:S(2)}) copy-start(f32[256,1024]{1,0:T(8,128)} %copy-done) | copy-start | bytes 3145732
  162.5 5.6 %copy-start.3 = (f32[256,2048]{1,0:T(8,128)S(1)}, f32[256,2048]{1,0:T(8,128)}, u32[]{:S(2)}) copy-start(f32[256,2048]{1,0:T(8,128)} %fusion.31) | copy-start | bytes 6291460
  169.9 5.0 %copy-start.5 = (bf16[256,1024]{1,0:T(8,128)(2,1)S(1)}, bf16[256,1024]{1,0:T(8,128)(2,1)}, u32[]{:S(2)}) copy-start(bf16[256,1024]{1,0:T(8,128)(2,1)} %copy-done.4) | copy-start | bytes 1572868
  169.9 5.0 %copy-start.7 = (bf16[256,1024]{1,0:T(8,128)(2,1)S(1)}, bf16[256,1024]{1,0:T(8,128)(2,1)}, u32[]{:S(2)}) copy-start(bf16[256,1024]{1,0:T(8,128)(2,1)} %copy-done.6) | copy-start | bytes 1572868
  171.7 16.6 %collective-permute-start.27 = (bf16[64,2176]{1,0:T(8,128)(2,1)}, bf16[64,2176]{1,0:T(8,128)(2,1)}, u32[]{:S(2)}, u32[]{:S(2)}) collective-permute-start(bf16[64,2176]{1,0:T(8,128)(2,1)} %get-tuple-element.78), channel_id=1, source_target_pairs={{0,2},{1,3},{2,4},{3,5},{4,6},{5,7},{6,0},{7,1},{8,10},{9,11},{10,... | collective-permute-start | bytes 835592 | tf_op jit(solution)/shard_map/ppermute | solution.py:24
  171.7 16.6 %collective-permute-start.28 = (bf16[64,2176]{1,0:T(8,128)(2,1)}, bf16[64,2176]{1,0:T(8,128)(2,1)}, u32[]{:S(2)}, u32[]{:S(2)}) collective-permute-start(bf16[64,2176]{1,0:T(8,128)(2,1)} %get-tuple-element.77), channel_id=1, source_target_pairs={{0,6},{1,7},{2,0},{3,1},{4,2},{5,3},{6,4},{7,5},{8,14},{9,15},{10,... | collective-permute-start | bytes 835592 | tf_op jit(solution)/shard_map/ppermute | solution.py:24
  174.9 13.3 %collective-permute-start.29 = (bf16[64,2176]{1,0:T(8,128)(2,1)S(1)}, bf16[64,2176]{1,0:T(8,128)(2,1)}, u32[]{:S(2)}, u32[]{:S(2)}) collective-permute-start(bf16[64,2176]{1,0:T(8,128)(2,1)S(1)} %get-tuple-element.76), channel_id=1, source_target_pairs={{0,4},{1,5},{2,6},{3,7},{4,0},{5,1},{6,2},{7,3},{8,12},{9,13},{10,... | collective-permute-start | bytes 835592 | tf_op jit(solution)/shard_map/ppermute | solution.py:24
  175.0 19.9 %copy-start.11 = (bf16[512,1024]{1,0:T(8,128)(2,1)}, bf16[512,1024]{1,0:T(8,128)(2,1)S(1)}, u32[]{:S(2)}) copy-start(bf16[512,1024]{1,0:T(8,128)(2,1)S(1)} %pad_maximum_fusion.2) | copy-start | bytes 3145732
  195.0 7.7 %copy-start.12 = (bf16[512,1024]{1,0:T(8,128)(2,1)S(1)}, bf16[512,1024]{1,0:T(8,128)(2,1)}, u32[]{:S(2)}) copy-start(bf16[512,1024]{1,0:T(8,128)(2,1)} %copy-done.11) | copy-start | bytes 3145732
  196.9 15.0 %all-to-all-start.1 = ((bf16[16,4,2560]{2,1,0:T(4,128)(2,1)}), bf16[16,4,2560]{2,1,0:T(4,128)(2,1)S(1)}, u32[]{:S(2)}, u32[]{:S(2)}) async-start(bf16[16,4,2560]{2,1,0:T(4,128)(2,1)} %pad_maximum_fusion.5), calls=%async_computation.1 | async-start | bytes 655360 | tf_op jit(solution)/shard_map/all_to_all | solution.py:231
  208.1 4.3 %copy-start.13 = (bf16[4,8192]{1,0:T(4,128)(2,1)S(1)}, bf16[4,8192]{1,0:T(4,128)(2,1)}, u32[]{:S(2)}) copy-start(bf16[4,8192]{1,0:T(4,128)(2,1)} %param.6) | copy-start | bytes 196612
  (8 other events, 15.1 us)

commit v7 on v5

--- a/solution.py
+++ b/solution.py
@@ -78,30 +78,25 @@
     return keep, gain_partial
 
 
-def sum_over_y(keep, gain, x):
-    n = keep.shape[1]
+def sum_over_y(near, far, gain, x):
+    n = near.shape[1]
 
     def piece(dy):
-        return lax.dynamic_slice(keep, ((dy - x) % XS * 32, 0), (32, n))
+        start = (dy - x) % XS * 32
+        halves = [lax.dynamic_slice(half, (start, 0), (32, n)) for half in (near, far)]
+        return jnp.concatenate(halves, axis=0)
 
     def gain_of(parts):
         return parts[:8].astype(F32) + parts[8:16].astype(F32)
 
-    if gain is not None:
-        parts = jnp.concatenate(parts_of(gain, 2) + [jnp.zeros((16, 128), BF16)], axis=0)
-        gains = {0: gain_of(parts)}
+    parts = jnp.concatenate(parts_of(gain, 2) + [jnp.zeros((48, 128), BF16)], axis=0)
+    gains = {0: gain_of(parts)}
     total = piece(0)
     for dy in (1, 3, 2):
-        message = piece(dy).astype(BF16)
-        if gain is not None:
-            message = jnp.concatenate([message, parts], axis=1)
-        got = send(message, y=dy)
+        got = send(jnp.concatenate([piece(dy).astype(BF16), parts], axis=1), y=dy)
         total = total + got[:, :n].astype(F32)
-        if gain is not None:
-            gains[dy] = gain_of(got[:, n:])
-    if gain is not None:
-        gain = (gains[0] + gains[2]) + (gains[1] + gains[3])
-    return total, gain
+        gains[dy] = gain_of(got[:, n:])
+    return total, (gains[0] + gains[2]) + (gains[1] + gains[3])
 
 
 def sum_over_row(near, far):
@@ -189,10 +184,10 @@
     near_core, _ = gather_half(near_block, x)
     far_estimate, far_normed, far_grad = normed_of(both_cores(far_core))
     far = partials(far_normed, far_grad)
-    near_core, far = lax.optimization_barrier((near_core, far))
+    near_core, far_own = lax.optimization_barrier((near_core, far[0]))
     near_estimate, near_normed, near_grad = normed_of(both_cores(near_core))
     near = partials(near_normed, near_grad)
-    sums = sum_over_row(near, far)
+    sums = sum_over_row(near, [far_own, far[1], far[2], far[3]])
     gate, up, hidden_grad = sums[:, :width], sums[:, width : 2 * width], sums[:, 2 * width :]
     sigma = jax.nn.sigmoid(gate)
     silu = gate * sigma
@@ -213,30 +208,27 @@
 
     near_partial = backward(units[0])
     near_keep, _ = sum_over_core(near_partial, None)
-    near_total, _ = sum_over_y(near_keep, None, x)
-    far_units, near_total = lax.optimization_barrier((units[1], near_total))
-    far_partial = backward(far_units)
+    far_partial = backward(units[1])
     gain_partial = jnp.sum(near_partial[:, 1024:] * near_estimate, axis=0) + jnp.sum(
         far_partial[:, 1024:] * far_estimate, axis=0
     )
     far_keep, gain = sum_over_core(far_partial, gain_partial.reshape(8, 128))
 
-    units = jnp.concatenate([units[0], far_units], axis=0)
+    units = jnp.concatenate(units, axis=0)
     hidden, gate_grad, up_grad = units[:, :width], units[:, width : 2 * width], units[:, 2 * width :]
     normed = jnp.concatenate([near_normed, far_normed], axis=0)
     grad_full = jnp.concatenate([near_grad, far_grad], axis=0)
     down_weight_grad = product_left_t(hidden, grad_full).astype(BF16)
     far_keep, down_weight_grad = lax.optimization_barrier((far_keep, down_weight_grad))
-    far_total, gain = sum_over_y(far_keep, gain, x)
-    normed, far_total = lax.optimization_barrier((normed, far_total))
+    total, gain = sum_over_y(near_keep, far_keep, gain, x)
+    normed, total = lax.optimization_barrier((normed, total))
     gate_weight_grad = product_left_t(normed, gate_grad).astype(BF16)
     up_weight_grad = product_left_t(normed, up_grad).astype(BF16)
 
     gain_parts = [p.reshape(4, 256) for p in parts_of(gain, 2)]
     gain_rows = jnp.broadcast_to(jnp.concatenate(gain_parts, axis=1)[None], (16, 4, 512))
-    total = jnp.zeros((64, 2048), BF16)
-    total = lax.dynamic_update_slice(total, near_total.astype(BF16), (z * 32, 0))
-    total = lax.dynamic_update_slice(total, far_total.astype(BF16), ((1 - z) * 32, 0))
+    total = total.astype(BF16)
+    total = jnp.where(z == 0, total, jnp.concatenate([total[32:], total[:32]], axis=0))
     message = jnp.concatenate([total.reshape(16, 4, 2048), gain_rows], axis=2)
     back = lax.all_to_all(message, ("h", "z", "x"), split_axis=0, concat_axis=0, tiled=True)
     back = back.reshape(HS, 8, 4, 2560).astype(F32)

time: 196 us -> 190 us (0.969)
  waiting for transfers between devices: 93.6 us -> 74.2 us
  local copies, waits for them, and re-layouts: 11.7 us -> 21.5 us
    ppermute x34 -> x31, waiting for transfers between devices: 81.2 us -> 65.4 us  [send(): return lax.ppermute(value, AXES, pairs)]
    unnamed x45 -> x58, local copies, waits for them, and re-layouts: 7.42 us -> 16.1 us
    all_to_all x1, waiting for transfers between devices: 3.59 us -> 0.01 us  [per_device(): lax.all_to_all(message, ('h', 'z', 'x'), split_axis=0, concat_axis=0, til...]
    ppermute x34 -> x31, starting transfers between devices: 39.7 us -> 38.5 us  [send(): return lax.ppermute(value, AXES, pairs)]
  transfers between devices with their start and end apart: 36 -> 33, of which waited for: 20 -> 15; matrix products, arithmetic and copies ran while one was open for 11% -> 20% of each run, Pallas kernels for 0% -> 0%
where the time goes in v7:
time: 190 us; the launch traced here: 189 us
  waiting for transfers between devices  74.2 us (39%)
  starting transfers between devices  52.8 us (28%)
  matrix products  28.7 us (15%)
  local copies, waits for them, and re-layouts  21.5 us (11%)
  other arithmetic  9.89 us (5%)
    ppermute x31, waiting for transfers between devices, send(): return lax.ppermute(value, AXES, pairs)  65.4 us
    ppermute x31, starting transfers between devices, send(): return lax.ppermute(value, AXES, pairs)  38.5 us
    unnamed x58, local copies, waits for them, and re-layouts  16.1 us
    dot_general x3, matrix products, product_left_t(): lax.dot_general(left, right, (((0,), (0,)), ((), ())), preferred_element_...  14.9 us
    all_to_all x1, waiting for transfers between devices, per_device(): lax.all_to_all(message.reshape(16, 4, 2176), ('h', 'z', 'x'), split_axis=...  8.83 us
    all_to_all x1, starting transfers between devices, per_device(): lax.all_to_all(message.reshape(16, 4, 2176), ('h', 'z', 'x'), split_axis=...  7.96 us
    dot_general x6, matrix products, product_right_t(): lax.dot_general(left, right, (((1,), (1,)), ((), ())), preferred_element_...  6.99 us
    dot_general x6, matrix products, product(): return jnp.dot(left, right, preferred_element_type=F32)  6.83 us
  transfers between devices with their start and end apart: 33, of which 15 were waited for; matrix products, arithmetic and copies ran while one was open for 20% of the time, Pallas kernels for 0%

profile of v7, /device:TPU:0, one launch (start us, length us, event | category | flops | bytes accessed | tf_op | source)
XLA Modules:
  0.0 188.6 jit_solution(13950787225179239958)
XLA Ops:
  4.0 8.0 %all-to-all-start = ((bf16[16,4,2176]{2,1,0:T(4,128)(2,1)}), bf16[16,4,2176]{2,1,0:T(4,128)(2,1)S(1)}, u32[]{:S(2)}, u32[]{:S(2)}) async-start(bf16[16,4,2176]{2,1,0:T(4,128)(2,1)} %bitcast.2), calls=%async_computation | async-start | bytes 557056 | tf_op jit(solution)/shard_map/all_to_all | solution.py:155
  12.0 8.8 %all-to-all-done = bf16[16,4,2176]{2,1,0:T(4,128)(2,1)S(1)} async-done(((bf16[16,4,2176]{2,1,0:T(4,128)(2,1)}), bf16[16,4,2176]{2,1,0:T(4,128)(2,1)S(1)}, u32[]{:S(2)}, u32[]{:S(2)}) %all-to-all-start) | async-done | bytes 278560 | tf_op jit(solution)/shard_map/all_to_all | solution.py:155
  21.0 1.6 collective-permute-start
  22.6 1.7 collective-permute-start.4
  24.3 2.0 %collective-permute-start.5 = (bf16[32,2176]{1,0:T(8,128)(2,1)S(1)}, bf16[32,2176]{1,0:T(8,128)(2,1)S(1)}, u32[]{:S(2)}, u32[]{:S(2)}) collective-permute-start(bf16[32,2176]{1,0:T(8,128)(2,1)S(1)} %get-tuple-element.31), channel_id=1, source_target_pairs={{0,4},{1,5},{2,6},{3,7},{4,0},{5,1},{6,2},{7,3},{8,12},{9,13},{10,... | collective-permute-start | bytes 417800 | tf_op jit(solution)/shard_map/ppermute | solution.py:24
  26.3 2.7 %collective-permute-done = bf16[32,2176]{1,0:T(8,128)(2,1)S(1)} collective-permute-done((bf16[32,2176]{1,0:T(8,128)(2,1)S(1)}, bf16[32,2176]{1,0:T(8,128)(2,1)S(1)}, u32[]{:S(2)}, u32[]{:S(2)}) %collective-permute-start) | collective-permute-done | bytes 139296 | tf_op jit(solution)/shard_map/ppermute | solution.py:24
  28.9 3.1 %collective-permute-start.2 = (bf16[32,2176]{1,0:T(8,128)(2,1)S(1)}, bf16[32,2176]{1,0:T(8,128)(2,1)S(1)}, u32[]{:S(2)}, u32[]{:S(2)}) collective-permute-start(bf16[32,2176]{1,0:T(8,128)(2,1)S(1)} %get-tuple-element.17), channel_id=1, source_target_pairs={{0,4},{1,5},{2,6},{3,7},{4,0},{5,1},{6,2},{7,3},{8,12},{9,13},{10,... | collective-permute-start | bytes 417800 | tf_op jit(solution)/shard_map/ppermute | solution.py:24
  32.0 2.0 %collective-permute-start.1 = (bf16[32,2176]{1,0:T(8,128)(2,1)S(1)}, bf16[32,2176]{1,0:T(8,128)(2,1)S(1)}, u32[]{:S(2)}, u32[]{:S(2)}) collective-permute-start(bf16[32,2176]{1,0:T(8,128)(2,1)S(1)} %get-tuple-element.17), channel_id=1, source_target_pairs={{0,6},{1,7},{2,0},{3,1},{4,2},{5,3},{6,4},{7,5},{8,14},{9,15},{10,... | collective-permute-start | bytes 417800 | tf_op jit(solution)/shard_map/ppermute | solution.py:24
  34.3 3.3 %collective-permute-done.1 = bf16[32,2176]{1,0:T(8,128)(2,1)S(1)} collective-permute-done((bf16[32,2176]{1,0:T(8,128)(2,1)S(1)}, bf16[32,2176]{1,0:T(8,128)(2,1)S(1)}, u32[]{:S(2)}, u32[]{:S(2)}) %collective-permute-start.1) | collective-permute-done | bytes 139296 | tf_op jit(solution)/shard_map/ppermute | solution.py:24
  40.3 1.1 fusion.71
  42.3 1.1 fusion.62
  44.3 2.6 %copy-done = f32[256,5376]{1,0:T(8,128)} copy-done((f32[256,5376]{1,0:T(8,128)}, f32[256,5376]{1,0:T(8,128)S(1)}, u32[]{:S(2)}) %copy-start) | copy-done | bytes 5505048
  48.0 1.4 collective-permute-start.8
  50.0 1.1 fusion.74
  52.1 1.1 fusion.73
  53.2 1.1 fusion.60
  54.7 1.9 collective-permute-start.15
  57.2 7.5 %collective-permute-done.11 = bf16[64,5376]{1,0:T(8,128)(2,1)S(1)} collective-permute-done((bf16[64,5376]{1,0:T(8,128)(2,1)S(1)}, bf16[64,5376]{1,0:T(8,128)(2,1)S(1)}, u32[]{:S(2)}, u32[]{:S(2)}) %collective-permute-start.11) | collective-permute-done | bytes 688160 | tf_op jit(solution)/shard_map/ppermute | solution.py:24
  65.7 1.3 collective-permute-start.12
  67.8 1.3 collective-permute-start.10
  69.0 10.7 %collective-permute-done.13 = bf16[32,5376]{1,0:T(8,128)(2,1)S(1)} collective-permute-done((bf16[32,5376]{1,0:T(8,128)(2,1)S(1)}, bf16[32,5376]{1,0:T(8,128)(2,1)S(1)}, u32[]{:S(2)}, u32[]{:S(2)}) %collective-permute-start.13) | collective-permute-done | bytes 344096 | tf_op jit(solution)/shard_map/ppermute | solution.py:24
  79.7 1.5 collective-permute-done.12
  81.7 3.0 %collective-permute-start.17 = (bf16[32,5376]{1,0:T(8,128)(2,1)S(1)}, bf16[32,5376]{1,0:T(8,128)(2,1)S(1)}, u32[]{:S(2)}, u32[]{:S(2)}) collective-permute-start(bf16[32,5376]{1,0:T(8,128)(2,1)S(1)} %get-tuple-element.23), channel_id=1, source_target_pairs={{0,48},{1,49},{2,50},{3,51},{4,52},{5,53},{6,54},{7,55},{8,56},{9,... | collective-permute-start | bytes 1032200 | tf_op jit(solution)/shard_map/ppermute | solution.py:24
  84.7 7.0 %collective-permute-done.16 = bf16[32,5376]{1,0:T(8,128)(2,1)S(1)} collective-permute-done((bf16[32,5376]{1,0:T(8,128)(2,1)S(1)}, bf16[32,5376]{1,0:T(8,128)(2,1)S(1)}, u32[]{:S(2)}, u32[]{:S(2)}) %collective-permute-start.16) | collective-permute-done | bytes 344096 | tf_op jit(solution)/shard_map/ppermute | solution.py:24
  92.3 1.4 constant_dynamic-update-slice_fusion.18
  93.7 3.2 %collective-permute-start.18 = (bf16[64,5376]{1,0:T(8,128)(2,1)}, bf16[64,5376]{1,0:T(8,128)(2,1)}, u32[]{:S(2)}, u32[]{:S(2)}) collective-permute-start(bf16[64,5376]{1,0:T(8,128)(2,1)} %get-tuple-element.78), channel_id=1, source_target_pairs={{0,48},{1,49},{2,50},{3,51},{4,52},{5,53},{6,54},{7,55},{8,56},{9,... | collective-permute-start | bytes 2064392 | tf_op jit(solution)/shard_map/ppermute | solution.py:24
  96.9 1.2 collective-permute-start.23
  99.3 11.4 %collective-permute-done.19 = bf16[64,5376]{1,0:T(8,128)(2,1)} collective-permute-done((bf16[64,5376]{1,0:T(8,128)(2,1)}, bf16[64,5376]{1,0:T(8,128)(2,1)}, u32[]{:S(2)}, u32[]{:S(2)}) %collective-permute-start.19) | collective-permute-done | bytes 688160 | tf_op jit(solution)/shard_map/ppermute | solution.py:24
  112.8 3.3 %collective-permute-start.21 = (bf16[32,5376]{1,0:T(8,128)(2,1)S(1)}, bf16[32,5376]{1,0:T(8,128)(2,1)S(1)}, u32[]{:S(2)}, u32[]{:S(2)}) collective-permute-start(bf16[32,5376]{1,0:T(8,128)(2,1)S(1)} %slice.429), channel_id=1, source_target_pairs={{0,48},{1,49},{2,50},{3,51},{4,52},{5,53},{6,54},{7,55},{8,56},{9,... | collective-permute-start | bytes 1032200 | tf_op jit(solution)/shard_map/ppermute | solution.py:24
  116.1 3.2 %collective-permute-start.24 = (bf16[64,5376]{1,0:T(8,128)(2,1)}, bf16[64,5376]{1,0:T(8,128)(2,1)S(1)}, u32[]{:S(2)}, u32[]{:S(2)}) collective-permute-start(bf16[64,5376]{1,0:T(8,128)(2,1)} %collective-permute-done.23), channel_id=1, source_target_pairs={{0,48},{1,49},{2,50},{3,51},{4,52},{5,53},{6,54},{7,55},{8,56},{9,... | collective-permute-start | bytes 2064392 | tf_op jit(solution)/shard_map/ppermute | solution.py:24
  119.4 2.0 %constant_dynamic-update-slice_fusion.17 = (bf16[512,5376]{1,0:T(8,128)(2,1)}, bf16[256,5376]{1,0:T(8,128)(2,1)S(1)}) fusion(bf16[512,5376]{1,0:T(8,128)(2,1)} %get-tuple-element.76, bf16[64,5376]{1,0:T(8,128)(2,1)} %collective-permute-done.18, bf16[256,5376]{1,0:T(8,128)(2,1)S(1)} %copy-done.3), kind=kLoop, calls=%fused_computation.163 | loop fusion | bytes 2064384
  121.4 2.3 %collective-permute-done.20 = bf16[32,5376]{1,0:T(8,128)(2,1)S(1)} collective-permute-done((bf16[32,5376]{1,0:T(8,128)(2,1)S(1)}, bf16[32,5376]{1,0:T(8,128)(2,1)S(1)}, u32[]{:S(2)}, u32[]{:S(2)}) %collective-permute-start.20) | collective-permute-done | bytes 344096 | tf_op jit(solution)/shard_map/ppermute | solution.py:24
  125.4 2.0 %constant_dynamic-update-slice_fusion.14 = (bf16[512,5376]{1,0:T(8,128)(2,1)}, bf16[256,5376]{1,0:T(8,128)(2,1)S(1)}) fusion(bf16[512,5376]{1,0:T(8,128)(2,1)} %get-tuple-element.81, bf16[64,5376]{1,0:T(8,128)(2,1)} %collective-permute-done.19, bf16[256,5376]{1,0:T(8,128)(2,1)S(1)} %get-tuple-element.82), kind=kLoop, calls=%fused_computation.160 | loop fusion | bytes 2064384
  129.5 1.2 fusion.15
  130.7 1.3 collective-permute-start.25
  132.0 1.2 multiply_reduce_fusion.1
  134.8 1.2 constant_dynamic-update-slice_fusion.13
  136.1 5.7 %collective-permute-done.25 = bf16[64,5376]{1,0:T(8,128)(2,1)S(1)} collective-permute-done((bf16[64,5376]{1,0:T(8,128)(2,1)S(1)}, bf16[64,5376]{1,0:T(8,128)(2,1)S(1)}, u32[]{:S(2)}, u32[]{:S(2)}) %collective-permute-start.25) | collective-permute-done | bytes 688160 | tf_op jit(solution)/shard_map/ppermute | solution.py:24
  143.2 1.1 fusion.10
  144.4 1.2 multiply_reduce_fusion
  145.9 4.0 %convolution_convert_fusion.2 = bf16[1792,1024]{1,0:T(8,128)(2,1)} fusion(bf16[512,5376]{1,0:T(8,128)(2,1)S(1)} %get-tuple-element.64, bf16[256,1024]{1,0:T(8,128)(2,1)S(1)} %slice.403, bf16[256,1024]{1,0:T(8,128)(2,1)S(1)} %slice.413), kind=kOutput, calls=%fused_computation.32 | convolution fusion | flops 1882980352 | bytes 6553600 | tf_op jit(solution)/shard_map/dot_general | solution.py:36
  150.4 2.5 %collective-permute-start.30 = (bf16[64,2176]{1,0:T(8,128)(2,1)S(1)}, bf16[64,2176]{1,0:T(8,128)(2,1)S(1)}, u32[]{:S(2)}, u32[]{:S(2)}) collective-permute-start(bf16[64,2176]{1,0:T(8,128)(2,1)S(1)} %get-tuple-element.90), channel_id=1, source_target_pairs={{0,4},{1,5},{2,6},{3,7},{4,0},{5,1},{6,2},{7,3},{8,12},{9,13},{10,... | collective-permute-start | bytes 835592 | tf_op jit(solution)/shard_map/ppermute | solution.py:24
  152.9 2.1 %collective-permute-start.29 = (bf16[64,2176]{1,0:T(8,128)(2,1)S(1)}, bf16[64,2176]{1,0:T(8,128)(2,1)S(1)}, u32[]{:S(2)}, u32[]{:S(2)}) collective-permute-start(bf16[64,2176]{1,0:T(8,128)(2,1)S(1)} %get-tuple-element.91), channel_id=1, source_target_pairs={{0,6},{1,7},{2,0},{3,1},{4,2},{5,3},{6,4},{7,5},{8,14},{9,15},{10,... | collective-permute-start | bytes 835592 | tf_op jit(solution)/shard_map/ppermute | solution.py:24
  155.0 6.4 %collective-permute-done.30 = bf16[64,2176]{1,0:T(8,128)(2,1)S(1)} collective-permute-done((bf16[64,2176]{1,0:T(8,128)(2,1)S(1)}, bf16[64,2176]{1,0:T(8,128)(2,1)S(1)}, u32[]{:S(2)}, u32[]{:S(2)}) %collective-permute-start.30) | collective-permute-done | bytes 278560 | tf_op jit(solution)/shard_map/ppermute | solution.py:24
  161.4 5.6 %collective-permute-done.29 = bf16[64,2176]{1,0:T(8,128)(2,1)S(1)} collective-permute-done((bf16[64,2176]{1,0:T(8,128)(2,1)S(1)}, bf16[64,2176]{1,0:T(8,128)(2,1)S(1)}, u32[]{:S(2)}, u32[]{:S(2)}) %collective-permute-start.29) | collective-permute-done | bytes 278560 | tf_op jit(solution)/shard_map/ppermute | solution.py:24
  168.4 6.4 %all-to-all-start.1 = ((bf16[16,4,2560]{2,1,0:T(4,128)(2,1)}), bf16[16,4,2560]{2,1,0:T(4,128)(2,1)S(1)}, u32[]{:S(2)}, u32[]{:S(2)}) async-start(bf16[16,4,2560]{2,1,0:T(4,128)(2,1)} %pad_maximum_fusion.5), calls=%async_computation.1 | async-start | bytes 655360 | tf_op jit(solution)/shard_map/all_to_all | solution.py:233
  174.8 5.5 %convolution_convert_fusion = bf16[1024,1792]{1,0:T(8,128)(2,1)} fusion(bf16[512,1024]{1,0:T(8,128)(2,1)S(1)} %copy-done.1, bf16[512,5376]{1,0:T(8,128)(2,1)} %copy-done.5), kind=kOutput, calls=%fused_computation.30 | convolution fusion | flops 1880883200 | bytes 6553600 | tf_op jit(solution)/shard_map/dot_general | solution.py:36
  180.2 5.5 %convolution_convert_fusion.1 = bf16[1024,1792]{1,0:T(8,128)(2,1)} fusion(bf16[512,1024]{1,0:T(8,128)(2,1)S(1)} %copy-done.1, bf16[512,5376]{1,0:T(8,128)(2,1)} %copy-done.5), kind=kOutput, calls=%fused_computation.31 | convolution fusion | flops 1880883200 | bytes 6553600 | tf_op jit(solution)/shard_map/dot_general | solution.py:36
  (182 shorter events, 29.1 us)
Async XLA Ops:
  0.6 23.6 %copy-start.4 = (f32[8192]{0:T(1024)S(1)}, f32[8192]{0:T(1024)}, u32[]{:S(2)}) copy-start(f32[8192]{0:T(1024)} %param.7) | copy-start | bytes 98308
  4.0 16.8 %all-to-all-start = ((bf16[16,4,2176]{2,1,0:T(4,128)(2,1)}), bf16[16,4,2176]{2,1,0:T(4,128)(2,1)S(1)}, u32[]{:S(2)}, u32[]{:S(2)}) async-start(bf16[16,4,2176]{2,1,0:T(4,128)(2,1)} %bitcast.2), calls=%async_computation | async-start | bytes 557056 | tf_op jit(solution)/shard_map/all_to_all | solution.py:155
  21.0 8.0 %collective-permute-start = (bf16[32,2176]{1,0:T(8,128)(2,1)S(1)}, bf16[32,2176]{1,0:T(8,128)(2,1)S(1)}, u32[]{:S(2)}, u32[]{:S(2)}) collective-permute-start(bf16[32,2176]{1,0:T(8,128)(2,1)S(1)} %get-tuple-element.31), channel_id=1, source_target_pairs={{0,2},{1,3},{2,4},{3,5},{4,6},{5,7},{6,0},{7,1},{8,10},{9,11},{10,... | collective-permute-start | bytes 417800 | tf_op jit(solution)/shard_map/ppermute | solution.py:24
  22.6 11.4 %collective-permute-start.4 = (bf16[32,2176]{1,0:T(8,128)(2,1)S(1)}, bf16[32,2176]{1,0:T(8,128)(2,1)S(1)}, u32[]{:S(2)}, u32[]{:S(2)}) collective-permute-start(bf16[32,2176]{1,0:T(8,128)(2,1)S(1)} %get-tuple-element.31), channel_id=1, source_target_pairs={{0,6},{1,7},{2,0},{3,1},{4,2},{5,3},{6,4},{7,5},{8,14},{9,15},{10,... | collective-permute-start | bytes 417800 | tf_op jit(solution)/shard_map/ppermute | solution.py:24
  24.3 9.7 %collective-permute-start.5 = (bf16[32,2176]{1,0:T(8,128)(2,1)S(1)}, bf16[32,2176]{1,0:T(8,128)(2,1)S(1)}, u32[]{:S(2)}, u32[]{:S(2)}) collective-permute-start(bf16[32,2176]{1,0:T(8,128)(2,1)S(1)} %get-tuple-element.31), channel_id=1, source_target_pairs={{0,4},{1,5},{2,6},{3,7},{4,0},{5,1},{6,2},{7,3},{8,12},{9,13},{10,... | collective-permute-start | bytes 417800 | tf_op jit(solution)/shard_map/ppermute | solution.py:24
  28.9 8.7 %collective-permute-start.3 = (bf16[32,2176]{1,0:T(8,128)(2,1)S(1)}, bf16[32,2176]{1,0:T(8,128)(2,1)S(1)}, u32[]{:S(2)}, u32[]{:S(2)}) collective-permute-start(bf16[32,2176]{1,0:T(8,128)(2,1)S(1)} %get-tuple-element.17), channel_id=1, source_target_pairs={{0,2},{1,3},{2,4},{3,5},{4,6},{5,7},{6,0},{7,1},{8,10},{9,11},{10,... | collective-permute-start | bytes 417800 | tf_op jit(solution)/shard_map/ppermute | solution.py:24
  28.9 8.6 %collective-permute-start.2 = (bf16[32,2176]{1,0:T(8,128)(2,1)S(1)}, bf16[32,2176]{1,0:T(8,128)(2,1)S(1)}, u32[]{:S(2)}, u32[]{:S(2)}) collective-permute-start(bf16[32,2176]{1,0:T(8,128)(2,1)S(1)} %get-tuple-element.17), channel_id=1, source_target_pairs={{0,4},{1,5},{2,6},{3,7},{4,0},{5,1},{6,2},{7,3},{8,12},{9,13},{10,... | collective-permute-start | bytes 417800 | tf_op jit(solution)/shard_map/ppermute | solution.py:24
  32.0 5.5 %collective-permute-start.1 = (bf16[32,2176]{1,0:T(8,128)(2,1)S(1)}, bf16[32,2176]{1,0:T(8,128)(2,1)S(1)}, u32[]{:S(2)}, u32[]{:S(2)}) collective-permute-start(bf16[32,2176]{1,0:T(8,128)(2,1)S(1)} %get-tuple-element.17), channel_id=1, source_target_pairs={{0,6},{1,7},{2,0},{3,1},{4,2},{5,3},{6,4},{7,5},{8,14},{9,15},{10,... | collective-permute-start | bytes 417800 | tf_op jit(solution)/shard_map/ppermute | solution.py:24
  34.1 3.6 %collective-permute-start.6 = (bf16[128,2176]{1,0:T(8,128)(2,1)S(1)}, bf16[128,2176]{1,0:T(8,128)(2,1)S(1)}, u32[]{:S(2)}, u32[]{:S(2)}) collective-permute-start(bf16[128,2176]{1,0:T(8,128)(2,1)S(1)} %constant_dynamic-update-slice_fusion.19), channel_id=1, source_target_pairs={{0,1},{1,0},{2,3},{3,2},{4,5},{5,4},{6,7},{7,6},{8,9},{9,8},{10,11... | collective-permute-start | bytes 1671176 | tf_op jit(solution)/shard_map/ppermute | solution.py:24
  34.3 4.0 %copy-start.8 = (bf16[1024,1792]{1,0:T(8,128)(2,1)S(1)}, bf16[1024,1792]{1,0:T(8,128)(2,1)}, u32[]{:S(2)}) copy-start(bf16[1024,1792]{1,0:T(8,128)(2,1)} %param.9) | copy-start | bytes 11010052
  38.2 2.0 %copy-start.11 = (bf16[1024,1792]{1,0:T(8,128)(2,1)S(1)}, bf16[1024,1792]{1,0:T(8,128)(2,1)}, u32[]{:S(2)}) copy-start(bf16[1024,1792]{1,0:T(8,128)(2,1)} %param.8) | copy-start | bytes 11010052
  40.3 2.0 %copy-start.6 = (bf16[1792,1024]{1,0:T(8,128)(2,1)S(1)}, bf16[1792,1024]{1,0:T(8,128)(2,1)}, u32[]{:S(2)}) copy-start(bf16[1792,1024]{1,0:T(8,128)(2,1)} %param.10) | copy-start | bytes 11010052
  44.1 2.7 %copy-start = (f32[256,5376]{1,0:T(8,128)}, f32[256,5376]{1,0:T(8,128)S(1)}, u32[]{:S(2)}) copy-start(f32[256,5376]{1,0:T(8,128)S(1)} %pad_maximum_fusion) | copy-start | bytes 16515076
  44.3 5.8 %copy-start.9 = (bf16[1024,1792]{1,0:T(8,128)(2,1)S(1)}, bf16[1024,1792]{1,0:T(8,128)(2,1)}, u32[]{:S(2)}) copy-start(bf16[1024,1792]{1,0:T(8,128)(2,1)} %param.9) | copy-start | bytes 11010052
  46.8 2.6 %collective-permute-start.7 = (bf16[128,2176]{1,0:T(8,128)(2,1)S(1)}, bf16[128,2176]{1,0:T(8,128)(2,1)S(1)}, u32[]{:S(2)}, u32[]{:S(2)}) collective-permute-start(bf16[128,2176]{1,0:T(8,128)(2,1)S(1)} %constant_dynamic-update-slice_fusion.23), channel_id=1, source_target_pairs={{0,1},{1,0},{2,3},{3,2},{4,5},{5,4},{6,7},{7,6},{8,9},{9,8},{10,11... | collective-permute-start | bytes 1671176 | tf_op jit(solution)/shard_map/ppermute | solution.py:24
  46.8 17.8 %collective-permute-start.11 = (bf16[64,5376]{1,0:T(8,128)(2,1)S(1)}, bf16[64,5376]{1,0:T(8,128)(2,1)S(1)}, u32[]{:S(2)}, u32[]{:S(2)}) collective-permute-start(bf16[64,5376]{1,0:T(8,128)(2,1)S(1)} %get-tuple-element.38), channel_id=1, source_target_pairs={{0,64},{1,65},{2,66},{3,67},{4,68},{5,69},{6,70},{7,71},{8,72},{9,... | collective-permute-start | bytes 2064392 | tf_op jit(solution)/shard_map/ppermute | solution.py:24
  47.4 18.3 %collective-permute-start.9 = (bf16[64,5376]{1,0:T(8,128)(2,1)S(1)}, bf16[64,5376]{1,0:T(8,128)(2,1)S(1)}, u32[]{:S(2)}, u32[]{:S(2)}) collective-permute-start(bf16[64,5376]{1,0:T(8,128)(2,1)S(1)} %get-tuple-element.39), channel_id=1, source_target_pairs={{0,48},{1,49},{2,50},{3,51},{4,52},{5,53},{6,54},{7,55},{8,56},{9,... | collective-permute-start | bytes 2064392 | tf_op jit(solution)/shard_map/ppermute | solution.py:24
  48.0 19.5 %collective-permute-start.8 = (bf16[64,5376]{1,0:T(8,128)(2,1)S(1)}, bf16[64,5376]{1,0:T(8,128)(2,1)S(1)}, u32[]{:S(2)}, u32[]{:S(2)}) collective-permute-start(bf16[64,5376]{1,0:T(8,128)(2,1)S(1)} %get-tuple-element.40), channel_id=1, source_target_pairs={{0,16},{1,17},{2,18},{3,19},{4,20},{5,21},{6,22},{7,23},{8,24},{9,... | collective-permute-start | bytes 2064392 | tf_op jit(solution)/shard_map/ppermute | solution.py:24
  50.0 2.0 %copy-start.12 = (bf16[1024,1792]{1,0:T(8,128)(2,1)S(1)}, bf16[1024,1792]{1,0:T(8,128)(2,1)}, u32[]{:S(2)}) copy-start(bf16[1024,1792]{1,0:T(8,128)(2,1)} %param.8) | copy-start | bytes 11010052
  54.7 26.7 %collective-permute-start.15 = (bf16[32,5376]{1,0:T(8,128)(2,1)S(1)}, bf16[32,5376]{1,0:T(8,128)(2,1)S(1)}, u32[]{:S(2)}, u32[]{:S(2)}) collective-permute-start(bf16[32,5376]{1,0:T(8,128)(2,1)S(1)} %get-tuple-element.36), channel_id=1, source_target_pairs={{0,48},{1,49},{2,50},{3,51},{4,52},{5,53},{6,54},{7,55},{8,56},{9,... | collective-permute-start | bytes 1032200 | tf_op jit(solution)/shard_map/ppermute | solution.py:24
  56.6 24.8 %collective-permute-start.14 = (bf16[32,5376]{1,0:T(8,128)(2,1)S(1)}, bf16[32,5376]{1,0:T(8,128)(2,1)S(1)}, u32[]{:S(2)}, u32[]{:S(2)}) collective-permute-start(bf16[32,5376]{1,0:T(8,128)(2,1)S(1)} %get-tuple-element.37), channel_id=1, source_target_pairs={{0,16},{1,17},{2,18},{3,19},{4,20},{5,21},{6,22},{7,23},{8,24},{9,... | collective-permute-start | bytes 1032200 | tf_op jit(solution)/shard_map/ppermute | solution.py:24
  57.2 10.4 %slice-start = ((f32[256,5376]{1,0:T(8,128)}), f32[64,5376]{1,0:T(8,128)S(1)}, s32[]{:S(2)}) async-start(f32[256,5376]{1,0:T(8,128)} %copy-done), calls=%async_computation.2 | async-start | bytes 2752512 | tf_op jit(solution)/shard_map/slice | solution.py:187
  64.9 14.9 %collective-permute-start.13 = (bf16[32,5376]{1,0:T(8,128)(2,1)S(1)}, bf16[32,5376]{1,0:T(8,128)(2,1)S(1)}, u32[]{:S(2)}, u32[]{:S(2)}) collective-permute-start(bf16[32,5376]{1,0:T(8,128)(2,1)S(1)} %get-tuple-element.79), channel_id=1, source_target_pairs={{0,48},{1,49},{2,50},{3,51},{4,52},{5,53},{6,54},{7,55},{8,56},{9,... | collective-permute-start | bytes 1032200 | tf_op jit(solution)/shard_map/ppermute | solution.py:24
  65.7 15.6 %collective-permute-start.12 = (bf16[32,5376]{1,0:T(8,128)(2,1)S(1)}, bf16[32,5376]{1,0:T(8,128)(2,1)S(1)}, u32[]{:S(2)}, u32[]{:S(2)}) collective-permute-start(bf16[32,5376]{1,0:T(8,128)(2,1)S(1)} %get-tuple-element.80), channel_id=1, source_target_pairs={{0,16},{1,17},{2,18},{3,19},{4,20},{5,21},{6,22},{7,23},{8,24},{9,... | collective-permute-start | bytes 1032200 | tf_op jit(solution)/shard_map/ppermute | solution.py:24
  67.8 17.0 %collective-permute-start.10 = (bf16[64,5376]{1,0:T(8,128)(2,1)S(1)}, bf16[64,5376]{1,0:T(8,128)(2,1)S(1)}, u32[]{:S(2)}, u32[]{:S(2)}) collective-permute-start(bf16[64,5376]{1,0:T(8,128)(2,1)S(1)} %add_convert_fusion), channel_id=1, source_target_pairs={{0,64},{1,65},{2,66},{3,67},{4,68},{5,69},{6,70},{7,71},{8,72},{9,... | collective-permute-start | bytes 2064392 | tf_op jit(solution)/shard_map/ppermute | solution.py:24
  81.4 10.3 %collective-permute-start.16 = (bf16[32,5376]{1,0:T(8,128)(2,1)S(1)}, bf16[32,5376]{1,0:T(8,128)(2,1)S(1)}, u32[]{:S(2)}, u32[]{:S(2)}) collective-permute-start(bf16[32,5376]{1,0:T(8,128)(2,1)S(1)} %get-tuple-element.20), channel_id=1, source_target_pairs={{0,16},{1,17},{2,18},{3,19},{4,20},{5,21},{6,22},{7,23},{8,24},{9,... | collective-permute-start | bytes 1032200 | tf_op jit(solution)/shard_map/ppermute | solution.py:24
  81.7 10.1 %collective-permute-start.17 = (bf16[32,5376]{1,0:T(8,128)(2,1)S(1)}, bf16[32,5376]{1,0:T(8,128)(2,1)S(1)}, u32[]{:S(2)}, u32[]{:S(2)}) collective-permute-start(bf16[32,5376]{1,0:T(8,128)(2,1)S(1)} %get-tuple-element.23), channel_id=1, source_target_pairs={{0,48},{1,49},{2,50},{3,51},{4,52},{5,53},{6,54},{7,55},{8,56},{9,... | collective-permute-start | bytes 1032200 | tf_op jit(solution)/shard_map/ppermute | solution.py:24
  93.7 17.0 %collective-permute-start.19 = (bf16[64,5376]{1,0:T(8,128)(2,1)}, bf16[64,5376]{1,0:T(8,128)(2,1)}, u32[]{:S(2)}, u32[]{:S(2)}) collective-permute-start(bf16[64,5376]{1,0:T(8,128)(2,1)} %get-tuple-element.78), channel_id=1, source_target_pairs={{0,16},{1,17},{2,18},{3,19},{4,20},{5,21},{6,22},{7,23},{8,24},{9,... | collective-permute-start | bytes 2064392 | tf_op jit(solution)/shard_map/ppermute | solution.py:24
  93.7 18.1 %collective-permute-start.18 = (bf16[64,5376]{1,0:T(8,128)(2,1)}, bf16[64,5376]{1,0:T(8,128)(2,1)}, u32[]{:S(2)}, u32[]{:S(2)}) collective-permute-start(bf16[64,5376]{1,0:T(8,128)(2,1)} %get-tuple-element.78), channel_id=1, source_target_pairs={{0,48},{1,49},{2,50},{3,51},{4,52},{5,53},{6,54},{7,55},{8,56},{9,... | collective-permute-start | bytes 2064392 | tf_op jit(solution)/shard_map/ppermute | solution.py:24
  96.9 19.2 %collective-permute-start.23 = (bf16[64,5376]{1,0:T(8,128)(2,1)}, bf16[64,5376]{1,0:T(8,128)(2,1)}, u32[]{:S(2)}, u32[]{:S(2)}) collective-permute-start(bf16[64,5376]{1,0:T(8,128)(2,1)} %get-tuple-element.78), channel_id=1, source_target_pairs={{0,64},{1,65},{2,66},{3,67},{4,68},{5,69},{6,70},{7,71},{8,72},{9,... | collective-permute-start | bytes 2064392 | tf_op jit(solution)/shard_map/ppermute | solution.py:24
  98.2 21.2 %copy-start.3 = (bf16[256,5376]{1,0:T(8,128)(2,1)S(1)}, bf16[256,5376]{1,0:T(8,128)(2,1)}, u32[]{:S(2)}) copy-start(bf16[256,5376]{1,0:T(8,128)(2,1)} %get-tuple-element.77) | copy-start | bytes 8257540
  111.7 12.0 %collective-permute-start.20 = (bf16[32,5376]{1,0:T(8,128)(2,1)S(1)}, bf16[32,5376]{1,0:T(8,128)(2,1)S(1)}, u32[]{:S(2)}, u32[]{:S(2)}) collective-permute-start(bf16[32,5376]{1,0:T(8,128)(2,1)S(1)} %slice.428), channel_id=1, source_target_pairs={{0,16},{1,17},{2,18},{3,19},{4,20},{5,21},{6,22},{7,23},{8,24},{9,... | collective-permute-start | bytes 1032200 | tf_op jit(solution)/shard_map/ppermute | solution.py:24
  112.8 11.8 %collective-permute-start.21 = (bf16[32,5376]{1,0:T(8,128)(2,1)S(1)}, bf16[32,5376]{1,0:T(8,128)(2,1)S(1)}, u32[]{:S(2)}, u32[]{:S(2)}) collective-permute-start(bf16[32,5376]{1,0:T(8,128)(2,1)S(1)} %slice.429), channel_id=1, source_target_pairs={{0,48},{1,49},{2,50},{3,51},{4,52},{5,53},{6,54},{7,55},{8,56},{9,... | collective-permute-start | bytes 1032200 | tf_op jit(solution)/shard_map/ppermute | solution.py:24
  116.1 25.8 %collective-permute-start.26 = (bf16[64,5376]{1,0:T(8,128)(2,1)}, bf16[64,5376]{1,0:T(8,128)(2,1)S(1)}, u32[]{:S(2)}, u32[]{:S(2)}) collective-permute-start(bf16[64,5376]{1,0:T(8,128)(2,1)} %collective-permute-done.23), channel_id=1, source_target_pairs={{0,16},{1,17},{2,18},{3,19},{4,20},{5,21},{6,22},{7,23},{8,24},{9,... | collective-permute-start | bytes 2064392 | tf_op jit(solution)/shard_map/ppermute | solution.py:24
  116.1 19.9 %collective-permute-start.24 = (bf16[64,5376]{1,0:T(8,128)(2,1)}, bf16[64,5376]{1,0:T(8,128)(2,1)S(1)}, u32[]{:S(2)}, u32[]{:S(2)}) collective-permute-start(bf16[64,5376]{1,0:T(8,128)(2,1)} %collective-permute-done.23), channel_id=1, source_target_pairs={{0,48},{1,49},{2,50},{3,51},{4,52},{5,53},{6,54},{7,55},{8,56},{9,... | collective-permute-start | bytes 2064392 | tf_op jit(solution)/shard_map/ppermute | solution.py:24
  121.4 6.1 %copy-start.7 = (bf16[1792,1024]{1,0:T(8,128)(2,1)S(1)}, bf16[1792,1024]{1,0:T(8,128)(2,1)}, u32[]{:S(2)}) copy-start(bf16[1792,1024]{1,0:T(8,128)(2,1)} %param.10) | copy-start | bytes 11010052
  127.5 2.0 %copy-start.10 = (bf16[1024,1792]{1,0:T(8,128)(2,1)S(1)}, bf16[1024,1792]{1,0:T(8,128)(2,1)}, u32[]{:S(2)}) copy-start(bf16[1024,1792]{1,0:T(8,128)(2,1)} %param.9) | copy-start | bytes 11010052
  129.5 2.5 %copy-start.13 = (bf16[1024,1792]{1,0:T(8,128)(2,1)S(1)}, bf16[1024,1792]{1,0:T(8,128)(2,1)}, u32[]{:S(2)}) copy-start(bf16[1024,1792]{1,0:T(8,128)(2,1)} %param.8) | copy-start | bytes 11010052
  130.7 11.1 %collective-permute-start.25 = (bf16[64,5376]{1,0:T(8,128)(2,1)S(1)}, bf16[64,5376]{1,0:T(8,128)(2,1)S(1)}, u32[]{:S(2)}, u32[]{:S(2)}) collective-permute-start(bf16[64,5376]{1,0:T(8,128)(2,1)S(1)} %pad_maximum_fusion.4), channel_id=1, source_target_pairs={{0,64},{1,65},{2,66},{3,67},{4,68},{5,69},{6,70},{7,71},{8,72},{9,... | collective-permute-start | bytes 2064392 | tf_op jit(solution)/shard_map/ppermute | solution.py:24
  132.0 2.2 %slice-start.1 = ((s8[5505024]{0:T(1024)(128)(4,1)}), s8[4194304]{0:T(1024)(128)(4,1)S(1)}, s32[]{:S(2)}) async-start(s8[5505024]{0:T(1024)(128)(4,1)} %bitcast.58), calls=%async_computation.3 | async-start | bytes 8388608
  133.5 16.3 %collective-permute-start.22 = (f32[128,2048]{1,0:T(8,128)S(1)}, f32[128,2048]{1,0:T(8,128)S(1)}, u32[]{:S(2)}, u32[]{:S(2)}) collective-permute-start(f32[128,2048]{1,0:T(8,128)S(1)} %fusion.6), channel_id=1, source_target_pairs={{0,1},{1,0},{2,3},{3,2},{4,5},{5,4},{6,7},{7,6},{8,9},{9,8},{10,11... | collective-permute-start | bytes 3145736 | tf_op jit(solution)/shard_map/ppermute | solution.py:24
  142.1 3.9 %copy-start.5 = (bf16[512,5376]{1,0:T(8,128)(2,1)}, bf16[512,5376]{1,0:T(8,128)(2,1)S(1)}, u32[]{:S(2)}) copy-start(bf16[512,5376]{1,0:T(8,128)(2,1)S(1)} %get-tuple-element.64) | copy-start | bytes 16515076
  145.8 4.2 %collective-permute-start.27 = (f32[136,2048]{1,0:T(8,128)S(1)}, f32[136,2048]{1,0:T(8,128)S(1)}, u32[]{:S(2)}, u32[]{:S(2)}) collective-permute-start(f32[136,2048]{1,0:T(8,128)S(1)} %constant_dynamic-update-slice_fusion.9), channel_id=1, source_target_pairs={{0,1},{1,0},{2,3},{3,2},{4,5},{5,4},{6,7},{7,6},{8,9},{9,8},{10,11... | collective-permute-start | bytes 3342344 | tf_op jit(solution)/shard_map/ppermute | solution.py:24
  150.4 11.1 %collective-permute-start.30 = (bf16[64,2176]{1,0:T(8,128)(2,1)S(1)}, bf16[64,2176]{1,0:T(8,128)(2,1)S(1)}, u32[]{:S(2)}, u32[]{:S(2)}) collective-permute-start(bf16[64,2176]{1,0:T(8,128)(2,1)S(1)} %get-tuple-element.90), channel_id=1, source_target_pairs={{0,4},{1,5},{2,6},{3,7},{4,0},{5,1},{6,2},{7,3},{8,12},{9,13},{10,... | collective-permute-start | bytes 835592 | tf_op jit(solution)/shard_map/ppermute | solution.py:24
  152.9 14.2 %collective-permute-start.29 = (bf16[64,2176]{1,0:T(8,128)(2,1)S(1)}, bf16[64,2176]{1,0:T(8,128)(2,1)S(1)}, u32[]{:S(2)}, u32[]{:S(2)}) collective-permute-start(bf16[64,2176]{1,0:T(8,128)(2,1)S(1)} %get-tuple-element.91), channel_id=1, source_target_pairs={{0,6},{1,7},{2,0},{3,1},{4,2},{5,3},{6,4},{7,5},{8,14},{9,15},{10,... | collective-permute-start | bytes 835592 | tf_op jit(solution)/shard_map/ppermute | solution.py:24
  155.0 12.1 %collective-permute-start.28 = (bf16[64,2176]{1,0:T(8,128)(2,1)S(1)}, bf16[64,2176]{1,0:T(8,128)(2,1)S(1)}, u32[]{:S(2)}, u32[]{:S(2)}) collective-permute-start(bf16[64,2176]{1,0:T(8,128)(2,1)S(1)} %get-tuple-element.92), channel_id=1, source_target_pairs={{0,2},{1,3},{2,4},{3,5},{4,6},{5,7},{6,0},{7,1},{8,10},{9,11},{10,... | collective-permute-start | bytes 835592 | tf_op jit(solution)/shard_map/ppermute | solution.py:24
  167.1 7.7 %copy-start.1 = (bf16[512,1024]{1,0:T(8,128)(2,1)S(1)}, bf16[512,1024]{1,0:T(8,128)(2,1)}, u32[]{:S(2)}) copy-start(bf16[512,1024]{1,0:T(8,128)(2,1)} %pad_maximum_fusion.2) | copy-start | bytes 3145732
  168.4 17.3 %all-to-all-start.1 = ((bf16[16,4,2560]{2,1,0:T(4,128)(2,1)}), bf16[16,4,2560]{2,1,0:T(4,128)(2,1)S(1)}, u32[]{:S(2)}, u32[]{:S(2)}) async-start(bf16[16,4,2560]{2,1,0:T(4,128)(2,1)} %pad_maximum_fusion.5), calls=%async_computation.1 | async-start | bytes 655360 | tf_op jit(solution)/shard_map/all_to_all | solution.py:233
  (2 other events, 2.8 us)

commit v8 on v7

v8 whole, which is shorter than its diff:
```python
import math

import jax
import jax.numpy as jnp
from jax import lax
from jax.experimental import pallas as pl
from jax.experimental.pallas import tpu as pltpu
from jax.sharding import Mesh, PartitionSpec as P

EPS = 1e-05
F32 = jnp.float32
BF16 = jnp.bfloat16
ZS, XS, HS, YS, CS = 2, 4, 2, 4, 2
AXES = ("z", "x", "h", "y", "core")


def send(value, z=0, x=0, h=0, y=0, c=0):
    pairs = []
    for z0 in range(ZS):
        for x0 in range(XS):
            for h0 in range(HS):
                for y0 in range(YS):
                    for c0 in range(CS):
                        source = (((z0 * XS + x0) * HS + h0) * YS + y0) * CS + c0
                        z1, x1, h1 = (z0 + z) % ZS, (x0 + x) % XS, (h0 + h) % HS
                        y1, c1 = (y0 + y) % YS, (c0 + c) % CS
                        pairs.append((source, (((z1 * XS + x1) * HS + h1) * YS + y1) * CS + c1))
    return lax.ppermute(value, AXES, pairs)


def contract(left, right, dims):
    return lax.dot_general(left, right, ((dims[:1], dims[1:]), ((), ())), preferred_element_type=F32)


def rounded(value):
    return lax.reduce_precision(value, 8, 7)


def parts_of(value, count):
    parts = []
    for _ in range(count):
        top = rounded(value)
        parts.append(top.astype(BF16))
        value = value - top
    return parts


def gather_half(own, x):
    n = own.shape[1]
    over_y = {0: own}
    for dy in (1, 3, 2):
        over_y[-dy % YS] = send(own, y=dy)
    core = jnp.zeros((128, n), own.dtype)
    for dy in range(YS):
        core = lax.dynamic_update_slice(core, over_y[dy], ((dy - x) % XS * 32, 0))
    return core, over_y[3]


TILE = 256


def call(kernel, grid, arrays, specs, outs, flops, scratch=()):
    size = sum(array.size * array.dtype.itemsize for array in arrays)
    size += sum(math.prod(shape) * jnp.dtype(dtype).itemsize for shape, dtype, _ in outs)
    return pl.pallas_call(
        kernel,
        grid=grid,
        in_specs=specs,
        out_specs=[spec for _, _, spec in outs],
        out_shape=[jax.ShapeDtypeStruct(shape, dtype) for shape, dtype, _ in outs],
        scratch_shapes=scratch,
        compiler_params=pltpu.CompilerParams(vmem_limit_bytes=28 * 1024 * 1024),
        cost_estimate=pl.CostEstimate(flops=flops, bytes_accessed=size, transcendentals=0),
    )(*arrays)


def whole(rows, columns):
    return pl.BlockSpec((rows, columns), lambda j: (0, 0))


def columns_at(rows, columns=3 * TILE):
    return pl.BlockSpec((rows, columns), lambda j: (0, j))


def weight_specs():
    return [columns_at(1024, TILE), columns_at(1024, TILE), pl.BlockSpec((TILE, 1024), lambda j: (j, 0))]


def estimates(core_ref, other_ref):
    for i in range(XS):
        for k, ref in enumerate((core_ref, other_ref)):
            rows = ref[i * 32 : i * 32 + 32, :]
            side = rows[:, 2048:].astype(F32)
            inverse = side[:, 0:1] + side[:, 1:2] + side[:, 2:3]
            yield i * 64 + k * 32, rows[:, :1024].astype(F32) * inverse, rows[:, 1024:2048]


def multiply_half(core, other, gain_block, weights, pieces):
    def kernel(core_ref, other_ref, gain_ref, gate_ref, up_ref, down_ref, normed, grad, *refs):
        @pl.when(pl.program_id(0) == 0)
        def _():
            for at, estimate, rows in estimates(core_ref, other_ref):
                normed[at : at + 32, :] = (estimate * gain_ref[...]).astype(BF16)
                grad[at : at + 32, :] = rows

        sums = (
            contract(normed[...], gate_ref[...], (1, 0)),
            contract(normed[...], up_ref[...], (1, 0)),
            contract(grad[...], down_ref[...], (1, 1)),
        )
        for (first, count, dtype), ref in zip(pieces, refs, strict=True):
            for k, value in enumerate(sums):
                ref[:, k * TILE : k * TILE + TILE] = value[first : first + count].astype(dtype)

    width = weights[0].shape[1]
    outs = [((256, 1024), BF16, whole(256, 1024))] * 2
    outs += [((rows, 3 * width), dtype, columns_at(rows)) for _, rows, dtype in pieces]
    specs = [whole(128, 2176), whole(128, 2176), whole(1, 1024)] + weight_specs()
    flops = 6 * 256 * 1024 * width
    return call(kernel, (width // TILE,), [core, other, gain_block, *weights], specs, outs, flops)


def finish_sums(near, q, top1, bottom1, top2, bottom2):
    def kernel(near_ref, q_ref, top1_ref, bottom1_ref, top2_ref, bottom2_ref, out_ref):
        for rows, one, two in (
            (slice(0, 32), top1_ref, top2_ref),
            (slice(32, 64), bottom1_ref, bottom2_ref),
        ):
            total = near_ref[rows, :] + q_ref[rows, :].astype(F32)
            total = total + one[...].astype(F32) + two[...].astype(F32)
            gate, up, grad = (total[:, k * TILE : k * TILE + TILE] for k in range(3))
            sigma = jax.nn.sigmoid(gate)
            silu = gate * sigma
            out_ref[rows, :TILE] = (silu * up).astype(BF16)
            gate_grad = grad * up * sigma * (1.0 + gate * (1.0 - sigma))
            out_ref[rows, TILE : 2 * TILE] = gate_grad.astype(BF16)
            out_ref[rows, 2 * TILE :] = (grad * silu).astype(BF16)

    width = near.shape[1]
    specs = [columns_at(64)] * 2 + [columns_at(32)] * 4
    outs = [((64, width), BF16, columns_at(64))]
    arrays = [near, q, top1, bottom1, top2, bottom2]
    return call(kernel, (width // (3 * TILE),), arrays, specs, outs, 64 * width * 8)[0]


def multiply_back(units, core, other, weights, gain_before):
    last = weights[0].shape[1] // TILE - 1
    with_before = gain_before is not None

    def kernel(*refs):
        unit_refs, refs = refs[:4], refs[4:]
        gate_ref, up_ref, down_ref, core_ref, other_ref, *refs = refs
        before_ref, refs = (refs[0], refs[1:]) if with_before else (None, refs)
        keep_ref, give_ref, gain_ref, out_sum, grad_sum = refs
        j = pl.program_id(0)

        @pl.when(j == 0)
        def _():
            out_sum[...] = jnp.zeros_like(out_sum)
            grad_sum[...] = jnp.zeros_like(grad_sum)

        unit = jnp.concatenate([ref[...] for ref in unit_refs], axis=0)
        out_sum[...] += contract(unit[:, :TILE], down_ref[...], (1, 0))
        grad_sum[...] += contract(unit[:, TILE : 2 * TILE], gate_ref[...], (1, 1)) + contract(
            unit[:, 2 * TILE :], up_ref[...], (1, 1)
        )

        @pl.when(j == last)
        def _():
            gain = before_ref[0:1, :] if with_before else jnp.zeros((1, 1024), F32)
            for at, estimate, _ in estimates(core_ref, other_ref):
                grad = grad_sum[at : at + 32, :]
                gain = gain + jnp.sum(grad * estimate, axis=0, keepdims=True)
                ref = give_ref if at // 32 % 2 else keep_ref
                to = at // 64 * 32
                ref[to : to + 32, :1024] = out_sum[at : at + 32, :]
                ref[to : to + 32, 1024:] = grad
            gain_ref[...] = jnp.broadcast_to(gain, (8, 1024))
            if with_before:
                give_ref[128:136, :1024] = jnp.broadcast_to(gain, (8, 1024))
                give_ref[128:136, 1024:] = jnp.broadcast_to(gain, (8, 1024))

    width = weights[0].shape[1]
    give = 136 if with_before else 128
    arrays = [*units, *weights, core, other] + ([gain_before] if with_before else [])
    specs = [columns_at(64)] * 4 + weight_specs() + [whole(128, 2176)] * 2
    specs += [whole(8, 1024)] if with_before else []
    outs = [((rows, 2048), F32, whole(rows, 2048)) for rows in (128, give)]
    outs += [((8, 1024), F32, whole(8, 1024))]
    scratch = [pltpu.VMEM((256, 1024), F32)] * 2
    flops = 6 * 256 * 1024 * width
    return call(kernel, (width // TILE,), arrays, specs, outs, flops, scratch)


def weight_grad(units, parts, sides, left):
    width = units[0].shape[1] // 3
    count = len(parts)

    def kernel(*refs):
        side = jnp.concatenate([ref[...] for ref in refs[8 * count : 8 * count + 2]], axis=0)
        for k in range(count):
            unit = jnp.concatenate([ref[...] for ref in refs[8 * k : 8 * k + 8]], axis=0)
            pair = (unit, side) if left else (side, unit)
            refs[8 * count + 2 + k][...] = contract(*pair, (0, 0)).astype(BF16)

    specs = [
        pl.BlockSpec((64, TILE), lambda j, part=part: (0, 3 * j + part))
        for part in parts
        for _ in units
    ]
    specs += [whole(256, 1024)] * 2
    if left:
        out = ((width, 1024), BF16, pl.BlockSpec((TILE, 1024), lambda j: (j, 0)))
    else:
        out = ((1024, width), BF16, columns_at(1024, TILE))
    arrays = [*units] * count + list(sides)
    flops = 2 * 512 * 1024 * width * count
    return call(kernel, (width // TILE,), arrays, specs, [out] * count, flops)


def sum_over_y(near, far, gain, x):
    n = near.shape[1]

    def piece(dy):
        start = (dy - x) % XS * 32
        halves = [lax.dynamic_slice(half, (start, 0), (32, n)) for half in (near, far)]
        return jnp.concatenate(halves, axis=0)

    def gain_of(parts):
        return parts[:8].astype(F32) + parts[8:16].astype(F32)

    parts = jnp.concatenate(parts_of(gain, 2) + [jnp.zeros((48, 128), BF16)], axis=0)
    gains = {0: gain_of(parts)}
    total = piece(0)
    for dy in (1, 3, 2):
        got = send(jnp.concatenate([piece(dy).astype(BF16), parts], axis=1), y=dy)
        total = total + got[:, :n].astype(F32)
        gains[dy] = gain_of(got[:, n:])
    return total, (gains[0] + gains[2]) + (gains[1] + gains[3])


def sum_over_row(far, near):
    own, to1, to2, to3 = far
    near0, near1_top, near1_bottom, near2, near3_top, near3_bottom = near
    m12 = send(to2, z=1).astype(F32)
    m11 = send(to1, x=1).astype(F32)
    m13 = send(to3, x=3).astype(F32)
    first1 = send(near1_bottom, x=1)
    first2 = send(near3_top, x=3)
    n1 = send((near2[:32] + m12[:32]).astype(BF16), x=1).astype(F32)
    n2 = send((near2[32:] + m12[32:]).astype(BF16), x=3).astype(F32)
    q = send((own + m11 + m13).astype(BF16), z=1)
    last1 = (near1_top + n1).astype(BF16)
    last2 = (near3_bottom + n2).astype(BF16)
    last1, last2, first1, first2 = lax.optimization_barrier((last1, last2, first1, first2))
    return finish_sums(near0, q, send(last1, x=1), first1, first2, send(last2, x=3))


def gather_over_row(own):
    h = own.shape[0] // 2
    a = send(own, x=1)
    b = send(own, x=3)
    p = send(own, z=1)
    a2 = send(a[:h], x=1)
    b2 = send(b[h:], x=3)
    pa = send(p, x=1)
    pb = send(p, x=3)
    across = jnp.concatenate([a2, b2], axis=0)
    p2 = send(across, z=1)
    return [own, b, across, a], [p, pb, p2, pa]


def per_device(inputs, rms_gain_vector, gate_weight, up_weight, down_weight, out_grad):
    z, x = lax.axis_index("z"), lax.axis_index("x")
    row = z * XS + x

    value_entries = inputs.astype(F32)
    inverse_rms = lax.rsqrt(jnp.mean(value_entries * value_entries, axis=1, keepdims=True) + EPS)
    side = jnp.concatenate(parts_of(inverse_rms, 3) + [jnp.zeros((4, 125), BF16)], axis=1)
    message = jnp.concatenate(
        [
            inputs.reshape(4, 8, 1024),
            out_grad.reshape(4, 8, 1024),
            jnp.broadcast_to(side[:, None, :], (4, 8, 128)),
        ],
        axis=2,
    )
    message = jnp.broadcast_to(jnp.transpose(message, (1, 0, 2))[None], (HS, 8, 4, 2176))
    block = lax.all_to_all(
        message.reshape(16, 4, 2176), ("h", "z", "x"), split_axis=0, concat_axis=0, tiled=True
    )
    block = block.reshape(64, 2176)
    gain_block = lax.dynamic_slice(rms_gain_vector, (row * 1024,), (1024,))

    gain_block = gain_block.reshape(1, 1024)
    weights = (gate_weight, up_weight, down_weight)

    far_core, first = gather_half(lax.dynamic_slice(block, ((1 - z) * 32, 0), (32, 2176)), x)
    near_block, _ = lax.optimization_barrier(
        (lax.dynamic_slice(block, (z * 32, 0), (32, 2176)), first)
    )
    near_core, _ = gather_half(near_block, x)
    far_tokens = (far_core, send(far_core, c=1))
    far_normed, far_grad, far_own, *far = multiply_half(
        *far_tokens,
        gain_block,
        weights,
        [(0, 64, F32), (64, 64, BF16), (128, 64, BF16), (192, 64, BF16)],
    )
    near_core, far_own = lax.optimization_barrier((near_core, far_own))
    near_tokens = (near_core, send(near_core, c=1))
    near_normed, near_grad, *near = multiply_half(
        *near_tokens,
        gain_block,
        weights,
        [
            (0, 64, F32),
            (64, 32, F32),
            (96, 32, BF16),
            (128, 64, F32),
            (192, 32, BF16),
            (224, 32, F32),
        ],
    )
    near_units, far_units = gather_over_row(sum_over_row([far_own, *far], near))

    near_keep, near_give, gain = multiply_back(near_units, *near_tokens, weights, None)
    near_keep = near_keep + send(near_give, c=1)
    far_keep, far_give, gain = multiply_back(far_units, *far_tokens, weights, gain)
    taken = send(far_give, c=1)
    far_keep = far_keep + taken[:128]
    gain = (gain[0] + taken[128, :1024]).reshape(8, 128)

    units = near_units + far_units
    (down_weight_grad,) = weight_grad(units, (0,), (near_grad, far_grad), True)
    far_keep, down_weight_grad = lax.optimization_barrier((far_keep, down_weight_grad))
    total, gain = sum_over_y(near_keep, far_keep, gain, x)
    near_normed, total = lax.optimization_barrier((near_normed, total))
    gate_weight_grad, up_weight_grad = weight_grad(
        units, (1, 2), (near_normed, far_normed), False
    )

    gain_parts = [p.reshape(4, 256) for p in parts_of(gain, 2)]
    gain_rows = jnp.broadcast_to(jnp.concatenate(gain_parts, axis=1)[None], (16, 4, 512))
    total = total.astype(BF16)
    total = jnp.where(z == 0, total, jnp.concatenate([total[32:], total[:32]], axis=0))
    message = jnp.concatenate([total.reshape(16, 4, 2048), gain_rows], axis=2)
    back = lax.all_to_all(message, ("h", "z", "x"), split_axis=0, concat_axis=0, tiled=True)
    back = back.reshape(HS, 8, 4, 2560).astype(F32)
    gain_grad = back[..., 2048:2304] + back[..., 2304:]
    gain_grad = (gain_grad[0] + gain_grad[1]).reshape(8192)
    back = back[0, :, :, :2048] + back[1, :, :, :2048]
    outputs = jnp.transpose(back[..., :1024].astype(BF16), (1, 0, 2)).reshape(4, 8192)
    normed_grad = jnp.transpose(back[..., 1024:], (1, 0, 2)).reshape(4, 8192)

    normalized = value_entries * inverse_rms
    scaled = normed_grad * rms_gain_vector
    input_gradient = inverse_rms * (
        scaled - normalized * jnp.mean(scaled * normalized, axis=1, keepdims=True)
    )
    return (
        outputs,
        input_gradient.astype(BF16),
        gain_grad,
        gate_weight_grad,
        up_weight_grad,
        down_weight_grad,
    )


def solution(mesh):
    fine = Mesh(mesh.devices.reshape(ZS, XS, HS, YS, CS), AXES)
    row, col = AXES[:2], AXES[2:]
    in_specs = (P(AXES, None), P(), P(row, col), P(row, col), P(col, row), P(AXES, None))
    out_specs = (P(AXES, None), P(AXES, None), P(), P(row, col), P(row, col), P(col, row))
    return jax.shard_map(
        per_device, mesh=fine, in_specs=in_specs, out_specs=out_specs, check_vma=False
    )
```

time: 190 us -> 210 us (1.11)
  Pallas kernels: 0 us -> 36.9 us
  matrix products: 28.7 us -> 0 us
  local copies, waits for them, and re-layouts: 21.5 us -> 29.9 us
  other arithmetic: 9.89 us -> 12.6 us
    pallas_call x0 -> x7, Pallas kernels: none -> 36.9 us  [call(): pl.pallas_call(kernel, grid=grid, in_specs=specs, out_specs=[spec for _,...]
    dot_general x15 -> x0, matrix products: 28.7 us -> none  [the longest x3 14.9 us: product_left_t(): lax.dot_general(left, right, (((0,), (0,)), ((), ())), preferred_element_...]
    unnamed x58 -> x78, local copies, waits for them, and re-layouts: 16.1 us -> 23.6 us
    add x6 -> x3, other arithmetic: 0.89 us -> 3.53 us  [the longest x1 1.43 us: per_device(): near_keep = near_keep + send(near_give, c=1)]
    concatenate x7 -> x0, other arithmetic: 2.2 us -> none  [the longest x1 1.04 us: per_device(): normed = jnp.concatenate([near_normed, far_normed], axis=0)]
  transfers between devices with their start and end apart: 33 -> 33, of which waited for: 15 -> 13; matrix products, arithmetic and copies ran while one was open for 20% -> 1% of each run, Pallas kernels for 0% -> 15%
where the time goes in v8:
time: 210 us; the launch traced here: 208 us
  waiting for transfers between devices  73.8 us (35%)
  starting transfers between devices  53.6 us (26%)
  Pallas kernels  36.9 us (18%)
  local copies, waits for them, and re-layouts  29.9 us (14%)
  other arithmetic  12.6 us (6%)
    ppermute x31, waiting for transfers between devices, send(): return lax.ppermute(value, AXES, pairs)  65 us
    ppermute x31, starting transfers between devices, send(): return lax.ppermute(value, AXES, pairs)  40.4 us
    pallas_call x7, Pallas kernels, call(): pl.pallas_call(kernel, grid=grid, in_specs=specs, out_specs=[spec for _,...  36.9 us
    unnamed x78, local copies, waits for them, and re-layouts  23.6 us
    all_to_all x1, waiting for transfers between devices, per_device(): lax.all_to_all(message.reshape(16, 4, 2176), ('h', 'z', 'x'), split_axis=...  8.83 us
    all_to_all x1, starting transfers between devices, per_device(): lax.all_to_all(message.reshape(16, 4, 2176), ('h', 'z', 'x'), split_axis=...  7.96 us
    all_to_all x1, starting transfers between devices, per_device(): lax.all_to_all(message, ('h', 'z', 'x'), split_axis=0, concat_axis=0, til...  5.22 us
  transfers between devices with their start and end apart: 33, of which 13 were waited for; matrix products, arithmetic and copies ran while one was open for 1% of the time, Pallas kernels for 15%

profile of v8, /device:TPU:0, one launch (start us, length us, event | category | flops | bytes accessed | tf_op | source)
XLA Modules:
  0.0 208.1 jit_solution(16517817997076156771)
XLA Ops:
  4.0 8.0 %all-to-all-start = ((bf16[16,4,2176]{2,1,0:T(4,128)(2,1)}), bf16[16,4,2176]{2,1,0:T(4,128)(2,1)S(1)}, u32[]{:S(2)}, u32[]{:S(2)}) async-start(bf16[16,4,2176]{2,1,0:T(4,128)(2,1)} %bitcast.2), calls=%async_computation | async-start | bytes 557056 | tf_op jit(solution)/shard_map/all_to_all | solution.py:289
  12.0 8.8 %all-to-all-done = bf16[16,4,2176]{2,1,0:T(4,128)(2,1)S(1)} async-done(((bf16[16,4,2176]{2,1,0:T(4,128)(2,1)}), bf16[16,4,2176]{2,1,0:T(4,128)(2,1)S(1)}, u32[]{:S(2)}, u32[]{:S(2)}) %all-to-all-start) | async-done | bytes 278560 | tf_op jit(solution)/shard_map/all_to_all | solution.py:289
  21.0 1.6 collective-permute-start
  22.6 1.7 collective-permute-start.4
  24.3 2.0 collective-permute-start.5
  26.3 2.5 %collective-permute-done = bf16[32,2176]{1,0:T(8,128)(2,1)S(1)} collective-permute-done((bf16[32,2176]{1,0:T(8,128)(2,1)S(1)}, bf16[32,2176]{1,0:T(8,128)(2,1)S(1)}, u32[]{:S(2)}, u32[]{:S(2)}) %collective-permute-start) | collective-permute-done | bytes 139296 | tf_op jit(solution)/shard_map/ppermute | solution.py:28
  28.8 3.2 %collective-permute-start.2 = (bf16[32,2176]{1,0:T(8,128)(2,1)S(1)}, bf16[32,2176]{1,0:T(8,128)(2,1)S(1)}, u32[]{:S(2)}, u32[]{:S(2)}) collective-permute-start(bf16[32,2176]{1,0:T(8,128)(2,1)S(1)} %get-tuple-element.39), channel_id=1, source_target_pairs={{0,4},{1,5},{2,6},{3,7},{4,0},{5,1},{6,2},{7,3},{8,12},{9,13},{10,... | collective-permute-start | bytes 417800 | tf_op jit(solution)/shard_map/ppermute | solution.py:28
  32.0 2.0 collective-permute-start.1
  34.3 3.1 %collective-permute-done.1 = bf16[32,2176]{1,0:T(8,128)(2,1)S(1)} collective-permute-done((bf16[32,2176]{1,0:T(8,128)(2,1)S(1)}, bf16[32,2176]{1,0:T(8,128)(2,1)S(1)}, u32[]{:S(2)}, u32[]{:S(2)}) %collective-permute-start.1) | collective-permute-done | bytes 139296 | tf_op jit(solution)/shard_map/ppermute | solution.py:28
  37.5 2.0 copy-done
  39.6 2.0 copy-done.2
  41.6 2.0 copy-done.4
  43.6 5.2 %shard_map.109 = (bf16[256,1024]{1,0:T(8,128)(2,1)S(1)}, bf16[256,1024]{1,0:T(8,128)(2,1)S(1)}, f32[64,5376]{1,0:T(8,128)S(1)}, bf16[64,5376]{1,0:T(8,128)(2,1)S...) custom-call(bf16[128,2176]{1,0:T(8,128)(2,1)S(1)} %constant_dynamic-update-slice_fusion.2.core_ref.refs_7_, ...), custom_call_target="tpu_custom_call" | custom-call | flops 2818572288 | bytes 16617472 | tf_op jit(solution)/shard_map/pallas_call | solution.py:65
  51.3 3.2 %collective-permute-start.9 = (bf16[64,5376]{1,0:T(8,128)(2,1)S(1)}, bf16[64,5376]{1,0:T(8,128)(2,1)S(1)}, u32[]{:S(2)}, u32[]{:S(2)}) collective-permute-start(bf16[64,5376]{1,0:T(8,128)(2,1)S(1)} %get-tuple-element.46), channel_id=1, source_target_pairs={{0,48},{1,49},{2,50},{3,51},{4,52},{5,53},{6,54},{7,55},{8,56},{9,... | collective-permute-start | bytes 2064392 | tf_op jit(solution)/shard_map/ppermute | solution.py:28
  54.5 5.5 %shard_map.110 = (bf16[256,1024]{1,0:T(8,128)(2,1)S(1)}, bf16[256,1024]{1,0:T(8,128)(2,1)S(1)}, f32[64,5376]{1,0:T(8,128)S(1)}, f32[32,5376]{1,0:T(8,128)S(1)}, ...) custom-call(bf16[128,2176]{1,0:T(8,128)(2,1)S(1)} %constant_dynamic-, ...), custom_call_target="tpu_custom_call" | custom-call | flops 2818572288 | bytes 17993728 | tf_op jit(solution)/shard_map/pallas_call | solution.py:65
  60.1 3.2 %collective-permute-start.15 = (bf16[32,5376]{1,0:T(8,128)(2,1)S(1)}, bf16[32,5376]{1,0:T(8,128)(2,1)S(1)}, u32[]{:S(2)}, u32[]{:S(2)}) collective-permute-start(bf16[32,5376]{1,0:T(8,128)(2,1)S(1)} %get-tuple-element.52), channel_id=1, source_target_pairs={{0,48},{1,49},{2,50},{3,51},{4,52},{5,53},{6,54},{7,55},{8,56},{9,... | collective-permute-start | bytes 1032200 | tf_op jit(solution)/shard_map/ppermute | solution.py:28
  63.3 5.1 %collective-permute-done.11 = bf16[64,5376]{1,0:T(8,128)(2,1)S(1)} collective-permute-done((bf16[64,5376]{1,0:T(8,128)(2,1)S(1)}, bf16[64,5376]{1,0:T(8,128)(2,1)S(1)}, u32[]{:S(2)}, u32[]{:S(2)}) %collective-permute-start.11) | collective-permute-done | bytes 688160 | tf_op jit(solution)/shard_map/ppermute | solution.py:28
  69.1 1.6 collective-permute-done.8
  70.9 1.4 collective-permute-start.10
  72.4 11.7 %collective-permute-done.13 = bf16[32,5376]{1,0:T(8,128)(2,1)S(1)} collective-permute-done((bf16[32,5376]{1,0:T(8,128)(2,1)S(1)}, bf16[32,5376]{1,0:T(8,128)(2,1)S(1)}, u32[]{:S(2)}, u32[]{:S(2)}) %collective-permute-start.13) | collective-permute-done | bytes 344096 | tf_op jit(solution)/shard_map/ppermute | solution.py:28
  84.9 3.2 %collective-permute-start.17 = (bf16[32,5376]{1,0:T(8,128)(2,1)S(1)}, bf16[32,5376]{1,0:T(8,128)(2,1)S(1)}, u32[]{:S(2)}, u32[]{:S(2)}) collective-permute-start(bf16[32,5376]{1,0:T(8,128)(2,1)S(1)} %add_convert_fusion.1), channel_id=1, source_target_pairs={{0,48},{1,49},{2,50},{3,51},{4,52},{5,53},{6,54},{7,55},{8,56},{9,... | collective-permute-start | bytes 1032200 | tf_op jit(solution)/shard_map/ppermute | solution.py:28
  88.2 7.3 %collective-permute-done.16.top1_ref = bf16[32,5376]{1,0:T(8,128)(2,1)S(1)} collective-permute-done((bf16[32,5376]{1,0:T(8,128)(2,1)S(1)}, bf16[32,5376]{1,0:T(8,128)(2,1)S(1)}, u32[]{:S(2)}, u32[]{:S(2)}) %collective-permute-start.16) | collective-permute-done | bytes 344096 | tf_op jit(solution)/shard_map/ppermute | solution.py:28
  97.5 2.3 %collective-permute-start.18 = (bf16[64,5376]{1,0:T(8,128)(2,1)S(1)}, bf16[64,5376]{1,0:T(8,128)(2,1)S(1)}, u32[]{:S(2)}, u32[]{:S(2)}) collective-permute-start(bf16[64,5376]{1,0:T(8,128)(2,1)S(1)} %shard_map.111.refs_0_.refs_8_), channel_id=1, source_target_pairs={{0,48},{1,49},{2,50},{3,51},{4,52},{5,53},{6,54},{7,55},{8,56},{9,... | collective-permute-start | bytes 2064392 | tf_op jit(solution)/shard_map/ppermute | solution.py:28
  99.8 1.3 collective-permute-start.23
  101.1 12.5 %collective-permute-done.19.refs_3_.refs_11_ = bf16[64,5376]{1,0:T(8,128)(2,1)S(1)} collective-permute-done((bf16[64,5376]{1,0:T(8,128)(2,1)S(1)}, bf16[64,5376]{1,0:T(8,128)(2,1)S(1)}, u32[]{:S(2)}, u32[]{:S(2)}) %collective-permute-start.19) | collective-permute-done | bytes 688160 | tf_op jit(solution)/shard_map/ppermute | solution.py:28
  113.7 3.3 %collective-permute-start.21 = (bf16[32,5376]{1,0:T(8,128)(2,1)S(1)}, bf16[32,5376]{1,0:T(8,128)(2,1)S(1)}, u32[]{:S(2)}, u32[]{:S(2)}) collective-permute-start(bf16[32,5376]{1,0:T(8,128)(2,1)S(1)} %slice.125), channel_id=1, source_target_pairs={{0,48},{1,49},{2,50},{3,51},{4,52},{5,53},{6,54},{7,55},{8,56},{9,... | collective-permute-start | bytes 1032200 | tf_op jit(solution)/shard_map/ppermute | solution.py:28
  117.0 3.2 %collective-permute-start.24 = (bf16[64,5376]{1,0:T(8,128)(2,1)S(1)}, bf16[64,5376]{1,0:T(8,128)(2,1)S(1)}, u32[]{:S(2)}, u32[]{:S(2)}) collective-permute-start(bf16[64,5376]{1,0:T(8,128)(2,1)S(1)} %collective-permute-done.23.refs_0_.refs_4_.refs_12_), channel_id=1, source_target_pairs={{0,48},{1,49},{2,50},{3,51},{4,52},{5,53},{6,54},{7,55},{8,56},{9,... | collective-permute-start | bytes 2064392 | tf_op jit(solution)/shard_map/ppermute | solution.py:28
  120.3 5.6 %collective-permute-done.20 = bf16[32,5376]{1,0:T(8,128)(2,1)S(1)} collective-permute-done((bf16[32,5376]{1,0:T(8,128)(2,1)S(1)}, bf16[32,5376]{1,0:T(8,128)(2,1)S(1)}, u32[]{:S(2)}, u32[]{:S(2)}) %collective-permute-start.20) | collective-permute-done | bytes 344096 | tf_op jit(solution)/shard_map/ppermute | solution.py:28
  126.0 1.4 collective-permute-start.25
  127.4 6.4 %shard_map.112 = (f32[128,2048]{1,0:T(8,128)S(1)}, f32[128,2048]{1,0:T(8,128)}, f32[8,1024]{1,0:T(8,128)S(1)}) custom-call(bf16[64,5376]{1,0:T(8,128)(2,1)S(1)} %shard_map.111.refs_0_.refs_8_, bf16[64,5376]{1,0:T(8,128)(2,1)S(1)} %collective-permute-done.18.refs_1_.refs_9_, bf16[64,5376]{1,0:T(8,128)(2,1)S(1)} %constant_dynamic-update-slice_fusion.refs_2_.refs_10_, ...), custom_call_target="tpu_custom_call" | custom-call | flops 2818572288 | bytes 17006592 | tf_op jit(solution)/shard_map/pallas_call | solution.py:65
  133.8 3.4 %collective-permute-done.26.refs_3_.refs_7_.refs_15_ = bf16[64,5376]{1,0:T(8,128)(2,1)S(1)} collective-permute-done((bf16[64,5376]{1,0:T(8,128)(2,1)S(1)}, bf16[64,5376]{1,0:T(8,128)(2,1)S(1)}, u32[]{:S(2)}, u32[]{:S(2)}) %collective-permute-start.26) | collective-permute-done | bytes 688160 | tf_op jit(solution)/shard_map/ppermute | solution.py:28
  137.2 6.4 %shard_map.113 = (f32[128,2048]{1,0:T(8,128)S(1)}, f32[136,2048]{1,0:T(8,128)}, f32[8,1024]{1,0:T(8,128)S(1)}) custom-call(bf16[64,5376]{1,0:T(8,128)(2,1)S(1)} %collective-permute-done.23.refs_0_.refs_4_.refs_12_, bf16[64,5376]{1,0:T(8,128)(2,1)S(1)} %collective-permute-done.24.refs_1_.refs_5_.refs_13_, ...), custom_call_target="tpu_custom_call" | custom-call | flops 2818572288 | bytes 17104896 | tf_op jit(solution)/shard_map/pallas_call | solution.py:65
  144.7 1.1 copy-done.7
  145.8 1.1 copy-done.10
  146.9 1.1 copy-done.13
  151.1 5.2 %shard_map.114 = bf16[1792,1024]{1,0:T(8,128)(2,1)} custom-call(bf16[64,5376]{1,0:T(8,128)(2,1)S(1)} %shard_map.111.refs_0_.refs_8_, bf16[64,5376]{1,0:T(8,128)(2,1)S(1)} %collective-permute-done.18.refs_1_.refs_9_, bf16[64,5376]{1,0:T(8,128)(2,1)S(1)} %constant_dynamic-update-slice_fusion.refs_2_.refs_10_, ...), custom_call_target="tpu_custom_call" | custom-call | flops 1879048192 | bytes 10223616 | tf_op jit(solution)/shard_map/pallas_call | solution.py:65
  156.3 1.4 add.176
  158.6 1.3 slice_add_fusion
  160.1 2.8 %collective-permute-start.30 = (bf16[64,2176]{1,0:T(8,128)(2,1)S(1)}, bf16[64,2176]{1,0:T(8,128)(2,1)S(1)}, u32[]{:S(2)}, u32[]{:S(2)}) collective-permute-start(bf16[64,2176]{1,0:T(8,128)(2,1)S(1)} %get-tuple-element.91), channel_id=1, source_target_pairs={{0,4},{1,5},{2,6},{3,7},{4,0},{5,1},{6,2},{7,3},{8,12},{9,13},{10,... | collective-permute-start | bytes 835592 | tf_op jit(solution)/shard_map/ppermute | solution.py:28
  162.9 2.0 collective-permute-start.29
  165.7 5.5 %collective-permute-done.30 = bf16[64,2176]{1,0:T(8,128)(2,1)S(1)} collective-permute-done((bf16[64,2176]{1,0:T(8,128)(2,1)S(1)}, bf16[64,2176]{1,0:T(8,128)(2,1)S(1)}, u32[]{:S(2)}, u32[]{:S(2)}) %collective-permute-start.30) | collective-permute-done | bytes 278560 | tf_op jit(solution)/shard_map/ppermute | solution.py:28
  171.2 5.9 %collective-permute-done.29 = bf16[64,2176]{1,0:T(8,128)(2,1)S(1)} collective-permute-done((bf16[64,2176]{1,0:T(8,128)(2,1)S(1)}, bf16[64,2176]{1,0:T(8,128)(2,1)S(1)}, u32[]{:S(2)}, u32[]{:S(2)}) %collective-permute-start.29) | collective-permute-done | bytes 278560 | tf_op jit(solution)/shard_map/ppermute | solution.py:28
  177.9 1.3 fusion.3
  179.9 1.8 maximum_select_fusion
  181.7 1.8 reshape.130
  183.5 1.8 pad_maximum_fusion
  185.3 5.2 %all-to-all-start.1 = ((bf16[16,4,2560]{2,1,0:T(4,128)(2,1)}), bf16[16,4,2560]{2,1,0:T(4,128)(2,1)}, u32[]{:S(2)}, u32[]{:S(2)}) async-start(bf16[16,4,2560]{2,1,0:T(4,128)(2,1)} %pad_maximum_fusion), calls=%async_computation.1 | async-start | bytes 655360 | tf_op jit(solution)/shard_map/all_to_all | solution.py:348
  196.0 7.2 %shard_map.115 = (bf16[1024,1792]{1,0:T(8,128)(2,1)}, bf16[1024,1792]{1,0:T(8,128)(2,1)}) custom-call(bf16[64,5376]{1,0:T(8,128)(2,1)S(1)} %shard_map.111.refs_0_.refs_8_, bf16[64,5376]{1,0:T(8,128)(2,1)S(1)} %collective-permute-done.18.refs_1_.refs_9_, bf16[64,5376]{1,0:T(8,128)(2,1)S(1)} %constant_dynamic-update-slice_fusion.refs_2_.refs_10_, ...), custom_call_target="tpu_custom_call" | custom-call | flops 3758096384 | bytes 19398656 | tf_op jit(solution)/shard_map/pallas_call | solution.py:65
  (166 shorter events, 27.8 us)
Async XLA Ops:
  3.2 19.4 %copy-start.35 = (f32[8192]{0:T(1024)S(1)}, f32[8192]{0:T(1024)}, u32[]{:S(2)}) copy-start(f32[8192]{0:T(1024)} %param.7) | copy-start | bytes 98308
  4.0 16.8 %all-to-all-start = ((bf16[16,4,2176]{2,1,0:T(4,128)(2,1)}), bf16[16,4,2176]{2,1,0:T(4,128)(2,1)S(1)}, u32[]{:S(2)}, u32[]{:S(2)}) async-start(bf16[16,4,2176]{2,1,0:T(4,128)(2,1)} %bitcast.2), calls=%async_computation | async-start | bytes 557056 | tf_op jit(solution)/shard_map/all_to_all | solution.py:289
  21.0 7.8 %collective-permute-start = (bf16[32,2176]{1,0:T(8,128)(2,1)S(1)}, bf16[32,2176]{1,0:T(8,128)(2,1)S(1)}, u32[]{:S(2)}, u32[]{:S(2)}) collective-permute-start(bf16[32,2176]{1,0:T(8,128)(2,1)S(1)} %get-tuple-element.75), channel_id=1, source_target_pairs={{0,2},{1,3},{2,4},{3,5},{4,6},{5,7},{6,0},{7,1},{8,10},{9,11},{10,... | collective-permute-start | bytes 417800 | tf_op jit(solution)/shard_map/ppermute | solution.py:28
  22.6 11.5 %collective-permute-start.4 = (bf16[32,2176]{1,0:T(8,128)(2,1)S(1)}, bf16[32,2176]{1,0:T(8,128)(2,1)S(1)}, u32[]{:S(2)}, u32[]{:S(2)}) collective-permute-start(bf16[32,2176]{1,0:T(8,128)(2,1)S(1)} %get-tuple-element.75), channel_id=1, source_target_pairs={{0,6},{1,7},{2,0},{3,1},{4,2},{5,3},{6,4},{7,5},{8,14},{9,15},{10,... | collective-permute-start | bytes 417800 | tf_op jit(solution)/shard_map/ppermute | solution.py:28
  24.3 9.8 %collective-permute-start.5 = (bf16[32,2176]{1,0:T(8,128)(2,1)S(1)}, bf16[32,2176]{1,0:T(8,128)(2,1)S(1)}, u32[]{:S(2)}, u32[]{:S(2)}) collective-permute-start(bf16[32,2176]{1,0:T(8,128)(2,1)S(1)} %get-tuple-element.75), channel_id=1, source_target_pairs={{0,4},{1,5},{2,6},{3,7},{4,0},{5,1},{6,2},{7,3},{8,12},{9,13},{10,... | collective-permute-start | bytes 417800 | tf_op jit(solution)/shard_map/ppermute | solution.py:28
  28.8 8.7 %collective-permute-start.3 = (bf16[32,2176]{1,0:T(8,128)(2,1)S(1)}, bf16[32,2176]{1,0:T(8,128)(2,1)S(1)}, u32[]{:S(2)}, u32[]{:S(2)}) collective-permute-start(bf16[32,2176]{1,0:T(8,128)(2,1)S(1)} %get-tuple-element.39), channel_id=1, source_target_pairs={{0,2},{1,3},{2,4},{3,5},{4,6},{5,7},{6,0},{7,1},{8,10},{9,11},{10,... | collective-permute-start | bytes 417800 | tf_op jit(solution)/shard_map/ppermute | solution.py:28
  28.8 8.6 %collective-permute-start.2 = (bf16[32,2176]{1,0:T(8,128)(2,1)S(1)}, bf16[32,2176]{1,0:T(8,128)(2,1)S(1)}, u32[]{:S(2)}, u32[]{:S(2)}) collective-permute-start(bf16[32,2176]{1,0:T(8,128)(2,1)S(1)} %get-tuple-element.39), channel_id=1, source_target_pairs={{0,4},{1,5},{2,6},{3,7},{4,0},{5,1},{6,2},{7,3},{8,12},{9,13},{10,... | collective-permute-start | bytes 417800 | tf_op jit(solution)/shard_map/ppermute | solution.py:28
  32.0 5.4 %collective-permute-start.1 = (bf16[32,2176]{1,0:T(8,128)(2,1)S(1)}, bf16[32,2176]{1,0:T(8,128)(2,1)S(1)}, u32[]{:S(2)}, u32[]{:S(2)}) collective-permute-start(bf16[32,2176]{1,0:T(8,128)(2,1)S(1)} %get-tuple-element.39), channel_id=1, source_target_pairs={{0,6},{1,7},{2,0},{3,1},{4,2},{5,3},{6,4},{7,5},{8,14},{9,15},{10,... | collective-permute-start | bytes 417800 | tf_op jit(solution)/shard_map/ppermute | solution.py:28
  34.2 3.3 %collective-permute-start.6 = (bf16[128,2176]{1,0:T(8,128)(2,1)S(1)}, bf16[128,2176]{1,0:T(8,128)(2,1)S(1)}, u32[]{:S(2)}, u32[]{:S(2)}) collective-permute-start(bf16[128,2176]{1,0:T(8,128)(2,1)S(1)} %constant_dynamic-update-slice_fusion.2.core_ref.refs_7_), channel_id=1, source_target_pairs={{0,1},{1,0},{2,3},{3,2},{4,5},{5,4},{6,7},{7,6},{8,9},{9,8},{10,11... | collective-permute-start | bytes 1671176 | tf_op jit(solution)/shard_map/ppermute | solution.py:28
  43.6 10.9 %copy-start.1 = (bf16[1024,1792]{1,0:T(8,128)(2,1)S(1)}, bf16[1024,1792]{1,0:T(8,128)(2,1)}, u32[]{:S(2)}) copy-start(bf16[1024,1792]{1,0:T(8,128)(2,1)} %refs_4_.3) | copy-start | bytes 11010052
  50.6 3.9 %collective-permute-start.7 = (bf16[128,2176]{1,0:T(8,128)(2,1)S(1)}, bf16[128,2176]{1,0:T(8,128)(2,1)S(1)}, u32[]{:S(2)}, u32[]{:S(2)}) collective-permute-start(bf16[128,2176]{1,0:T(8,128)(2,1)S(1)} %constant_dynamic-update-slice_fusion.6.core_ref.refs_7_), channel_id=1, source_target_pairs={{0,1},{1,0},{2,3},{3,2},{4,5},{5,4},{6,7},{7,6},{8,9},{9,8},{10,11... | collective-permute-start | bytes 1671176 | tf_op jit(solution)/shard_map/ppermute | solution.py:28
  50.6 17.8 %collective-permute-start.11 = (bf16[64,5376]{1,0:T(8,128)(2,1)S(1)}, bf16[64,5376]{1,0:T(8,128)(2,1)S(1)}, u32[]{:S(2)}, u32[]{:S(2)}) collective-permute-start(bf16[64,5376]{1,0:T(8,128)(2,1)S(1)} %get-tuple-element.49), channel_id=1, source_target_pairs={{0,64},{1,65},{2,66},{3,67},{4,68},{5,69},{6,70},{7,71},{8,72},{9,... | collective-permute-start | bytes 2064392 | tf_op jit(solution)/shard_map/ppermute | solution.py:28
  51.3 19.5 %collective-permute-start.8 = (bf16[64,5376]{1,0:T(8,128)(2,1)S(1)}, bf16[64,5376]{1,0:T(8,128)(2,1)S(1)}, u32[]{:S(2)}, u32[]{:S(2)}) collective-permute-start(bf16[64,5376]{1,0:T(8,128)(2,1)S(1)} %get-tuple-element.45), channel_id=1, source_target_pairs={{0,16},{1,17},{2,18},{3,19},{4,20},{5,21},{6,22},{7,23},{8,24},{9,... | collective-permute-start | bytes 2064392 | tf_op jit(solution)/shard_map/ppermute | solution.py:28
  51.3 19.5 %collective-permute-start.9 = (bf16[64,5376]{1,0:T(8,128)(2,1)S(1)}, bf16[64,5376]{1,0:T(8,128)(2,1)S(1)}, u32[]{:S(2)}, u32[]{:S(2)}) collective-permute-start(bf16[64,5376]{1,0:T(8,128)(2,1)S(1)} %get-tuple-element.46), channel_id=1, source_target_pairs={{0,48},{1,49},{2,50},{3,51},{4,52},{5,53},{6,54},{7,55},{8,56},{9,... | collective-permute-start | bytes 2064392 | tf_op jit(solution)/shard_map/ppermute | solution.py:28
  60.0 8.6 %copy-start.24 = (bf16[256,1024]{1,0:T(8,128)(2,1)}, bf16[256,1024]{1,0:T(8,128)(2,1)S(1)}, u32[]{:S(2)}) copy-start(bf16[256,1024]{1,0:T(8,128)(2,1)S(1)} %get-tuple-element.62.refs_8_) | copy-start | bytes 1572868
  60.0 8.6 %copy-start.28 = (bf16[256,1024]{1,0:T(8,128)(2,1)}, bf16[256,1024]{1,0:T(8,128)(2,1)S(1)}, u32[]{:S(2)}) copy-start(bf16[256,1024]{1,0:T(8,128)(2,1)S(1)} %get-tuple-element.67.refs_16_) | copy-start | bytes 1572868
  60.0 24.8 %collective-permute-start.14 = (bf16[32,5376]{1,0:T(8,128)(2,1)S(1)}, bf16[32,5376]{1,0:T(8,128)(2,1)S(1)}, u32[]{:S(2)}, u32[]{:S(2)}) collective-permute-start(bf16[32,5376]{1,0:T(8,128)(2,1)S(1)} %get-tuple-element.51), channel_id=1, source_target_pairs={{0,16},{1,17},{2,18},{3,19},{4,20},{5,21},{6,22},{7,23},{8,24},{9,... | collective-permute-start | bytes 1032200 | tf_op jit(solution)/shard_map/ppermute | solution.py:28
  60.1 24.7 %collective-permute-start.15 = (bf16[32,5376]{1,0:T(8,128)(2,1)S(1)}, bf16[32,5376]{1,0:T(8,128)(2,1)S(1)}, u32[]{:S(2)}, u32[]{:S(2)}) collective-permute-start(bf16[32,5376]{1,0:T(8,128)(2,1)S(1)} %get-tuple-element.52), channel_id=1, source_target_pairs={{0,48},{1,49},{2,50},{3,51},{4,52},{5,53},{6,54},{7,55},{8,56},{9,... | collective-permute-start | bytes 1032200 | tf_op jit(solution)/shard_map/ppermute | solution.py:28
  68.7 15.4 %collective-permute-start.13 = (bf16[32,5376]{1,0:T(8,128)(2,1)S(1)}, bf16[32,5376]{1,0:T(8,128)(2,1)S(1)}, u32[]{:S(2)}, u32[]{:S(2)}) collective-permute-start(bf16[32,5376]{1,0:T(8,128)(2,1)S(1)} %get-tuple-element.78), channel_id=1, source_target_pairs={{0,48},{1,49},{2,50},{3,51},{4,52},{5,53},{6,54},{7,55},{8,56},{9,... | collective-permute-start | bytes 1032200 | tf_op jit(solution)/shard_map/ppermute | solution.py:28
  70.9 17.2 %collective-permute-start.10 = (bf16[64,5376]{1,0:T(8,128)(2,1)S(1)}, bf16[64,5376]{1,0:T(8,128)(2,1)S(1)}, u32[]{:S(2)}, u32[]{:S(2)}) collective-permute-start(bf16[64,5376]{1,0:T(8,128)(2,1)S(1)} %add_convert_fusion), channel_id=1, source_target_pairs={{0,64},{1,65},{2,66},{3,67},{4,68},{5,69},{6,70},{7,71},{8,72},{9,... | collective-permute-start | bytes 2064392 | tf_op jit(solution)/shard_map/ppermute | solution.py:28
  72.4 12.4 %collective-permute-start.12 = (bf16[32,5376]{1,0:T(8,128)(2,1)S(1)}, bf16[32,5376]{1,0:T(8,128)(2,1)S(1)}, u32[]{:S(2)}, u32[]{:S(2)}) collective-permute-start(bf16[32,5376]{1,0:T(8,128)(2,1)S(1)} %get-tuple-element.79), channel_id=1, source_target_pairs={{0,16},{1,17},{2,18},{3,19},{4,20},{5,21},{6,22},{7,23},{8,24},{9,... | collective-permute-start | bytes 1032200 | tf_op jit(solution)/shard_map/ppermute | solution.py:28
  84.9 10.7 %collective-permute-start.16 = (bf16[32,5376]{1,0:T(8,128)(2,1)S(1)}, bf16[32,5376]{1,0:T(8,128)(2,1)S(1)}, u32[]{:S(2)}, u32[]{:S(2)}) collective-permute-start(bf16[32,5376]{1,0:T(8,128)(2,1)S(1)} %add_convert_fusion.2), channel_id=1, source_target_pairs={{0,16},{1,17},{2,18},{3,19},{4,20},{5,21},{6,22},{7,23},{8,24},{9,... | collective-permute-start | bytes 1032200 | tf_op jit(solution)/shard_map/ppermute | solution.py:28
  84.9 10.6 %collective-permute-start.17 = (bf16[32,5376]{1,0:T(8,128)(2,1)S(1)}, bf16[32,5376]{1,0:T(8,128)(2,1)S(1)}, u32[]{:S(2)}, u32[]{:S(2)}) collective-permute-start(bf16[32,5376]{1,0:T(8,128)(2,1)S(1)} %add_convert_fusion.1), channel_id=1, source_target_pairs={{0,48},{1,49},{2,50},{3,51},{4,52},{5,53},{6,54},{7,55},{8,56},{9,... | collective-permute-start | bytes 1032200 | tf_op jit(solution)/shard_map/ppermute | solution.py:28
  95.5 31.9 %copy-start.3 = (bf16[1024,1792]{1,0:T(8,128)(2,1)S(1)}, bf16[1024,1792]{1,0:T(8,128)(2,1)}, u32[]{:S(2)}) copy-start(bf16[1024,1792]{1,0:T(8,128)(2,1)} %refs_5_.3) | copy-start | bytes 11010052
  96.5 17.1 %collective-permute-start.19 = (bf16[64,5376]{1,0:T(8,128)(2,1)S(1)}, bf16[64,5376]{1,0:T(8,128)(2,1)S(1)}, u32[]{:S(2)}, u32[]{:S(2)}) collective-permute-start(bf16[64,5376]{1,0:T(8,128)(2,1)S(1)} %shard_map.111.refs_0_.refs_8_), channel_id=1, source_target_pairs={{0,16},{1,17},{2,18},{3,19},{4,20},{5,21},{6,22},{7,23},{8,24},{9,... | collective-permute-start | bytes 2064392 | tf_op jit(solution)/shard_map/ppermute | solution.py:28
  97.5 16.2 %collective-permute-start.18 = (bf16[64,5376]{1,0:T(8,128)(2,1)S(1)}, bf16[64,5376]{1,0:T(8,128)(2,1)S(1)}, u32[]{:S(2)}, u32[]{:S(2)}) collective-permute-start(bf16[64,5376]{1,0:T(8,128)(2,1)S(1)} %shard_map.111.refs_0_.refs_8_), channel_id=1, source_target_pairs={{0,48},{1,49},{2,50},{3,51},{4,52},{5,53},{6,54},{7,55},{8,56},{9,... | collective-permute-start | bytes 2064392 | tf_op jit(solution)/shard_map/ppermute | solution.py:28
  99.8 17.2 %collective-permute-start.23 = (bf16[64,5376]{1,0:T(8,128)(2,1)S(1)}, bf16[64,5376]{1,0:T(8,128)(2,1)S(1)}, u32[]{:S(2)}, u32[]{:S(2)}) collective-permute-start(bf16[64,5376]{1,0:T(8,128)(2,1)S(1)} %shard_map.111.refs_0_.refs_8_), channel_id=1, source_target_pairs={{0,64},{1,65},{2,66},{3,67},{4,68},{5,69},{6,70},{7,71},{8,72},{9,... | collective-permute-start | bytes 2064392 | tf_op jit(solution)/shard_map/ppermute | solution.py:28
  113.6 12.3 %collective-permute-start.20 = (bf16[32,5376]{1,0:T(8,128)(2,1)S(1)}, bf16[32,5376]{1,0:T(8,128)(2,1)S(1)}, u32[]{:S(2)}, u32[]{:S(2)}) collective-permute-start(bf16[32,5376]{1,0:T(8,128)(2,1)S(1)} %slice.124), channel_id=1, source_target_pairs={{0,16},{1,17},{2,18},{3,19},{4,20},{5,21},{6,22},{7,23},{8,24},{9,... | collective-permute-start | bytes 1032200 | tf_op jit(solution)/shard_map/ppermute | solution.py:28
  113.7 12.2 %collective-permute-start.21 = (bf16[32,5376]{1,0:T(8,128)(2,1)S(1)}, bf16[32,5376]{1,0:T(8,128)(2,1)S(1)}, u32[]{:S(2)}, u32[]{:S(2)}) collective-permute-start(bf16[32,5376]{1,0:T(8,128)(2,1)S(1)} %slice.125), channel_id=1, source_target_pairs={{0,48},{1,49},{2,50},{3,51},{4,52},{5,53},{6,54},{7,55},{8,56},{9,... | collective-permute-start | bytes 1032200 | tf_op jit(solution)/shard_map/ppermute | solution.py:28
  117.0 20.2 %copy-start.6 = (bf16[64,5376]{1,0:T(8,128)(2,1)}, bf16[64,5376]{1,0:T(8,128)(2,1)S(1)}, u32[]{:S(2)}) copy-start(bf16[64,5376]{1,0:T(8,128)(2,1)S(1)} %collective-permute-done.23.refs_0_.refs_4_.refs_12_) | copy-start | bytes 2064388
  117.0 20.1 %collective-permute-start.26 = (bf16[64,5376]{1,0:T(8,128)(2,1)S(1)}, bf16[64,5376]{1,0:T(8,128)(2,1)S(1)}, u32[]{:S(2)}, u32[]{:S(2)}) collective-permute-start(bf16[64,5376]{1,0:T(8,128)(2,1)S(1)} %collective-permute-done.23.refs_0_.refs_4_.refs_12_), channel_id=1, source_target_pairs={{0,16},{1,17},{2,18},{3,19},{4,20},{5,21},{6,22},{7,23},{8,24},{9,... | collective-permute-start | bytes 2064392 | tf_op jit(solution)/shard_map/ppermute | solution.py:28
  117.0 20.1 %collective-permute-start.24 = (bf16[64,5376]{1,0:T(8,128)(2,1)S(1)}, bf16[64,5376]{1,0:T(8,128)(2,1)S(1)}, u32[]{:S(2)}, u32[]{:S(2)}) collective-permute-start(bf16[64,5376]{1,0:T(8,128)(2,1)S(1)} %collective-permute-done.23.refs_0_.refs_4_.refs_12_), channel_id=1, source_target_pairs={{0,48},{1,49},{2,50},{3,51},{4,52},{5,53},{6,54},{7,55},{8,56},{9,... | collective-permute-start | bytes 2064392 | tf_op jit(solution)/shard_map/ppermute | solution.py:28
  126.0 11.2 %collective-permute-start.25 = (bf16[64,5376]{1,0:T(8,128)(2,1)S(1)}, bf16[64,5376]{1,0:T(8,128)(2,1)S(1)}, u32[]{:S(2)}, u32[]{:S(2)}) collective-permute-start(bf16[64,5376]{1,0:T(8,128)(2,1)S(1)} %constant_dynamic-update-slice_fusion.refs_2_.refs_10_), channel_id=1, source_target_pairs={{0,64},{1,65},{2,66},{3,67},{4,68},{5,69},{6,70},{7,71},{8,72},{9,... | collective-permute-start | bytes 2064392 | tf_op jit(solution)/shard_map/ppermute | solution.py:28
  127.4 9.8 %copy-start.5 = (bf16[1792,1024]{1,0:T(8,128)(2,1)S(1)}, bf16[1792,1024]{1,0:T(8,128)(2,1)}, u32[]{:S(2)}) copy-start(bf16[1792,1024]{1,0:T(8,128)(2,1)} %refs_6_.3) | copy-start | bytes 11010052
  133.8 9.9 %copy-start.18 = (f32[128,2048]{1,0:T(8,128)}, f32[128,2048]{1,0:T(8,128)S(1)}, u32[]{:S(2)}) copy-start(f32[128,2048]{1,0:T(8,128)S(1)} %get-tuple-element.57) | copy-start | bytes 3145732
  133.8 22.6 %collective-permute-start.22 = (f32[128,2048]{1,0:T(8,128)}, f32[128,2048]{1,0:T(8,128)}, u32[]{:S(2)}, u32[]{:S(2)}) collective-permute-start(f32[128,2048]{1,0:T(8,128)} %get-tuple-element.58), channel_id=1, source_target_pairs={{0,1},{1,0},{2,3},{3,2},{4,5},{5,4},{6,7},{7,6},{8,9},{9,8},{10,11... | collective-permute-start | bytes 3145736 | tf_op jit(solution)/shard_map/ppermute | solution.py:28
  137.2 6.5 %copy-start.9 = (bf16[64,5376]{1,0:T(8,128)(2,1)}, bf16[64,5376]{1,0:T(8,128)(2,1)S(1)}, u32[]{:S(2)}) copy-start(bf16[64,5376]{1,0:T(8,128)(2,1)S(1)} %collective-permute-done.26.refs_3_.refs_7_.refs_15_) | copy-start | bytes 2064388
  137.2 6.5 %copy-start.12 = (bf16[64,5376]{1,0:T(8,128)(2,1)}, bf16[64,5376]{1,0:T(8,128)(2,1)S(1)}, u32[]{:S(2)}) copy-start(bf16[64,5376]{1,0:T(8,128)(2,1)S(1)} %collective-permute-done.24.refs_1_.refs_5_.refs_13_) | copy-start | bytes 2064388
  137.2 6.5 %copy-start.15 = (bf16[64,5376]{1,0:T(8,128)(2,1)}, bf16[64,5376]{1,0:T(8,128)(2,1)S(1)}, u32[]{:S(2)}) copy-start(bf16[64,5376]{1,0:T(8,128)(2,1)S(1)} %collective-permute-done.25.refs_2_.refs_6_.refs_14_) | copy-start | bytes 2064388
  144.7 13.2 %collective-permute-start.27 = (f32[136,2048]{1,0:T(8,128)}, f32[136,2048]{1,0:T(8,128)}, u32[]{:S(2)}, u32[]{:S(2)}) collective-permute-start(f32[136,2048]{1,0:T(8,128)} %get-tuple-element.61), channel_id=1, source_target_pairs={{0,1},{1,0},{2,3},{3,2},{4,5},{5,4},{6,7},{7,6},{8,9},{9,8},{10,11... | collective-permute-start | bytes 3342344 | tf_op jit(solution)/shard_map/ppermute | solution.py:28
  151.1 5.2 %copy-start.19 = (f32[128,2048]{1,0:T(8,128)S(1)}, f32[128,2048]{1,0:T(8,128)}, u32[]{:S(2)}) copy-start(f32[128,2048]{1,0:T(8,128)} %copy-done.18) | copy-start | bytes 3145732
  156.3 2.3 %copy-start.21 = (f32[128,2048]{1,0:T(8,128)S(1)}, f32[128,2048]{1,0:T(8,128)}, u32[]{:S(2)}) copy-start(f32[128,2048]{1,0:T(8,128)} %copy-done.20) | copy-start | bytes 3145732
  160.1 11.1 %collective-permute-start.30 = (bf16[64,2176]{1,0:T(8,128)(2,1)S(1)}, bf16[64,2176]{1,0:T(8,128)(2,1)S(1)}, u32[]{:S(2)}, u32[]{:S(2)}) collective-permute-start(bf16[64,2176]{1,0:T(8,128)(2,1)S(1)} %get-tuple-element.91), channel_id=1, source_target_pairs={{0,4},{1,5},{2,6},{3,7},{4,0},{5,1},{6,2},{7,3},{8,12},{9,13},{10,... | collective-permute-start | bytes 835592 | tf_op jit(solution)/shard_map/ppermute | solution.py:28
  162.9 14.2 %collective-permute-start.29 = (bf16[64,2176]{1,0:T(8,128)(2,1)S(1)}, bf16[64,2176]{1,0:T(8,128)(2,1)S(1)}, u32[]{:S(2)}, u32[]{:S(2)}) collective-permute-start(bf16[64,2176]{1,0:T(8,128)(2,1)S(1)} %get-tuple-element.92), channel_id=1, source_target_pairs={{0,6},{1,7},{2,0},{3,1},{4,2},{5,3},{6,4},{7,5},{8,14},{9,15},{10,... | collective-permute-start | bytes 835592 | tf_op jit(solution)/shard_map/ppermute | solution.py:28
  164.9 12.1 %collective-permute-start.28 = (bf16[64,2176]{1,0:T(8,128)(2,1)S(1)}, bf16[64,2176]{1,0:T(8,128)(2,1)S(1)}, u32[]{:S(2)}, u32[]{:S(2)}) collective-permute-start(bf16[64,2176]{1,0:T(8,128)(2,1)S(1)} %get-tuple-element.93), channel_id=1, source_target_pairs={{0,2},{1,3},{2,4},{3,5},{4,6},{5,7},{6,0},{7,1},{8,10},{9,11},{10,... | collective-permute-start | bytes 835592 | tf_op jit(solution)/shard_map/ppermute | solution.py:28
  171.2 5.9 %copy-start.32 = (bf16[64,2176]{1,0:T(8,128)(2,1)}, bf16[64,2176]{1,0:T(8,128)(2,1)S(1)}, u32[]{:S(2)}) copy-start(bf16[64,2176]{1,0:T(8,128)(2,1)S(1)} %collective-permute-done.30) | copy-start | bytes 835588
  179.9 10.6 %copy-start.27 = (bf16[256,1024]{1,0:T(8,128)(2,1)S(1)}, bf16[256,1024]{1,0:T(8,128)(2,1)}, u32[]{:S(2)}) copy-start(bf16[256,1024]{1,0:T(8,128)(2,1)} %copy-done.26) | copy-start | bytes 1572868
  185.3 17.9 %all-to-all-start.1 = ((bf16[16,4,2560]{2,1,0:T(4,128)(2,1)}), bf16[16,4,2560]{2,1,0:T(4,128)(2,1)}, u32[]{:S(2)}, u32[]{:S(2)}) async-start(bf16[16,4,2560]{2,1,0:T(4,128)(2,1)} %pad_maximum_fusion), calls=%async_computation.1 | async-start | bytes 655360 | tf_op jit(solution)/shard_map/all_to_all | solution.py:348
  (21 other events, 25.1 us)

commit v9 on v7

--- a/solution.py
+++ b/solution.py
@@ -61,21 +61,22 @@
 
 
 def both_cores(core):
-    both = (core, send(core, c=1))
-    return jnp.concatenate([v[i * 32 : i * 32 + 32] for i in range(XS) for v in both], axis=0)
+    return jnp.concatenate([core, send(core, c=1)], axis=0)
+
+
+def by_core(blocks):
+    return jnp.concatenate([b[:32] for b in blocks] + [b[32:] for b in blocks], axis=0)
 
 
 def sum_over_core(partial, gain_partial):
-    n = partial.shape[1]
-    split = [partial[i * 32 : i * 32 + 32] for i in range(2 * XS)]
-    give = split[1::2]
+    give = partial[128:]
     if gain_partial is not None:
-        give = give + [jnp.pad(gain_partial, ((0, 0), (0, n - 128)))]
-    taken = send(jnp.concatenate(give, axis=0), c=1)
-    keep = jnp.concatenate(split[::2], axis=0) + taken[:128]
+        gain_rows = jnp.pad(gain_partial, ((0, 0), (0, partial.shape[1] - 128)))
+        give = jnp.concatenate([give, gain_rows], axis=0)
+    taken = send(give, c=1)
     if gain_partial is not None:
         gain_partial = gain_partial + taken[128:, :128]
-    return keep, gain_partial
+    return partial[:128] + taken[:128], gain_partial
 
 
 def sum_over_y(near, far, gain, x):
@@ -99,23 +100,23 @@
     return total, (gains[0] + gains[2]) + (gains[1] + gains[3])
 
 
-def sum_over_row(near, far):
-    m12 = send(far[2].astype(BF16), z=1).astype(F32)
-    m11 = send(far[1].astype(BF16), x=1).astype(F32)
-    m13 = send(far[3].astype(BF16), x=3).astype(F32)
-    h = near[0].shape[0] // 2
-    first1 = send(near[1][h:].astype(BF16), x=1)
-    first2 = send(near[3][:h].astype(BF16), x=3)
-    a02 = near[2] + m12
-    n1 = send(a02[:h].astype(BF16), x=1).astype(F32)
-    n2 = send(a02[h:].astype(BF16), x=3).astype(F32)
-    q = send((far[0] + m11 + m13).astype(BF16), z=1).astype(F32)
-    last1 = (near[1][:h] + n1).astype(BF16)
-    last2 = (near[3][h:] + n2).astype(BF16)
+def sum_over_row(far, near):
+    own, to1, to2, to3 = far
+    near0, near1_top, near1_bottom, near2, near3_top, near3_bottom = near
+    m12 = send(to2, z=1).astype(F32)
+    m11 = send(to1, x=1).astype(F32)
+    m13 = send(to3, x=3).astype(F32)
+    first1 = send(near1_bottom, x=1)
+    first2 = send(near3_top, x=3)
+    n1 = send((near2[:32] + m12[:32]).astype(BF16), x=1).astype(F32)
+    n2 = send((near2[32:] + m12[32:]).astype(BF16), x=3).astype(F32)
+    q = send((own + m11 + m13).astype(BF16), z=1)
+    last1 = (near1_top + n1).astype(BF16)
+    last2 = (near3_bottom + n2).astype(BF16)
     last1, last2, first1, first2 = lax.optimization_barrier((last1, last2, first1, first2))
-    r1 = jnp.concatenate([send(last1, x=1), first1], axis=0).astype(F32)
-    r2 = jnp.concatenate([first2, send(last2, x=3)], axis=0).astype(F32)
-    return near[0] + q + r1 + r2
+    one = jnp.concatenate([send(last1, x=1), first1], axis=0).astype(F32)
+    two = jnp.concatenate([first2, send(last2, x=3)], axis=0).astype(F32)
+    return near0 + q.astype(F32) + one + two
 
 
 def gather_over_row(own):
@@ -129,10 +130,7 @@
     pb = send(p, x=3)
     across = jnp.concatenate([a2, b2], axis=0)
     p2 = send(across, z=1)
-    return (
-        jnp.concatenate([own, b, across, a], axis=0),
-        jnp.concatenate([p, pb, p2, pa], axis=0),
-    )
+    return [own, b, across, a], [p, pb, p2, pa]
 
 
 def per_device(inputs, rms_gain_vector, gate_weight, up_weight, down_weight, out_grad):
@@ -168,14 +166,20 @@
         return estimate, (estimate * gain_block).astype(BF16), tokens[:, 1024:2048]
 
     def partials(normed, grad):
-        return jnp.concatenate(
-            [
-                product(normed, gate_weight),
-                product(normed, up_weight),
-                product_right_t(grad, down_weight),
-            ],
-            axis=1,
-        ).reshape(4, 64, 3 * width)
+        sums = [
+            product(normed, gate_weight),
+            product(normed, up_weight),
+            product_right_t(grad, down_weight),
+        ]
+
+        def block(dx, dtype, cores=(0, 1)):
+            rows = [
+                jnp.concatenate([value[c * 128 + dx * 32 :][:32] for value in sums], axis=1)
+                for c in cores
+            ]
+            return jnp.concatenate(rows, axis=0).astype(dtype)
+
+        return block
 
     far_core, first = gather_half(lax.dynamic_slice(block, ((1 - z) * 32, 0), (32, 2176)), x)
     near_block, _ = lax.optimization_barrier(
@@ -184,10 +188,19 @@
     near_core, _ = gather_half(near_block, x)
     far_estimate, far_normed, far_grad = normed_of(both_cores(far_core))
     far = partials(far_normed, far_grad)
-    near_core, far_own = lax.optimization_barrier((near_core, far[0]))
+    far = [far(0, F32), far(1, BF16), far(2, BF16), far(3, BF16)]
+    near_core, far[0] = lax.optimization_barrier((near_core, far[0]))
     near_estimate, near_normed, near_grad = normed_of(both_cores(near_core))
     near = partials(near_normed, near_grad)
-    sums = sum_over_row(near, [far_own, far[1], far[2], far[3]])
+    near = [
+        near(0, F32),
+        near(1, F32, (0,)),
+        near(1, BF16, (1,)),
+        near(2, F32),
+        near(3, BF16, (0,)),
+        near(3, F32, (1,)),
+    ]
+    sums = sum_over_row(far, near)
     gate, up, hidden_grad = sums[:, :width], sums[:, width : 2 * width], sums[:, 2 * width :]
     sigma = jax.nn.sigmoid(gate)
     silu = gate * sigma
@@ -199,31 +212,38 @@
         ],
         axis=1,
     )
-    units = gather_over_row(units)
+    near_units, far_units = gather_over_row(units)
+    near_units = by_core(lax.optimization_barrier(near_units))
+    far_units = by_core(lax.optimization_barrier(far_units))
 
     def backward(units):
         hidden, gate_grad, up_grad = units[:, :width], units[:, width : 2 * width], units[:, 2 * width :]
         grad = product_right_t(gate_grad, gate_weight) + product_right_t(up_grad, up_weight)
         return jnp.concatenate([product(hidden, down_weight), grad], axis=1)
 
-    near_partial = backward(units[0])
+    near_partial = backward(near_units)
     near_keep, _ = sum_over_core(near_partial, None)
-    far_partial = backward(units[1])
+    far_partial = backward(far_units)
     gain_partial = jnp.sum(near_partial[:, 1024:] * near_estimate, axis=0) + jnp.sum(
         far_partial[:, 1024:] * far_estimate, axis=0
     )
     far_keep, gain = sum_over_core(far_partial, gain_partial.reshape(8, 128))
 
-    units = jnp.concatenate(units, axis=0)
-    hidden, gate_grad, up_grad = units[:, :width], units[:, width : 2 * width], units[:, 2 * width :]
-    normed = jnp.concatenate([near_normed, far_normed], axis=0)
+    *late, far_keep = lax.optimization_barrier((near_units, far_units, far_keep))
+
+    def of_all(part):
+        return jnp.concatenate(
+            [unit[:, part * width : (part + 1) * width] for unit in late], axis=0
+        )
+
     grad_full = jnp.concatenate([near_grad, far_grad], axis=0)
-    down_weight_grad = product_left_t(hidden, grad_full).astype(BF16)
-    far_keep, down_weight_grad = lax.optimization_barrier((far_keep, down_weight_grad))
+    down_weight_grad = product_left_t(of_all(0), grad_full).astype(BF16)
     total, gain = sum_over_y(near_keep, far_keep, gain, x)
-    normed, total = lax.optimization_barrier((normed, total))
-    gate_weight_grad = product_left_t(normed, gate_grad).astype(BF16)
-    up_weight_grad = product_left_t(normed, up_grad).astype(BF16)
+    normed, total, down_weight_grad = lax.optimization_barrier(
+        (jnp.concatenate([near_normed, far_normed], axis=0), total, down_weight_grad)
+    )
+    gate_weight_grad = product_left_t(normed, of_all(1)).astype(BF16)
+    up_weight_grad = product_left_t(normed, of_all(2)).astype(BF16)
 
     gain_parts = [p.reshape(4, 256) for p in parts_of(gain, 2)]
     gain_rows = jnp.broadcast_to(jnp.concatenate(gain_parts, axis=1)[None], (16, 4, 512))

time: 190 us -> 179 us (0.942)
  local copies, waits for them, and re-layouts: 21.5 us -> 11.1 us
  other arithmetic: 9.89 us -> 12.2 us
  matrix products: 28.7 us -> 26.7 us
  waiting for transfers between devices: 74.2 us -> 72.3 us
    unnamed x58 -> x57, local copies, waits for them, and re-layouts: 16.1 us -> 4.46 us
    slice x5 -> x14, local copies, waits for them, and re-layouts: 0.23 us -> 3.49 us  [the longest x2 2.92 us: of_all(): unit[:, part * width:(part + 1) * width]]
    add x3, other arithmetic: 0.51 us -> 3.43 us  [the longest x2 3.16 us: sum_over_core(): return (partial[:128] + taken[:128], gain_partial)]
    ppermute x31, starting transfers between devices: 38.5 us -> 40.8 us  [send(): return lax.ppermute(value, AXES, pairs)]
    ppermute x31, waiting for transfers between devices: 65.4 us -> 63.5 us  [send(): return lax.ppermute(value, AXES, pairs)]
  transfers between devices with their start and end apart: 33 -> 33, of which waited for: 15 -> 14; matrix products, arithmetic and copies ran while one was open for 20% -> 18% of each run, Pallas kernels for 0% -> 0%
where the time goes in v9:
time: 179 us; the launch traced here: 178 us
  waiting for transfers between devices  72.3 us (40%)
  starting transfers between devices  53.5 us (30%)
  matrix products  26.7 us (15%)
  other arithmetic  12.2 us (7%)
  local copies, waits for them, and re-layouts  11.1 us (6%)
    ppermute x31, waiting for transfers between devices, send(): return lax.ppermute(value, AXES, pairs)  63.5 us
    ppermute x31, starting transfers between devices, send(): return lax.ppermute(value, AXES, pairs)  40.8 us
    dot_general x3, matrix products, product_left_t(): lax.dot_general(left, right, (((0,), (0,)), ((), ())), preferred_element_...  13.2 us
    all_to_all x1, waiting for transfers between devices, per_device(): lax.all_to_all(message.reshape(16, 4, 2176), ('h', 'z', 'x'), split_axis=...  8.83 us
    all_to_all x1, starting transfers between devices, per_device(): lax.all_to_all(message.reshape(16, 4, 2176), ('h', 'z', 'x'), split_axis=...  7.96 us
    dot_general x6, matrix products, product_right_t(): lax.dot_general(left, right, (((1,), (1,)), ((), ())), preferred_element_...  6.9 us
    dot_general x6, matrix products, product(): return jnp.dot(left, right, preferred_element_type=F32)  6.66 us
    all_to_all x1, starting transfers between devices, per_device(): lax.all_to_all(message, ('h', 'z', 'x'), split_axis=0, concat_axis=0, til...  4.7 us
  transfers between devices with their start and end apart: 33, of which 14 were waited for; matrix products, arithmetic and copies ran while one was open for 18% of the time, Pallas kernels for 0%

profile of v9, /device:TPU:0, one launch (start us, length us, event | category | flops | bytes accessed | tf_op | source)
XLA Modules:
  0.0 177.5 jit_solution(3099223107802756262)
XLA Ops:
  4.0 8.0 %all-to-all-start = ((bf16[16,4,2176]{2,1,0:T(4,128)(2,1)}), bf16[16,4,2176]{2,1,0:T(4,128)(2,1)S(1)}, u32[]{:S(2)}, u32[]{:S(2)}) async-start(bf16[16,4,2176]{2,1,0:T(4,128)(2,1)} %bitcast.2), calls=%async_computation | async-start | bytes 557056 | tf_op jit(solution)/shard_map/all_to_all | solution.py:153
  12.0 8.8 %all-to-all-done = bf16[16,4,2176]{2,1,0:T(4,128)(2,1)S(1)} async-done(((bf16[16,4,2176]{2,1,0:T(4,128)(2,1)}), bf16[16,4,2176]{2,1,0:T(4,128)(2,1)S(1)}, u32[]{:S(2)}, u32[]{:S(2)}) %all-to-all-start) | async-done | bytes 278560 | tf_op jit(solution)/shard_map/all_to_all | solution.py:153
  21.0 1.6 collective-permute-start
  22.6 1.7 collective-permute-start.4
  24.3 2.0 %collective-permute-start.5 = (bf16[32,2176]{1,0:T(8,128)(2,1)S(1)}, bf16[32,2176]{1,0:T(8,128)(2,1)S(1)}, u32[]{:S(2)}, u32[]{:S(2)}) collective-permute-start(bf16[32,2176]{1,0:T(8,128)(2,1)S(1)} %get-tuple-element.51), channel_id=1, source_target_pairs={{0,4},{1,5},{2,6},{3,7},{4,0},{5,1},{6,2},{7,3},{8,12},{9,13},{10,... | collective-permute-start | bytes 417800 | tf_op jit(solution)/shard_map/ppermute | solution.py:24
  26.3 2.5 %collective-permute-done = bf16[32,2176]{1,0:T(8,128)(2,1)S(1)} collective-permute-done((bf16[32,2176]{1,0:T(8,128)(2,1)S(1)}, bf16[32,2176]{1,0:T(8,128)(2,1)S(1)}, u32[]{:S(2)}, u32[]{:S(2)}) %collective-permute-start) | collective-permute-done | bytes 139296 | tf_op jit(solution)/shard_map/ppermute | solution.py:24
  28.8 3.2 %collective-permute-start.2 = (bf16[32,2176]{1,0:T(8,128)(2,1)S(1)}, bf16[32,2176]{1,0:T(8,128)(2,1)S(1)}, u32[]{:S(2)}, u32[]{:S(2)}) collective-permute-start(bf16[32,2176]{1,0:T(8,128)(2,1)S(1)} %get-tuple-element.27), channel_id=1, source_target_pairs={{0,4},{1,5},{2,6},{3,7},{4,0},{5,1},{6,2},{7,3},{8,12},{9,13},{10,... | collective-permute-start | bytes 417800 | tf_op jit(solution)/shard_map/ppermute | solution.py:24
  32.0 2.0 %collective-permute-start.1 = (bf16[32,2176]{1,0:T(8,128)(2,1)S(1)}, bf16[32,2176]{1,0:T(8,128)(2,1)S(1)}, u32[]{:S(2)}, u32[]{:S(2)}) collective-permute-start(bf16[32,2176]{1,0:T(8,128)(2,1)S(1)} %get-tuple-element.27), channel_id=1, source_target_pairs={{0,6},{1,7},{2,0},{3,1},{4,2},{5,3},{6,4},{7,5},{8,14},{9,15},{10,... | collective-permute-start | bytes 417800 | tf_op jit(solution)/shard_map/ppermute | solution.py:24
  34.3 3.1 %collective-permute-done.1 = bf16[32,2176]{1,0:T(8,128)(2,1)S(1)} collective-permute-done((bf16[32,2176]{1,0:T(8,128)(2,1)S(1)}, bf16[32,2176]{1,0:T(8,128)(2,1)S(1)}, u32[]{:S(2)}, u32[]{:S(2)}) %collective-permute-start.1) | collective-permute-done | bytes 139296 | tf_op jit(solution)/shard_map/ppermute | solution.py:24
  37.6 1.2 fusion.76
  39.2 1.6 copy-done
  44.8 3.0 %collective-permute-start.9 = (bf16[64,5376]{1,0:T(8,128)(2,1)S(1)}, bf16[64,5376]{1,0:T(8,128)(2,1)S(1)}, u32[]{:S(2)}, u32[]{:S(2)}) collective-permute-start(bf16[64,5376]{1,0:T(8,128)(2,1)S(1)} %maximum_maximum_fusion.2), channel_id=1, source_target_pairs={{0,48},{1,49},{2,50},{3,51},{4,52},{5,53},{6,54},{7,55},{8,56},{9,... | collective-permute-start | bytes 2064392 | tf_op jit(solution)/shard_map/ppermute | solution.py:24
  49.3 1.1 fusion.81
  50.4 1.1 fusion.80
  51.5 1.2 fusion.79
  53.1 3.3 %collective-permute-start.15 = (bf16[32,5376]{1,0:T(8,128)(2,1)S(1)}, bf16[32,5376]{1,0:T(8,128)(2,1)S(1)}, u32[]{:S(2)}, u32[]{:S(2)}) collective-permute-start(bf16[32,5376]{1,0:T(8,128)(2,1)S(1)} %pad_maximum_fusion.6), channel_id=1, source_target_pairs={{0,48},{1,49},{2,50},{3,51},{4,52},{5,53},{6,54},{7,55},{8,56},{9,... | collective-permute-start | bytes 1032200 | tf_op jit(solution)/shard_map/ppermute | solution.py:24
  56.5 8.9 %collective-permute-done.11 = bf16[64,5376]{1,0:T(8,128)(2,1)S(1)} collective-permute-done((bf16[64,5376]{1,0:T(8,128)(2,1)S(1)}, bf16[64,5376]{1,0:T(8,128)(2,1)S(1)}, u32[]{:S(2)}, u32[]{:S(2)}) %collective-permute-start.11) | collective-permute-done | bytes 688160 | tf_op jit(solution)/shard_map/ppermute | solution.py:24
  67.0 1.7 collective-permute-start.12
  68.7 8.9 %collective-permute-done.13 = bf16[32,5376]{1,0:T(8,128)(2,1)S(1)} collective-permute-done((bf16[32,5376]{1,0:T(8,128)(2,1)S(1)}, bf16[32,5376]{1,0:T(8,128)(2,1)S(1)}, u32[]{:S(2)}, u32[]{:S(2)}) %collective-permute-start.13) | collective-permute-done | bytes 344096 | tf_op jit(solution)/shard_map/ppermute | solution.py:24
  78.4 3.2 %collective-permute-start.17 = (bf16[32,5376]{1,0:T(8,128)(2,1)S(1)}, bf16[32,5376]{1,0:T(8,128)(2,1)S(1)}, u32[]{:S(2)}, u32[]{:S(2)}) collective-permute-start(bf16[32,5376]{1,0:T(8,128)(2,1)S(1)} %fusion.31), channel_id=1, source_target_pairs={{0,48},{1,49},{2,50},{3,51},{4,52},{5,53},{6,54},{7,55},{8,56},{9,... | collective-permute-start | bytes 1032200 | tf_op jit(solution)/shard_map/ppermute | solution.py:24
  81.6 1.2 collective-permute-done.10
  82.8 6.4 %collective-permute-done.16 = bf16[32,5376]{1,0:T(8,128)(2,1)S(1)} collective-permute-done((bf16[32,5376]{1,0:T(8,128)(2,1)S(1)}, bf16[32,5376]{1,0:T(8,128)(2,1)S(1)}, u32[]{:S(2)}, u32[]{:S(2)}) %collective-permute-start.16) | collective-permute-done | bytes 344096 | tf_op jit(solution)/shard_map/ppermute | solution.py:24
  89.7 1.2 collective-permute-start.19
  90.9 2.1 %collective-permute-start.18 = (bf16[64,5376]{1,0:T(8,128)(2,1)S(1)}, bf16[64,5376]{1,0:T(8,128)(2,1)S(1)}, u32[]{:S(2)}, u32[]{:S(2)}) collective-permute-start(bf16[64,5376]{1,0:T(8,128)(2,1)S(1)} %pad_maximum_fusion.3), channel_id=1, source_target_pairs={{0,48},{1,49},{2,50},{3,51},{4,52},{5,53},{6,54},{7,55},{8,56},{9,... | collective-permute-start | bytes 2064392 | tf_op jit(solution)/shard_map/ppermute | solution.py:24
  93.7 13.3 %collective-permute-done.19 = bf16[64,5376]{1,0:T(8,128)(2,1)S(1)} collective-permute-done((bf16[64,5376]{1,0:T(8,128)(2,1)S(1)}, bf16[64,5376]{1,0:T(8,128)(2,1)S(1)}, u32[]{:S(2)}, u32[]{:S(2)}) %collective-permute-start.19) | collective-permute-done | bytes 688160 | tf_op jit(solution)/shard_map/ppermute | solution.py:24
  107.2 3.3 %collective-permute-start.21 = (bf16[32,5376]{1,0:T(8,128)(2,1)S(1)}, bf16[32,5376]{1,0:T(8,128)(2,1)S(1)}, u32[]{:S(2)}, u32[]{:S(2)}) collective-permute-start(bf16[32,5376]{1,0:T(8,128)(2,1)S(1)} %slice.645), channel_id=1, source_target_pairs={{0,48},{1,49},{2,50},{3,51},{4,52},{5,53},{6,54},{7,55},{8,56},{9,... | collective-permute-start | bytes 1032200 | tf_op jit(solution)/shard_map/ppermute | solution.py:24
  110.5 3.2 %collective-permute-start.24 = (bf16[64,5376]{1,0:T(8,128)(2,1)S(1)}, bf16[64,5376]{1,0:T(8,128)(2,1)S(1)}, u32[]{:S(2)}, u32[]{:S(2)}) collective-permute-start(bf16[64,5376]{1,0:T(8,128)(2,1)S(1)} %collective-permute-done.23), channel_id=1, source_target_pairs={{0,48},{1,49},{2,50},{3,51},{4,52},{5,53},{6,54},{7,55},{8,56},{9,... | collective-permute-start | bytes 2064392 | tf_op jit(solution)/shard_map/ppermute | solution.py:24
  113.7 5.6 %collective-permute-done.20 = bf16[32,5376]{1,0:T(8,128)(2,1)S(1)} collective-permute-done((bf16[32,5376]{1,0:T(8,128)(2,1)S(1)}, bf16[32,5376]{1,0:T(8,128)(2,1)S(1)}, u32[]{:S(2)}, u32[]{:S(2)}) %collective-permute-start.20) | collective-permute-done | bytes 344096 | tf_op jit(solution)/shard_map/ppermute | solution.py:24
  120.6 1.1 fusion.26
  121.8 1.1 fusion.24
  122.9 1.2 multiply_reduce_fusion.1
  124.1 1.2 pad_maximum_fusion.1
  125.3 5.5 %collective-permute-done.26 = bf16[64,5376]{1,0:T(8,128)(2,1)S(1)} collective-permute-done((bf16[64,5376]{1,0:T(8,128)(2,1)S(1)}, bf16[64,5376]{1,0:T(8,128)(2,1)S(1)}, u32[]{:S(2)}, u32[]{:S(2)}) %collective-permute-start.26) | collective-permute-done | bytes 688160 | tf_op jit(solution)/shard_map/ppermute | solution.py:24
  131.1 1.1 fusion.19
  132.2 1.2 multiply_reduce_fusion
  133.4 1.1 fusion.21
  134.6 1.2 select_maximum_fusion
  136.0 1.8 %fusion.14 = f32[128,2048]{1,0:T(8,128)S(1)} fusion(f32[128,2048]{1,0:T(8,128)} %collective-permute-done.22, f32[256,1024]{1,0:T(8,128)} %copy-done.3, f32[256,1024]{1,0:T(8,128)} %copy-done.4), kind=kLoop, calls=%fused_computation.37 | loop fusion | flops 524288 | bytes 4194304 | tf_op jit(solution)/shard_map/add | solution.py:79
  139.0 1.4 fusion.12
  140.5 1.4 fusion.60
  142.7 2.7 %collective-permute-start.30 = (bf16[64,2176]{1,0:T(8,128)(2,1)S(1)}, bf16[64,2176]{1,0:T(8,128)(2,1)S(1)}, u32[]{:S(2)}, u32[]{:S(2)}) collective-permute-start(bf16[64,2176]{1,0:T(8,128)(2,1)S(1)} %get-tuple-element.126), channel_id=1, source_target_pairs={{0,4},{1,5},{2,6},{3,7},{4,0},{5,1},{6,2},{7,3},{8,12},{9,13},{10,... | collective-permute-start | bytes 835592 | tf_op jit(solution)/shard_map/ppermute | solution.py:24
  145.4 2.1 %collective-permute-start.29 = (bf16[64,2176]{1,0:T(8,128)(2,1)S(1)}, bf16[64,2176]{1,0:T(8,128)(2,1)S(1)}, u32[]{:S(2)}, u32[]{:S(2)}) collective-permute-start(bf16[64,2176]{1,0:T(8,128)(2,1)S(1)} %get-tuple-element.127), channel_id=1, source_target_pairs={{0,6},{1,7},{2,0},{3,1},{4,2},{5,3},{6,4},{7,5},{8,14},{9,15},{10,... | collective-permute-start | bytes 835592 | tf_op jit(solution)/shard_map/ppermute | solution.py:24
  147.5 1.5 fusion.61
  148.9 3.9 %convolution_convert_fusion.2 = bf16[1792,1024]{1,0:T(8,128)(2,1)} fusion(bf16[256,1792]{1,0:T(8,128)(2,1)S(1)} %get-tuple-element.59, bf16[256,1792]{1,0:T(8,128)(2,1)S(1)} %get-tuple-element.56, bf16[256,1024]{1,0:T(8,128)(2,1)S(1)} %pad_maximum_fusion.4, bf16[256,1024]{1,0:T(8,128)(2,1)S(1)} %slice.598), kind=kOutput, calls=%fused_computation.2 | convolution fusion | flops 1886650368 | bytes 6553600 | tf_op jit(solution)/shard_map/dot_general | solution.py:36
  153.8 5.6 %collective-permute-done.29 = bf16[64,2176]{1,0:T(8,128)(2,1)S(1)} collective-permute-done((bf16[64,2176]{1,0:T(8,128)(2,1)S(1)}, bf16[64,2176]{1,0:T(8,128)(2,1)S(1)}, u32[]{:S(2)}, u32[]{:S(2)}) %collective-permute-start.29) | collective-permute-done | bytes 278560 | tf_op jit(solution)/shard_map/ppermute | solution.py:24
  160.7 4.7 %all-to-all-start.1 = ((bf16[16,4,2560]{2,1,0:T(4,128)(2,1)}), bf16[16,4,2560]{2,1,0:T(4,128)(2,1)S(1)}, u32[]{:S(2)}, u32[]{:S(2)}) async-start(bf16[16,4,2560]{2,1,0:T(4,128)(2,1)} %pad_maximum_fusion.7), calls=%async_computation.1 | async-start | bytes 655360 | tf_op jit(solution)/shard_map/all_to_all | solution.py:253
  165.4 5.3 %convolution_convert_fusion = bf16[1024,1792]{1,0:T(8,128)(2,1)} fusion(bf16[512,1024]{1,0:T(8,128)(2,1)S(1)} %pad_maximum_fusion.2, bf16[256,1792]{1,0:T(8,128)(2,1)} %get-tuple-element.57, bf16[256,1792]{1,0:T(8,128)(2,1)S(1)} %copy-done.15), kind=kOutput, calls=%fused_computation | convolution fusion | flops 1884553216 | bytes 6553600 | tf_op jit(solution)/shard_map/dot_general | solution.py:36
  170.7 4.0 %convolution_convert_fusion.1 = bf16[1024,1792]{1,0:T(8,128)(2,1)} fusion(bf16[512,1024]{1,0:T(8,128)(2,1)S(1)} %pad_maximum_fusion.2, bf16[256,1792]{1,0:T(8,128)(2,1)S(1)} %copy-done.16, bf16[256,1792]{1,0:T(8,128)(2,1)S(1)} %copy-done.14), kind=kOutput, calls=%fused_computation.1 | convolution fusion | flops 1884553216 | bytes 6553600 | tf_op jit(solution)/shard_map/dot_general | solution.py:36
  (188 shorter events, 22.6 us)
Async XLA Ops:
  2.1 20.5 %copy-start.17 = (f32[8192]{0:T(1024)S(1)}, f32[8192]{0:T(1024)}, u32[]{:S(2)}) copy-start(f32[8192]{0:T(1024)} %param.7) | copy-start | bytes 98308
  4.0 16.8 %all-to-all-start = ((bf16[16,4,2176]{2,1,0:T(4,128)(2,1)}), bf16[16,4,2176]{2,1,0:T(4,128)(2,1)S(1)}, u32[]{:S(2)}, u32[]{:S(2)}) async-start(bf16[16,4,2176]{2,1,0:T(4,128)(2,1)} %bitcast.2), calls=%async_computation | async-start | bytes 557056 | tf_op jit(solution)/shard_map/all_to_all | solution.py:153
  21.0 7.8 %collective-permute-start = (bf16[32,2176]{1,0:T(8,128)(2,1)S(1)}, bf16[32,2176]{1,0:T(8,128)(2,1)S(1)}, u32[]{:S(2)}, u32[]{:S(2)}) collective-permute-start(bf16[32,2176]{1,0:T(8,128)(2,1)S(1)} %get-tuple-element.51), channel_id=1, source_target_pairs={{0,2},{1,3},{2,4},{3,5},{4,6},{5,7},{6,0},{7,1},{8,10},{9,11},{10,... | collective-permute-start | bytes 417800 | tf_op jit(solution)/shard_map/ppermute | solution.py:24
  22.6 11.5 %collective-permute-start.4 = (bf16[32,2176]{1,0:T(8,128)(2,1)S(1)}, bf16[32,2176]{1,0:T(8,128)(2,1)S(1)}, u32[]{:S(2)}, u32[]{:S(2)}) collective-permute-start(bf16[32,2176]{1,0:T(8,128)(2,1)S(1)} %get-tuple-element.51), channel_id=1, source_target_pairs={{0,6},{1,7},{2,0},{3,1},{4,2},{5,3},{6,4},{7,5},{8,14},{9,15},{10,... | collective-permute-start | bytes 417800 | tf_op jit(solution)/shard_map/ppermute | solution.py:24
  24.3 9.8 %collective-permute-start.5 = (bf16[32,2176]{1,0:T(8,128)(2,1)S(1)}, bf16[32,2176]{1,0:T(8,128)(2,1)S(1)}, u32[]{:S(2)}, u32[]{:S(2)}) collective-permute-start(bf16[32,2176]{1,0:T(8,128)(2,1)S(1)} %get-tuple-element.51), channel_id=1, source_target_pairs={{0,4},{1,5},{2,6},{3,7},{4,0},{5,1},{6,2},{7,3},{8,12},{9,13},{10,... | collective-permute-start | bytes 417800 | tf_op jit(solution)/shard_map/ppermute | solution.py:24
  28.8 8.7 %collective-permute-start.3 = (bf16[32,2176]{1,0:T(8,128)(2,1)S(1)}, bf16[32,2176]{1,0:T(8,128)(2,1)S(1)}, u32[]{:S(2)}, u32[]{:S(2)}) collective-permute-start(bf16[32,2176]{1,0:T(8,128)(2,1)S(1)} %get-tuple-element.27), channel_id=1, source_target_pairs={{0,2},{1,3},{2,4},{3,5},{4,6},{5,7},{6,0},{7,1},{8,10},{9,11},{10,... | collective-permute-start | bytes 417800 | tf_op jit(solution)/shard_map/ppermute | solution.py:24
  28.8 8.6 %collective-permute-start.2 = (bf16[32,2176]{1,0:T(8,128)(2,1)S(1)}, bf16[32,2176]{1,0:T(8,128)(2,1)S(1)}, u32[]{:S(2)}, u32[]{:S(2)}) collective-permute-start(bf16[32,2176]{1,0:T(8,128)(2,1)S(1)} %get-tuple-element.27), channel_id=1, source_target_pairs={{0,4},{1,5},{2,6},{3,7},{4,0},{5,1},{6,2},{7,3},{8,12},{9,13},{10,... | collective-permute-start | bytes 417800 | tf_op jit(solution)/shard_map/ppermute | solution.py:24
  32.0 5.4 %collective-permute-start.1 = (bf16[32,2176]{1,0:T(8,128)(2,1)S(1)}, bf16[32,2176]{1,0:T(8,128)(2,1)S(1)}, u32[]{:S(2)}, u32[]{:S(2)}) collective-permute-start(bf16[32,2176]{1,0:T(8,128)(2,1)S(1)} %get-tuple-element.27), channel_id=1, source_target_pairs={{0,6},{1,7},{2,0},{3,1},{4,2},{5,3},{6,4},{7,5},{8,14},{9,15},{10,... | collective-permute-start | bytes 417800 | tf_op jit(solution)/shard_map/ppermute | solution.py:24
  34.0 3.6 %copy-start.2 = (bf16[1792,1024]{1,0:T(8,128)(2,1)S(1)}, bf16[1792,1024]{1,0:T(8,128)(2,1)}, u32[]{:S(2)}) copy-start(bf16[1792,1024]{1,0:T(8,128)(2,1)} %param.10) | copy-start | bytes 11010052
  34.2 3.3 %collective-permute-start.6 = (bf16[128,2176]{1,0:T(8,128)(2,1)S(1)}, bf16[128,2176]{1,0:T(8,128)(2,1)S(1)}, u32[]{:S(2)}, u32[]{:S(2)}) collective-permute-start(bf16[128,2176]{1,0:T(8,128)(2,1)S(1)} %constant_dynamic-update-slice_fusion.4), channel_id=1, source_target_pairs={{0,1},{1,0},{2,3},{3,2},{4,5},{5,4},{6,7},{7,6},{8,9},{9,8},{10,11... | collective-permute-start | bytes 1671176 | tf_op jit(solution)/shard_map/ppermute | solution.py:24
  38.8 2.0 %copy-start = (bf16[1024,1792]{1,0:T(8,128)(2,1)S(1)}, bf16[1024,1792]{1,0:T(8,128)(2,1)}, u32[]{:S(2)}) copy-start(bf16[1024,1792]{1,0:T(8,128)(2,1)} %param.8) | copy-start | bytes 11010052
  40.8 2.0 %copy-start.1 = (bf16[1024,1792]{1,0:T(8,128)(2,1)S(1)}, bf16[1024,1792]{1,0:T(8,128)(2,1)}, u32[]{:S(2)}) copy-start(bf16[1024,1792]{1,0:T(8,128)(2,1)} %param.9) | copy-start | bytes 11010052
  44.2 4.6 %collective-permute-start.7 = (bf16[128,2176]{1,0:T(8,128)(2,1)S(1)}, bf16[128,2176]{1,0:T(8,128)(2,1)S(1)}, u32[]{:S(2)}, u32[]{:S(2)}) collective-permute-start(bf16[128,2176]{1,0:T(8,128)(2,1)S(1)} %constant_dynamic-update-slice_fusion.8), channel_id=1, source_target_pairs={{0,1},{1,0},{2,3},{3,2},{4,5},{5,4},{6,7},{7,6},{8,9},{9,8},{10,11... | collective-permute-start | bytes 1671176 | tf_op jit(solution)/shard_map/ppermute | solution.py:24
  44.3 21.6 %collective-permute-start.8 = (bf16[64,5376]{1,0:T(8,128)(2,1)S(1)}, bf16[64,5376]{1,0:T(8,128)(2,1)S(1)}, u32[]{:S(2)}, u32[]{:S(2)}) collective-permute-start(bf16[64,5376]{1,0:T(8,128)(2,1)S(1)} %maximum_maximum_fusion.1), channel_id=1, source_target_pairs={{0,16},{1,17},{2,18},{3,19},{4,20},{5,21},{6,22},{7,23},{8,24},{9,... | collective-permute-start | bytes 2064392 | tf_op jit(solution)/shard_map/ppermute | solution.py:24
  44.8 21.2 %collective-permute-start.9 = (bf16[64,5376]{1,0:T(8,128)(2,1)S(1)}, bf16[64,5376]{1,0:T(8,128)(2,1)S(1)}, u32[]{:S(2)}, u32[]{:S(2)}) collective-permute-start(bf16[64,5376]{1,0:T(8,128)(2,1)S(1)} %maximum_maximum_fusion.2), channel_id=1, source_target_pairs={{0,48},{1,49},{2,50},{3,51},{4,52},{5,53},{6,54},{7,55},{8,56},{9,... | collective-permute-start | bytes 2064392 | tf_op jit(solution)/shard_map/ppermute | solution.py:24
  47.8 17.5 %collective-permute-start.11 = (bf16[64,5376]{1,0:T(8,128)(2,1)S(1)}, bf16[64,5376]{1,0:T(8,128)(2,1)S(1)}, u32[]{:S(2)}, u32[]{:S(2)}) collective-permute-start(bf16[64,5376]{1,0:T(8,128)(2,1)S(1)} %maximum_maximum_fusion.3), channel_id=1, source_target_pairs={{0,64},{1,65},{2,66},{3,67},{4,68},{5,69},{6,70},{7,71},{8,72},{9,... | collective-permute-start | bytes 2064392 | tf_op jit(solution)/shard_map/ppermute | solution.py:24
  53.0 25.3 %collective-permute-start.14 = (bf16[32,5376]{1,0:T(8,128)(2,1)S(1)}, bf16[32,5376]{1,0:T(8,128)(2,1)S(1)}, u32[]{:S(2)}, u32[]{:S(2)}) collective-permute-start(bf16[32,5376]{1,0:T(8,128)(2,1)S(1)} %pad_maximum_fusion.5), channel_id=1, source_target_pairs={{0,16},{1,17},{2,18},{3,19},{4,20},{5,21},{6,22},{7,23},{8,24},{9,... | collective-permute-start | bytes 1032200 | tf_op jit(solution)/shard_map/ppermute | solution.py:24
  53.1 25.2 %collective-permute-start.15 = (bf16[32,5376]{1,0:T(8,128)(2,1)S(1)}, bf16[32,5376]{1,0:T(8,128)(2,1)S(1)}, u32[]{:S(2)}, u32[]{:S(2)}) collective-permute-start(bf16[32,5376]{1,0:T(8,128)(2,1)S(1)} %pad_maximum_fusion.6), channel_id=1, source_target_pairs={{0,48},{1,49},{2,50},{3,51},{4,52},{5,53},{6,54},{7,55},{8,56},{9,... | collective-permute-start | bytes 1032200 | tf_op jit(solution)/shard_map/ppermute | solution.py:24
  65.6 12.0 %collective-permute-start.13 = (bf16[32,5376]{1,0:T(8,128)(2,1)S(1)}, bf16[32,5376]{1,0:T(8,128)(2,1)S(1)}, u32[]{:S(2)}, u32[]{:S(2)}) collective-permute-start(bf16[32,5376]{1,0:T(8,128)(2,1)S(1)} %get-tuple-element.87), channel_id=1, source_target_pairs={{0,48},{1,49},{2,50},{3,51},{4,52},{5,53},{6,54},{7,55},{8,56},{9,... | collective-permute-start | bytes 1032200 | tf_op jit(solution)/shard_map/ppermute | solution.py:24
  66.2 16.5 %collective-permute-start.10 = (bf16[64,5376]{1,0:T(8,128)(2,1)S(1)}, bf16[64,5376]{1,0:T(8,128)(2,1)S(1)}, u32[]{:S(2)}, u32[]{:S(2)}) collective-permute-start(bf16[64,5376]{1,0:T(8,128)(2,1)S(1)} %add_convert_fusion), channel_id=1, source_target_pairs={{0,64},{1,65},{2,66},{3,67},{4,68},{5,69},{6,70},{7,71},{8,72},{9,... | collective-permute-start | bytes 2064392 | tf_op jit(solution)/shard_map/ppermute | solution.py:24
  67.0 11.2 %collective-permute-start.12 = (bf16[32,5376]{1,0:T(8,128)(2,1)S(1)}, bf16[32,5376]{1,0:T(8,128)(2,1)S(1)}, u32[]{:S(2)}, u32[]{:S(2)}) collective-permute-start(bf16[32,5376]{1,0:T(8,128)(2,1)S(1)} %get-tuple-element.88), channel_id=1, source_target_pairs={{0,16},{1,17},{2,18},{3,19},{4,20},{5,21},{6,22},{7,23},{8,24},{9,... | collective-permute-start | bytes 1032200 | tf_op jit(solution)/shard_map/ppermute | solution.py:24
  78.3 10.8 %collective-permute-start.16 = (bf16[32,5376]{1,0:T(8,128)(2,1)S(1)}, bf16[32,5376]{1,0:T(8,128)(2,1)S(1)}, u32[]{:S(2)}, u32[]{:S(2)}) collective-permute-start(bf16[32,5376]{1,0:T(8,128)(2,1)S(1)} %fusion.30), channel_id=1, source_target_pairs={{0,16},{1,17},{2,18},{3,19},{4,20},{5,21},{6,22},{7,23},{8,24},{9,... | collective-permute-start | bytes 1032200 | tf_op jit(solution)/shard_map/ppermute | solution.py:24
  78.4 10.8 %collective-permute-start.17 = (bf16[32,5376]{1,0:T(8,128)(2,1)S(1)}, bf16[32,5376]{1,0:T(8,128)(2,1)S(1)}, u32[]{:S(2)}, u32[]{:S(2)}) collective-permute-start(bf16[32,5376]{1,0:T(8,128)(2,1)S(1)} %fusion.31), channel_id=1, source_target_pairs={{0,48},{1,49},{2,50},{3,51},{4,52},{5,53},{6,54},{7,55},{8,56},{9,... | collective-permute-start | bytes 1032200 | tf_op jit(solution)/shard_map/ppermute | solution.py:24
  89.7 17.3 %collective-permute-start.19 = (bf16[64,5376]{1,0:T(8,128)(2,1)S(1)}, bf16[64,5376]{1,0:T(8,128)(2,1)S(1)}, u32[]{:S(2)}, u32[]{:S(2)}) collective-permute-start(bf16[64,5376]{1,0:T(8,128)(2,1)S(1)} %pad_maximum_fusion.3), channel_id=1, source_target_pairs={{0,16},{1,17},{2,18},{3,19},{4,20},{5,21},{6,22},{7,23},{8,24},{9,... | collective-permute-start | bytes 2064392 | tf_op jit(solution)/shard_map/ppermute | solution.py:24
  90.9 16.2 %collective-permute-start.18 = (bf16[64,5376]{1,0:T(8,128)(2,1)S(1)}, bf16[64,5376]{1,0:T(8,128)(2,1)S(1)}, u32[]{:S(2)}, u32[]{:S(2)}) collective-permute-start(bf16[64,5376]{1,0:T(8,128)(2,1)S(1)} %pad_maximum_fusion.3), channel_id=1, source_target_pairs={{0,48},{1,49},{2,50},{3,51},{4,52},{5,53},{6,54},{7,55},{8,56},{9,... | collective-permute-start | bytes 2064392 | tf_op jit(solution)/shard_map/ppermute | solution.py:24
  93.0 17.4 %collective-permute-start.23 = (bf16[64,5376]{1,0:T(8,128)(2,1)S(1)}, bf16[64,5376]{1,0:T(8,128)(2,1)S(1)}, u32[]{:S(2)}, u32[]{:S(2)}) collective-permute-start(bf16[64,5376]{1,0:T(8,128)(2,1)S(1)} %pad_maximum_fusion.3), channel_id=1, source_target_pairs={{0,64},{1,65},{2,66},{3,67},{4,68},{5,69},{6,70},{7,71},{8,72},{9,... | collective-permute-start | bytes 2064392 | tf_op jit(solution)/shard_map/ppermute | solution.py:24
  107.0 12.3 %collective-permute-start.20 = (bf16[32,5376]{1,0:T(8,128)(2,1)S(1)}, bf16[32,5376]{1,0:T(8,128)(2,1)S(1)}, u32[]{:S(2)}, u32[]{:S(2)}) collective-permute-start(bf16[32,5376]{1,0:T(8,128)(2,1)S(1)} %slice.644), channel_id=1, source_target_pairs={{0,16},{1,17},{2,18},{3,19},{4,20},{5,21},{6,22},{7,23},{8,24},{9,... | collective-permute-start | bytes 1032200 | tf_op jit(solution)/shard_map/ppermute | solution.py:24
  107.2 12.2 %collective-permute-start.21 = (bf16[32,5376]{1,0:T(8,128)(2,1)S(1)}, bf16[32,5376]{1,0:T(8,128)(2,1)S(1)}, u32[]{:S(2)}, u32[]{:S(2)}) collective-permute-start(bf16[32,5376]{1,0:T(8,128)(2,1)S(1)} %slice.645), channel_id=1, source_target_pairs={{0,48},{1,49},{2,50},{3,51},{4,52},{5,53},{6,54},{7,55},{8,56},{9,... | collective-permute-start | bytes 1032200 | tf_op jit(solution)/shard_map/ppermute | solution.py:24
  110.4 20.3 %collective-permute-start.26 = (bf16[64,5376]{1,0:T(8,128)(2,1)S(1)}, bf16[64,5376]{1,0:T(8,128)(2,1)S(1)}, u32[]{:S(2)}, u32[]{:S(2)}) collective-permute-start(bf16[64,5376]{1,0:T(8,128)(2,1)S(1)} %collective-permute-done.23), channel_id=1, source_target_pairs={{0,16},{1,17},{2,18},{3,19},{4,20},{5,21},{6,22},{7,23},{8,24},{9,... | collective-permute-start | bytes 2064392 | tf_op jit(solution)/shard_map/ppermute | solution.py:24
  110.5 20.3 %collective-permute-start.24 = (bf16[64,5376]{1,0:T(8,128)(2,1)S(1)}, bf16[64,5376]{1,0:T(8,128)(2,1)S(1)}, u32[]{:S(2)}, u32[]{:S(2)}) collective-permute-start(bf16[64,5376]{1,0:T(8,128)(2,1)S(1)} %collective-permute-done.23), channel_id=1, source_target_pairs={{0,48},{1,49},{2,50},{3,51},{4,52},{5,53},{6,54},{7,55},{8,56},{9,... | collective-permute-start | bytes 2064392 | tf_op jit(solution)/shard_map/ppermute | solution.py:24
  119.4 11.4 %collective-permute-start.25 = (bf16[64,5376]{1,0:T(8,128)(2,1)S(1)}, bf16[64,5376]{1,0:T(8,128)(2,1)S(1)}, u32[]{:S(2)}, u32[]{:S(2)}) collective-permute-start(bf16[64,5376]{1,0:T(8,128)(2,1)S(1)} %constant_dynamic-update-slice_fusion.2), channel_id=1, source_target_pairs={{0,64},{1,65},{2,66},{3,67},{4,68},{5,69},{6,70},{7,71},{8,72},{9,... | collective-permute-start | bytes 2064392 | tf_op jit(solution)/shard_map/ppermute | solution.py:24
  120.6 2.3 %copy-start.9 = (bf16[256,5376]{1,0:T(8,128)(2,1)}, bf16[256,5376]{1,0:T(8,128)(2,1)S(1)}, u32[]{:S(2)}) copy-start(bf16[256,5376]{1,0:T(8,128)(2,1)S(1)} %slice_dynamic-update-slice_fusion.8) | copy-start | bytes 8257540
  121.8 2.3 %copy-start.3 = (f32[256,1024]{1,0:T(8,128)}, f32[256,1024]{1,0:T(8,128)S(1)}, u32[]{:S(2)}) copy-start(f32[256,1024]{1,0:T(8,128)S(1)} %fusion.26) | copy-start | bytes 3145732
  124.1 6.7 %copy-start.4 = (f32[256,1024]{1,0:T(8,128)}, f32[256,1024]{1,0:T(8,128)S(1)}, u32[]{:S(2)}) copy-start(f32[256,1024]{1,0:T(8,128)S(1)} %get-tuple-element.144) | copy-start | bytes 3145732
  125.3 10.8 %collective-permute-start.22 = (f32[128,2048]{1,0:T(8,128)}, f32[128,2048]{1,0:T(8,128)}, u32[]{:S(2)}, u32[]{:S(2)}) collective-permute-start(f32[128,2048]{1,0:T(8,128)} %pad_maximum_fusion.1), channel_id=1, source_target_pairs={{0,1},{1,0},{2,3},{3,2},{4,5},{5,4},{6,7},{7,6},{8,9},{9,8},{10,11... | collective-permute-start | bytes 3145736 | tf_op jit(solution)/shard_map/ppermute | solution.py:24
  131.1 2.3 %copy-start.11 = (bf16[256,5376]{1,0:T(8,128)(2,1)}, bf16[256,5376]{1,0:T(8,128)(2,1)S(1)}, u32[]{:S(2)}) copy-start(bf16[256,5376]{1,0:T(8,128)(2,1)S(1)} %slice_dynamic-update-slice_fusion) | copy-start | bytes 8257540
  135.9 3.1 %collective-permute-start.27 = (f32[136,2048]{1,0:T(8,128)}, f32[136,2048]{1,0:T(8,128)}, u32[]{:S(2)}, u32[]{:S(2)}) collective-permute-start(f32[136,2048]{1,0:T(8,128)} %select_maximum_fusion), channel_id=1, source_target_pairs={{0,1},{1,0},{2,3},{3,2},{4,5},{5,4},{6,7},{7,6},{8,9},{9,8},{10,11... | collective-permute-start | bytes 3342344 | tf_op jit(solution)/shard_map/ppermute | solution.py:24
  136.0 3.0 %copy-start.6 = (f32[256,1024]{1,0:T(8,128)S(1)}, f32[256,1024]{1,0:T(8,128)}, u32[]{:S(2)}) copy-start(f32[256,1024]{1,0:T(8,128)} %copy-done.5) | copy-start | bytes 3145732
  136.0 3.0 %copy-start.8 = (f32[256,1024]{1,0:T(8,128)S(1)}, f32[256,1024]{1,0:T(8,128)}, u32[]{:S(2)}) copy-start(f32[256,1024]{1,0:T(8,128)} %copy-done.7) | copy-start | bytes 3145732
  137.9 2.5 %copy-start.10 = (bf16[256,5376]{1,0:T(8,128)(2,1)S(1)}, bf16[256,5376]{1,0:T(8,128)(2,1)}, u32[]{:S(2)}) copy-start(bf16[256,5376]{1,0:T(8,128)(2,1)} %copy-done.9) | copy-start | bytes 8257540
  140.5 7.0 %copy-start.12 = (bf16[256,5376]{1,0:T(8,128)(2,1)S(1)}, bf16[256,5376]{1,0:T(8,128)(2,1)}, u32[]{:S(2)}) copy-start(bf16[256,5376]{1,0:T(8,128)(2,1)} %copy-done.11) | copy-start | bytes 8257540
  142.7 11.1 %collective-permute-start.30 = (bf16[64,2176]{1,0:T(8,128)(2,1)S(1)}, bf16[64,2176]{1,0:T(8,128)(2,1)S(1)}, u32[]{:S(2)}, u32[]{:S(2)}) collective-permute-start(bf16[64,2176]{1,0:T(8,128)(2,1)S(1)} %get-tuple-element.126), channel_id=1, source_target_pairs={{0,4},{1,5},{2,6},{3,7},{4,0},{5,1},{6,2},{7,3},{8,12},{9,13},{10,... | collective-permute-start | bytes 835592 | tf_op jit(solution)/shard_map/ppermute | solution.py:24
  145.4 14.0 %collective-permute-start.29 = (bf16[64,2176]{1,0:T(8,128)(2,1)S(1)}, bf16[64,2176]{1,0:T(8,128)(2,1)S(1)}, u32[]{:S(2)}, u32[]{:S(2)}) collective-permute-start(bf16[64,2176]{1,0:T(8,128)(2,1)S(1)} %get-tuple-element.127), channel_id=1, source_target_pairs={{0,6},{1,7},{2,0},{3,1},{4,2},{5,3},{6,4},{7,5},{8,14},{9,15},{10,... | collective-permute-start | bytes 835592 | tf_op jit(solution)/shard_map/ppermute | solution.py:24
  147.4 11.9 %collective-permute-start.28 = (bf16[64,2176]{1,0:T(8,128)(2,1)S(1)}, bf16[64,2176]{1,0:T(8,128)(2,1)S(1)}, u32[]{:S(2)}, u32[]{:S(2)}) collective-permute-start(bf16[64,2176]{1,0:T(8,128)(2,1)S(1)} %get-tuple-element.128), channel_id=1, source_target_pairs={{0,2},{1,3},{2,4},{3,5},{4,6},{5,7},{6,0},{7,1},{8,10},{9,11},{10,... | collective-permute-start | bytes 835592 | tf_op jit(solution)/shard_map/ppermute | solution.py:24
  159.5 5.8 %copy-start.15 = (bf16[256,1792]{1,0:T(8,128)(2,1)S(1)}, bf16[256,1792]{1,0:T(8,128)(2,1)}, u32[]{:S(2)}) copy-start(bf16[256,1792]{1,0:T(8,128)(2,1)} %get-tuple-element.54) | copy-start | bytes 2752516
  160.7 14.0 %all-to-all-start.1 = ((bf16[16,4,2560]{2,1,0:T(4,128)(2,1)}), bf16[16,4,2560]{2,1,0:T(4,128)(2,1)S(1)}, u32[]{:S(2)}, u32[]{:S(2)}) async-start(bf16[16,4,2560]{2,1,0:T(4,128)(2,1)} %pad_maximum_fusion.7), calls=%async_computation.1 | async-start | bytes 655360 | tf_op jit(solution)/shard_map/all_to_all | solution.py:253
  165.4 5.3 %copy-start.14 = (bf16[256,1792]{1,0:T(8,128)(2,1)S(1)}, bf16[256,1792]{1,0:T(8,128)(2,1)}, u32[]{:S(2)}) copy-start(bf16[256,1792]{1,0:T(8,128)(2,1)} %get-tuple-element.55) | copy-start | bytes 2752516
  165.4 5.3 %copy-start.16 = (bf16[256,1792]{1,0:T(8,128)(2,1)S(1)}, bf16[256,1792]{1,0:T(8,128)(2,1)}, u32[]{:S(2)}) copy-start(bf16[256,1792]{1,0:T(8,128)(2,1)} %get-tuple-element.58) | copy-start | bytes 2752516
  (3 other events, 3.7 us)

commit v10 on v9

--- a/solution.py
+++ b/solution.py
@@ -68,15 +68,20 @@
     return jnp.concatenate([b[:32] for b in blocks] + [b[32:] for b in blocks], axis=0)
 
 
+def gain_of(parts):
+    return parts[:8].astype(F32) + parts[8:16].astype(F32)
+
+
 def sum_over_core(partial, gain_partial):
-    give = partial[128:]
+    give = partial[128:].astype(BF16)
     if gain_partial is not None:
-        gain_rows = jnp.pad(gain_partial, ((0, 0), (0, partial.shape[1] - 128)))
-        give = jnp.concatenate([give, gain_rows], axis=0)
+        gain_rows = jnp.concatenate(parts_of(gain_partial, 2), axis=0)
+        padded = jnp.pad(gain_rows, ((0, 0), (0, partial.shape[1] - 128)))
+        give = jnp.concatenate([give, padded], axis=0)
     taken = send(give, c=1)
     if gain_partial is not None:
-        gain_partial = gain_partial + taken[128:, :128]
-    return partial[:128] + taken[:128], gain_partial
+        gain_partial = gain_of(gain_rows) + gain_of(taken[128:, :128])
+    return partial[:128] + taken[:128].astype(F32), gain_partial
 
 
 def sum_over_y(near, far, gain, x):
@@ -86,9 +91,6 @@
         start = (dy - x) % XS * 32
         halves = [lax.dynamic_slice(half, (start, 0), (32, n)) for half in (near, far)]
         return jnp.concatenate(halves, axis=0)
-
-    def gain_of(parts):
-        return parts[:8].astype(F32) + parts[8:16].astype(F32)
 
     parts = jnp.concatenate(parts_of(gain, 2) + [jnp.zeros((48, 128), BF16)], axis=0)
     gains = {0: gain_of(parts)}
@@ -110,7 +112,7 @@
     first2 = send(near3_top, x=3)
     n1 = send((near2[:32] + m12[:32]).astype(BF16), x=1).astype(F32)
     n2 = send((near2[32:] + m12[32:]).astype(BF16), x=3).astype(F32)
-    q = send((own + m11 + m13).astype(BF16), z=1)
+    q = send((own.astype(F32) + m11 + m13).astype(BF16), z=1)
     last1 = (near1_top + n1).astype(BF16)
     last2 = (near3_bottom + n2).astype(BF16)
     last1, last2, first1, first2 = lax.optimization_barrier((last1, last2, first1, first2))
@@ -188,7 +190,7 @@
     near_core, _ = gather_half(near_block, x)
     far_estimate, far_normed, far_grad = normed_of(both_cores(far_core))
     far = partials(far_normed, far_grad)
-    far = [far(0, F32), far(1, BF16), far(2, BF16), far(3, BF16)]
+    far = [far(0, BF16), far(1, BF16), far(2, BF16), far(3, BF16)]
     near_core, far[0] = lax.optimization_barrier((near_core, far[0]))
     near_estimate, near_normed, near_grad = normed_of(both_cores(near_core))
     near = partials(near_normed, near_grad)
@@ -201,6 +203,9 @@
         near(3, F32, (1,)),
     ]
     sums = sum_over_row(far, near)
+    normed = jnp.concatenate([near_normed, far_normed], axis=0)
+    grad_full = jnp.concatenate([near_grad, far_grad], axis=0)
+    normed, grad_full, sums = lax.optimization_barrier((normed, grad_full, sums))
     gate, up, hidden_grad = sums[:, :width], sums[:, width : 2 * width], sums[:, 2 * width :]
     sigma = jax.nn.sigmoid(gate)
     silu = gate * sigma
@@ -213,11 +218,14 @@
         axis=1,
     )
     near_units, far_units = gather_over_row(units)
-    near_units = by_core(lax.optimization_barrier(near_units))
-    far_units = by_core(lax.optimization_barrier(far_units))
+    def parts_by_core(blocks):
+        blocks = lax.optimization_barrier(blocks)
+        return [by_core([b[:, k * width : (k + 1) * width] for b in blocks]) for k in range(3)]
+
+    near_units, far_units = parts_by_core(near_units), parts_by_core(far_units)
 
     def backward(units):
-        hidden, gate_grad, up_grad = units[:, :width], units[:, width : 2 * width], units[:, 2 * width :]
+        hidden, gate_grad, up_grad = units
         grad = product_right_t(gate_grad, gate_weight) + product_right_t(up_grad, up_weight)
         return jnp.concatenate([product(hidden, down_weight), grad], axis=1)
 
@@ -229,18 +237,15 @@
     )
     far_keep, gain = sum_over_core(far_partial, gain_partial.reshape(8, 128))
 
-    *late, far_keep = lax.optimization_barrier((near_units, far_units, far_keep))
+    near_units, far_units, far_keep = lax.optimization_barrier((near_units, far_units, far_keep))
 
     def of_all(part):
-        return jnp.concatenate(
-            [unit[:, part * width : (part + 1) * width] for unit in late], axis=0
-        )
-
-    grad_full = jnp.concatenate([near_grad, far_grad], axis=0)
+        return jnp.concatenate([near_units[part], far_units[part]], axis=0)
+
     down_weight_grad = product_left_t(of_all(0), grad_full).astype(BF16)
     total, gain = sum_over_y(near_keep, far_keep, gain, x)
     normed, total, down_weight_grad = lax.optimization_barrier(
-        (jnp.concatenate([near_normed, far_normed], axis=0), total, down_weight_grad)
+        (normed, total, down_weight_grad)
     )
     gate_weight_grad = product_left_t(normed, of_all(1)).astype(BF16)
     up_weight_grad = product_left_t(normed, of_all(2)).astype(BF16)

time: 179 us -> 178 us (level)
  local copies, waits for them, and re-layouts: 11.1 us -> 17.3 us
  other arithmetic: 12.2 us -> 8.4 us
  waiting for transfers between devices: 72.3 us -> 70.5 us
    unnamed x57, local copies, waits for them, and re-layouts: 4.46 us -> 12 us
    add x3 -> x2, other arithmetic: 3.16 us -> 0.22 us  [sum_over_core(): return (partial[:128] + taken[:128].astype(F32), gain_partial)]
    slice x2 -> x0, local copies, waits for them, and re-layouts: 2.92 us -> none  [of_all(): unit[:, part * width:(part + 1) * width]]
    ppermute x31, waiting for transfers between devices: 63.5 us -> 60.6 us  [send(): return lax.ppermute(value, AXES, pairs)]
  transfers between devices with their start and end apart: 33 -> 33, of which waited for: 14 -> 16; matrix products, arithmetic and copies ran while one was open for 18% -> 19% of each run, Pallas kernels for 0% -> 0%
where the time goes in v10:
time: 178 us
  waiting for transfers between devices  70.5 us (40%)
  starting transfers between devices  54.4 us (31%)
  matrix products  25.6 us (14%)
  local copies, waits for them, and re-layouts  17.3 us (10%)
  other arithmetic  8.4 us (5%)
    ppermute x31, waiting for transfers between devices, send(): return lax.ppermute(value, AXES, pairs)  60.6 us
    ppermute x31, starting transfers between devices, send(): return lax.ppermute(value, AXES, pairs)  40 us
    unnamed x57, local copies, waits for them, and re-layouts  12 us
    dot_general x3, matrix products, product_left_t(): lax.dot_general(left, right, (((0,), (0,)), ((), ())), preferred_element_...  11.9 us
    all_to_all x1, waiting for transfers between devices, per_device(): lax.all_to_all(message.reshape(16, 4, 2176), ('h', 'z', 'x'), split_axis=...  8.83 us
    all_to_all x1, starting transfers between devices, per_device(): lax.all_to_all(message.reshape(16, 4, 2176), ('h', 'z', 'x'), split_axis=...  7.96 us
    dot_general x6, matrix products, product_right_t(): lax.dot_general(left, right, (((1,), (1,)), ((), ())), preferred_element_...  6.94 us
    dot_general x6, matrix products, product(): return jnp.dot(left, right, preferred_element_type=F32)  6.75 us
  transfers between devices with their start and end apart: 33, of which 16 were waited for; matrix products, arithmetic and copies ran while one was open for 19% of the time, Pallas kernels for 0%

profile of v10, /device:TPU:0, one launch (start us, length us, event | category | flops | bytes accessed | tf_op | source)
XLA Modules:
  0.0 177.8 jit_solution(3250595043337913579)
XLA Ops:
  4.0 8.0 %all-to-all-start = ((bf16[16,4,2176]{2,1,0:T(4,128)(2,1)}), bf16[16,4,2176]{2,1,0:T(4,128)(2,1)S(1)}, u32[]{:S(2)}, u32[]{:S(2)}) async-start(bf16[16,4,2176]{2,1,0:T(4,128)(2,1)} %bitcast.2), calls=%async_computation | async-start | bytes 557056 | tf_op jit(solution)/shard_map/all_to_all | solution.py:155
  12.0 8.8 %all-to-all-done = bf16[16,4,2176]{2,1,0:T(4,128)(2,1)S(1)} async-done(((bf16[16,4,2176]{2,1,0:T(4,128)(2,1)}), bf16[16,4,2176]{2,1,0:T(4,128)(2,1)S(1)}, u32[]{:S(2)}, u32[]{:S(2)}) %all-to-all-start) | async-done | bytes 278560 | tf_op jit(solution)/shard_map/all_to_all | solution.py:155
  21.0 1.6 collective-permute-start
  22.6 1.7 collective-permute-start.4
  24.3 2.0 %collective-permute-start.5 = (bf16[32,2176]{1,0:T(8,128)(2,1)S(1)}, bf16[32,2176]{1,0:T(8,128)(2,1)S(1)}, u32[]{:S(2)}, u32[]{:S(2)}) collective-permute-start(bf16[32,2176]{1,0:T(8,128)(2,1)S(1)} %get-tuple-element.65), channel_id=1, source_target_pairs={{0,4},{1,5},{2,6},{3,7},{4,0},{5,1},{6,2},{7,3},{8,12},{9,13},{10,... | collective-permute-start | bytes 417800 | tf_op jit(solution)/shard_map/ppermute | solution.py:24
  26.3 2.5 %collective-permute-done = bf16[32,2176]{1,0:T(8,128)(2,1)S(1)} collective-permute-done((bf16[32,2176]{1,0:T(8,128)(2,1)S(1)}, bf16[32,2176]{1,0:T(8,128)(2,1)S(1)}, u32[]{:S(2)}, u32[]{:S(2)}) %collective-permute-start) | collective-permute-done | bytes 139296 | tf_op jit(solution)/shard_map/ppermute | solution.py:24
  28.8 1.1 collective-permute-start.1
  30.8 1.4 collective-permute-start.3
  32.5 1.9 %collective-permute-done.1 = bf16[32,2176]{1,0:T(8,128)(2,1)S(1)} collective-permute-done((bf16[32,2176]{1,0:T(8,128)(2,1)S(1)}, bf16[32,2176]{1,0:T(8,128)(2,1)S(1)}, u32[]{:S(2)}, u32[]{:S(2)}) %collective-permute-start.1) | collective-permute-done | bytes 139296 | tf_op jit(solution)/shard_map/ppermute | solution.py:24
  34.4 2.2 %collective-permute-done.2 = bf16[32,2176]{1,0:T(8,128)(2,1)S(1)} collective-permute-done((bf16[32,2176]{1,0:T(8,128)(2,1)S(1)}, bf16[32,2176]{1,0:T(8,128)(2,1)S(1)}, u32[]{:S(2)}, u32[]{:S(2)}) %collective-permute-start.2) | collective-permute-done | bytes 139296 | tf_op jit(solution)/shard_map/ppermute | solution.py:24
  36.6 1.4 collective-permute-done.3
  38.1 1.2 convolution_convert_fusion.3
  39.7 1.6 copy-done
  41.3 1.1 convolution_convert_fusion.4
  43.3 1.1 convolution_convert_fusion.5
  45.7 1.3 collective-permute-start.8
  47.0 1.6 collective-permute-start.11
  48.9 1.2 fusion.65
  50.3 1.2 fusion.66
  51.4 1.1 fusion.67
  53.2 3.3 %collective-permute-start.15 = (bf16[32,5376]{1,0:T(8,128)(2,1)S(1)}, bf16[32,5376]{1,0:T(8,128)(2,1)S(1)}, u32[]{:S(2)}, u32[]{:S(2)}) collective-permute-start(bf16[32,5376]{1,0:T(8,128)(2,1)S(1)} %pad_maximum_fusion.8), channel_id=1, source_target_pairs={{0,48},{1,49},{2,50},{3,51},{4,52},{5,53},{6,54},{7,55},{8,56},{9,... | collective-permute-start | bytes 1032200 | tf_op jit(solution)/shard_map/ppermute | solution.py:24
  56.6 7.8 %collective-permute-done.11 = bf16[64,5376]{1,0:T(8,128)(2,1)S(1)} collective-permute-done((bf16[64,5376]{1,0:T(8,128)(2,1)S(1)}, bf16[64,5376]{1,0:T(8,128)(2,1)S(1)}, u32[]{:S(2)}, u32[]{:S(2)}) %collective-permute-start.11) | collective-permute-done | bytes 688160 | tf_op jit(solution)/shard_map/ppermute | solution.py:24
  66.8 2.9 %collective-permute-start.13 = (bf16[32,5376]{1,0:T(8,128)(2,1)S(1)}, bf16[32,5376]{1,0:T(8,128)(2,1)S(1)}, u32[]{:S(2)}, u32[]{:S(2)}) collective-permute-start(bf16[32,5376]{1,0:T(8,128)(2,1)S(1)} %get-tuple-element.89), channel_id=1, source_target_pairs={{0,48},{1,49},{2,50},{3,51},{4,52},{5,53},{6,54},{7,55},{8,56},{9,... | collective-permute-start | bytes 1032200 | tf_op jit(solution)/shard_map/ppermute | solution.py:24
  69.8 9.5 %collective-permute-done.12 = bf16[32,5376]{1,0:T(8,128)(2,1)S(1)} collective-permute-done((bf16[32,5376]{1,0:T(8,128)(2,1)S(1)}, bf16[32,5376]{1,0:T(8,128)(2,1)S(1)}, u32[]{:S(2)}, u32[]{:S(2)}) %collective-permute-start.12) | collective-permute-done | bytes 344096 | tf_op jit(solution)/shard_map/ppermute | solution.py:24
  79.5 3.2 %collective-permute-start.17 = (bf16[32,5376]{1,0:T(8,128)(2,1)S(1)}, bf16[32,5376]{1,0:T(8,128)(2,1)S(1)}, u32[]{:S(2)}, u32[]{:S(2)}) collective-permute-start(bf16[32,5376]{1,0:T(8,128)(2,1)S(1)} %fusion.20), channel_id=1, source_target_pairs={{0,48},{1,49},{2,50},{3,51},{4,52},{5,53},{6,54},{7,55},{8,56},{9,... | collective-permute-start | bytes 1032200 | tf_op jit(solution)/shard_map/ppermute | solution.py:24
  84.9 5.2 %collective-permute-done.16 = bf16[32,5376]{1,0:T(8,128)(2,1)S(1)} collective-permute-done((bf16[32,5376]{1,0:T(8,128)(2,1)S(1)}, bf16[32,5376]{1,0:T(8,128)(2,1)S(1)}, u32[]{:S(2)}, u32[]{:S(2)}) %collective-permute-start.16) | collective-permute-done | bytes 344096 | tf_op jit(solution)/shard_map/ppermute | solution.py:24
  90.7 3.2 %collective-permute-start.18 = (bf16[64,5376]{1,0:T(8,128)(2,1)S(1)}, bf16[64,5376]{1,0:T(8,128)(2,1)}, u32[]{:S(2)}, u32[]{:S(2)}) collective-permute-start(bf16[64,5376]{1,0:T(8,128)(2,1)S(1)} %pad_maximum_fusion.4), channel_id=1, source_target_pairs={{0,48},{1,49},{2,50},{3,51},{4,52},{5,53},{6,54},{7,55},{8,56},{9,... | collective-permute-start | bytes 2064392 | tf_op jit(solution)/shard_map/ppermute | solution.py:24
  94.0 1.3 collective-permute-start.23
  95.2 12.5 %collective-permute-done.19 = bf16[64,5376]{1,0:T(8,128)(2,1)S(1)} collective-permute-done((bf16[64,5376]{1,0:T(8,128)(2,1)S(1)}, bf16[64,5376]{1,0:T(8,128)(2,1)S(1)}, u32[]{:S(2)}, u32[]{:S(2)}) %collective-permute-start.19) | collective-permute-done | bytes 688160 | tf_op jit(solution)/shard_map/ppermute | solution.py:24
  110.4 3.3 %collective-permute-start.21 = (bf16[32,5376]{1,0:T(8,128)(2,1)S(1)}, bf16[32,5376]{1,0:T(8,128)(2,1)S(1)}, u32[]{:S(2)}, u32[]{:S(2)}) collective-permute-start(bf16[32,5376]{1,0:T(8,128)(2,1)S(1)} %slice.809), channel_id=1, source_target_pairs={{0,48},{1,49},{2,50},{3,51},{4,52},{5,53},{6,54},{7,55},{8,56},{9,... | collective-permute-start | bytes 1032200 | tf_op jit(solution)/shard_map/ppermute | solution.py:24
  113.9 1.8 collective-permute-start.26
  115.7 6.1 %collective-permute-done.20 = bf16[32,5376]{1,0:T(8,128)(2,1)S(1)} collective-permute-done((bf16[32,5376]{1,0:T(8,128)(2,1)}, bf16[32,5376]{1,0:T(8,128)(2,1)S(1)}, u32[]{:S(2)}, u32[]{:S(2)}) %collective-permute-start.20) | collective-permute-done | bytes 344096 | tf_op jit(solution)/shard_map/ppermute | solution.py:24
  122.2 1.7 collective-permute-start.25
  125.1 1.2 slice_dynamic-update-slice_fusion.26
  127.2 1.1 fusion.69
  131.3 1.2 multiply_reduce_fusion.1
  135.6 1.1 fusion.70
  136.7 1.1 fusion.71
  137.8 1.2 multiply_reduce_fusion
  139.5 1.7 collective-permute-done.27
  142.3 1.3 collective-permute-start.28
  143.6 1.5 collective-permute-start.30
  145.1 4.0 %convolution_convert_fusion.2 = bf16[1792,1024]{1,0:T(8,128)(2,1)} fusion(bf16[512,1024]{1,0:T(8,128)(2,1)S(1)} %copy-done.11, bf16[256,1792]{1,0:T(8,128)(2,1)S(1)} %get-tuple-element.53, bf16[256,1792]{1,0:T(8,128)(2,1)S(1)} %get-tuple-element.52), kind=kOutput, calls=%fused_computation.2 | convolution fusion | flops 1884553216 | bytes 6553600 | tf_op jit(solution)/shard_map/dot_general | solution.py:36
  149.1 2.0 %collective-permute-done.29 = bf16[64,2176]{1,0:T(8,128)(2,1)S(1)} collective-permute-done((bf16[64,2176]{1,0:T(8,128)(2,1)S(1)}, bf16[64,2176]{1,0:T(8,128)(2,1)S(1)}, u32[]{:S(2)}, u32[]{:S(2)}) %collective-permute-start.29) | collective-permute-done | bytes 278560 | tf_op jit(solution)/shard_map/ppermute | solution.py:24
  151.1 6.9 %collective-permute-done.28 = bf16[64,2176]{1,0:T(8,128)(2,1)S(1)} collective-permute-done((bf16[64,2176]{1,0:T(8,128)(2,1)S(1)}, bf16[64,2176]{1,0:T(8,128)(2,1)S(1)}, u32[]{:S(2)}, u32[]{:S(2)}) %collective-permute-start.28) | collective-permute-done | bytes 278560 | tf_op jit(solution)/shard_map/ppermute | solution.py:24
  159.3 6.5 %all-to-all-start.1 = ((bf16[16,4,2560]{2,1,0:T(4,128)(2,1)}), bf16[16,4,2560]{2,1,0:T(4,128)(2,1)S(1)}, u32[]{:S(2)}, u32[]{:S(2)}) async-start(bf16[16,4,2560]{2,1,0:T(4,128)(2,1)} %pad_maximum_fusion.9), calls=%async_computation.1 | async-start | bytes 655360 | tf_op jit(solution)/shard_map/all_to_all | solution.py:258
  165.9 4.0 %convolution_convert_fusion.1 = bf16[1024,1792]{1,0:T(8,128)(2,1)} fusion(bf16[512,1024]{1,0:T(8,128)(2,1)S(1)} %copy-done.10, bf16[256,1792]{1,0:T(8,128)(2,1)S(1)} %get-tuple-element.58, bf16[256,1792]{1,0:T(8,128)(2,1)S(1)} %copy-done.15), kind=kOutput, calls=%fused_computation.1 | convolution fusion | flops 1884553216 | bytes 6553600 | tf_op jit(solution)/shard_map/dot_general | solution.py:36
  169.8 4.0 %convolution_convert_fusion = bf16[1024,1792]{1,0:T(8,128)(2,1)} fusion(bf16[512,1024]{1,0:T(8,128)(2,1)S(1)} %copy-done.10, bf16[256,1792]{1,0:T(8,128)(2,1)S(1)} %copy-done.17, bf16[256,1792]{1,0:T(8,128)(2,1)S(1)} %copy-done.9), kind=kOutput, calls=%fused_computation | convolution fusion | flops 1884553216 | bytes 6553600 | tf_op jit(solution)/shard_map/dot_general | solution.py:36
  (186 shorter events, 31.8 us)
Async XLA Ops:
  3.2 21.1 %copy-start.13 = (f32[8192]{0:T(1024)S(1)}, f32[8192]{0:T(1024)}, u32[]{:S(2)}) copy-start(f32[8192]{0:T(1024)} %param.7) | copy-start | bytes 98308
  4.0 16.8 %all-to-all-start = ((bf16[16,4,2176]{2,1,0:T(4,128)(2,1)}), bf16[16,4,2176]{2,1,0:T(4,128)(2,1)S(1)}, u32[]{:S(2)}, u32[]{:S(2)}) async-start(bf16[16,4,2176]{2,1,0:T(4,128)(2,1)} %bitcast.2), calls=%async_computation | async-start | bytes 557056 | tf_op jit(solution)/shard_map/all_to_all | solution.py:155
  21.0 7.8 %collective-permute-start = (bf16[32,2176]{1,0:T(8,128)(2,1)S(1)}, bf16[32,2176]{1,0:T(8,128)(2,1)S(1)}, u32[]{:S(2)}, u32[]{:S(2)}) collective-permute-start(bf16[32,2176]{1,0:T(8,128)(2,1)S(1)} %get-tuple-element.65), channel_id=1, source_target_pairs={{0,2},{1,3},{2,4},{3,5},{4,6},{5,7},{6,0},{7,1},{8,10},{9,11},{10,... | collective-permute-start | bytes 417800 | tf_op jit(solution)/shard_map/ppermute | solution.py:24
  22.6 9.6 %collective-permute-start.4 = (bf16[32,2176]{1,0:T(8,128)(2,1)S(1)}, bf16[32,2176]{1,0:T(8,128)(2,1)S(1)}, u32[]{:S(2)}, u32[]{:S(2)}) collective-permute-start(bf16[32,2176]{1,0:T(8,128)(2,1)S(1)} %get-tuple-element.65), channel_id=1, source_target_pairs={{0,6},{1,7},{2,0},{3,1},{4,2},{5,3},{6,4},{7,5},{8,14},{9,15},{10,... | collective-permute-start | bytes 417800 | tf_op jit(solution)/shard_map/ppermute | solution.py:24
  24.3 7.9 %collective-permute-start.5 = (bf16[32,2176]{1,0:T(8,128)(2,1)S(1)}, bf16[32,2176]{1,0:T(8,128)(2,1)S(1)}, u32[]{:S(2)}, u32[]{:S(2)}) collective-permute-start(bf16[32,2176]{1,0:T(8,128)(2,1)S(1)} %get-tuple-element.65), channel_id=1, source_target_pairs={{0,4},{1,5},{2,6},{3,7},{4,0},{5,1},{6,2},{7,3},{8,12},{9,13},{10,... | collective-permute-start | bytes 417800 | tf_op jit(solution)/shard_map/ppermute | solution.py:24
  28.8 5.6 %collective-permute-start.1 = (bf16[32,2176]{1,0:T(8,128)(2,1)S(1)}, bf16[32,2176]{1,0:T(8,128)(2,1)S(1)}, u32[]{:S(2)}, u32[]{:S(2)}) collective-permute-start(bf16[32,2176]{1,0:T(8,128)(2,1)S(1)} %get-tuple-element.34), channel_id=1, source_target_pairs={{0,6},{1,7},{2,0},{3,1},{4,2},{5,3},{6,4},{7,5},{8,14},{9,15},{10,... | collective-permute-start | bytes 417800 | tf_op jit(solution)/shard_map/ppermute | solution.py:24
  29.9 6.7 %collective-permute-start.2 = (bf16[32,2176]{1,0:T(8,128)(2,1)S(1)}, bf16[32,2176]{1,0:T(8,128)(2,1)S(1)}, u32[]{:S(2)}, u32[]{:S(2)}) collective-permute-start(bf16[32,2176]{1,0:T(8,128)(2,1)S(1)} %get-tuple-element.34), channel_id=1, source_target_pairs={{0,4},{1,5},{2,6},{3,7},{4,0},{5,1},{6,2},{7,3},{8,12},{9,13},{10,... | collective-permute-start | bytes 417800 | tf_op jit(solution)/shard_map/ppermute | solution.py:24
  30.8 7.2 %collective-permute-start.3 = (bf16[32,2176]{1,0:T(8,128)(2,1)S(1)}, bf16[32,2176]{1,0:T(8,128)(2,1)S(1)}, u32[]{:S(2)}, u32[]{:S(2)}) collective-permute-start(bf16[32,2176]{1,0:T(8,128)(2,1)S(1)} %get-tuple-element.34), channel_id=1, source_target_pairs={{0,2},{1,3},{2,4},{3,5},{4,6},{5,7},{6,0},{7,1},{8,10},{9,11},{10,... | collective-permute-start | bytes 417800 | tf_op jit(solution)/shard_map/ppermute | solution.py:24
  32.2 5.8 %copy-start.2 = (bf16[1792,1024]{1,0:T(8,128)(2,1)S(1)}, bf16[1792,1024]{1,0:T(8,128)(2,1)}, u32[]{:S(2)}) copy-start(bf16[1792,1024]{1,0:T(8,128)(2,1)} %param.10) | copy-start | bytes 11010052
  32.3 5.7 %collective-permute-start.6 = (bf16[128,2176]{1,0:T(8,128)(2,1)S(1)}, bf16[128,2176]{1,0:T(8,128)(2,1)S(1)}, u32[]{:S(2)}, u32[]{:S(2)}) collective-permute-start(bf16[128,2176]{1,0:T(8,128)(2,1)S(1)} %constant_dynamic-update-slice_fusion.4), channel_id=1, source_target_pairs={{0,1},{1,0},{2,3},{3,2},{4,5},{5,4},{6,7},{7,6},{8,9},{9,8},{10,11... | collective-permute-start | bytes 1671176 | tf_op jit(solution)/shard_map/ppermute | solution.py:24
  39.2 2.0 %copy-start = (bf16[1024,1792]{1,0:T(8,128)(2,1)S(1)}, bf16[1024,1792]{1,0:T(8,128)(2,1)}, u32[]{:S(2)}) copy-start(bf16[1024,1792]{1,0:T(8,128)(2,1)} %param.9) | copy-start | bytes 11010052
  41.3 2.0 %copy-start.4 = (bf16[1024,1792]{1,0:T(8,128)(2,1)S(1)}, bf16[1024,1792]{1,0:T(8,128)(2,1)}, u32[]{:S(2)}) copy-start(bf16[1024,1792]{1,0:T(8,128)(2,1)} %param.8) | copy-start | bytes 11010052
  44.6 4.0 %collective-permute-start.7 = (bf16[128,2176]{1,0:T(8,128)(2,1)S(1)}, bf16[128,2176]{1,0:T(8,128)(2,1)S(1)}, u32[]{:S(2)}, u32[]{:S(2)}) collective-permute-start(bf16[128,2176]{1,0:T(8,128)(2,1)S(1)} %constant_dynamic-update-slice_fusion.8), channel_id=1, source_target_pairs={{0,1},{1,0},{2,3},{3,2},{4,5},{5,4},{6,7},{7,6},{8,9},{9,8},{10,11... | collective-permute-start | bytes 1671176 | tf_op jit(solution)/shard_map/ppermute | solution.py:24
  44.7 20.8 %collective-permute-start.9 = (bf16[64,5376]{1,0:T(8,128)(2,1)S(1)}, bf16[64,5376]{1,0:T(8,128)(2,1)S(1)}, u32[]{:S(2)}, u32[]{:S(2)}) collective-permute-start(bf16[64,5376]{1,0:T(8,128)(2,1)S(1)} %maximum_maximum_fusion.2), channel_id=1, source_target_pairs={{0,48},{1,49},{2,50},{3,51},{4,52},{5,53},{6,54},{7,55},{8,56},{9,... | collective-permute-start | bytes 2064392 | tf_op jit(solution)/shard_map/ppermute | solution.py:24
  45.7 19.8 %collective-permute-start.8 = (bf16[64,5376]{1,0:T(8,128)(2,1)S(1)}, bf16[64,5376]{1,0:T(8,128)(2,1)S(1)}, u32[]{:S(2)}, u32[]{:S(2)}) collective-permute-start(bf16[64,5376]{1,0:T(8,128)(2,1)S(1)} %maximum_maximum_fusion.1), channel_id=1, source_target_pairs={{0,16},{1,17},{2,18},{3,19},{4,20},{5,21},{6,22},{7,23},{8,24},{9,... | collective-permute-start | bytes 2064392 | tf_op jit(solution)/shard_map/ppermute | solution.py:24
  47.0 17.3 %collective-permute-start.11 = (bf16[64,5376]{1,0:T(8,128)(2,1)S(1)}, bf16[64,5376]{1,0:T(8,128)(2,1)S(1)}, u32[]{:S(2)}, u32[]{:S(2)}) collective-permute-start(bf16[64,5376]{1,0:T(8,128)(2,1)S(1)} %maximum_maximum_fusion.3), channel_id=1, source_target_pairs={{0,64},{1,65},{2,66},{3,67},{4,68},{5,69},{6,70},{7,71},{8,72},{9,... | collective-permute-start | bytes 2064392 | tf_op jit(solution)/shard_map/ppermute | solution.py:24
  52.9 26.5 %collective-permute-start.14 = (bf16[32,5376]{1,0:T(8,128)(2,1)S(1)}, bf16[32,5376]{1,0:T(8,128)(2,1)S(1)}, u32[]{:S(2)}, u32[]{:S(2)}) collective-permute-start(bf16[32,5376]{1,0:T(8,128)(2,1)S(1)} %pad_maximum_fusion.7), channel_id=1, source_target_pairs={{0,16},{1,17},{2,18},{3,19},{4,20},{5,21},{6,22},{7,23},{8,24},{9,... | collective-permute-start | bytes 1032200 | tf_op jit(solution)/shard_map/ppermute | solution.py:24
  53.2 26.2 %collective-permute-start.15 = (bf16[32,5376]{1,0:T(8,128)(2,1)S(1)}, bf16[32,5376]{1,0:T(8,128)(2,1)S(1)}, u32[]{:S(2)}, u32[]{:S(2)}) collective-permute-start(bf16[32,5376]{1,0:T(8,128)(2,1)S(1)} %pad_maximum_fusion.8), channel_id=1, source_target_pairs={{0,48},{1,49},{2,50},{3,51},{4,52},{5,53},{6,54},{7,55},{8,56},{9,... | collective-permute-start | bytes 1032200 | tf_op jit(solution)/shard_map/ppermute | solution.py:24
  64.6 14.7 %collective-permute-start.12 = (bf16[32,5376]{1,0:T(8,128)(2,1)S(1)}, bf16[32,5376]{1,0:T(8,128)(2,1)S(1)}, u32[]{:S(2)}, u32[]{:S(2)}) collective-permute-start(bf16[32,5376]{1,0:T(8,128)(2,1)S(1)} %get-tuple-element.90), channel_id=1, source_target_pairs={{0,16},{1,17},{2,18},{3,19},{4,20},{5,21},{6,22},{7,23},{8,24},{9,... | collective-permute-start | bytes 1032200 | tf_op jit(solution)/shard_map/ppermute | solution.py:24
  65.8 19.1 %collective-permute-start.10 = (bf16[64,5376]{1,0:T(8,128)(2,1)S(1)}, bf16[64,5376]{1,0:T(8,128)(2,1)S(1)}, u32[]{:S(2)}, u32[]{:S(2)}) collective-permute-start(bf16[64,5376]{1,0:T(8,128)(2,1)S(1)} %add_convert_fusion), channel_id=1, source_target_pairs={{0,64},{1,65},{2,66},{3,67},{4,68},{5,69},{6,70},{7,71},{8,72},{9,... | collective-permute-start | bytes 2064392 | tf_op jit(solution)/shard_map/ppermute | solution.py:24
  66.8 12.5 %collective-permute-start.13 = (bf16[32,5376]{1,0:T(8,128)(2,1)S(1)}, bf16[32,5376]{1,0:T(8,128)(2,1)S(1)}, u32[]{:S(2)}, u32[]{:S(2)}) collective-permute-start(bf16[32,5376]{1,0:T(8,128)(2,1)S(1)} %get-tuple-element.89), channel_id=1, source_target_pairs={{0,48},{1,49},{2,50},{3,51},{4,52},{5,53},{6,54},{7,55},{8,56},{9,... | collective-permute-start | bytes 1032200 | tf_op jit(solution)/shard_map/ppermute | solution.py:24
  79.4 10.6 %collective-permute-start.16 = (bf16[32,5376]{1,0:T(8,128)(2,1)S(1)}, bf16[32,5376]{1,0:T(8,128)(2,1)S(1)}, u32[]{:S(2)}, u32[]{:S(2)}) collective-permute-start(bf16[32,5376]{1,0:T(8,128)(2,1)S(1)} %fusion.19), channel_id=1, source_target_pairs={{0,16},{1,17},{2,18},{3,19},{4,20},{5,21},{6,22},{7,23},{8,24},{9,... | collective-permute-start | bytes 1032200 | tf_op jit(solution)/shard_map/ppermute | solution.py:24
  79.5 10.6 %collective-permute-start.17 = (bf16[32,5376]{1,0:T(8,128)(2,1)S(1)}, bf16[32,5376]{1,0:T(8,128)(2,1)S(1)}, u32[]{:S(2)}, u32[]{:S(2)}) collective-permute-start(bf16[32,5376]{1,0:T(8,128)(2,1)S(1)} %fusion.20), channel_id=1, source_target_pairs={{0,48},{1,49},{2,50},{3,51},{4,52},{5,53},{6,54},{7,55},{8,56},{9,... | collective-permute-start | bytes 1032200 | tf_op jit(solution)/shard_map/ppermute | solution.py:24
  90.7 17.1 %collective-permute-start.19 = (bf16[64,5376]{1,0:T(8,128)(2,1)S(1)}, bf16[64,5376]{1,0:T(8,128)(2,1)S(1)}, u32[]{:S(2)}, u32[]{:S(2)}) collective-permute-start(bf16[64,5376]{1,0:T(8,128)(2,1)S(1)} %pad_maximum_fusion.4), channel_id=1, source_target_pairs={{0,16},{1,17},{2,18},{3,19},{4,20},{5,21},{6,22},{7,23},{8,24},{9,... | collective-permute-start | bytes 2064392 | tf_op jit(solution)/shard_map/ppermute | solution.py:24
  90.7 18.6 %collective-permute-start.18 = (bf16[64,5376]{1,0:T(8,128)(2,1)S(1)}, bf16[64,5376]{1,0:T(8,128)(2,1)}, u32[]{:S(2)}, u32[]{:S(2)}) collective-permute-start(bf16[64,5376]{1,0:T(8,128)(2,1)S(1)} %pad_maximum_fusion.4), channel_id=1, source_target_pairs={{0,48},{1,49},{2,50},{3,51},{4,52},{5,53},{6,54},{7,55},{8,56},{9,... | collective-permute-start | bytes 2064392 | tf_op jit(solution)/shard_map/ppermute | solution.py:24
  94.0 19.7 %collective-permute-start.23 = (bf16[64,5376]{1,0:T(8,128)(2,1)S(1)}, bf16[64,5376]{1,0:T(8,128)(2,1)}, u32[]{:S(2)}, u32[]{:S(2)}) collective-permute-start(bf16[64,5376]{1,0:T(8,128)(2,1)S(1)} %pad_maximum_fusion.4), channel_id=1, source_target_pairs={{0,64},{1,65},{2,66},{3,67},{4,68},{5,69},{6,70},{7,71},{8,72},{9,... | collective-permute-start | bytes 2064392 | tf_op jit(solution)/shard_map/ppermute | solution.py:24
  109.4 12.4 %collective-permute-start.20 = (bf16[32,5376]{1,0:T(8,128)(2,1)}, bf16[32,5376]{1,0:T(8,128)(2,1)S(1)}, u32[]{:S(2)}, u32[]{:S(2)}) collective-permute-start(bf16[32,5376]{1,0:T(8,128)(2,1)} %slice.808), channel_id=1, source_target_pairs={{0,16},{1,17},{2,18},{3,19},{4,20},{5,21},{6,22},{7,23},{8,24},{9,... | collective-permute-start | bytes 1032200 | tf_op jit(solution)/shard_map/ppermute | solution.py:24
  110.4 11.8 %collective-permute-start.21 = (bf16[32,5376]{1,0:T(8,128)(2,1)S(1)}, bf16[32,5376]{1,0:T(8,128)(2,1)S(1)}, u32[]{:S(2)}, u32[]{:S(2)}) collective-permute-start(bf16[32,5376]{1,0:T(8,128)(2,1)S(1)} %slice.809), channel_id=1, source_target_pairs={{0,48},{1,49},{2,50},{3,51},{4,52},{5,53},{6,54},{7,55},{8,56},{9,... | collective-permute-start | bytes 1032200 | tf_op jit(solution)/shard_map/ppermute | solution.py:24
  113.7 19.6 %collective-permute-start.24 = (bf16[64,5376]{1,0:T(8,128)(2,1)}, bf16[64,5376]{1,0:T(8,128)(2,1)S(1)}, u32[]{:S(2)}, u32[]{:S(2)}) collective-permute-start(bf16[64,5376]{1,0:T(8,128)(2,1)} %collective-permute-done.23), channel_id=1, source_target_pairs={{0,48},{1,49},{2,50},{3,51},{4,52},{5,53},{6,54},{7,55},{8,56},{9,... | collective-permute-start | bytes 2064392 | tf_op jit(solution)/shard_map/ppermute | solution.py:24
  113.9 19.4 %collective-permute-start.26 = (bf16[64,5376]{1,0:T(8,128)(2,1)}, bf16[64,5376]{1,0:T(8,128)(2,1)S(1)}, u32[]{:S(2)}, u32[]{:S(2)}) collective-permute-start(bf16[64,5376]{1,0:T(8,128)(2,1)} %collective-permute-done.23), channel_id=1, source_target_pairs={{0,16},{1,17},{2,18},{3,19},{4,20},{5,21},{6,22},{7,23},{8,24},{9,... | collective-permute-start | bytes 2064392 | tf_op jit(solution)/shard_map/ppermute | solution.py:24
  121.8 3.2 %copy-start.7 = (bf16[64,5376]{1,0:T(8,128)(2,1)S(1)}, bf16[64,5376]{1,0:T(8,128)(2,1)}, u32[]{:S(2)}) copy-start(bf16[64,5376]{1,0:T(8,128)(2,1)} %copy-done.6) | copy-start | bytes 2064388
  122.2 11.1 %collective-permute-start.25 = (bf16[64,5376]{1,0:T(8,128)(2,1)S(1)}, bf16[64,5376]{1,0:T(8,128)(2,1)S(1)}, u32[]{:S(2)}, u32[]{:S(2)}) collective-permute-start(bf16[64,5376]{1,0:T(8,128)(2,1)S(1)} %constant_dynamic-update-slice_fusion.2), channel_id=1, source_target_pairs={{0,64},{1,65},{2,66},{3,67},{4,68},{5,69},{6,70},{7,71},{8,72},{9,... | collective-permute-start | bytes 2064392 | tf_op jit(solution)/shard_map/ppermute | solution.py:24
  125.0 2.2 %copy-start.5 = (bf16[1024,1792]{1,0:T(8,128)(2,1)S(1)}, bf16[1024,1792]{1,0:T(8,128)(2,1)}, u32[]{:S(2)}) copy-start(bf16[1024,1792]{1,0:T(8,128)(2,1)} %param.8) | copy-start | bytes 11010052
  126.4 4.0 %copy-start.8 = (bf16[256,1792]{1,0:T(8,128)(2,1)}, bf16[256,1792]{1,0:T(8,128)(2,1)S(1)}, u32[]{:S(2)}) copy-start(bf16[256,1792]{1,0:T(8,128)(2,1)S(1)} %get-tuple-element.59) | copy-start | bytes 2752516
  127.2 2.0 %copy-start.3 = (bf16[1792,1024]{1,0:T(8,128)(2,1)S(1)}, bf16[1792,1024]{1,0:T(8,128)(2,1)}, u32[]{:S(2)}) copy-start(bf16[1792,1024]{1,0:T(8,128)(2,1)} %param.10) | copy-start | bytes 11010052
  129.2 2.0 %copy-start.1 = (bf16[1024,1792]{1,0:T(8,128)(2,1)S(1)}, bf16[1024,1792]{1,0:T(8,128)(2,1)}, u32[]{:S(2)}) copy-start(bf16[1024,1792]{1,0:T(8,128)(2,1)} %param.9) | copy-start | bytes 11010052
  132.5 6.8 %collective-permute-start.22 = (bf16[128,2048]{1,0:T(8,128)(2,1)S(1)}, bf16[128,2048]{1,0:T(8,128)(2,1)S(1)}, u32[]{:S(2)}, u32[]{:S(2)}) collective-permute-start(bf16[128,2048]{1,0:T(8,128)(2,1)S(1)} %fusion.16), channel_id=1, source_target_pairs={{0,1},{1,0},{2,3},{3,2},{4,5},{5,4},{6,7},{7,6},{8,9},{9,8},{10,11... | collective-permute-start | bytes 1572872 | tf_op jit(solution)/shard_map/ppermute | solution.py:24
  135.6 2.3 %copy-start.16 = (bf16[256,1792]{1,0:T(8,128)(2,1)}, bf16[256,1792]{1,0:T(8,128)(2,1)S(1)}, u32[]{:S(2)}) copy-start(bf16[256,1792]{1,0:T(8,128)(2,1)S(1)} %get-tuple-element.60) | copy-start | bytes 2752516
  139.2 2.1 %collective-permute-start.27 = (bf16[144,2048]{1,0:T(8,128)(2,1)S(1)}, bf16[144,2048]{1,0:T(8,128)(2,1)S(1)}, u32[]{:S(2)}, u32[]{:S(2)}) collective-permute-start(bf16[144,2048]{1,0:T(8,128)(2,1)S(1)} %pad_maximum_fusion.5), channel_id=1, source_target_pairs={{0,1},{1,0},{2,3},{3,2},{4,5},{5,4},{6,7},{7,6},{8,9},{9,8},{10,11... | collective-permute-start | bytes 1769480 | tf_op jit(solution)/shard_map/ppermute | solution.py:24
  141.4 3.7 %copy-start.11 = (bf16[512,1024]{1,0:T(8,128)(2,1)S(1)}, bf16[512,1024]{1,0:T(8,128)(2,1)}, u32[]{:S(2)}) copy-start(bf16[512,1024]{1,0:T(8,128)(2,1)} %pad_maximum_fusion.3) | copy-start | bytes 3145732
  141.5 9.6 %collective-permute-start.29 = (bf16[64,2176]{1,0:T(8,128)(2,1)S(1)}, bf16[64,2176]{1,0:T(8,128)(2,1)S(1)}, u32[]{:S(2)}, u32[]{:S(2)}) collective-permute-start(bf16[64,2176]{1,0:T(8,128)(2,1)S(1)} %get-tuple-element.183), channel_id=1, source_target_pairs={{0,6},{1,7},{2,0},{3,1},{4,2},{5,3},{6,4},{7,5},{8,14},{9,15},{10,... | collective-permute-start | bytes 835592 | tf_op jit(solution)/shard_map/ppermute | solution.py:24
  142.3 15.7 %collective-permute-start.28 = (bf16[64,2176]{1,0:T(8,128)(2,1)S(1)}, bf16[64,2176]{1,0:T(8,128)(2,1)S(1)}, u32[]{:S(2)}, u32[]{:S(2)}) collective-permute-start(bf16[64,2176]{1,0:T(8,128)(2,1)S(1)} %get-tuple-element.184), channel_id=1, source_target_pairs={{0,2},{1,3},{2,4},{3,5},{4,6},{5,7},{6,0},{7,1},{8,10},{9,11},{10,... | collective-permute-start | bytes 835592 | tf_op jit(solution)/shard_map/ppermute | solution.py:24
  143.6 14.4 %collective-permute-start.30 = (bf16[64,2176]{1,0:T(8,128)(2,1)S(1)}, bf16[64,2176]{1,0:T(8,128)(2,1)S(1)}, u32[]{:S(2)}, u32[]{:S(2)}) collective-permute-start(bf16[64,2176]{1,0:T(8,128)(2,1)S(1)} %get-tuple-element.182), channel_id=1, source_target_pairs={{0,4},{1,5},{2,6},{3,7},{4,0},{5,1},{6,2},{7,3},{8,12},{9,13},{10,... | collective-permute-start | bytes 835592 | tf_op jit(solution)/shard_map/ppermute | solution.py:24
  158.2 7.6 %copy-start.10 = (bf16[512,1024]{1,0:T(8,128)(2,1)S(1)}, bf16[512,1024]{1,0:T(8,128)(2,1)}, u32[]{:S(2)}) copy-start(bf16[512,1024]{1,0:T(8,128)(2,1)} %pad_maximum_fusion.2) | copy-start | bytes 3145732
  158.2 7.6 %copy-start.15 = (bf16[256,1792]{1,0:T(8,128)(2,1)S(1)}, bf16[256,1792]{1,0:T(8,128)(2,1)}, u32[]{:S(2)}) copy-start(bf16[256,1792]{1,0:T(8,128)(2,1)} %copy-done.14) | copy-start | bytes 2752516
  159.3 15.5 %all-to-all-start.1 = ((bf16[16,4,2560]{2,1,0:T(4,128)(2,1)}), bf16[16,4,2560]{2,1,0:T(4,128)(2,1)S(1)}, u32[]{:S(2)}, u32[]{:S(2)}) async-start(bf16[16,4,2560]{2,1,0:T(4,128)(2,1)} %pad_maximum_fusion.9), calls=%async_computation.1 | async-start | bytes 655360 | tf_op jit(solution)/shard_map/all_to_all | solution.py:258
  165.8 4.0 %copy-start.9 = (bf16[256,1792]{1,0:T(8,128)(2,1)S(1)}, bf16[256,1792]{1,0:T(8,128)(2,1)}, u32[]{:S(2)}) copy-start(bf16[256,1792]{1,0:T(8,128)(2,1)} %copy-done.8) | copy-start | bytes 2752516
  165.9 4.0 %copy-start.17 = (bf16[256,1792]{1,0:T(8,128)(2,1)S(1)}, bf16[256,1792]{1,0:T(8,128)(2,1)}, u32[]{:S(2)}) copy-start(bf16[256,1792]{1,0:T(8,128)(2,1)} %copy-done.16) | copy-start | bytes 2752516
  (3 other events, 4.0 us)

commit v11 on v10

--- a/solution.py
+++ b/solution.py
@@ -73,8 +73,9 @@
 
 
 def sum_over_core(partial, gain_partial):
-    give = partial[128:].astype(BF16)
+    give = partial[128:]
     if gain_partial is not None:
+        give = give.astype(BF16)
         gain_rows = jnp.concatenate(parts_of(gain_partial, 2), axis=0)
         padded = jnp.pad(gain_rows, ((0, 0), (0, partial.shape[1] - 128)))
         give = jnp.concatenate([give, padded], axis=0)

time: 178 us -> 178 us (level)
  no operation moved by 1% of the time
where the time goes in v11:
time: 178 us
  waiting for transfers between devices  70.4 us (40%)
  starting transfers between devices  54.4 us (31%)
  matrix products  25.6 us (14%)
  local copies, waits for them, and re-layouts  17.3 us (10%)
  other arithmetic  8.44 us (5%)
    ppermute x31, waiting for transfers between devices, send(): return lax.ppermute(value, AXES, pairs)  60.5 us
    ppermute x31, starting transfers between devices, send(): return lax.ppermute(value, AXES, pairs)  40 us
    unnamed x57, local copies, waits for them, and re-layouts  12 us
    dot_general x3, matrix products, product_left_t(): lax.dot_general(left, right, (((0,), (0,)), ((), ())), preferred_element_...  11.9 us
    all_to_all x1, waiting for transfers between devices, per_device(): lax.all_to_all(message.reshape(16, 4, 2176), ('h', 'z', 'x'), split_axis=...  8.83 us
    all_to_all x1, starting transfers between devices, per_device(): lax.all_to_all(message.reshape(16, 4, 2176), ('h', 'z', 'x'), split_axis=...  7.96 us
    dot_general x6, matrix products, product_right_t(): lax.dot_general(left, right, (((1,), (1,)), ((), ())), preferred_element_...  6.94 us
    dot_general x6, matrix products, product(): return jnp.dot(left, right, preferred_element_type=F32)  6.75 us
  transfers between devices with their start and end apart: 33, of which 16 were waited for; matrix products, arithmetic and copies ran while one was open for 19% of the time, Pallas kernels for 0%

profile of v11, /device:TPU:0, one launch (start us, length us, event | category | flops | bytes accessed | tf_op | source)
XLA Modules:
  0.0 177.8 jit_solution(529976014227060235)
XLA Ops:
  4.0 8.0 %all-to-all-start = ((bf16[16,4,2176]{2,1,0:T(4,128)(2,1)}), bf16[16,4,2176]{2,1,0:T(4,128)(2,1)S(1)}, u32[]{:S(2)}, u32[]{:S(2)}) async-start(bf16[16,4,2176]{2,1,0:T(4,128)(2,1)} %bitcast.2), calls=%async_computation | async-start | bytes 557056 | tf_op jit(solution)/shard_map/all_to_all | solution.py:156
  12.0 8.8 %all-to-all-done = bf16[16,4,2176]{2,1,0:T(4,128)(2,1)S(1)} async-done(((bf16[16,4,2176]{2,1,0:T(4,128)(2,1)}), bf16[16,4,2176]{2,1,0:T(4,128)(2,1)S(1)}, u32[]{:S(2)}, u32[]{:S(2)}) %all-to-all-start) | async-done | bytes 278560 | tf_op jit(solution)/shard_map/all_to_all | solution.py:156
  21.0 1.6 collective-permute-start
  22.6 1.7 collective-permute-start.4
  24.3 2.0 %collective-permute-start.5 = (bf16[32,2176]{1,0:T(8,128)(2,1)S(1)}, bf16[32,2176]{1,0:T(8,128)(2,1)S(1)}, u32[]{:S(2)}, u32[]{:S(2)}) collective-permute-start(bf16[32,2176]{1,0:T(8,128)(2,1)S(1)} %get-tuple-element.65), channel_id=1, source_target_pairs={{0,4},{1,5},{2,6},{3,7},{4,0},{5,1},{6,2},{7,3},{8,12},{9,13},{10,... | collective-permute-start | bytes 417800 | tf_op jit(solution)/shard_map/ppermute | solution.py:24
  26.3 2.5 %collective-permute-done = bf16[32,2176]{1,0:T(8,128)(2,1)S(1)} collective-permute-done((bf16[32,2176]{1,0:T(8,128)(2,1)S(1)}, bf16[32,2176]{1,0:T(8,128)(2,1)S(1)}, u32[]{:S(2)}, u32[]{:S(2)}) %collective-permute-start) | collective-permute-done | bytes 139296 | tf_op jit(solution)/shard_map/ppermute | solution.py:24
  28.8 1.1 collective-permute-start.1
  30.8 1.4 collective-permute-start.3
  32.5 1.9 %collective-permute-done.1 = bf16[32,2176]{1,0:T(8,128)(2,1)S(1)} collective-permute-done((bf16[32,2176]{1,0:T(8,128)(2,1)S(1)}, bf16[32,2176]{1,0:T(8,128)(2,1)S(1)}, u32[]{:S(2)}, u32[]{:S(2)}) %collective-permute-start.1) | collective-permute-done | bytes 139296 | tf_op jit(solution)/shard_map/ppermute | solution.py:24
  34.4 2.2 %collective-permute-done.2 = bf16[32,2176]{1,0:T(8,128)(2,1)S(1)} collective-permute-done((bf16[32,2176]{1,0:T(8,128)(2,1)S(1)}, bf16[32,2176]{1,0:T(8,128)(2,1)S(1)}, u32[]{:S(2)}, u32[]{:S(2)}) %collective-permute-start.2) | collective-permute-done | bytes 139296 | tf_op jit(solution)/shard_map/ppermute | solution.py:24
  36.6 1.4 collective-permute-done.3
  38.1 1.2 convolution_convert_fusion.3
  39.7 1.6 copy-done
  41.3 1.1 convolution_convert_fusion.4
  43.3 1.1 convolution_convert_fusion.5
  45.7 1.3 collective-permute-start.8
  47.0 1.6 collective-permute-start.11
  48.9 1.2 fusion.64
  50.3 1.2 fusion.65
  51.4 1.1 fusion.66
  53.2 3.3 %collective-permute-start.15 = (bf16[32,5376]{1,0:T(8,128)(2,1)S(1)}, bf16[32,5376]{1,0:T(8,128)(2,1)S(1)}, u32[]{:S(2)}, u32[]{:S(2)}) collective-permute-start(bf16[32,5376]{1,0:T(8,128)(2,1)S(1)} %pad_maximum_fusion.8), channel_id=1, source_target_pairs={{0,48},{1,49},{2,50},{3,51},{4,52},{5,53},{6,54},{7,55},{8,56},{9,... | collective-permute-start | bytes 1032200 | tf_op jit(solution)/shard_map/ppermute | solution.py:24
  56.6 7.8 %collective-permute-done.11 = bf16[64,5376]{1,0:T(8,128)(2,1)S(1)} collective-permute-done((bf16[64,5376]{1,0:T(8,128)(2,1)S(1)}, bf16[64,5376]{1,0:T(8,128)(2,1)S(1)}, u32[]{:S(2)}, u32[]{:S(2)}) %collective-permute-start.11) | collective-permute-done | bytes 688160 | tf_op jit(solution)/shard_map/ppermute | solution.py:24
  66.8 2.9 %collective-permute-start.13 = (bf16[32,5376]{1,0:T(8,128)(2,1)S(1)}, bf16[32,5376]{1,0:T(8,128)(2,1)S(1)}, u32[]{:S(2)}, u32[]{:S(2)}) collective-permute-start(bf16[32,5376]{1,0:T(8,128)(2,1)S(1)} %get-tuple-element.89), channel_id=1, source_target_pairs={{0,48},{1,49},{2,50},{3,51},{4,52},{5,53},{6,54},{7,55},{8,56},{9,... | collective-permute-start | bytes 1032200 | tf_op jit(solution)/shard_map/ppermute | solution.py:24
  69.8 9.5 %collective-permute-done.12 = bf16[32,5376]{1,0:T(8,128)(2,1)S(1)} collective-permute-done((bf16[32,5376]{1,0:T(8,128)(2,1)S(1)}, bf16[32,5376]{1,0:T(8,128)(2,1)S(1)}, u32[]{:S(2)}, u32[]{:S(2)}) %collective-permute-start.12) | collective-permute-done | bytes 344096 | tf_op jit(solution)/shard_map/ppermute | solution.py:24
  79.5 3.2 %collective-permute-start.17 = (bf16[32,5376]{1,0:T(8,128)(2,1)S(1)}, bf16[32,5376]{1,0:T(8,128)(2,1)S(1)}, u32[]{:S(2)}, u32[]{:S(2)}) collective-permute-start(bf16[32,5376]{1,0:T(8,128)(2,1)S(1)} %fusion.19), channel_id=1, source_target_pairs={{0,48},{1,49},{2,50},{3,51},{4,52},{5,53},{6,54},{7,55},{8,56},{9,... | collective-permute-start | bytes 1032200 | tf_op jit(solution)/shard_map/ppermute | solution.py:24
  84.9 5.2 %collective-permute-done.16 = bf16[32,5376]{1,0:T(8,128)(2,1)S(1)} collective-permute-done((bf16[32,5376]{1,0:T(8,128)(2,1)S(1)}, bf16[32,5376]{1,0:T(8,128)(2,1)S(1)}, u32[]{:S(2)}, u32[]{:S(2)}) %collective-permute-start.16) | collective-permute-done | bytes 344096 | tf_op jit(solution)/shard_map/ppermute | solution.py:24
  90.7 3.2 %collective-permute-start.18 = (bf16[64,5376]{1,0:T(8,128)(2,1)S(1)}, bf16[64,5376]{1,0:T(8,128)(2,1)}, u32[]{:S(2)}, u32[]{:S(2)}) collective-permute-start(bf16[64,5376]{1,0:T(8,128)(2,1)S(1)} %pad_maximum_fusion.4), channel_id=1, source_target_pairs={{0,48},{1,49},{2,50},{3,51},{4,52},{5,53},{6,54},{7,55},{8,56},{9,... | collective-permute-start | bytes 2064392 | tf_op jit(solution)/shard_map/ppermute | solution.py:24
  94.0 1.3 collective-permute-start.23
  95.2 12.5 %collective-permute-done.19 = bf16[64,5376]{1,0:T(8,128)(2,1)S(1)} collective-permute-done((bf16[64,5376]{1,0:T(8,128)(2,1)S(1)}, bf16[64,5376]{1,0:T(8,128)(2,1)S(1)}, u32[]{:S(2)}, u32[]{:S(2)}) %collective-permute-start.19) | collective-permute-done | bytes 688160 | tf_op jit(solution)/shard_map/ppermute | solution.py:24
  110.4 3.3 %collective-permute-start.21 = (bf16[32,5376]{1,0:T(8,128)(2,1)S(1)}, bf16[32,5376]{1,0:T(8,128)(2,1)S(1)}, u32[]{:S(2)}, u32[]{:S(2)}) collective-permute-start(bf16[32,5376]{1,0:T(8,128)(2,1)S(1)} %slice.808), channel_id=1, source_target_pairs={{0,48},{1,49},{2,50},{3,51},{4,52},{5,53},{6,54},{7,55},{8,56},{9,... | collective-permute-start | bytes 1032200 | tf_op jit(solution)/shard_map/ppermute | solution.py:24
  113.9 1.8 collective-permute-start.26
  115.7 6.1 %collective-permute-done.20 = bf16[32,5376]{1,0:T(8,128)(2,1)S(1)} collective-permute-done((bf16[32,5376]{1,0:T(8,128)(2,1)}, bf16[32,5376]{1,0:T(8,128)(2,1)S(1)}, u32[]{:S(2)}, u32[]{:S(2)}) %collective-permute-start.20) | collective-permute-done | bytes 344096 | tf_op jit(solution)/shard_map/ppermute | solution.py:24
  122.2 1.7 collective-permute-start.25
  125.1 1.2 slice_dynamic-update-slice_fusion.26
  127.2 1.1 fusion.68
  131.3 1.2 multiply_reduce_fusion.1
  135.6 1.1 fusion.70
  136.7 1.2 multiply_reduce_fusion
  137.9 1.1 fusion.69
  139.5 1.7 collective-permute-done.27
  142.3 1.3 collective-permute-start.28
  143.6 1.5 collective-permute-start.30
  145.1 4.0 %convolution_convert_fusion.2 = bf16[1792,1024]{1,0:T(8,128)(2,1)} fusion(bf16[512,1024]{1,0:T(8,128)(2,1)S(1)} %copy-done.11, bf16[256,1792]{1,0:T(8,128)(2,1)S(1)} %get-tuple-element.53, bf16[256,1792]{1,0:T(8,128)(2,1)S(1)} %get-tuple-element.52), kind=kOutput, calls=%fused_computation.2 | convolution fusion | flops 1884553216 | bytes 6553600 | tf_op jit(solution)/shard_map/dot_general | solution.py:36
  149.1 2.0 %collective-permute-done.29 = bf16[64,2176]{1,0:T(8,128)(2,1)S(1)} collective-permute-done((bf16[64,2176]{1,0:T(8,128)(2,1)S(1)}, bf16[64,2176]{1,0:T(8,128)(2,1)S(1)}, u32[]{:S(2)}, u32[]{:S(2)}) %collective-permute-start.29) | collective-permute-done | bytes 278560 | tf_op jit(solution)/shard_map/ppermute | solution.py:24
  151.1 6.9 %collective-permute-done.28 = bf16[64,2176]{1,0:T(8,128)(2,1)S(1)} collective-permute-done((bf16[64,2176]{1,0:T(8,128)(2,1)S(1)}, bf16[64,2176]{1,0:T(8,128)(2,1)S(1)}, u32[]{:S(2)}, u32[]{:S(2)}) %collective-permute-start.28) | collective-permute-done | bytes 278560 | tf_op jit(solution)/shard_map/ppermute | solution.py:24
  159.4 6.4 %all-to-all-start.1 = ((bf16[16,4,2560]{2,1,0:T(4,128)(2,1)}), bf16[16,4,2560]{2,1,0:T(4,128)(2,1)S(1)}, u32[]{:S(2)}, u32[]{:S(2)}) async-start(bf16[16,4,2560]{2,1,0:T(4,128)(2,1)} %pad_maximum_fusion.9), calls=%async_computation.1 | async-start | bytes 655360 | tf_op jit(solution)/shard_map/all_to_all | solution.py:259
  165.9 4.0 %convolution_convert_fusion.1 = bf16[1024,1792]{1,0:T(8,128)(2,1)} fusion(bf16[512,1024]{1,0:T(8,128)(2,1)S(1)} %copy-done.10, bf16[256,1792]{1,0:T(8,128)(2,1)S(1)} %get-tuple-element.58, bf16[256,1792]{1,0:T(8,128)(2,1)S(1)} %copy-done.15), kind=kOutput, calls=%fused_computation.1 | convolution fusion | flops 1884553216 | bytes 6553600 | tf_op jit(solution)/shard_map/dot_general | solution.py:36
  169.8 4.0 %convolution_convert_fusion = bf16[1024,1792]{1,0:T(8,128)(2,1)} fusion(bf16[512,1024]{1,0:T(8,128)(2,1)S(1)} %copy-done.10, bf16[256,1792]{1,0:T(8,128)(2,1)S(1)} %copy-done.17, bf16[256,1792]{1,0:T(8,128)(2,1)S(1)} %copy-done.9), kind=kOutput, calls=%fused_computation | convolution fusion | flops 1884553216 | bytes 6553600 | tf_op jit(solution)/shard_map/dot_general | solution.py:36
  (186 shorter events, 31.8 us)
Async XLA Ops:
  3.2 21.1 %copy-start.13 = (f32[8192]{0:T(1024)S(1)}, f32[8192]{0:T(1024)}, u32[]{:S(2)}) copy-start(f32[8192]{0:T(1024)} %param.7) | copy-start | bytes 98308
  4.0 16.8 %all-to-all-start = ((bf16[16,4,2176]{2,1,0:T(4,128)(2,1)}), bf16[16,4,2176]{2,1,0:T(4,128)(2,1)S(1)}, u32[]{:S(2)}, u32[]{:S(2)}) async-start(bf16[16,4,2176]{2,1,0:T(4,128)(2,1)} %bitcast.2), calls=%async_computation | async-start | bytes 557056 | tf_op jit(solution)/shard_map/all_to_all | solution.py:156
  21.0 7.8 %collective-permute-start = (bf16[32,2176]{1,0:T(8,128)(2,1)S(1)}, bf16[32,2176]{1,0:T(8,128)(2,1)S(1)}, u32[]{:S(2)}, u32[]{:S(2)}) collective-permute-start(bf16[32,2176]{1,0:T(8,128)(2,1)S(1)} %get-tuple-element.65), channel_id=1, source_target_pairs={{0,2},{1,3},{2,4},{3,5},{4,6},{5,7},{6,0},{7,1},{8,10},{9,11},{10,... | collective-permute-start | bytes 417800 | tf_op jit(solution)/shard_map/ppermute | solution.py:24
  22.6 9.6 %collective-permute-start.4 = (bf16[32,2176]{1,0:T(8,128)(2,1)S(1)}, bf16[32,2176]{1,0:T(8,128)(2,1)S(1)}, u32[]{:S(2)}, u32[]{:S(2)}) collective-permute-start(bf16[32,2176]{1,0:T(8,128)(2,1)S(1)} %get-tuple-element.65), channel_id=1, source_target_pairs={{0,6},{1,7},{2,0},{3,1},{4,2},{5,3},{6,4},{7,5},{8,14},{9,15},{10,... | collective-permute-start | bytes 417800 | tf_op jit(solution)/shard_map/ppermute | solution.py:24
  24.3 7.9 %collective-permute-start.5 = (bf16[32,2176]{1,0:T(8,128)(2,1)S(1)}, bf16[32,2176]{1,0:T(8,128)(2,1)S(1)}, u32[]{:S(2)}, u32[]{:S(2)}) collective-permute-start(bf16[32,2176]{1,0:T(8,128)(2,1)S(1)} %get-tuple-element.65), channel_id=1, source_target_pairs={{0,4},{1,5},{2,6},{3,7},{4,0},{5,1},{6,2},{7,3},{8,12},{9,13},{10,... | collective-permute-start | bytes 417800 | tf_op jit(solution)/shard_map/ppermute | solution.py:24
  28.8 5.6 %collective-permute-start.1 = (bf16[32,2176]{1,0:T(8,128)(2,1)S(1)}, bf16[32,2176]{1,0:T(8,128)(2,1)S(1)}, u32[]{:S(2)}, u32[]{:S(2)}) collective-permute-start(bf16[32,2176]{1,0:T(8,128)(2,1)S(1)} %get-tuple-element.34), channel_id=1, source_target_pairs={{0,6},{1,7},{2,0},{3,1},{4,2},{5,3},{6,4},{7,5},{8,14},{9,15},{10,... | collective-permute-start | bytes 417800 | tf_op jit(solution)/shard_map/ppermute | solution.py:24
  29.9 6.7 %collective-permute-start.2 = (bf16[32,2176]{1,0:T(8,128)(2,1)S(1)}, bf16[32,2176]{1,0:T(8,128)(2,1)S(1)}, u32[]{:S(2)}, u32[]{:S(2)}) collective-permute-start(bf16[32,2176]{1,0:T(8,128)(2,1)S(1)} %get-tuple-element.34), channel_id=1, source_target_pairs={{0,4},{1,5},{2,6},{3,7},{4,0},{5,1},{6,2},{7,3},{8,12},{9,13},{10,... | collective-permute-start | bytes 417800 | tf_op jit(solution)/shard_map/ppermute | solution.py:24
  30.8 7.2 %collective-permute-start.3 = (bf16[32,2176]{1,0:T(8,128)(2,1)S(1)}, bf16[32,2176]{1,0:T(8,128)(2,1)S(1)}, u32[]{:S(2)}, u32[]{:S(2)}) collective-permute-start(bf16[32,2176]{1,0:T(8,128)(2,1)S(1)} %get-tuple-element.34), channel_id=1, source_target_pairs={{0,2},{1,3},{2,4},{3,5},{4,6},{5,7},{6,0},{7,1},{8,10},{9,11},{10,... | collective-permute-start | bytes 417800 | tf_op jit(solution)/shard_map/ppermute | solution.py:24
  32.2 5.8 %copy-start.4 = (bf16[1792,1024]{1,0:T(8,128)(2,1)S(1)}, bf16[1792,1024]{1,0:T(8,128)(2,1)}, u32[]{:S(2)}) copy-start(bf16[1792,1024]{1,0:T(8,128)(2,1)} %param.10) | copy-start | bytes 11010052
  32.3 5.7 %collective-permute-start.6 = (bf16[128,2176]{1,0:T(8,128)(2,1)S(1)}, bf16[128,2176]{1,0:T(8,128)(2,1)S(1)}, u32[]{:S(2)}, u32[]{:S(2)}) collective-permute-start(bf16[128,2176]{1,0:T(8,128)(2,1)S(1)} %constant_dynamic-update-slice_fusion.4), channel_id=1, source_target_pairs={{0,1},{1,0},{2,3},{3,2},{4,5},{5,4},{6,7},{7,6},{8,9},{9,8},{10,11... | collective-permute-start | bytes 1671176 | tf_op jit(solution)/shard_map/ppermute | solution.py:24
  39.2 2.0 %copy-start = (bf16[1024,1792]{1,0:T(8,128)(2,1)S(1)}, bf16[1024,1792]{1,0:T(8,128)(2,1)}, u32[]{:S(2)}) copy-start(bf16[1024,1792]{1,0:T(8,128)(2,1)} %param.9) | copy-start | bytes 11010052
  41.3 2.0 %copy-start.2 = (bf16[1024,1792]{1,0:T(8,128)(2,1)S(1)}, bf16[1024,1792]{1,0:T(8,128)(2,1)}, u32[]{:S(2)}) copy-start(bf16[1024,1792]{1,0:T(8,128)(2,1)} %param.8) | copy-start | bytes 11010052
  44.6 4.0 %collective-permute-start.7 = (bf16[128,2176]{1,0:T(8,128)(2,1)S(1)}, bf16[128,2176]{1,0:T(8,128)(2,1)S(1)}, u32[]{:S(2)}, u32[]{:S(2)}) collective-permute-start(bf16[128,2176]{1,0:T(8,128)(2,1)S(1)} %constant_dynamic-update-slice_fusion.8), channel_id=1, source_target_pairs={{0,1},{1,0},{2,3},{3,2},{4,5},{5,4},{6,7},{7,6},{8,9},{9,8},{10,11... | collective-permute-start | bytes 1671176 | tf_op jit(solution)/shard_map/ppermute | solution.py:24
  44.7 20.8 %collective-permute-start.9 = (bf16[64,5376]{1,0:T(8,128)(2,1)S(1)}, bf16[64,5376]{1,0:T(8,128)(2,1)S(1)}, u32[]{:S(2)}, u32[]{:S(2)}) collective-permute-start(bf16[64,5376]{1,0:T(8,128)(2,1)S(1)} %maximum_maximum_fusion.2), channel_id=1, source_target_pairs={{0,48},{1,49},{2,50},{3,51},{4,52},{5,53},{6,54},{7,55},{8,56},{9,... | collective-permute-start | bytes 2064392 | tf_op jit(solution)/shard_map/ppermute | solution.py:24
  45.7 19.8 %collective-permute-start.8 = (bf16[64,5376]{1,0:T(8,128)(2,1)S(1)}, bf16[64,5376]{1,0:T(8,128)(2,1)S(1)}, u32[]{:S(2)}, u32[]{:S(2)}) collective-permute-start(bf16[64,5376]{1,0:T(8,128)(2,1)S(1)} %maximum_maximum_fusion.1), channel_id=1, source_target_pairs={{0,16},{1,17},{2,18},{3,19},{4,20},{5,21},{6,22},{7,23},{8,24},{9,... | collective-permute-start | bytes 2064392 | tf_op jit(solution)/shard_map/ppermute | solution.py:24
  47.0 17.3 %collective-permute-start.11 = (bf16[64,5376]{1,0:T(8,128)(2,1)S(1)}, bf16[64,5376]{1,0:T(8,128)(2,1)S(1)}, u32[]{:S(2)}, u32[]{:S(2)}) collective-permute-start(bf16[64,5376]{1,0:T(8,128)(2,1)S(1)} %maximum_maximum_fusion.3), channel_id=1, source_target_pairs={{0,64},{1,65},{2,66},{3,67},{4,68},{5,69},{6,70},{7,71},{8,72},{9,... | collective-permute-start | bytes 2064392 | tf_op jit(solution)/shard_map/ppermute | solution.py:24
  52.9 26.5 %collective-permute-start.14 = (bf16[32,5376]{1,0:T(8,128)(2,1)S(1)}, bf16[32,5376]{1,0:T(8,128)(2,1)S(1)}, u32[]{:S(2)}, u32[]{:S(2)}) collective-permute-start(bf16[32,5376]{1,0:T(8,128)(2,1)S(1)} %pad_maximum_fusion.7), channel_id=1, source_target_pairs={{0,16},{1,17},{2,18},{3,19},{4,20},{5,21},{6,22},{7,23},{8,24},{9,... | collective-permute-start | bytes 1032200 | tf_op jit(solution)/shard_map/ppermute | solution.py:24
  53.2 26.2 %collective-permute-start.15 = (bf16[32,5376]{1,0:T(8,128)(2,1)S(1)}, bf16[32,5376]{1,0:T(8,128)(2,1)S(1)}, u32[]{:S(2)}, u32[]{:S(2)}) collective-permute-start(bf16[32,5376]{1,0:T(8,128)(2,1)S(1)} %pad_maximum_fusion.8), channel_id=1, source_target_pairs={{0,48},{1,49},{2,50},{3,51},{4,52},{5,53},{6,54},{7,55},{8,56},{9,... | collective-permute-start | bytes 1032200 | tf_op jit(solution)/shard_map/ppermute | solution.py:24
  64.6 14.7 %collective-permute-start.12 = (bf16[32,5376]{1,0:T(8,128)(2,1)S(1)}, bf16[32,5376]{1,0:T(8,128)(2,1)S(1)}, u32[]{:S(2)}, u32[]{:S(2)}) collective-permute-start(bf16[32,5376]{1,0:T(8,128)(2,1)S(1)} %get-tuple-element.90), channel_id=1, source_target_pairs={{0,16},{1,17},{2,18},{3,19},{4,20},{5,21},{6,22},{7,23},{8,24},{9,... | collective-permute-start | bytes 1032200 | tf_op jit(solution)/shard_map/ppermute | solution.py:24
  65.8 19.1 %collective-permute-start.10 = (bf16[64,5376]{1,0:T(8,128)(2,1)S(1)}, bf16[64,5376]{1,0:T(8,128)(2,1)S(1)}, u32[]{:S(2)}, u32[]{:S(2)}) collective-permute-start(bf16[64,5376]{1,0:T(8,128)(2,1)S(1)} %add_convert_fusion), channel_id=1, source_target_pairs={{0,64},{1,65},{2,66},{3,67},{4,68},{5,69},{6,70},{7,71},{8,72},{9,... | collective-permute-start | bytes 2064392 | tf_op jit(solution)/shard_map/ppermute | solution.py:24
  66.8 12.5 %collective-permute-start.13 = (bf16[32,5376]{1,0:T(8,128)(2,1)S(1)}, bf16[32,5376]{1,0:T(8,128)(2,1)S(1)}, u32[]{:S(2)}, u32[]{:S(2)}) collective-permute-start(bf16[32,5376]{1,0:T(8,128)(2,1)S(1)} %get-tuple-element.89), channel_id=1, source_target_pairs={{0,48},{1,49},{2,50},{3,51},{4,52},{5,53},{6,54},{7,55},{8,56},{9,... | collective-permute-start | bytes 1032200 | tf_op jit(solution)/shard_map/ppermute | solution.py:24
  79.4 10.6 %collective-permute-start.16 = (bf16[32,5376]{1,0:T(8,128)(2,1)S(1)}, bf16[32,5376]{1,0:T(8,128)(2,1)S(1)}, u32[]{:S(2)}, u32[]{:S(2)}) collective-permute-start(bf16[32,5376]{1,0:T(8,128)(2,1)S(1)} %fusion.18), channel_id=1, source_target_pairs={{0,16},{1,17},{2,18},{3,19},{4,20},{5,21},{6,22},{7,23},{8,24},{9,... | collective-permute-start | bytes 1032200 | tf_op jit(solution)/shard_map/ppermute | solution.py:24
  79.5 10.6 %collective-permute-start.17 = (bf16[32,5376]{1,0:T(8,128)(2,1)S(1)}, bf16[32,5376]{1,0:T(8,128)(2,1)S(1)}, u32[]{:S(2)}, u32[]{:S(2)}) collective-permute-start(bf16[32,5376]{1,0:T(8,128)(2,1)S(1)} %fusion.19), channel_id=1, source_target_pairs={{0,48},{1,49},{2,50},{3,51},{4,52},{5,53},{6,54},{7,55},{8,56},{9,... | collective-permute-start | bytes 1032200 | tf_op jit(solution)/shard_map/ppermute | solution.py:24
  90.7 17.1 %collective-permute-start.19 = (bf16[64,5376]{1,0:T(8,128)(2,1)S(1)}, bf16[64,5376]{1,0:T(8,128)(2,1)S(1)}, u32[]{:S(2)}, u32[]{:S(2)}) collective-permute-start(bf16[64,5376]{1,0:T(8,128)(2,1)S(1)} %pad_maximum_fusion.4), channel_id=1, source_target_pairs={{0,16},{1,17},{2,18},{3,19},{4,20},{5,21},{6,22},{7,23},{8,24},{9,... | collective-permute-start | bytes 2064392 | tf_op jit(solution)/shard_map/ppermute | solution.py:24
  90.7 18.6 %collective-permute-start.18 = (bf16[64,5376]{1,0:T(8,128)(2,1)S(1)}, bf16[64,5376]{1,0:T(8,128)(2,1)}, u32[]{:S(2)}, u32[]{:S(2)}) collective-permute-start(bf16[64,5376]{1,0:T(8,128)(2,1)S(1)} %pad_maximum_fusion.4), channel_id=1, source_target_pairs={{0,48},{1,49},{2,50},{3,51},{4,52},{5,53},{6,54},{7,55},{8,56},{9,... | collective-permute-start | bytes 2064392 | tf_op jit(solution)/shard_map/ppermute | solution.py:24
  94.0 19.7 %collective-permute-start.23 = (bf16[64,5376]{1,0:T(8,128)(2,1)S(1)}, bf16[64,5376]{1,0:T(8,128)(2,1)}, u32[]{:S(2)}, u32[]{:S(2)}) collective-permute-start(bf16[64,5376]{1,0:T(8,128)(2,1)S(1)} %pad_maximum_fusion.4), channel_id=1, source_target_pairs={{0,64},{1,65},{2,66},{3,67},{4,68},{5,69},{6,70},{7,71},{8,72},{9,... | collective-permute-start | bytes 2064392 | tf_op jit(solution)/shard_map/ppermute | solution.py:24
  109.4 12.4 %collective-permute-start.20 = (bf16[32,5376]{1,0:T(8,128)(2,1)}, bf16[32,5376]{1,0:T(8,128)(2,1)S(1)}, u32[]{:S(2)}, u32[]{:S(2)}) collective-permute-start(bf16[32,5376]{1,0:T(8,128)(2,1)} %slice.807), channel_id=1, source_target_pairs={{0,16},{1,17},{2,18},{3,19},{4,20},{5,21},{6,22},{7,23},{8,24},{9,... | collective-permute-start | bytes 1032200 | tf_op jit(solution)/shard_map/ppermute | solution.py:24
  110.4 11.8 %collective-permute-start.21 = (bf16[32,5376]{1,0:T(8,128)(2,1)S(1)}, bf16[32,5376]{1,0:T(8,128)(2,1)S(1)}, u32[]{:S(2)}, u32[]{:S(2)}) collective-permute-start(bf16[32,5376]{1,0:T(8,128)(2,1)S(1)} %slice.808), channel_id=1, source_target_pairs={{0,48},{1,49},{2,50},{3,51},{4,52},{5,53},{6,54},{7,55},{8,56},{9,... | collective-permute-start | bytes 1032200 | tf_op jit(solution)/shard_map/ppermute | solution.py:24
  113.7 19.6 %collective-permute-start.24 = (bf16[64,5376]{1,0:T(8,128)(2,1)}, bf16[64,5376]{1,0:T(8,128)(2,1)S(1)}, u32[]{:S(2)}, u32[]{:S(2)}) collective-permute-start(bf16[64,5376]{1,0:T(8,128)(2,1)} %collective-permute-done.23), channel_id=1, source_target_pairs={{0,48},{1,49},{2,50},{3,51},{4,52},{5,53},{6,54},{7,55},{8,56},{9,... | collective-permute-start | bytes 2064392 | tf_op jit(solution)/shard_map/ppermute | solution.py:24
  113.9 19.4 %collective-permute-start.26 = (bf16[64,5376]{1,0:T(8,128)(2,1)}, bf16[64,5376]{1,0:T(8,128)(2,1)S(1)}, u32[]{:S(2)}, u32[]{:S(2)}) collective-permute-start(bf16[64,5376]{1,0:T(8,128)(2,1)} %collective-permute-done.23), channel_id=1, source_target_pairs={{0,16},{1,17},{2,18},{3,19},{4,20},{5,21},{6,22},{7,23},{8,24},{9,... | collective-permute-start | bytes 2064392 | tf_op jit(solution)/shard_map/ppermute | solution.py:24
  121.8 3.2 %copy-start.7 = (bf16[64,5376]{1,0:T(8,128)(2,1)S(1)}, bf16[64,5376]{1,0:T(8,128)(2,1)}, u32[]{:S(2)}) copy-start(bf16[64,5376]{1,0:T(8,128)(2,1)} %copy-done.6) | copy-start | bytes 2064388
  122.2 11.1 %collective-permute-start.25 = (bf16[64,5376]{1,0:T(8,128)(2,1)S(1)}, bf16[64,5376]{1,0:T(8,128)(2,1)S(1)}, u32[]{:S(2)}, u32[]{:S(2)}) collective-permute-start(bf16[64,5376]{1,0:T(8,128)(2,1)S(1)} %constant_dynamic-update-slice_fusion.2), channel_id=1, source_target_pairs={{0,64},{1,65},{2,66},{3,67},{4,68},{5,69},{6,70},{7,71},{8,72},{9,... | collective-permute-start | bytes 2064392 | tf_op jit(solution)/shard_map/ppermute | solution.py:24
  125.0 2.2 %copy-start.3 = (bf16[1024,1792]{1,0:T(8,128)(2,1)S(1)}, bf16[1024,1792]{1,0:T(8,128)(2,1)}, u32[]{:S(2)}) copy-start(bf16[1024,1792]{1,0:T(8,128)(2,1)} %param.8) | copy-start | bytes 11010052
  126.4 2.0 %copy-start.14 = (bf16[256,1792]{1,0:T(8,128)(2,1)}, bf16[256,1792]{1,0:T(8,128)(2,1)S(1)}, u32[]{:S(2)}) copy-start(bf16[256,1792]{1,0:T(8,128)(2,1)S(1)} %get-tuple-element.57) | copy-start | bytes 2752516
  126.4 4.0 %copy-start.8 = (bf16[256,1792]{1,0:T(8,128)(2,1)}, bf16[256,1792]{1,0:T(8,128)(2,1)S(1)}, u32[]{:S(2)}) copy-start(bf16[256,1792]{1,0:T(8,128)(2,1)S(1)} %get-tuple-element.59) | copy-start | bytes 2752516
  127.2 2.0 %copy-start.5 = (bf16[1792,1024]{1,0:T(8,128)(2,1)S(1)}, bf16[1792,1024]{1,0:T(8,128)(2,1)}, u32[]{:S(2)}) copy-start(bf16[1792,1024]{1,0:T(8,128)(2,1)} %param.10) | copy-start | bytes 11010052
  129.2 2.0 %copy-start.1 = (bf16[1024,1792]{1,0:T(8,128)(2,1)S(1)}, bf16[1024,1792]{1,0:T(8,128)(2,1)}, u32[]{:S(2)}) copy-start(bf16[1024,1792]{1,0:T(8,128)(2,1)} %param.9) | copy-start | bytes 11010052
  132.5 6.8 %collective-permute-start.22 = (f32[128,2048]{1,0:T(8,128)S(1)}, f32[128,2048]{1,0:T(8,128)S(1)}, u32[]{:S(2)}, u32[]{:S(2)}) collective-permute-start(f32[128,2048]{1,0:T(8,128)S(1)} %pad_maximum_fusion.1), channel_id=1, source_target_pairs={{0,1},{1,0},{2,3},{3,2},{4,5},{5,4},{6,7},{7,6},{8,9},{9,8},{10,11... | collective-permute-start | bytes 3145736 | tf_op jit(solution)/shard_map/ppermute | solution.py:24
  139.2 2.1 %collective-permute-start.27 = (bf16[144,2048]{1,0:T(8,128)(2,1)S(1)}, bf16[144,2048]{1,0:T(8,128)(2,1)S(1)}, u32[]{:S(2)}, u32[]{:S(2)}) collective-permute-start(bf16[144,2048]{1,0:T(8,128)(2,1)S(1)} %pad_maximum_fusion.5), channel_id=1, source_target_pairs={{0,1},{1,0},{2,3},{3,2},{4,5},{5,4},{6,7},{7,6},{8,9},{9,8},{10,11... | collective-permute-start | bytes 1769480 | tf_op jit(solution)/shard_map/ppermute | solution.py:24
  141.4 3.7 %copy-start.11 = (bf16[512,1024]{1,0:T(8,128)(2,1)S(1)}, bf16[512,1024]{1,0:T(8,128)(2,1)}, u32[]{:S(2)}) copy-start(bf16[512,1024]{1,0:T(8,128)(2,1)} %pad_maximum_fusion.3) | copy-start | bytes 3145732
  141.6 9.6 %collective-permute-start.29 = (bf16[64,2176]{1,0:T(8,128)(2,1)S(1)}, bf16[64,2176]{1,0:T(8,128)(2,1)S(1)}, u32[]{:S(2)}, u32[]{:S(2)}) collective-permute-start(bf16[64,2176]{1,0:T(8,128)(2,1)S(1)} %get-tuple-element.183), channel_id=1, source_target_pairs={{0,6},{1,7},{2,0},{3,1},{4,2},{5,3},{6,4},{7,5},{8,14},{9,15},{10,... | collective-permute-start | bytes 835592 | tf_op jit(solution)/shard_map/ppermute | solution.py:24
  142.3 15.7 %collective-permute-start.28 = (bf16[64,2176]{1,0:T(8,128)(2,1)S(1)}, bf16[64,2176]{1,0:T(8,128)(2,1)S(1)}, u32[]{:S(2)}, u32[]{:S(2)}) collective-permute-start(bf16[64,2176]{1,0:T(8,128)(2,1)S(1)} %get-tuple-element.184), channel_id=1, source_target_pairs={{0,2},{1,3},{2,4},{3,5},{4,6},{5,7},{6,0},{7,1},{8,10},{9,11},{10,... | collective-permute-start | bytes 835592 | tf_op jit(solution)/shard_map/ppermute | solution.py:24
  143.6 14.4 %collective-permute-start.30 = (bf16[64,2176]{1,0:T(8,128)(2,1)S(1)}, bf16[64,2176]{1,0:T(8,128)(2,1)S(1)}, u32[]{:S(2)}, u32[]{:S(2)}) collective-permute-start(bf16[64,2176]{1,0:T(8,128)(2,1)S(1)} %get-tuple-element.182), channel_id=1, source_target_pairs={{0,4},{1,5},{2,6},{3,7},{4,0},{5,1},{6,2},{7,3},{8,12},{9,13},{10,... | collective-permute-start | bytes 835592 | tf_op jit(solution)/shard_map/ppermute | solution.py:24
  158.3 7.6 %copy-start.10 = (bf16[512,1024]{1,0:T(8,128)(2,1)S(1)}, bf16[512,1024]{1,0:T(8,128)(2,1)}, u32[]{:S(2)}) copy-start(bf16[512,1024]{1,0:T(8,128)(2,1)} %pad_maximum_fusion.2) | copy-start | bytes 3145732
  158.3 7.6 %copy-start.15 = (bf16[256,1792]{1,0:T(8,128)(2,1)S(1)}, bf16[256,1792]{1,0:T(8,128)(2,1)}, u32[]{:S(2)}) copy-start(bf16[256,1792]{1,0:T(8,128)(2,1)} %copy-done.14) | copy-start | bytes 2752516
  159.4 15.5 %all-to-all-start.1 = ((bf16[16,4,2560]{2,1,0:T(4,128)(2,1)}), bf16[16,4,2560]{2,1,0:T(4,128)(2,1)S(1)}, u32[]{:S(2)}, u32[]{:S(2)}) async-start(bf16[16,4,2560]{2,1,0:T(4,128)(2,1)} %pad_maximum_fusion.9), calls=%async_computation.1 | async-start | bytes 655360 | tf_op jit(solution)/shard_map/all_to_all | solution.py:259
  165.9 4.0 %copy-start.9 = (bf16[256,1792]{1,0:T(8,128)(2,1)S(1)}, bf16[256,1792]{1,0:T(8,128)(2,1)}, u32[]{:S(2)}) copy-start(bf16[256,1792]{1,0:T(8,128)(2,1)} %copy-done.8) | copy-start | bytes 2752516
  165.9 4.0 %copy-start.17 = (bf16[256,1792]{1,0:T(8,128)(2,1)S(1)}, bf16[256,1792]{1,0:T(8,128)(2,1)}, u32[]{:S(2)}) copy-start(bf16[256,1792]{1,0:T(8,128)(2,1)} %copy-done.16) | copy-start | bytes 2752516
  (3 other events, 3.2 us)
